TPU v7x, 32 devices: a whole 2x2x4 slice. The times are simulated.
32 devices in a mesh: section: 4 (over y, x), tm: 8 (over z, core).
Axes of the slice: x: 2, y: 2, z: 4, core: 2. Of those that a mesh axis runs over, the one named last changes fastest.
Arguments:
- signal: bfloat16 [4, 4096, 256], P(None, 'tm'), may hold values from -6 to 6
- skip_cot: bfloat16 [4, 4096, 256], P(None, 'tm'), may hold values from -6 to 6
- res_cot: bfloat16 [4, 4096, 256], P(None, 'tm'), may hold values from -6 to 6
- w_tap: bfloat16 [4, 256, 512], P('section'), may hold values from -0.25 to 0.25
- w_now: bfloat16 [4, 256, 512], P('section'), may hold values from -0.25 to 0.25
- w_res: bfloat16 [4, 256, 256], P('section'), may hold values from -0.375 to 0.375
- w_skip: bfloat16 [4, 256, 256], P('section'), may hold values from -0.375 to 0.375
Outputs:
- skip_total: bfloat16 [4, 4096, 256], P(None, 'tm')
- input_grads: bfloat16 [4, 4, 4096, 256], P('section', None, 'tm')
- grad_tap: float32 [4, 256, 512], P('section')
- grad_now: float32 [4, 256, 512], P('section')
- grad_res: float32 [4, 256, 256], P('section')
- grad_skip: float32 [4, 256, 256], P('section')
All inputs are finite; a program needn't handle non-finite values.
Results may differ from a plain program's by a relative error of at most 0.01.
Values may be sent and summed in bfloat16 or wider, within the bound.
No kernel may reach another device: no remote copies, remote signals or barrier semaphores. Data moves between devices by JAX's collectives and lax.ppermute only.
A program may use at most 64 MiB of HBM per device.

v0:
```python
import math

import jax
import jax.numpy as jnp
from jax import lax
from jax.sharding import PartitionSpec as P

SPAN = 4


def passed_along(x, axis, by):
    size = lax.axis_size(axis)
    pairs = [(i, i + by) for i in range(size) if 0 <= i + by < size]
    return lax.ppermute(x, axis, pairs)


def flat_dot(left, right):
    result = jnp.dot(left.reshape(-1, left.shape[-1]), right, preferred_element_type=jnp.float32)
    return result.reshape(left.shape[:-1] + (right.shape[-1],))


def rows_spanning(left, right):
    return lax.dot_general(
        left.reshape(-1, left.shape[-1]),
        right.reshape(-1, right.shape[-1]),
        (((0,), (0,)), ((), ())),
        preferred_element_type=jnp.float32,
    )


def tap_rows(values, chosen, delayed):
    result = jnp.zeros_like(values)
    for layer_number, selected in chosen:
        if delayed:
            arrived = passed_along(values, "tm", SPAN << layer_number)
        else:
            arrived = passed_along(values, "tm", -(SPAN << layer_number))
        result = jnp.where(selected, arrived, result)
    return result


def gate_parts(tapped, layer_in, weights):
    pre = flat_dot(tapped, weights[0]) + flat_dot(layer_in, weights[1])
    half_width = pre.shape[-1] // 2
    return (jnp.tanh(pre[..., :half_width]), jax.nn.sigmoid(pre[..., half_width:]))


def layer_forward(layer_in, weights, chosen):
    tapped = tap_rows(layer_in, chosen, True)
    tanh_part, sigmoid_part = gate_parts(tapped, layer_in, weights)
    gated = (tanh_part * sigmoid_part).astype(jnp.bfloat16)
    stream_out = (layer_in.astype(jnp.float32) + flat_dot(gated, weights[2])).astype(jnp.bfloat16)
    return (tapped, stream_out, flat_dot(gated, weights[3]))


def layer_backward(layer_in, tapped, grad_out, skip_grad, weights, chosen):
    tanh_part, sigmoid_part = gate_parts(tapped, layer_in, weights)
    gated = (tanh_part * sigmoid_part).astype(jnp.bfloat16)
    grad_gated = flat_dot(grad_out, weights[2].T) + flat_dot(skip_grad, weights[3].T)
    grad_pre = jnp.concatenate(
        [
            grad_gated * sigmoid_part * (1.0 - tanh_part * tanh_part),
            grad_gated * tanh_part * sigmoid_part * (1.0 - sigmoid_part),
        ],
        axis=-1,
    ).astype(jnp.bfloat16)
    terms = (
        rows_spanning(tapped, grad_pre),
        rows_spanning(layer_in, grad_pre),
        rows_spanning(gated, grad_out),
        rows_spanning(gated, skip_grad),
    )
    back_term = flat_dot(grad_pre, weights[0].T).astype(jnp.bfloat16)
    arrived = tap_rows(back_term, chosen, False)
    grad_in = (
        grad_out.astype(jnp.float32)
        + flat_dot(grad_pre, weights[1].T)
        + arrived.astype(jnp.float32)
    )
    return (grad_in.astype(jnp.bfloat16), terms)


def keep_slot(holding_rows, micro_index, in_range, value):
    former = lax.dynamic_slice_in_dim(holding_rows, micro_index, 1, 0)
    return lax.dynamic_update_slice_in_dim(
        holding_rows, jnp.where(in_range, value, former), micro_index, 0
    )


def run_layers(signal, skip_cot, res_cot, w_tap, w_now, w_res, w_skip, section_index, sections):
    number, seq_rows, channels = signal.shape
    weights = (w_tap[0], w_now[0], w_res[0], w_skip[0])
    total_steps = number + sections - 1
    saved_in = jnp.zeros((number, seq_rows, channels), jnp.bfloat16)
    saved_tap = jnp.zeros((number, seq_rows, channels), jnp.bfloat16)
    skip_running_sum = jnp.zeros((number, seq_rows, w_skip.shape[2]), jnp.float32)
    received = jnp.zeros((1, seq_rows, channels), jnp.bfloat16)
    for moment in range(total_steps):
        chosen = [
            (layer_number, section_index == layer_number)
            for layer_number in range(sections)
            if 0 <= moment - layer_number < number
        ]
        position = moment - section_index
        in_range = (position >= 0) & (position < number)
        micro_index = jnp.clip(position, 0, number - 1)
        incoming = signal[min(moment, number - 1)][None]
        layer_in = jnp.where(section_index == 0, incoming, received)
        tapped, stream_out, skip_term = layer_forward(layer_in, weights, chosen)
        saved_in = keep_slot(saved_in, micro_index, in_range, layer_in)
        saved_tap = keep_slot(saved_tap, micro_index, in_range, tapped)
        skip_running_sum = keep_slot(skip_running_sum, micro_index, in_range, skip_term)
        if moment + 1 < total_steps:
            received = passed_along(stream_out, "section", 1)
    skip_total = lax.psum(skip_running_sum, "section").astype(jnp.bfloat16)
    partial_sums = [
        jnp.zeros(weights[0].shape, jnp.float32),
        jnp.zeros(weights[1].shape, jnp.float32),
        jnp.zeros(weights[2].shape, jnp.float32),
        jnp.zeros(weights[3].shape, jnp.float32),
    ]
    input_grads = jnp.zeros((number, seq_rows, channels), jnp.bfloat16)
    received = jnp.zeros((1, seq_rows, channels), jnp.bfloat16)
    for moment in range(total_steps):
        chosen = [
            (layer_number, section_index == layer_number)
            for layer_number in range(sections)
            if 0 <= moment - (sections - 1 - layer_number) < number
        ]
        position = moment - (sections - 1 - section_index)
        in_range = (position >= 0) & (position < number)
        micro_index = jnp.clip(position, 0, number - 1)
        top_grad = lax.dynamic_slice_in_dim(res_cot, micro_index, 1, 0)
        grad_out = jnp.where(section_index == sections - 1, top_grad, received)
        layer_in = lax.dynamic_slice_in_dim(saved_in, micro_index, 1, 0)
        tapped = lax.dynamic_slice_in_dim(saved_tap, micro_index, 1, 0)
        skip_grad = lax.dynamic_slice_in_dim(skip_cot, micro_index, 1, 0)
        grad_in, terms = layer_backward(layer_in, tapped, grad_out, skip_grad, weights, chosen)
        factor = in_range.astype(jnp.float32)
        partial_sums = [partial_sums[spot] + factor * terms[spot] for spot in range(4)]
        input_grads = keep_slot(input_grads, micro_index, in_range, grad_in)
        if moment + 1 < total_steps:
            received = passed_along(grad_in, "section", -1)
    return (skip_total, input_grads, tuple((part[None] for part in partial_sums)))


def body(signal, skip_cot, res_cot, w_tap, w_now, w_res, w_skip):
    sections = lax.axis_size("section")
    shards = lax.axis_size("tm")
    section_index = lax.axis_index("section")
    number, seq_rows, channels = signal.shape
    skip_total, input_grads, partial_sums = run_layers(
        signal, skip_cot, res_cot, w_tap, w_now, w_res, w_skip, section_index, sections
    )
    summed = lax.psum((partial_sums[0], partial_sums[1], partial_sums[2], partial_sums[3]), "tm")
    grad_scale = 1.0 / math.sqrt(number * seq_rows * shards)
    return (
        skip_total,
        input_grads[None],
        summed[0] * grad_scale,
        summed[1] * grad_scale,
        summed[2] * grad_scale,
        summed[3] * grad_scale,
    )


def solution(mesh):
    in_specs = (
        P(None, "tm", None),
        P(None, "tm", None),
        P(None, "tm", None),
        P("section", None, None),
        P("section", None, None),
        P("section", None, None),
        P("section", None, None),
    )
    out_specs = (
        P(None, "tm", None),
        P("section", None, "tm", None),
        P("section", None, None),
        P("section", None, None),
        P("section", None, None),
        P("section", None, None),
    )
    return jax.shard_map(body, mesh=mesh, in_specs=in_specs, out_specs=out_specs, check_vma=False)
```

profile of v0, /device:TPU:0, one launch (start us, length us, event | category | flops | bytes accessed | tf_op | source)
XLA Modules:
  0.0 310.0 jit_solution(4123571970916382570)
XLA Ops:
  8.4 6.0 %collective-permute-start = (bf16[1,512,256]{2,1,0:T(8,128)(2,1)S(1)}, bf16[1,512,256]{2,1,0:T(8,128)(2,1)S(1)}, u32[]{:S(2)}, u32[]{:S(2)}) collective-permute-start(bf16[1,512,256]{2,1,0:T(8,128)(2,1)S(1)} %get-tuple-element.23), channel_id=1, source_target_pairs={{0,4},{1,5},{2,6},{3,7},{8,12},{9,13},{10,14},{11,15},{16,20},{17,... | collective-permute-start | bytes 786440 | tf_op jit(solution)/shard_map/ppermute | solution.py:14
  28.1 4.7 %collective-permute-done.1 = bf16[1,512,256]{2,1,0:T(8,128)(2,1)S(1)} collective-permute-done((bf16[1,512,256]{2,1,0:T(8,128)(2,1)S(1)}, bf16[1,512,256]{2,1,0:T(8,128)(2,1)S(1)}, u32[]{:S(2)}, u32[]{:S(2)}) %collective-permute-start.1) | collective-permute-done | bytes 262176 | tf_op jit(solution)/shard_map/ppermute | solution.py:14
  35.5 4.0 %collective-permute-done.3 = bf16[1,512,256]{2,1,0:T(8,128)(2,1)S(1)} collective-permute-done((bf16[1,512,256]{2,1,0:T(8,128)(2,1)S(1)}, bf16[1,512,256]{2,1,0:T(8,128)(2,1)S(1)}, u32[]{:S(2)}, u32[]{:S(2)}) %collective-permute-start.3) | collective-permute-done | bytes 262176 | tf_op jit(solution)/shard_map/ppermute | solution.py:14
  40.3 4.4 %collective-permute-start.4 = (bf16[1,512,256]{2,1,0:T(8,128)(2,1)S(1)}, bf16[1,512,256]{2,1,0:T(8,128)(2,1)S(1)}, u32[]{:S(2)}, u32[]{:S(2)}) collective-permute-start(bf16[1,512,256]{2,1,0:T(8,128)(2,1)S(1)} %add_convert_fusion.11), channel_id=1, source_target_pairs={{0,8},{8,16},{16,24},{1,9},{9,17},{17,25},{2,10},{10,18},{18,26},{... | collective-permute-start | bytes 786440 | tf_op jit(solution)/shard_map/ppermute | solution.py:14
  49.4 5.3 %collective-permute-start.6 = (bf16[1,512,256]{2,1,0:T(8,128)(2,1)S(1)}, bf16[1,512,256]{2,1,0:T(8,128)(2,1)S(1)}, u32[]{:S(2)}, u32[]{:S(2)}) collective-permute-start(bf16[1,512,256]{2,1,0:T(8,128)(2,1)S(1)} %get-tuple-element.19), channel_id=1, source_target_pairs={{0,4},{1,5},{2,6},{3,7},{8,12},{9,13},{10,14},{11,15},{16,20},{17,... | collective-permute-start | bytes 786440 | tf_op jit(solution)/shard_map/ppermute | solution.py:14
  59.3 4.4 %collective-permute-start.7 = (bf16[1,512,256]{2,1,0:T(8,128)(2,1)S(1)}, bf16[1,512,256]{2,1,0:T(8,128)(2,1)S(1)}, u32[]{:S(2)}, u32[]{:S(2)}) collective-permute-start(bf16[1,512,256]{2,1,0:T(8,128)(2,1)S(1)} %add_convert_fusion.10), channel_id=1, source_target_pairs={{0,8},{8,16},{16,24},{1,9},{9,17},{17,25},{2,10},{10,18},{18,26},{... | collective-permute-start | bytes 786440 | tf_op jit(solution)/shard_map/ppermute | solution.py:14
  68.3 5.3 %collective-permute-start.9 = (bf16[1,512,256]{2,1,0:T(8,128)(2,1)S(1)}, bf16[1,512,256]{2,1,0:T(8,128)(2,1)S(1)}, u32[]{:S(2)}, u32[]{:S(2)}) collective-permute-start(bf16[1,512,256]{2,1,0:T(8,128)(2,1)S(1)} %get-tuple-element.17), channel_id=1, source_target_pairs={{0,4},{1,5},{2,6},{3,7},{8,12},{9,13},{10,14},{11,15},{16,20},{17,... | collective-permute-start | bytes 786440 | tf_op jit(solution)/shard_map/ppermute | solution.py:14
  73.9 3.6 %collective-permute-done.9 = bf16[1,512,256]{2,1,0:T(8,128)(2,1)S(1)} collective-permute-done((bf16[1,512,256]{2,1,0:T(8,128)(2,1)S(1)}, bf16[1,512,256]{2,1,0:T(8,128)(2,1)S(1)}, u32[]{:S(2)}, u32[]{:S(2)}) %collective-permute-start.9) | collective-permute-done | bytes 262176 | tf_op jit(solution)/shard_map/ppermute | solution.py:14
  78.2 5.2 %collective-permute-start.10 = (bf16[1,512,256]{2,1,0:T(8,128)(2,1)S(1)}, bf16[1,512,256]{2,1,0:T(8,128)(2,1)S(1)}, u32[]{:S(2)}, u32[]{:S(2)}) collective-permute-start(bf16[1,512,256]{2,1,0:T(8,128)(2,1)S(1)} %add_convert_fusion.9), channel_id=1, source_target_pairs={{0,8},{8,16},{16,24},{1,9},{9,17},{17,25},{2,10},{10,18},{18,26},{... | collective-permute-start | bytes 786440 | tf_op jit(solution)/shard_map/ppermute | solution.py:14
  83.9 3.6 %collective-permute-done.10 = bf16[1,512,256]{2,1,0:T(8,128)(2,1)S(1)} collective-permute-done((bf16[1,512,256]{2,1,0:T(8,128)(2,1)S(1)}, bf16[1,512,256]{2,1,0:T(8,128)(2,1)S(1)}, u32[]{:S(2)}, u32[]{:S(2)}) %collective-permute-start.10) | collective-permute-done | bytes 262176 | tf_op jit(solution)/shard_map/ppermute | solution.py:14
  89.3 5.6 %collective-permute-start.12 = (bf16[1,512,256]{2,1,0:T(8,128)(2,1)S(1)}, bf16[1,512,256]{2,1,0:T(8,128)(2,1)S(1)}, u32[]{:S(2)}, u32[]{:S(2)}) collective-permute-start(bf16[1,512,256]{2,1,0:T(8,128)(2,1)S(1)} %add_convert_fusion.8), channel_id=1, source_target_pairs={{0,8},{8,16},{16,24},{1,9},{9,17},{17,25},{2,10},{10,18},{18,26},{... | collective-permute-start | bytes 786440 | tf_op jit(solution)/shard_map/ppermute | solution.py:14
  95.3 4.7 %collective-permute-done.12 = bf16[1,512,256]{2,1,0:T(8,128)(2,1)S(1)} collective-permute-done((bf16[1,512,256]{2,1,0:T(8,128)(2,1)S(1)}, bf16[1,512,256]{2,1,0:T(8,128)(2,1)S(1)}, u32[]{:S(2)}, u32[]{:S(2)}) %collective-permute-start.12) | collective-permute-done | bytes 262176 | tf_op jit(solution)/shard_map/ppermute | solution.py:14
  101.8 5.6 %collective-permute-start.14 = (bf16[1,512,256]{2,1,0:T(8,128)(2,1)S(1)}, bf16[1,512,256]{2,1,0:T(8,128)(2,1)S(1)}, u32[]{:S(2)}, u32[]{:S(2)}) collective-permute-start(bf16[1,512,256]{2,1,0:T(8,128)(2,1)S(1)} %add_convert_fusion.7), channel_id=1, source_target_pairs={{0,8},{8,16},{16,24},{1,9},{9,17},{17,25},{2,10},{10,18},{18,26},{... | collective-permute-start | bytes 786440 | tf_op jit(solution)/shard_map/ppermute | solution.py:14
  122.3 9.6 %collective-permute-done.17 = bf16[1,512,256]{2,1,0:T(8,128)(2,1)S(1)} collective-permute-done((bf16[1,512,256]{2,1,0:T(8,128)(2,1)S(1)}, bf16[1,512,256]{2,1,0:T(8,128)(2,1)S(1)}, u32[]{:S(2)}, u32[]{:S(2)}) %collective-permute-start.17) | collective-permute-done | bytes 262176 | tf_op jit(solution)/shard_map/ppermute | solution.py:14
  136.5 10.7 %collective-permute-done.19 = bf16[1,512,256]{2,1,0:T(8,128)(2,1)S(1)} collective-permute-done((bf16[1,512,256]{2,1,0:T(8,128)(2,1)S(1)}, bf16[1,512,256]{2,1,0:T(8,128)(2,1)S(1)}, u32[]{:S(2)}, u32[]{:S(2)}) %collective-permute-start.19) | collective-permute-done | bytes 262176 | tf_op jit(solution)/shard_map/ppermute | solution.py:14
  151.8 7.0 %collective-permute-done.21 = bf16[1,512,256]{2,1,0:T(8,128)(2,1)S(1)} collective-permute-done((bf16[1,512,256]{2,1,0:T(8,128)(2,1)S(1)}, bf16[1,512,256]{2,1,0:T(8,128)(2,1)S(1)}, u32[]{:S(2)}, u32[]{:S(2)}) %collective-permute-start.21) | collective-permute-done | bytes 262176 | tf_op jit(solution)/shard_map/ppermute | solution.py:14
  162.2 8.1 %collective-permute-done.23 = bf16[1,512,256]{2,1,0:T(8,128)(2,1)S(1)} collective-permute-done((bf16[1,512,256]{2,1,0:T(8,128)(2,1)S(1)}, bf16[1,512,256]{2,1,0:T(8,128)(2,1)S(1)}, u32[]{:S(2)}, u32[]{:S(2)}) %collective-permute-start.23) | collective-permute-done | bytes 262176 | tf_op jit(solution)/shard_map/ppermute | solution.py:14
  172.7 7.5 %collective-permute-done.24 = bf16[1,512,256]{2,1,0:T(8,128)(2,1)S(1)} collective-permute-done((bf16[1,512,256]{2,1,0:T(8,128)(2,1)S(1)}, bf16[1,512,256]{2,1,0:T(8,128)(2,1)S(1)}, u32[]{:S(2)}, u32[]{:S(2)}) %collective-permute-start.24) | collective-permute-done | bytes 262176 | tf_op jit(solution)/shard_map/ppermute | solution.py:14
  183.6 7.2 %collective-permute-done.26 = bf16[1,512,256]{2,1,0:T(8,128)(2,1)S(1)} collective-permute-done((bf16[1,512,256]{2,1,0:T(8,128)(2,1)S(1)}, bf16[1,512,256]{2,1,0:T(8,128)(2,1)S(1)}, u32[]{:S(2)}, u32[]{:S(2)}) %collective-permute-start.26) | collective-permute-done | bytes 262176 | tf_op jit(solution)/shard_map/ppermute | solution.py:14
  193.3 7.3 %collective-permute-done.27 = bf16[1,512,256]{2,1,0:T(8,128)(2,1)S(1)} collective-permute-done((bf16[1,512,256]{2,1,0:T(8,128)(2,1)S(1)}, bf16[1,512,256]{2,1,0:T(8,128)(2,1)S(1)}, u32[]{:S(2)}, u32[]{:S(2)}) %collective-permute-start.27) | collective-permute-done | bytes 262176 | tf_op jit(solution)/shard_map/ppermute | solution.py:14
  204.0 7.2 %collective-permute-done.29 = bf16[1,512,256]{2,1,0:T(8,128)(2,1)S(1)} collective-permute-done((bf16[1,512,256]{2,1,0:T(8,128)(2,1)S(1)}, bf16[1,512,256]{2,1,0:T(8,128)(2,1)S(1)}, u32[]{:S(2)}, u32[]{:S(2)}) %collective-permute-start.29) | collective-permute-done | bytes 262176 | tf_op jit(solution)/shard_map/ppermute | solution.py:14
  213.9 7.0 %collective-permute-done.30 = bf16[1,512,256]{2,1,0:T(8,128)(2,1)S(1)} collective-permute-done((bf16[1,512,256]{2,1,0:T(8,128)(2,1)S(1)}, bf16[1,512,256]{2,1,0:T(8,128)(2,1)S(1)}, u32[]{:S(2)}, u32[]{:S(2)}) %collective-permute-start.30) | collective-permute-done | bytes 262176 | tf_op jit(solution)/shard_map/ppermute | solution.py:14
  228.3 63.4 %all-reduce.5 = bf16[4,512,256]{2,1,0:T(8,128)(2,1)} all-reduce(f32[4,512,256]{2,1,0:T(8,128)} %copy-done.3), channel_id=1, replica_groups=mesh['section'=4,'tm'=8] {'section'}, use_global_device_ids=true, to_apply=%region_0.1 | all-reduce | flops 524288 | bytes 3145728 | tf_op jit(solution)/shard_map/psum | solution.py:115
  293.8 5.2 %all-reduce.4.cloned.1.call-done = (f32[1,256,512]{2,1,0:T(8,128)}, f32[1,256,512]{2,1,0:T(8,128)}, f32[1,256,256]{2,1,0:T(8,128)}, f32[1,256,256]{2,1,0:T(8,128)}) async-done(((f32[1,256,512]{2,1,0:T(8,128)}, f32[1,256,512]{2,1,0:T(8,128)}, f32[1,256,256]{2,1,0:T(8,128)}, f32[1,256,256]{2,1,0:T(8,128)}), (f32[1,256,512]{2,1,0:T(8,128)}, f32[1,256,512]{2,1,0:T(8,128)}, f32[1,256,256]{2,1,0:T(8,128)}, ...) | async-done | bytes 1572880 | tf_op jit(solution)/shard_map/psum | solution.py:155
  (210 shorter events, 92.1 us)
Async XLA Ops:
  7.2 291.8 %all-reduce.4.cloned.1.call-start = ((), (), s32[]{:S(2)}) async-start(), calls=%async_computation | async-start | bytes 3145728 | tf_op jit(solution)/shard_map/psum | solution.py:155
  8.4 14.8 %collective-permute-start = (bf16[1,512,256]{2,1,0:T(8,128)(2,1)S(1)}, bf16[1,512,256]{2,1,0:T(8,128)(2,1)S(1)}, u32[]{:S(2)}, u32[]{:S(2)}) collective-permute-start(bf16[1,512,256]{2,1,0:T(8,128)(2,1)S(1)} %get-tuple-element.23), channel_id=1, source_target_pairs={{0,4},{1,5},{2,6},{3,7},{8,12},{9,13},{10,14},{11,15},{16,20},{17,... | collective-permute-start | bytes 786440 | tf_op jit(solution)/shard_map/ppermute | solution.py:14
  24.0 8.8 %collective-permute-start.1 = (bf16[1,512,256]{2,1,0:T(8,128)(2,1)S(1)}, bf16[1,512,256]{2,1,0:T(8,128)(2,1)S(1)}, u32[]{:S(2)}, u32[]{:S(2)}) collective-permute-start(bf16[1,512,256]{2,1,0:T(8,128)(2,1)S(1)} %fusion.39), channel_id=1, source_target_pairs={{0,8},{8,16},{16,24},{1,9},{9,17},{17,25},{2,10},{10,18},{18,26},{... | collective-permute-start | bytes 786440 | tf_op jit(solution)/shard_map/ppermute | solution.py:14
  33.6 5.9 %collective-permute-start.3 = (bf16[1,512,256]{2,1,0:T(8,128)(2,1)S(1)}, bf16[1,512,256]{2,1,0:T(8,128)(2,1)S(1)}, u32[]{:S(2)}, u32[]{:S(2)}) collective-permute-start(bf16[1,512,256]{2,1,0:T(8,128)(2,1)S(1)} %get-tuple-element.21), channel_id=1, source_target_pairs={{0,4},{1,5},{2,6},{3,7},{8,12},{9,13},{10,14},{11,15},{16,20},{17,... | collective-permute-start | bytes 786440 | tf_op jit(solution)/shard_map/ppermute | solution.py:14
  40.3 8.3 %collective-permute-start.4 = (bf16[1,512,256]{2,1,0:T(8,128)(2,1)S(1)}, bf16[1,512,256]{2,1,0:T(8,128)(2,1)S(1)}, u32[]{:S(2)}, u32[]{:S(2)}) collective-permute-start(bf16[1,512,256]{2,1,0:T(8,128)(2,1)S(1)} %add_convert_fusion.11), channel_id=1, source_target_pairs={{0,8},{8,16},{16,24},{1,9},{9,17},{17,25},{2,10},{10,18},{18,26},{... | collective-permute-start | bytes 786440 | tf_op jit(solution)/shard_map/ppermute | solution.py:14
  48.7 6.3 %collective-permute-start.5 = (bf16[1,512,256]{2,1,0:T(8,128)(2,1)S(1)}, bf16[1,512,256]{2,1,0:T(8,128)(2,1)S(1)}, u32[]{:S(2)}, u32[]{:S(2)}) collective-permute-start(bf16[1,512,256]{2,1,0:T(8,128)(2,1)S(1)} %get-tuple-element.19), channel_id=1, source_target_pairs={} | collective-permute-start | bytes 786440 | tf_op jit(solution)/shard_map/ppermute | solution.py:14
  49.4 9.2 %collective-permute-start.6 = (bf16[1,512,256]{2,1,0:T(8,128)(2,1)S(1)}, bf16[1,512,256]{2,1,0:T(8,128)(2,1)S(1)}, u32[]{:S(2)}, u32[]{:S(2)}) collective-permute-start(bf16[1,512,256]{2,1,0:T(8,128)(2,1)S(1)} %get-tuple-element.19), channel_id=1, source_target_pairs={{0,4},{1,5},{2,6},{3,7},{8,12},{9,13},{10,14},{11,15},{16,20},{17,... | collective-permute-start | bytes 786440 | tf_op jit(solution)/shard_map/ppermute | solution.py:14
  59.3 8.3 %collective-permute-start.7 = (bf16[1,512,256]{2,1,0:T(8,128)(2,1)S(1)}, bf16[1,512,256]{2,1,0:T(8,128)(2,1)S(1)}, u32[]{:S(2)}, u32[]{:S(2)}) collective-permute-start(bf16[1,512,256]{2,1,0:T(8,128)(2,1)S(1)} %add_convert_fusion.10), channel_id=1, source_target_pairs={{0,8},{8,16},{16,24},{1,9},{9,17},{17,25},{2,10},{10,18},{18,26},{... | collective-permute-start | bytes 786440 | tf_op jit(solution)/shard_map/ppermute | solution.py:14
  67.6 6.3 %collective-permute-start.8 = (bf16[1,512,256]{2,1,0:T(8,128)(2,1)S(1)}, bf16[1,512,256]{2,1,0:T(8,128)(2,1)S(1)}, u32[]{:S(2)}, u32[]{:S(2)}) collective-permute-start(bf16[1,512,256]{2,1,0:T(8,128)(2,1)S(1)} %get-tuple-element.17), channel_id=1, source_target_pairs={} | collective-permute-start | bytes 786440 | tf_op jit(solution)/shard_map/ppermute | solution.py:14
  68.3 9.2 %collective-permute-start.9 = (bf16[1,512,256]{2,1,0:T(8,128)(2,1)S(1)}, bf16[1,512,256]{2,1,0:T(8,128)(2,1)S(1)}, u32[]{:S(2)}, u32[]{:S(2)}) collective-permute-start(bf16[1,512,256]{2,1,0:T(8,128)(2,1)S(1)} %get-tuple-element.17), channel_id=1, source_target_pairs={{0,4},{1,5},{2,6},{3,7},{8,12},{9,13},{10,14},{11,15},{16,20},{17,... | collective-permute-start | bytes 786440 | tf_op jit(solution)/shard_map/ppermute | solution.py:14
  78.2 9.2 %collective-permute-start.10 = (bf16[1,512,256]{2,1,0:T(8,128)(2,1)S(1)}, bf16[1,512,256]{2,1,0:T(8,128)(2,1)S(1)}, u32[]{:S(2)}, u32[]{:S(2)}) collective-permute-start(bf16[1,512,256]{2,1,0:T(8,128)(2,1)S(1)} %add_convert_fusion.9), channel_id=1, source_target_pairs={{0,8},{8,16},{16,24},{1,9},{9,17},{17,25},{2,10},{10,18},{18,26},{... | collective-permute-start | bytes 786440 | tf_op jit(solution)/shard_map/ppermute | solution.py:14
  89.3 10.7 %collective-permute-start.12 = (bf16[1,512,256]{2,1,0:T(8,128)(2,1)S(1)}, bf16[1,512,256]{2,1,0:T(8,128)(2,1)S(1)}, u32[]{:S(2)}, u32[]{:S(2)}) collective-permute-start(bf16[1,512,256]{2,1,0:T(8,128)(2,1)S(1)} %add_convert_fusion.8), channel_id=1, source_target_pairs={{0,8},{8,16},{16,24},{1,9},{9,17},{17,25},{2,10},{10,18},{18,26},{... | collective-permute-start | bytes 786440 | tf_op jit(solution)/shard_map/ppermute | solution.py:14
  101.8 9.5 %collective-permute-start.14 = (bf16[1,512,256]{2,1,0:T(8,128)(2,1)S(1)}, bf16[1,512,256]{2,1,0:T(8,128)(2,1)S(1)}, u32[]{:S(2)}, u32[]{:S(2)}) collective-permute-start(bf16[1,512,256]{2,1,0:T(8,128)(2,1)S(1)} %add_convert_fusion.7), channel_id=1, source_target_pairs={{0,8},{8,16},{16,24},{1,9},{9,17},{17,25},{2,10},{10,18},{18,26},{... | collective-permute-start | bytes 786440 | tf_op jit(solution)/shard_map/ppermute | solution.py:14
  116.0 3.9 %collective-permute-start.16 = (bf16[1,512,256]{2,1,0:T(8,128)(2,1)S(1)}, bf16[1,512,256]{2,1,0:T(8,128)(2,1)S(1)}, u32[]{:S(2)}, u32[]{:S(2)}) collective-permute-start(bf16[1,512,256]{2,1,0:T(8,128)(2,1)S(1)} %fusion.52), channel_id=1, source_target_pairs={} | collective-permute-start | bytes 786440 | tf_op jit(solution)/shard_map/ppermute | solution.py:14
  120.3 11.6 %collective-permute-start.17 = (bf16[1,512,256]{2,1,0:T(8,128)(2,1)S(1)}, bf16[1,512,256]{2,1,0:T(8,128)(2,1)S(1)}, u32[]{:S(2)}, u32[]{:S(2)}) collective-permute-start(bf16[1,512,256]{2,1,0:T(8,128)(2,1)S(1)} %get-tuple-element.46), channel_id=1, source_target_pairs={{8,0},{16,8},{24,16},{9,1},{17,9},{25,17},{10,2},{18,10},{26,18},{... | collective-permute-start | bytes 786440 | tf_op jit(solution)/shard_map/ppermute | solution.py:14
  134.5 12.7 %collective-permute-start.19 = (bf16[1,512,256]{2,1,0:T(8,128)(2,1)S(1)}, bf16[1,512,256]{2,1,0:T(8,128)(2,1)S(1)}, u32[]{:S(2)}, u32[]{:S(2)}) collective-permute-start(bf16[1,512,256]{2,1,0:T(8,128)(2,1)S(1)} %get-tuple-element.48), channel_id=1, source_target_pairs={{8,0},{16,8},{24,16},{9,1},{17,9},{25,17},{10,2},{18,10},{26,18},{... | collective-permute-start | bytes 786440 | tf_op jit(solution)/shard_map/ppermute | solution.py:14
  149.7 9.0 %collective-permute-start.21 = (bf16[1,512,256]{2,1,0:T(8,128)(2,1)S(1)}, bf16[1,512,256]{2,1,0:T(8,128)(2,1)S(1)}, u32[]{:S(2)}, u32[]{:S(2)}) collective-permute-start(bf16[1,512,256]{2,1,0:T(8,128)(2,1)S(1)} %get-tuple-element.50), channel_id=1, source_target_pairs={{8,0},{16,8},{24,16},{9,1},{17,9},{25,17},{10,2},{18,10},{26,18},{... | collective-permute-start | bytes 786440 | tf_op jit(solution)/shard_map/ppermute | solution.py:14
  160.2 10.0 %collective-permute-start.23 = (bf16[1,512,256]{2,1,0:T(8,128)(2,1)S(1)}, bf16[1,512,256]{2,1,0:T(8,128)(2,1)S(1)}, u32[]{:S(2)}, u32[]{:S(2)}) collective-permute-start(bf16[1,512,256]{2,1,0:T(8,128)(2,1)S(1)} %fusion.55), channel_id=1, source_target_pairs={{4,0},{5,1},{6,2},{7,3},{12,8},{13,9},{14,10},{15,11},{20,16},{21,... | collective-permute-start | bytes 786440 | tf_op jit(solution)/shard_map/ppermute | solution.py:14
  170.6 9.6 %collective-permute-start.24 = (bf16[1,512,256]{2,1,0:T(8,128)(2,1)S(1)}, bf16[1,512,256]{2,1,0:T(8,128)(2,1)S(1)}, u32[]{:S(2)}, u32[]{:S(2)}) collective-permute-start(bf16[1,512,256]{2,1,0:T(8,128)(2,1)S(1)} %get-tuple-element.52), channel_id=1, source_target_pairs={{8,0},{16,8},{24,16},{9,1},{17,9},{25,17},{10,2},{18,10},{26,18},{... | collective-permute-start | bytes 786440 | tf_op jit(solution)/shard_map/ppermute | solution.py:14
  181.7 9.2 %collective-permute-start.26 = (bf16[1,512,256]{2,1,0:T(8,128)(2,1)S(1)}, bf16[1,512,256]{2,1,0:T(8,128)(2,1)S(1)}, u32[]{:S(2)}, u32[]{:S(2)}) collective-permute-start(bf16[1,512,256]{2,1,0:T(8,128)(2,1)S(1)} %fusion.56), channel_id=1, source_target_pairs={{4,0},{5,1},{6,2},{7,3},{12,8},{13,9},{14,10},{15,11},{20,16},{21,... | collective-permute-start | bytes 786440 | tf_op jit(solution)/shard_map/ppermute | solution.py:14
  191.3 9.3 %collective-permute-start.27 = (bf16[1,512,256]{2,1,0:T(8,128)(2,1)S(1)}, bf16[1,512,256]{2,1,0:T(8,128)(2,1)S(1)}, u32[]{:S(2)}, u32[]{:S(2)}) collective-permute-start(bf16[1,512,256]{2,1,0:T(8,128)(2,1)S(1)} %get-tuple-element.54), channel_id=1, source_target_pairs={{8,0},{16,8},{24,16},{9,1},{17,9},{25,17},{10,2},{18,10},{26,18},{... | collective-permute-start | bytes 786440 | tf_op jit(solution)/shard_map/ppermute | solution.py:14
  202.1 9.2 %collective-permute-start.29 = (bf16[1,512,256]{2,1,0:T(8,128)(2,1)S(1)}, bf16[1,512,256]{2,1,0:T(8,128)(2,1)S(1)}, u32[]{:S(2)}, u32[]{:S(2)}) collective-permute-start(bf16[1,512,256]{2,1,0:T(8,128)(2,1)S(1)} %fusion.57), channel_id=1, source_target_pairs={{4,0},{5,1},{6,2},{7,3},{12,8},{13,9},{14,10},{15,11},{20,16},{21,... | collective-permute-start | bytes 786440 | tf_op jit(solution)/shard_map/ppermute | solution.py:14
  211.7 9.3 %collective-permute-start.30 = (bf16[1,512,256]{2,1,0:T(8,128)(2,1)S(1)}, bf16[1,512,256]{2,1,0:T(8,128)(2,1)S(1)}, u32[]{:S(2)}, u32[]{:S(2)}) collective-permute-start(bf16[1,512,256]{2,1,0:T(8,128)(2,1)S(1)} %get-tuple-element.56), channel_id=1, source_target_pairs={{8,0},{16,8},{24,16},{9,1},{17,9},{25,17},{10,2},{18,10},{26,18},{... | collective-permute-start | bytes 786440 | tf_op jit(solution)/shard_map/ppermute | solution.py:14
  226.0 66.7 %collective-permute-start.31 = (bf16[1,512,256]{2,1,0:T(8,128)(2,1)}, bf16[1,512,256]{2,1,0:T(8,128)(2,1)S(1)}, u32[]{:S(2)}, u32[]{:S(2)}) collective-permute-start(bf16[1,512,256]{2,1,0:T(8,128)(2,1)} %fusion.58), channel_id=1, source_target_pairs={{4,0},{5,1},{6,2},{7,3},{12,8},{13,9},{14,10},{15,11},{20,16},{21,... | collective-permute-start | bytes 786440 | tf_op jit(solution)/shard_map/ppermute | solution.py:14
  (27 other events, 267.6 us)
Sparse Core Ops, SparseCore 0:
  228.5 70.5 all-reduce.3
where the time goes:
time: 311 us; the launch traced here: 310 us
  waiting for transfers between devices  111 us (36%)
  starting transfers between devices  68.9 us (22%)
  blocking collectives  63.4 us (20%)
  matrix products  40.6 us (13%)
  between operations  15.4 us (5%)
  other arithmetic  8.19 us (3%)
    ppermute x32, waiting for transfers between devices, passed_along(): return lax.ppermute(x, axis, pairs)  106 us
    ppermute x32, starting transfers between devices, passed_along(): return lax.ppermute(x, axis, pairs)  68.9 us
    psum x1, blocking collectives, run_layers(): skip_total = lax.psum(skip_running_sum, 'section').astype(jnp.bfloat16)  63.4 us
    dot_general x69, matrix products, flat_dot(): jnp.dot(left.reshape(-1, left.shape[-1]), right, preferred_element_type=j...  29.2 us
    dot_general x28, matrix products, rows_spanning(): lax.dot_general(left.reshape(-1, left.shape[-1]), right.reshape(-1, right...  11.4 us
  transfers between devices with their start and end apart: 33, of which 19 were waited for; matrix products, arithmetic and copies ran while one was open for 8% of the time, Pallas kernels for 0%

commit v1 on v0

--- a/solution.py
+++ b/solution.py
@@ -1,8 +1,11 @@
+import functools
 import math
 
 import jax
 import jax.numpy as jnp
 from jax import lax
+from jax.experimental import pallas as pl
+from jax.experimental.pallas import tpu as pltpu
 from jax.sharding import PartitionSpec as P
 
 SPAN = 4
@@ -144,7 +147,7 @@
     return (skip_total, input_grads, tuple((part[None] for part in partial_sums)))
 
 
-def body(signal, skip_cot, res_cot, w_tap, w_now, w_res, w_skip):
+def pipelined_body(signal, skip_cot, res_cot, w_tap, w_now, w_res, w_skip):
     sections = lax.axis_size("section")
     shards = lax.axis_size("tm")
     section_index = lax.axis_index("section")
@@ -164,6 +167,199 @@
     )
 
 
+def narrow_dot(left, right):
+    return lax.dot_general(left, right, (((1,), (0,)), ((), ())), preferred_element_type=jnp.float32)
+
+
+def rows_dot(left, right):
+    return lax.dot_general(left, right, (((0,), (0,)), ((), ())), preferred_element_type=jnp.float32)
+
+
+def stack_kernel(
+    layers, section_ref, signal, tapped, skip_cot, res_cot, weights,
+    skip_out, grad_out, back_out, sums,
+    turned, h_all, gated_all, dz_all, g_all, tanh_all, sig_all,
+):
+    section = section_ref[0]
+    seqs, seq_rows, channels = signal.shape
+    half = channels
+    now = slice(0, 2 * half)
+    res = slice(2 * half, 2 * half + channels)
+    skip = slice(2 * half + channels, 2 * half + 2 * channels)
+    tap = slice(2 * half + 2 * channels, 4 * half + 2 * channels)
+    first_slot = section
+
+    @pl.when(pl.program_id(0) == 0)
+    def _():
+        sums[...] = jnp.zeros(sums.shape, jnp.float32)
+        for k in range(layers):
+            turned[k] = weights[jnp.bitwise_xor(k, section), :, : 4 * half].T
+        turned[layers, : 2 * half] = weights[first_slot, :, tap].T
+
+    places = [slice(i * seq_rows, (i + 1) * seq_rows) for i in range(seqs)]
+    odd = jnp.bitwise_and(section, seqs - 1)
+    tap_at = [jnp.bitwise_xor(i, odd) for i in range(seqs)]
+    for i, rows in enumerate(places):
+        h_all[0, rows] = signal[i]
+        g_all[layers, rows] = res_cot[i]
+    for k in range(layers):
+        slot = jnp.bitwise_xor(k, section)
+        for i, rows in enumerate(places):
+            pre = narrow_dot(h_all[k, rows], weights[slot, :, now])
+            if k == 0:
+                pre = pre + narrow_dot(tapped[tap_at[i]], weights[first_slot, :, tap])
+            tanh_part = jnp.tanh(pre[:, :half])
+            sig_part = 0.5 * jnp.tanh(0.5 * pre[:, half:]) + 0.5
+            tanh_all[k, rows] = tanh_part
+            sig_all[k, rows] = sig_part
+            gated_all[k, rows] = (tanh_part * sig_part).astype(jnp.bfloat16)
+        if k + 1 < layers:
+            for rows in places:
+                stream = narrow_dot(gated_all[k, rows], weights[slot, :, res])
+                h_all[k + 1, rows] = (h_all[k, rows].astype(jnp.float32) + stream).astype(jnp.bfloat16)
+    for i, rows in enumerate(places):
+        total = narrow_dot(gated_all[0, rows], weights[first_slot, :, skip])
+        for k in range(1, layers):
+            total = total + narrow_dot(gated_all[k, rows], weights[jnp.bitwise_xor(k, section), :, skip])
+        skip_out[i] = total.astype(jnp.bfloat16)
+    for k in reversed(range(layers)):
+        for i, rows in enumerate(places):
+            du = narrow_dot(g_all[k + 1, rows], turned[k, res]) + narrow_dot(skip_cot[i], turned[k, skip])
+            tanh_part = tanh_all[k, rows]
+            sig_part = sig_all[k, rows]
+            scaled = du * sig_part
+            dz_all[k, rows, :half] = (scaled * (1.0 - tanh_part * tanh_part)).astype(jnp.bfloat16)
+            dz_all[k, rows, half:] = (scaled * (tanh_part * (1.0 - sig_part))).astype(jnp.bfloat16)
+        for i, rows in enumerate(places):
+            if k == 0:
+                back_out[i] = narrow_dot(dz_all[0, rows], turned[layers, : 2 * half]).astype(jnp.bfloat16)
+            below = narrow_dot(dz_all[k, rows], turned[k, now])
+            g_all[k, rows] = (g_all[k + 1, rows].astype(jnp.float32) + below).astype(jnp.bfloat16)
+    for i, rows in enumerate(places):
+        grad_out[i] = g_all[section, rows]
+        sums[:, : 2 * half] += rows_dot(tapped[tap_at[i]], dz_all[section, rows])
+        sums[:, 2 * half : 4 * half] += rows_dot(h_all[section, rows], dz_all[section, rows])
+        sums[:, 4 * half : 4 * half + channels] += rows_dot(gated_all[section, rows], g_all[section + 1, rows])
+        sums[:, 4 * half + channels :] += rows_dot(gated_all[section, rows], skip_cot[i])
+
+
+def layer_stack(section_index, signal, tapped, skip_cot, res_cot, weights):
+    number, seq_rows, channels = signal.shape
+    layers, _, width = weights.shape
+    seqs = 2
+    rows = seqs * seq_rows
+    block = pl.BlockSpec((seqs, seq_rows, channels), lambda b, s: (b, 0, 0))
+    tapped_block = pl.BlockSpec((seqs, seq_rows, channels), lambda b, s: (jnp.bitwise_xor(b, s[0] // seqs), 0, 0))
+    whole = pl.BlockSpec(weights.shape, lambda b, s: (0, 0, 0))
+    sums_shape = (channels, 6 * channels)
+    stream = jax.ShapeDtypeStruct(signal.shape, jnp.bfloat16)
+    return pl.pallas_call(
+        functools.partial(stack_kernel, layers),
+        grid_spec=pltpu.PrefetchScalarGridSpec(
+            num_scalar_prefetch=1,
+            grid=(number // seqs,),
+            in_specs=[block, tapped_block, block, block, whole],
+            out_specs=[block, block, block, pl.BlockSpec(sums_shape, lambda b, s: (0, 0))],
+            scratch_shapes=[
+                pltpu.VMEM((layers + 1, 4 * channels, channels), jnp.bfloat16),
+                pltpu.VMEM((layers, rows, channels), jnp.bfloat16),
+                pltpu.VMEM((layers, rows, channels), jnp.bfloat16),
+                pltpu.VMEM((layers, rows, 2 * channels), jnp.bfloat16),
+                pltpu.VMEM((layers + 1, rows, channels), jnp.bfloat16),
+                pltpu.VMEM((layers, rows, channels), jnp.float32),
+                pltpu.VMEM((layers, rows, channels), jnp.float32),
+            ],
+        ),
+        out_shape=[stream, stream, stream, jax.ShapeDtypeStruct(sums_shape, jnp.float32)],
+        compiler_params=pltpu.CompilerParams(vmem_limit_bytes=60 * 2**20),
+        name="layer_stack",
+    )(section_index.astype(jnp.int32).reshape(1), signal, tapped, skip_cot, res_cot, weights)
+
+
+def swapped(x, axis, by):
+    return lax.ppermute(x, axis, [(i, i ^ by) for i in range(lax.axis_size(axis))])
+
+
+def gather_weights(w_tap, w_now, w_res, w_skip, sections, core):
+    own = jnp.concatenate([w_now[0], w_res[0], w_skip[0], w_tap[0]], axis=1)
+    half_rows = own.shape[0] // 2
+    own_half = lax.dynamic_slice_in_dim(own, core * half_rows, half_rows, 0)
+    mine = jnp.stack([swapped(own_half, "section", m) for m in range(1, sections)])
+    other = swapped(mine, "tm", 1)
+    low = jnp.where(core == 0, mine, other)
+    high = jnp.where(core == 0, other, mine)
+    return jnp.concatenate([own[None], jnp.concatenate([low, high], axis=1)])
+
+
+def gather_tapped(signal, section_index, sections):
+    part = lax.dynamic_index_in_dim(signal, section_index, 0, False)
+    arrived = passed_along(part, "tm", SPAN)
+    return jnp.stack([arrived] + [swapped(arrived, "section", m) for m in range(1, sections)])
+
+
+def sum_over_shards(partial, core, place, places):
+    rows, width = partial.shape
+    halves = partial.reshape(2, rows // 2, width)
+    sent = lax.dynamic_index_in_dim(halves, 1 - core, 0, False).astype(jnp.bfloat16)
+    kept = lax.dynamic_index_in_dim(halves, core, 0, False)
+    kept = kept + swapped(sent, "tm", 1).astype(jnp.float32)
+    pieces = kept.reshape(places, rows // 2 // places, width)
+    total = lax.dynamic_index_in_dim(pieces, place, 0, False)
+    for m in range(1, places):
+        sent = lax.dynamic_index_in_dim(pieces, place ^ m, 0, False).astype(jnp.bfloat16)
+        total = total + swapped(sent, "tm", 2 * m).astype(jnp.float32)
+    total = total.astype(jnp.bfloat16)
+    by_distance = jnp.stack([total] + [swapped(total, "tm", 2 * m) for m in range(1, places)])
+    half = jnp.concatenate([lax.dynamic_index_in_dim(by_distance, place ^ q, 0, False) for q in range(places)])
+    other = swapped(half, "tm", 1)
+    low = jnp.where(core == 0, half, other)
+    high = jnp.where(core == 0, other, half)
+    return jnp.concatenate([low, high]).astype(jnp.float32)
+
+
+def stacked_body(signal, skip_cot, res_cot, w_tap, w_now, w_res, w_skip):
+    sections = lax.axis_size("section")
+    shards = lax.axis_size("tm")
+    section_index = lax.axis_index("section")
+    shard_index = lax.axis_index("tm")
+    core = shard_index % 2
+    place = shard_index // 2
+    number, seq_rows, channels = signal.shape
+    tapped = gather_tapped(signal, section_index, sections)
+    weights = gather_weights(w_tap, w_now, w_res, w_skip, sections, core)
+    skip_total, grads, back, sums = layer_stack(section_index, signal, tapped, skip_cot, res_cot, weights)
+    arrived = jnp.stack(
+        [
+            lax.ppermute(back[j], ("section", "tm"), [(j * shards + t + SPAN, t) for t in range(shards - SPAN)])
+            for j in range(number)
+        ]
+    )
+    input_grads = (grads.astype(jnp.float32) + arrived.astype(jnp.float32)).astype(jnp.bfloat16)
+    grad_scale = 1.0 / math.sqrt(number * seq_rows * shards)
+    summed = sum_over_shards(sums, core, place, shards // 2) * grad_scale
+    gate = 2 * channels
+    grad_tap = jnp.where(section_index == 0, summed[:, :gate], 0.0)
+    return (
+        skip_total,
+        input_grads[None],
+        grad_tap[None],
+        summed[None, :, gate : 2 * gate],
+        summed[None, :, 2 * gate : 2 * gate + channels],
+        summed[None, :, 2 * gate + channels :],
+    )
+
+
+def body(signal, skip_cot, res_cot, w_tap, w_now, w_res, w_skip):
+    sections = lax.axis_size("section")
+    shards = lax.axis_size("tm")
+    number, seq_rows, channels = signal.shape
+    one_live_tap = SPAN < shards <= 2 * SPAN
+    square = w_res.shape[1:] == (channels, channels) and w_skip.shape[1:] == (channels, channels)
+    if one_live_tap and square and number == sections and sections == 4 and shards == 8:
+        return stacked_body(signal, skip_cot, res_cot, w_tap, w_now, w_res, w_skip)
+    return pipelined_body(signal, skip_cot, res_cot, w_tap, w_now, w_res, w_skip)
+
+
 def solution(mesh):
     in_specs = (
         P(None, "tm", None),

time: 311 us -> 128 us (0.41)
  blocking collectives: 63.4 us -> 0 us
  waiting for transfers between devices: 111 us -> 61.9 us
  matrix products: 40.6 us -> 0 us
  starting transfers between devices: 68.9 us -> 33.2 us
  Pallas kernels: 0 us -> 17.3 us
  between operations: 15.4 us -> 0.88 us
    ppermute x32 -> x1, waiting for transfers between devices: 106 us -> 6.25 us  [passed_along(): return lax.ppermute(x, axis, pairs)]
    ppermute x32 -> x1, starting transfers between devices: 68.9 us -> 4.51 us  [passed_along(): return lax.ppermute(x, axis, pairs)]
    psum x1 -> x0, blocking collectives: 63.4 us -> none  [run_layers(): skip_total = lax.psum(skip_running_sum, 'section').astype(jnp.bfloat16)]
    ppermute x0 -> x19, waiting for transfers between devices: none -> 55.7 us  [the longest x15 46.2 us: swapped(): lax.ppermute(x, axis, [(i, i ^ by) for i in range(lax.axis_size(axis))])]
    dot_general x97 -> x0, matrix products: 40.6 us -> none  [the longest x69 29.2 us: flat_dot(): jnp.dot(left.reshape(-1, left.shape[-1]), right, preferred_element_type=j...]
    ppermute x0 -> x19, starting transfers between devices: none -> 28.7 us  [the longest x15 23.5 us: swapped(): lax.ppermute(x, axis, [(i, i ^ by) for i in range(lax.axis_size(axis))])]
    pallas_call x0 -> x1, Pallas kernels: none -> 17.3 us  [layer_stack(): pl.pallas_call(functools.partial(stack_kernel, layers), grid_spec=pltpu.P...]
    psum x1 -> x0, waiting for transfers between devices: 5.25 us -> none  [body(): lax.psum((partial_sums[0], partial_sums[1], partial_sums[2], partial_sums...]
  transfers between devices with their start and end apart: 33 -> 20, of which waited for: 19 -> 13; matrix products, arithmetic and copies ran while one was open for 8% -> 4% of each run, Pallas kernels for 0% -> 0%
where the time goes in v1:
time: 128 us
  waiting for transfers between devices  61.9 us (48%)
  starting transfers between devices  33.2 us (26%)
  Pallas kernels  17.3 us (14%)
  other arithmetic  10.6 us (8%)
  local copies, waits for them, and re-layouts  3.99 us (3%)
    ppermute x15, waiting for transfers between devices, swapped(): lax.ppermute(x, axis, [(i, i ^ by) for i in range(lax.axis_size(axis))])  46.2 us
    ppermute x15, starting transfers between devices, swapped(): lax.ppermute(x, axis, [(i, i ^ by) for i in range(lax.axis_size(axis))])  23.5 us
    pallas_call x1, Pallas kernels, layer_stack(): pl.pallas_call(functools.partial(stack_kernel, layers), grid_spec=pltpu.P...  17.3 us
    ppermute x4, waiting for transfers between devices, stacked_body(): lax.ppermute(back[j], ('section', 'tm'), [(j * shards + t + SPAN, t) for...  9.42 us
    ppermute x1, waiting for transfers between devices, passed_along(): return lax.ppermute(x, axis, pairs)  6.25 us
    ppermute x4, starting transfers between devices, stacked_body(): lax.ppermute(back[j], ('section', 'tm'), [(j * shards + t + SPAN, t) for...  5.28 us
    ppermute x1, starting transfers between devices, passed_along(): return lax.ppermute(x, axis, pairs)  4.51 us
  transfers between devices with their start and end apart: 20, of which 13 were waited for; matrix products, arithmetic and copies ran while one was open for 4% of the time, Pallas kernels for 0%

profile of v1, /device:TPU:0, one launch (start us, length us, event | category | flops | bytes accessed | tf_op | source)
XLA Modules:
  0.0 127.9 jit_solution(5904912830416199963)
XLA Ops:
  2.0 3.0 %collective-permute-start.4 = (bf16[128,1536]{1,0:T(8,128)(2,1)S(1)}, bf16[128,1536]{1,0:T(8,128)(2,1)S(1)}, u32[]{:S(2)}, u32[]{:S(2)}) collective-permute-start(bf16[128,1536]{1,0:T(8,128)(2,1)S(1)} %constant_dynamic-slice_fusion), channel_id=1, source_target_pairs={{0,8},{8,0},{16,24},{24,16},{1,9},{9,1},{17,25},{25,17},{2,10},{10... | collective-permute-start | bytes 1179656 | tf_op jit(solution)/shard_map/ppermute | solution.py:280
  5.0 1.5 %collective-permute-start.5 = (bf16[128,1536]{1,0:T(8,128)(2,1)S(1)}, bf16[128,1536]{1,0:T(8,128)(2,1)S(1)}, u32[]{:S(2)}, u32[]{:S(2)}) collective-permute-start(bf16[128,1536]{1,0:T(8,128)(2,1)S(1)} %constant_dynamic-slice_fusion), channel_id=1, source_target_pairs={{0,16},{8,24},{16,0},{24,8},{1,17},{9,25},{17,1},{25,9},{2,18},{10... | collective-permute-start | bytes 1179656 | tf_op jit(solution)/shard_map/ppermute | solution.py:280
  6.5 8.4 %collective-permute-done.4 = bf16[128,1536]{1,0:T(8,128)(2,1)S(1)} collective-permute-done((bf16[128,1536]{1,0:T(8,128)(2,1)S(1)}, bf16[128,1536]{1,0:T(8,128)(2,1)S(1)}, u32[]{:S(2)}, u32[]{:S(2)}) %collective-permute-start.4) | collective-permute-done | bytes 393248 | tf_op jit(solution)/shard_map/ppermute | solution.py:280
  14.9 9.1 %collective-permute-done.5 = bf16[128,1536]{1,0:T(8,128)(2,1)S(1)} collective-permute-done((bf16[128,1536]{1,0:T(8,128)(2,1)S(1)}, bf16[128,1536]{1,0:T(8,128)(2,1)S(1)}, u32[]{:S(2)}, u32[]{:S(2)}) %collective-permute-start.5) | collective-permute-done | bytes 393248 | tf_op jit(solution)/shard_map/ppermute | solution.py:280
  26.1 4.5 %collective-permute-start = (bf16[512,256]{1,0:T(8,128)(2,1)S(1)}, bf16[512,256]{1,0:T(8,128)(2,1)S(1)}, u32[]{:S(2)}, u32[]{:S(2)}) collective-permute-start(bf16[512,256]{1,0:T(8,128)(2,1)S(1)} %dynamic-slice_bitcast_fusion), channel_id=1, source_target_pairs={{0,4},{1,5},{2,6},{3,7},{8,12},{9,13},{10,14},{11,15},{16,20},{17,... | collective-permute-start | bytes 786440 | tf_op jit(solution)/shard_map/ppermute | solution.py:17
  30.6 6.2 %collective-permute-done = bf16[512,256]{1,0:T(8,128)(2,1)S(1)} collective-permute-done((bf16[512,256]{1,0:T(8,128)(2,1)S(1)}, bf16[512,256]{1,0:T(8,128)(2,1)S(1)}, u32[]{:S(2)}, u32[]{:S(2)}) %collective-permute-start) | collective-permute-done | bytes 262176 | tf_op jit(solution)/shard_map/ppermute | solution.py:17
  38.9 1.4 %collective-permute-start.3 = (bf16[512,256]{1,0:T(8,128)(2,1)S(1)}, bf16[512,256]{1,0:T(8,128)(2,1)}, u32[]{:S(2)}, u32[]{:S(2)}) collective-permute-start(bf16[512,256]{1,0:T(8,128)(2,1)S(1)} %collective-permute-done), channel_id=1, source_target_pairs={{0,24},{8,16},{16,8},{24,0},{1,25},{9,17},{17,9},{25,1},{2,26},{10... | collective-permute-start | bytes 786440 | tf_op jit(solution)/shard_map/ppermute | solution.py:280
  40.4 5.8 %collective-permute-done.1 = bf16[512,256]{1,0:T(8,128)(2,1)} collective-permute-done((bf16[512,256]{1,0:T(8,128)(2,1)S(1)}, bf16[512,256]{1,0:T(8,128)(2,1)}, u32[]{:S(2)}, u32[]{:S(2)}) %collective-permute-start.1) | collective-permute-done | bytes 262176 | tf_op jit(solution)/shard_map/ppermute | solution.py:280
  46.2 3.6 %collective-permute-done.2 = bf16[512,256]{1,0:T(8,128)(2,1)} collective-permute-done((bf16[512,256]{1,0:T(8,128)(2,1)S(1)}, bf16[512,256]{1,0:T(8,128)(2,1)}, u32[]{:S(2)}, u32[]{:S(2)}) %collective-permute-start.2) | collective-permute-done | bytes 262176 | tf_op jit(solution)/shard_map/ppermute | solution.py:280
  49.7 1.7 %collective-permute-done.3 = bf16[512,256]{1,0:T(8,128)(2,1)} collective-permute-done((bf16[512,256]{1,0:T(8,128)(2,1)S(1)}, bf16[512,256]{1,0:T(8,128)(2,1)}, u32[]{:S(2)}, u32[]{:S(2)}) %collective-permute-start.3) | collective-permute-done | bytes 262176 | tf_op jit(solution)/shard_map/ppermute | solution.py:280
  51.5 2.2 %pad_maximum_fusion.1.tapped = bf16[4,512,256]{2,1,0:T(8,128)(2,1)} fusion(bf16[1,512,256]{2,1,0:T(8,128)(2,1)} %bitcast.5, bf16[1,512,256]{2,1,0:T(8,128)(2,1)} %bitcast.4, bf16[1,512,256]{2,1,0:T(8,128)(2,1)} %bitcast.3, bf16[1,512,256]{2,1,0:T(8,128)(2,1)S(1)} %bitcast.87), kind=kLoop, calls=%fused_computation.7 | loop fusion | flops 1572864 | bytes 2097152 | tf_op jit(solution)/shard_map/stack | solution.py:297
  53.9 1.9 %maximum_maximum_fusion.weights = bf16[4,256,1536]{2,1,0:T(8,128)(2,1)} fusion(bf16[3,128,1536]{2,1,0:T(8,128)(2,1)S(1)} %get-tuple-element.15, bf16[3,128,1536]{2,1,0:T(8,128)(2,1)S(1)} %get-tuple-element.14, bf16[1,256,1536]{2,1,0:T(8,128)(2,1)S(1)} %get-tuple-element.29), kind=kLoop, calls=%fused_computation | loop fusion | flops 9437184 | bytes 6291456 | tf_op jit(solution)/shard_map/concatenate | solution.py:291
  55.8 17.3 %layer_stack.1 = (bf16[4,512,256]{2,1,0:T(8,128)(2,1)}, bf16[4,512,256]{2,1,0:T(8,128)(2,1)}, bf16[4,512,256]{2,1,0:T(8,128)(2,1)}, f32[256,1536]{1,0:T(8,128)}) custom-call(s32[1]{0:T(128)} %bitcast.section_ref, bf16[4,512,256]{2,1,0:T(8,128)(2,1)} %signal.1, bf16[4,512,256]{2,1,0:T(8,128)(2,1)} %pad_maximum_fusion.1.tapped, bf16[4,512,256]{2,1,0:T(8,128)(2,1)} %skip_cot.1, ...), custom_call_target="tpu_custom_call" | custom-call | tf_op jit(solution)/shard_map/layer_stack/pallas_call | solution.py:256
  74.3 1.7 %collective-permute-done.12 = bf16[128,1536]{1,0:T(8,128)(2,1)S(1)} collective-permute-done((bf16[128,1536]{1,0:T(8,128)(2,1)S(1)}, bf16[128,1536]{1,0:T(8,128)(2,1)S(1)}, u32[]{:S(2)}, u32[]{:S(2)}) %collective-permute-start.12) | collective-permute-done | bytes 393248 | tf_op jit(solution)/shard_map/ppermute | solution.py:280
  77.3 7.5 %collective-permute-start.13 = (bf16[32,1536]{1,0:T(8,128)(2,1)S(1)}, bf16[32,1536]{1,0:T(8,128)(2,1)S(1)}, u32[]{:S(2)}, u32[]{:S(2)}) collective-permute-start(bf16[32,1536]{1,0:T(8,128)(2,1)S(1)} %get-tuple-element.26), channel_id=1, source_target_pairs={{0,2},{1,3},{2,0},{3,1},{4,6},{5,7},{6,4},{7,5},{8,10},{9,11},{10,... | collective-permute-start | bytes 294920 | tf_op jit(solution)/shard_map/ppermute | solution.py:280
  84.7 3.4 %collective-permute-start.14 = (bf16[32,1536]{1,0:T(8,128)(2,1)S(1)}, bf16[32,1536]{1,0:T(8,128)(2,1)S(1)}, u32[]{:S(2)}, u32[]{:S(2)}) collective-permute-start(bf16[32,1536]{1,0:T(8,128)(2,1)S(1)} %get-tuple-element.28), channel_id=1, source_target_pairs={{0,4},{1,5},{2,6},{3,7},{4,0},{5,1},{6,2},{7,3},{8,12},{9,13},{10,... | collective-permute-start | bytes 294920 | tf_op jit(solution)/shard_map/ppermute | solution.py:280
  88.1 7.8 %collective-permute-done.14 = bf16[32,1536]{1,0:T(8,128)(2,1)S(1)} collective-permute-done((bf16[32,1536]{1,0:T(8,128)(2,1)S(1)}, bf16[32,1536]{1,0:T(8,128)(2,1)S(1)}, u32[]{:S(2)}, u32[]{:S(2)}) %collective-permute-start.14) | collective-permute-done | bytes 98336 | tf_op jit(solution)/shard_map/ppermute | solution.py:280
  96.0 1.9 %collective-permute-start.16 = (bf16[32,1536]{1,0:T(8,128)(2,1)S(1)}, bf16[32,1536]{1,0:T(8,128)(2,1)S(1)}, u32[]{:S(2)}, u32[]{:S(2)}) collective-permute-start(bf16[32,1536]{1,0:T(8,128)(2,1)S(1)} %fusion.5), channel_id=1, source_target_pairs={{0,2},{1,3},{2,0},{3,1},{4,6},{5,7},{6,4},{7,5},{8,10},{9,11},{10,... | collective-permute-start | bytes 294920 | tf_op jit(solution)/shard_map/ppermute | solution.py:280
  99.1 1.3 %collective-permute-start.18 = (bf16[32,1536]{1,0:T(8,128)(2,1)S(1)}, bf16[32,1536]{1,0:T(8,128)(2,1)S(1)}, u32[]{:S(2)}, u32[]{:S(2)}) collective-permute-start(bf16[32,1536]{1,0:T(8,128)(2,1)S(1)} %fusion.5), channel_id=1, source_target_pairs={{0,6},{1,7},{2,4},{3,5},{4,2},{5,3},{6,0},{7,1},{8,14},{9,15},{10,... | collective-permute-start | bytes 294920 | tf_op jit(solution)/shard_map/ppermute | solution.py:280
  101.3 1.4 %collective-permute-start.8 = (bf16[512,256]{1,0:T(8,128)(2,1)}, bf16[512,256]{1,0:T(8,128)(2,1)S(1)}, u32[]{:S(2)}, u32[]{:S(2)}) collective-permute-start(bf16[512,256]{1,0:T(8,128)(2,1)} %get-tuple-element.20), channel_id=1, source_target_pairs={{4,0},{5,1},{6,2},{7,3}} | collective-permute-start | bytes 786440 | tf_op jit(solution)/shard_map/ppermute | solution.py:333
  102.7 1.3 %collective-permute-start.9 = (bf16[512,256]{1,0:T(8,128)(2,1)}, bf16[512,256]{1,0:T(8,128)(2,1)S(1)}, u32[]{:S(2)}, u32[]{:S(2)}) collective-permute-start(bf16[512,256]{1,0:T(8,128)(2,1)} %get-tuple-element.23), channel_id=1, source_target_pairs={{12,0},{13,1},{14,2},{15,3}} | collective-permute-start | bytes 786440 | tf_op jit(solution)/shard_map/ppermute | solution.py:333
  105.4 8.2 %collective-permute-done.17 = bf16[32,1536]{1,0:T(8,128)(2,1)S(1)} collective-permute-done((bf16[32,1536]{1,0:T(8,128)(2,1)S(1)}, bf16[32,1536]{1,0:T(8,128)(2,1)S(1)}, u32[]{:S(2)}, u32[]{:S(2)}) %collective-permute-start.17) | collective-permute-done | bytes 98336 | tf_op jit(solution)/shard_map/ppermute | solution.py:280
  115.0 5.1 %collective-permute-done.8 = bf16[512,256]{1,0:T(8,128)(2,1)S(1)} collective-permute-done((bf16[512,256]{1,0:T(8,128)(2,1)}, bf16[512,256]{1,0:T(8,128)(2,1)S(1)}, u32[]{:S(2)}, u32[]{:S(2)}) %collective-permute-start.8) | collective-permute-done | bytes 262176 | tf_op jit(solution)/shard_map/ppermute | solution.py:333
  121.0 3.5 %collective-permute-done.11 = bf16[512,256]{1,0:T(8,128)(2,1)S(1)} collective-permute-done((bf16[512,256]{1,0:T(8,128)(2,1)S(1)}, bf16[512,256]{1,0:T(8,128)(2,1)S(1)}, u32[]{:S(2)}, u32[]{:S(2)}) %collective-permute-start.11) | collective-permute-done | bytes 262176 | tf_op jit(solution)/shard_map/ppermute | solution.py:333
  (41 shorter events, 17.4 us)
Async XLA Ops:
  2.0 12.9 %collective-permute-start.4 = (bf16[128,1536]{1,0:T(8,128)(2,1)S(1)}, bf16[128,1536]{1,0:T(8,128)(2,1)S(1)}, u32[]{:S(2)}, u32[]{:S(2)}) collective-permute-start(bf16[128,1536]{1,0:T(8,128)(2,1)S(1)} %constant_dynamic-slice_fusion), channel_id=1, source_target_pairs={{0,8},{8,0},{16,24},{24,16},{1,9},{9,1},{17,25},{25,17},{2,10},{10... | collective-permute-start | bytes 1179656 | tf_op jit(solution)/shard_map/ppermute | solution.py:280
  5.0 19.0 %collective-permute-start.5 = (bf16[128,1536]{1,0:T(8,128)(2,1)S(1)}, bf16[128,1536]{1,0:T(8,128)(2,1)S(1)}, u32[]{:S(2)}, u32[]{:S(2)}) collective-permute-start(bf16[128,1536]{1,0:T(8,128)(2,1)S(1)} %constant_dynamic-slice_fusion), channel_id=1, source_target_pairs={{0,16},{8,24},{16,0},{24,8},{1,17},{9,25},{17,1},{25,9},{2,18},{10... | collective-permute-start | bytes 1179656 | tf_op jit(solution)/shard_map/ppermute | solution.py:280
  6.5 17.5 %collective-permute-start.6 = (bf16[128,1536]{1,0:T(8,128)(2,1)S(1)}, bf16[128,1536]{1,0:T(8,128)(2,1)S(1)}, u32[]{:S(2)}, u32[]{:S(2)}) collective-permute-start(bf16[128,1536]{1,0:T(8,128)(2,1)S(1)} %constant_dynamic-slice_fusion), channel_id=1, source_target_pairs={{0,24},{8,16},{16,8},{24,0},{1,25},{9,17},{17,9},{25,1},{2,26},{10... | collective-permute-start | bytes 1179656 | tf_op jit(solution)/shard_map/ppermute | solution.py:280
  25.1 28.6 %collective-permute-start.7 = (bf16[3,128,1536]{2,1,0:T(8,128)(2,1)}, bf16[3,128,1536]{2,1,0:T(8,128)(2,1)S(1)}, u32[]{:S(2)}, u32[]{:S(2)}) collective-permute-start(bf16[3,128,1536]{2,1,0:T(8,128)(2,1)} %pad_maximum_fusion), channel_id=1, source_target_pairs={{0,1},{1,0},{2,3},{3,2},{4,5},{5,4},{6,7},{7,6},{8,9},{9,8},{10,11... | collective-permute-start | bytes 3538952 | tf_op jit(solution)/shard_map/ppermute | solution.py:280
  26.1 10.8 %collective-permute-start = (bf16[512,256]{1,0:T(8,128)(2,1)S(1)}, bf16[512,256]{1,0:T(8,128)(2,1)S(1)}, u32[]{:S(2)}, u32[]{:S(2)}) collective-permute-start(bf16[512,256]{1,0:T(8,128)(2,1)S(1)} %dynamic-slice_bitcast_fusion), channel_id=1, source_target_pairs={{0,4},{1,5},{2,6},{3,7},{8,12},{9,13},{10,14},{11,15},{16,20},{17,... | collective-permute-start | bytes 786440 | tf_op jit(solution)/shard_map/ppermute | solution.py:17
  36.9 9.3 %collective-permute-start.1 = (bf16[512,256]{1,0:T(8,128)(2,1)S(1)}, bf16[512,256]{1,0:T(8,128)(2,1)}, u32[]{:S(2)}, u32[]{:S(2)}) collective-permute-start(bf16[512,256]{1,0:T(8,128)(2,1)S(1)} %collective-permute-done), channel_id=1, source_target_pairs={{0,8},{8,0},{16,24},{24,16},{1,9},{9,1},{17,25},{25,17},{2,10},{10... | collective-permute-start | bytes 786440 | tf_op jit(solution)/shard_map/ppermute | solution.py:280
  38.1 11.7 %collective-permute-start.2 = (bf16[512,256]{1,0:T(8,128)(2,1)S(1)}, bf16[512,256]{1,0:T(8,128)(2,1)}, u32[]{:S(2)}, u32[]{:S(2)}) collective-permute-start(bf16[512,256]{1,0:T(8,128)(2,1)S(1)} %collective-permute-done), channel_id=1, source_target_pairs={{0,16},{8,24},{16,0},{24,8},{1,17},{9,25},{17,1},{25,9},{2,18},{10... | collective-permute-start | bytes 786440 | tf_op jit(solution)/shard_map/ppermute | solution.py:280
  38.9 12.6 %collective-permute-start.3 = (bf16[512,256]{1,0:T(8,128)(2,1)S(1)}, bf16[512,256]{1,0:T(8,128)(2,1)}, u32[]{:S(2)}, u32[]{:S(2)}) collective-permute-start(bf16[512,256]{1,0:T(8,128)(2,1)S(1)} %collective-permute-done), channel_id=1, source_target_pairs={{0,24},{8,16},{16,8},{24,0},{1,25},{9,17},{17,9},{25,1},{2,26},{10... | collective-permute-start | bytes 786440 | tf_op jit(solution)/shard_map/ppermute | solution.py:280
  74.2 1.8 %collective-permute-start.12 = (bf16[128,1536]{1,0:T(8,128)(2,1)S(1)}, bf16[128,1536]{1,0:T(8,128)(2,1)S(1)}, u32[]{:S(2)}, u32[]{:S(2)}) collective-permute-start(bf16[128,1536]{1,0:T(8,128)(2,1)S(1)} %fusion.2), channel_id=1, source_target_pairs={{0,1},{1,0},{2,3},{3,2},{4,5},{5,4},{6,7},{7,6},{8,9},{9,8},{10,11... | collective-permute-start | bytes 1179656 | tf_op jit(solution)/shard_map/ppermute | solution.py:280
  74.3 26.1 %copy-start.1 = (bf16[4,512,256]{2,1,0:T(8,128)(2,1)S(1)}, bf16[4,512,256]{2,1,0:T(8,128)(2,1)}, u32[]{:S(2)}) copy-start(bf16[4,512,256]{2,1,0:T(8,128)(2,1)} %get-tuple-element.12) | copy-start | bytes 3145732
  77.3 10.8 %collective-permute-start.13 = (bf16[32,1536]{1,0:T(8,128)(2,1)S(1)}, bf16[32,1536]{1,0:T(8,128)(2,1)S(1)}, u32[]{:S(2)}, u32[]{:S(2)}) collective-permute-start(bf16[32,1536]{1,0:T(8,128)(2,1)S(1)} %get-tuple-element.26), channel_id=1, source_target_pairs={{0,2},{1,3},{2,0},{3,1},{4,6},{5,7},{6,4},{7,5},{8,10},{9,11},{10,... | collective-permute-start | bytes 294920 | tf_op jit(solution)/shard_map/ppermute | solution.py:280
  84.7 11.2 %collective-permute-start.14 = (bf16[32,1536]{1,0:T(8,128)(2,1)S(1)}, bf16[32,1536]{1,0:T(8,128)(2,1)S(1)}, u32[]{:S(2)}, u32[]{:S(2)}) collective-permute-start(bf16[32,1536]{1,0:T(8,128)(2,1)S(1)} %get-tuple-element.28), channel_id=1, source_target_pairs={{0,4},{1,5},{2,6},{3,7},{4,0},{5,1},{6,2},{7,3},{8,12},{9,13},{10,... | collective-permute-start | bytes 294920 | tf_op jit(solution)/shard_map/ppermute | solution.py:280
  88.1 7.8 %collective-permute-start.15 = (bf16[32,1536]{1,0:T(8,128)(2,1)S(1)}, bf16[32,1536]{1,0:T(8,128)(2,1)S(1)}, u32[]{:S(2)}, u32[]{:S(2)}) collective-permute-start(bf16[32,1536]{1,0:T(8,128)(2,1)S(1)} %get-tuple-element.27), channel_id=1, source_target_pairs={{0,6},{1,7},{2,4},{3,5},{4,2},{5,3},{6,0},{7,1},{8,14},{9,15},{10,... | collective-permute-start | bytes 294920 | tf_op jit(solution)/shard_map/ppermute | solution.py:280
  96.0 8.1 %collective-permute-start.16 = (bf16[32,1536]{1,0:T(8,128)(2,1)S(1)}, bf16[32,1536]{1,0:T(8,128)(2,1)S(1)}, u32[]{:S(2)}, u32[]{:S(2)}) collective-permute-start(bf16[32,1536]{1,0:T(8,128)(2,1)S(1)} %fusion.5), channel_id=1, source_target_pairs={{0,2},{1,3},{2,0},{3,1},{4,6},{5,7},{6,4},{7,5},{8,10},{9,11},{10,... | collective-permute-start | bytes 294920 | tf_op jit(solution)/shard_map/ppermute | solution.py:280
  97.9 15.6 %collective-permute-start.17 = (bf16[32,1536]{1,0:T(8,128)(2,1)S(1)}, bf16[32,1536]{1,0:T(8,128)(2,1)S(1)}, u32[]{:S(2)}, u32[]{:S(2)}) collective-permute-start(bf16[32,1536]{1,0:T(8,128)(2,1)S(1)} %fusion.5), channel_id=1, source_target_pairs={{0,4},{1,5},{2,6},{3,7},{4,0},{5,1},{6,2},{7,3},{8,12},{9,13},{10,... | collective-permute-start | bytes 294920 | tf_op jit(solution)/shard_map/ppermute | solution.py:280
  99.1 15.7 %collective-permute-start.18 = (bf16[32,1536]{1,0:T(8,128)(2,1)S(1)}, bf16[32,1536]{1,0:T(8,128)(2,1)S(1)}, u32[]{:S(2)}, u32[]{:S(2)}) collective-permute-start(bf16[32,1536]{1,0:T(8,128)(2,1)S(1)} %fusion.5), channel_id=1, source_target_pairs={{0,6},{1,7},{2,4},{3,5},{4,2},{5,3},{6,0},{7,1},{8,14},{9,15},{10,... | collective-permute-start | bytes 294920 | tf_op jit(solution)/shard_map/ppermute | solution.py:280
  101.3 23.1 %copy-start = (bf16[4,512,256]{2,1,0:T(8,128)(2,1)S(1)}, bf16[4,512,256]{2,1,0:T(8,128)(2,1)}, u32[]{:S(2)}) copy-start(bf16[4,512,256]{2,1,0:T(8,128)(2,1)} %get-tuple-element.11) | copy-start | bytes 3145732
  101.3 18.8 %collective-permute-start.8 = (bf16[512,256]{1,0:T(8,128)(2,1)}, bf16[512,256]{1,0:T(8,128)(2,1)S(1)}, u32[]{:S(2)}, u32[]{:S(2)}) collective-permute-start(bf16[512,256]{1,0:T(8,128)(2,1)} %get-tuple-element.20), channel_id=1, source_target_pairs={{4,0},{5,1},{6,2},{7,3}} | collective-permute-start | bytes 786440 | tf_op jit(solution)/shard_map/ppermute | solution.py:333
  102.7 17.6 %collective-permute-start.9 = (bf16[512,256]{1,0:T(8,128)(2,1)}, bf16[512,256]{1,0:T(8,128)(2,1)S(1)}, u32[]{:S(2)}, u32[]{:S(2)}) collective-permute-start(bf16[512,256]{1,0:T(8,128)(2,1)} %get-tuple-element.23), channel_id=1, source_target_pairs={{12,0},{13,1},{14,2},{15,3}} | collective-permute-start | bytes 786440 | tf_op jit(solution)/shard_map/ppermute | solution.py:333
  104.1 16.9 %collective-permute-start.10 = (bf16[512,256]{1,0:T(8,128)(2,1)}, bf16[512,256]{1,0:T(8,128)(2,1)S(1)}, u32[]{:S(2)}, u32[]{:S(2)}) collective-permute-start(bf16[512,256]{1,0:T(8,128)(2,1)} %get-tuple-element.22), channel_id=1, source_target_pairs={{20,0},{21,1},{22,2},{23,3}} | collective-permute-start | bytes 786440 | tf_op jit(solution)/shard_map/ppermute | solution.py:333
  113.5 11.0 %collective-permute-start.11 = (bf16[512,256]{1,0:T(8,128)(2,1)S(1)}, bf16[512,256]{1,0:T(8,128)(2,1)S(1)}, u32[]{:S(2)}, u32[]{:S(2)}) collective-permute-start(bf16[512,256]{1,0:T(8,128)(2,1)S(1)} %get-tuple-element.21), channel_id=1, source_target_pairs={{28,0},{29,1},{30,2},{31,3}} | collective-permute-start | bytes 786440 | tf_op jit(solution)/shard_map/ppermute | solution.py:333
  114.9 10.7 %collective-permute-start.19 = (bf16[128,1536]{1,0:T(8,128)(2,1)S(1)}, bf16[128,1536]{1,0:T(8,128)(2,1)S(1)}, u32[]{:S(2)}, u32[]{:S(2)}) collective-permute-start(bf16[128,1536]{1,0:T(8,128)(2,1)S(1)} %pad_maximum_fusion.4), channel_id=1, source_target_pairs={{0,1},{1,0},{2,3},{3,2},{4,5},{5,4},{6,7},{7,6},{8,9},{9,8},{10,11... | collective-permute-start | bytes 1179656 | tf_op jit(solution)/shard_map/ppermute | solution.py:280

commit v2 on v0

--- a/solution.py
+++ b/solution.py
@@ -1,11 +1,15 @@
+import functools
 import math
 
 import jax
 import jax.numpy as jnp
 from jax import lax
+from jax.experimental import pallas as pl
+from jax.experimental.pallas import tpu as pltpu
 from jax.sharding import PartitionSpec as P
 
 SPAN = 4
+FIRST_DILATION = 2048
 
 
 def passed_along(x, axis, by):
@@ -144,7 +148,7 @@
     return (skip_total, input_grads, tuple((part[None] for part in partial_sums)))
 
 
-def body(signal, skip_cot, res_cot, w_tap, w_now, w_res, w_skip):
+def pipelined_body(signal, skip_cot, res_cot, w_tap, w_now, w_res, w_skip):
     sections = lax.axis_size("section")
     shards = lax.axis_size("tm")
     section_index = lax.axis_index("section")
@@ -164,6 +168,296 @@
     )
 
 
+def narrow_dot(left, right):
+    return lax.dot_general(left, right, (((1,), (0,)), ((), ())), preferred_element_type=jnp.float32)
+
+
+def rows_dot(left, right):
+    return lax.dot_general(left, right, (((0,), (0,)), ((), ())), preferred_element_type=jnp.float32)
+
+
+def turned_dot(left, right):
+    return lax.dot_general(left, right, (((1,), (1,)), ((), ())), preferred_element_type=jnp.float32)
+
+
+def stack_kernel(layers, last, *refs):
+    refs = list(refs)
+    take = lambda count: [refs.pop(0) for _ in range(count)]
+    signal, skip_cot, res_cot = take(3)
+    taps = take(layers - 1 if last else 1)
+    own = take(4)
+    mine = take(layers - 1)
+    other = take(layers - 1)
+    if last:
+        sums_in, _, _ = take(3)
+        skip_out, grad_out, sent_out, kept_out = take(4)
+    else:
+        skip_out, grad_out, back_out, sums = take(4)
+    weights, cot, tapped, h_all, gated_all, dz_all, g_all, tanh_all, sig_all, skip_total = take(10)
+    weights_here, stream_here, tap_here, skip_gone, grad_gone = take(5)
+    if last:
+        sums, sums_here = take(2)
+    section = lax.axis_index("section")
+    core = lax.rem(lax.axis_index("tm"), 2)
+    _, seqs, seq_rows, channels = h_all.shape
+    half = channels
+    now = slice(0, 2 * half)
+    res = slice(2 * half, 2 * half + channels)
+    skip = slice(2 * half + channels, 2 * half + 2 * channels)
+    tap = slice(2 * half + 2 * channels, 4 * half + 2 * channels)
+    low_rows = channels // 2
+    these = [jnp.bitwise_xor(section, i + 1) if last else section for i in range(seqs)]
+
+    def start_streams(source, target, there):
+        for i in range(seqs):
+            pltpu.make_async_copy(source.at[these[i]], target.at[i], there).start()
+
+    def wait_streams(target, there):
+        pltpu.make_async_copy(target, target, there).wait()
+
+    start_streams(signal, h_all.at[0], stream_here.at[0])
+    for ref, cols in zip(own, (now, res, skip, tap)):
+        pltpu.make_async_copy(ref.at[0], weights.at[section, :, cols], weights_here.at[section]).start()
+    for by in range(1, layers):
+        slot = jnp.bitwise_xor(section, by)
+        for ref, side in ((mine[by - 1], core), (other[by - 1], 1 - core)):
+            rows = pl.ds(pl.multiple_of(side * low_rows, low_rows), low_rows)
+            pltpu.make_async_copy(ref, weights.at[slot, rows], weights_here.at[slot]).start()
+    for i, ref in enumerate(taps):
+        pltpu.make_async_copy(ref, tapped.at[i], tap_here).start()
+    start_streams(skip_cot, cot, stream_here.at[1])
+    start_streams(res_cot, g_all.at[layers], stream_here.at[2])
+    if last:
+        sums_copy = pltpu.make_async_copy(sums_in, sums, sums_here)
+        sums_copy.start()
+
+    wait_streams(h_all.at[0], stream_here.at[0])
+    for k in range(layers):
+        pltpu.make_async_copy(weights.at[k], weights.at[k], weights_here.at[k]).wait()
+        if k == 0:
+            pltpu.make_async_copy(tapped, tapped, tap_here).wait()
+        for i in range(seqs):
+            pre = narrow_dot(h_all[k, i], weights[k, :, now])
+            if k == 0:
+                pre = pre + narrow_dot(tapped[i], weights[0, :, tap])
+            tanh_part = jnp.tanh(pre[:, :half])
+            sig_part = 0.5 * jnp.tanh(0.5 * pre[:, half:]) + 0.5
+            tanh_all[k, i] = tanh_part
+            sig_all[k, i] = sig_part
+            gated_all[k, i] = (tanh_part * sig_part).astype(jnp.bfloat16)
+        if k + 1 < layers:
+            for i in range(seqs):
+                stream = narrow_dot(gated_all[k, i], weights[k, :, res])
+                h_all[k + 1, i] = (h_all[k, i].astype(jnp.float32) + stream).astype(jnp.bfloat16)
+    wait_streams(cot, stream_here.at[1])
+    wait_streams(g_all.at[layers], stream_here.at[2])
+    for i in range(seqs):
+        total = narrow_dot(gated_all[0, i], weights[0, :, skip])
+        for k in range(1, layers):
+            total = total + narrow_dot(gated_all[k, i], weights[k, :, skip])
+        skip_total[i] = total.astype(jnp.bfloat16)
+    for i in range(seqs):
+        pltpu.make_async_copy(skip_total.at[i], skip_out.at[these[i]], skip_gone).start()
+    for k in reversed(range(layers)):
+        for i in range(seqs):
+            du = turned_dot(g_all[k + 1, i], weights[k, :, res]) + turned_dot(cot[i], weights[k, :, skip])
+            tanh_part = tanh_all[k, i]
+            sig_part = sig_all[k, i]
+            scaled = du * sig_part
+            dz_all[k, i, :, :half] = (scaled * (1.0 - tanh_part * tanh_part)).astype(jnp.bfloat16)
+            dz_all[k, i, :, half:] = (scaled * (tanh_part * (1.0 - sig_part))).astype(jnp.bfloat16)
+        for i in range(seqs):
+            below = turned_dot(dz_all[k, i], weights[k, :, now])
+            g_all[k, i] = (g_all[k + 1, i].astype(jnp.float32) + below).astype(jnp.bfloat16)
+    for i in range(seqs):
+        pltpu.make_async_copy(g_all.at[section, i], grad_out.at[these[i]], grad_gone).start()
+    if last:
+        sums_copy.wait()
+    else:
+        back_out[...] = turned_dot(dz_all[0, 0], weights[0, :, tap]).astype(jnp.bfloat16)
+    for i in range(seqs):
+        products = (
+            rows_dot(tapped[i], dz_all[section, i]),
+            rows_dot(h_all[section, i], dz_all[section, i]),
+            rows_dot(gated_all[section, i], g_all[section + 1, i]),
+            rows_dot(gated_all[section, i], cot[i]),
+        )
+        spots = (slice(0, 2 * half), slice(2 * half, 4 * half), slice(4 * half, 4 * half + channels), slice(4 * half + channels, None))
+        for spot, product in zip(spots, products):
+            if i == 0 and not last:
+                sums[:, spot] = product
+            else:
+                sums[:, spot] += product
+    if last:
+        kept_out[...] = sums[pl.ds(pl.multiple_of(core * low_rows, low_rows), low_rows)]
+        sent_out[...] = sums[pl.ds(pl.multiple_of((1 - core) * low_rows, low_rows), low_rows)].astype(jnp.bfloat16)
+    wait_streams(skip_total, skip_gone)
+    wait_streams(cot, grad_gone)
+
+
+def layer_stack(signal, skip_cot, res_cot, taps, own, mine, other, earlier=None):
+    number, seq_rows, channels = signal.shape
+    layers = len(mine) + 1
+    seqs = len(taps)
+    last = earlier is not None
+    width = 6 * channels
+    anywhere = pl.BlockSpec(memory_space=pl.ANY)
+    far = pl.BlockSpec(memory_space=pltpu.HBM)
+    near = pl.BlockSpec(memory_space=pltpu.VMEM)
+    stream = jax.ShapeDtypeStruct(signal.shape, jnp.bfloat16)
+    operands = [signal, skip_cot, res_cot, *taps, *own, *mine, *other]
+    rows = lambda *shape: pltpu.VMEM((*shape, seqs, seq_rows, channels), jnp.bfloat16)
+    scratch = [
+        pltpu.VMEM((layers, channels, width), jnp.bfloat16),
+        rows(),
+        rows(),
+        rows(layers),
+        rows(layers),
+        pltpu.VMEM((layers, seqs, seq_rows, 2 * channels), jnp.bfloat16),
+        rows(layers + 1),
+        pltpu.VMEM((layers, seqs, seq_rows, channels), jnp.float32),
+        pltpu.VMEM((layers, seqs, seq_rows, channels), jnp.float32),
+        rows(),
+        pltpu.SemaphoreType.DMA((layers,)),
+        pltpu.SemaphoreType.DMA((3,)),
+        pltpu.SemaphoreType.DMA,
+        pltpu.SemaphoreType.DMA,
+        pltpu.SemaphoreType.DMA,
+    ]
+    in_specs = [far] * 3 + [anywhere] * (len(operands) - 3)
+    aliases = {}
+    if last:
+        skip_total, grads, sums = earlier
+        in_specs += [anywhere, far, far]
+        aliases = {len(operands) + 1: 0, len(operands) + 2: 1}
+        operands += [sums, skip_total, grads]
+        shapes = [((channels // 2, width), jnp.bfloat16), ((channels // 2, width), jnp.float32)]
+        scratch += [pltpu.VMEM((channels, width), jnp.float32), pltpu.SemaphoreType.DMA]
+    else:
+        shapes = [((seq_rows, channels), jnp.bfloat16), ((channels, width), jnp.float32)]
+    flops = 2 * 22 * layers * seqs * seq_rows * channels * channels
+    return pl.pallas_call(
+        functools.partial(stack_kernel, layers, last),
+        in_specs=in_specs,
+        out_specs=[far, far, near, near],
+        out_shape=[stream, stream] + [jax.ShapeDtypeStruct(*shape) for shape in shapes],
+        scratch_shapes=scratch,
+        input_output_aliases=aliases,
+        compiler_params=pltpu.CompilerParams(vmem_limit_bytes=(48 if last else 24) * 2**20),
+        cost_estimate=pl.CostEstimate(flops=flops, bytes_accessed=16 * seqs * seq_rows * channels, transcendentals=0),
+        name="layer_stack",
+    )(*operands)
+
+
+def spread_kernel(places, kept, got, own_out, *outs):
+    place = lax.axis_index("tm") // 2
+    piece_rows = own_out.shape[0]
+    for by in range(places):
+        rows = pl.ds(pl.multiple_of(jnp.bitwise_xor(place, by) * piece_rows, piece_rows), piece_rows)
+        total = kept[rows] + got[rows].astype(jnp.float32)
+        if by == 0:
+            own_out[...] = total
+        else:
+            outs[by - 1][...] = total.astype(jnp.bfloat16)
+
+
+def final_kernel(places, scale, *refs):
+    shard = lax.axis_index("tm")
+    place, core = shard // 2, lax.rem(shard, 2)
+    pieces, other, outs = refs[:places], refs[places], refs[places + 1 :]
+    piece_rows = pieces[0].shape[0]
+    live = jnp.where(lax.axis_index("section") == 0, scale, 0.0)
+    for side, values in ((core, [ref[...] for ref in pieces]), (1 - core, [other[i] for i in range(places)])):
+        for by, value in enumerate(values):
+            at = (side * places + jnp.bitwise_xor(place, by)) * piece_rows
+            rows = pl.ds(pl.multiple_of(at, piece_rows), piece_rows)
+            value = value.astype(jnp.float32)
+            column = 0
+            for i, out in enumerate(outs):
+                width = out.shape[2]
+                out[0, rows, :] = value[:, column : column + width] * (live if i == 0 else scale)
+                column += width
+
+
+def local_call(kernel, name, operands, out_shape):
+    near = pl.BlockSpec(memory_space=pltpu.VMEM)
+    return pl.pallas_call(
+        kernel,
+        in_specs=[near] * len(operands),
+        out_specs=[near] * len(out_shape),
+        out_shape=out_shape,
+        compiler_params=pltpu.CompilerParams(vmem_limit_bytes=12 * 2**20),
+        name=name,
+    )(*operands)
+
+
+def swapped(x, axis, by):
+    return lax.ppermute(x, axis, [(i, i ^ by) for i in range(lax.axis_size(axis))])
+
+
+def sum_over_shards(sent, kept, places, scale):
+    rows, width = kept.shape
+    piece = (rows // places, width)
+    got = swapped(sent, "tm", 1)
+    narrow = jax.ShapeDtypeStruct(piece, jnp.bfloat16)
+    own, *pieces = local_call(
+        functools.partial(spread_kernel, places), "spread", [kept, got],
+        [jax.ShapeDtypeStruct(piece, jnp.float32)] + [narrow] * (places - 1),
+    )
+    arrived = [swapped(value, "tm", 2 * (by + 1)) for by, value in enumerate(pieces)]
+    total = sum([value.astype(jnp.float32) for value in arrived], own).astype(jnp.bfloat16)
+    by_distance = [total] + [swapped(total, "tm", 2 * by) for by in range(1, places)]
+    other = swapped(jnp.stack(by_distance), "tm", 1)
+    channels = width // 6
+    out_shape = [jax.ShapeDtypeStruct((1, 2 * rows, cols), jnp.float32) for cols in (2 * channels, 2 * channels, channels, channels)]
+    return local_call(functools.partial(final_kernel, places, scale), "place_sums", by_distance + [other], out_shape)
+
+
+def stacked_body(signal, skip_cot, res_cot, w_tap, w_now, w_res, w_skip):
+    sections = lax.axis_size("section")
+    shards = lax.axis_size("tm")
+    section = lax.axis_index("section")
+    core = lax.axis_index("tm") % 2
+    number, seq_rows, channels = signal.shape
+    span = FIRST_DILATION // seq_rows
+
+    tap = passed_along(lax.dynamic_index_in_dim(signal, section, 0, False), "tm", span)
+    packed = jnp.concatenate([w_now[0], w_res[0], w_skip[0], w_tap[0]], axis=1)
+    half_rows = packed.shape[0] // 2
+    own_half = lax.dynamic_slice_in_dim(packed, core * half_rows, half_rows, 0)
+    mine = [swapped(own_half, "section", by) for by in range(1, sections)]
+    tap, mine = lax.optimization_barrier((tap, mine))
+    other = [swapped(piece, "tm", 1) for piece in mine]
+    taps = [tap] + [swapped(tap, "section", by) for by in range(1, sections)]
+
+    own = (w_now, w_res, w_skip, w_tap)
+    streams = (signal, skip_cot, res_cot)
+    skip_total, grads, back, sums = layer_stack(*streams, taps[:1], own, mine, other)
+    back = passed_along(back, "tm", -span)
+    skip_total, grads, sent, kept = layer_stack(*streams, taps[1:], own, mine, other, (skip_total, grads, sums))
+    sent, back = lax.optimization_barrier((sent, back))
+    arrived = [lax.ppermute(back, "section", [(by, 0)]) for by in range(1, sections)]
+    first = jnp.where(section == 0, back, jnp.zeros_like(back))
+    grad_scale = 1.0 / math.sqrt(number * seq_rows * shards)
+    summed = sum_over_shards(sent, kept, shards // 2, grad_scale)
+    back_total = jnp.stack([first] + arrived).astype(jnp.float32)
+    input_grads = (grads.astype(jnp.float32) + back_total).astype(jnp.bfloat16)
+    return (skip_total, input_grads[None], *summed)
+
+
+def body(signal, skip_cot, res_cot, w_tap, w_now, w_res, w_skip):
+    sections = lax.axis_size("section")
+    shards = lax.axis_size("tm")
+    number, seq_rows, channels = signal.shape
+    span, beyond = divmod(FIRST_DILATION, seq_rows)
+    one_live_tap = beyond == 0 and span < shards <= 2 * span
+    square = w_res.shape[1:] == (channels, channels) and w_skip.shape[1:] == (channels, channels)
+    pairs = sections == number == 4 and shards % 2 == 0 and shards & (shards - 1) == 0
+    if one_live_tap and square and pairs:
+        return stacked_body(signal, skip_cot, res_cot, w_tap, w_now, w_res, w_skip)
+    return pipelined_body(signal, skip_cot, res_cot, w_tap, w_now, w_res, w_skip)
+
+
 def solution(mesh):
     in_specs = (
         P(None, "tm", None),

time: 311 us -> 89.3 us (0.29)
  waiting for transfers between devices: 111 us -> 33.5 us
  blocking collectives: 63.4 us -> 0 us
  starting transfers between devices: 68.9 us -> 27.8 us
  matrix products: 40.6 us -> 0 us
  Pallas kernels: 0 us -> 18.4 us
  between operations: 15.4 us -> 0.87 us
  other arithmetic: 8.19 us -> 2.53 us
  local copies, waits for them, and re-layouts: 2.06 us -> 5.83 us
    ppermute x32 -> x2, waiting for transfers between devices: 106 us -> 8.38 us  [passed_along(): return lax.ppermute(x, axis, pairs)]
    psum x1 -> x0, blocking collectives: 63.4 us -> none  [run_layers(): skip_total = lax.psum(skip_running_sum, 'section').astype(jnp.bfloat16)]
    ppermute x32 -> x2, starting transfers between devices: 68.9 us -> 6.4 us  [passed_along(): return lax.ppermute(x, axis, pairs)]
    dot_general x97 -> x0, matrix products: 40.6 us -> none  [the longest x69 29.2 us: flat_dot(): jnp.dot(left.reshape(-1, left.shape[-1]), right, preferred_element_type=j...]
    ppermute x0 -> x20, waiting for transfers between devices: none -> 25.1 us  [the longest x17 17.9 us: swapped(): lax.ppermute(x, axis, [(i, i ^ by) for i in range(lax.axis_size(axis))])]
    ppermute x0 -> x20, starting transfers between devices: none -> 21.4 us  [the longest x17 17.5 us: swapped(): lax.ppermute(x, axis, [(i, i ^ by) for i in range(lax.axis_size(axis))])]
    pallas_call x0 -> x4, Pallas kernels: none -> 18.4 us  [the longest x2 17.1 us: layer_stack(): pl.pallas_call(functools.partial(stack_kernel, layers, last), in_specs=in...]
    psum x1 -> x0, waiting for transfers between devices: 5.25 us -> none  [body(): lax.psum((partial_sums[0], partial_sums[1], partial_sums[2], partial_sums...]
  transfers between devices with their start and end apart: 33 -> 22, of which waited for: 19 -> 10; matrix products, arithmetic and copies ran while one was open for 8% -> 3% of each run, Pallas kernels for 0% -> 19%
where the time goes in v2:
time: 89.3 us; the launch traced here: 88.9 us
  waiting for transfers between devices  33.5 us (38%)
  starting transfers between devices  27.8 us (31%)
  Pallas kernels  18.4 us (21%)
  local copies, waits for them, and re-layouts  5.83 us (7%)
  other arithmetic  2.53 us (3%)
    ppermute x17, waiting for transfers between devices, swapped(): lax.ppermute(x, axis, [(i, i ^ by) for i in range(lax.axis_size(axis))])  17.9 us
    ppermute x17, starting transfers between devices, swapped(): lax.ppermute(x, axis, [(i, i ^ by) for i in range(lax.axis_size(axis))])  17.5 us
    pallas_call x2, Pallas kernels, layer_stack(): pl.pallas_call(functools.partial(stack_kernel, layers, last), in_specs=in...  17.1 us
    ppermute x2, waiting for transfers between devices, passed_along(): return lax.ppermute(x, axis, pairs)  8.38 us
    ppermute x3, waiting for transfers between devices, stacked_body(): lax.ppermute(back, 'section', [(by, 0)])  7.2 us
    ppermute x2, starting transfers between devices, passed_along(): return lax.ppermute(x, axis, pairs)  6.4 us
    unnamed x16, local copies, waits for them, and re-layouts  4.86 us
    ppermute x3, starting transfers between devices, stacked_body(): lax.ppermute(back, 'section', [(by, 0)])  3.85 us
  transfers between devices with their start and end apart: 22, of which 10 were waited for; matrix products, arithmetic and copies ran while one was open for 3% of the time, Pallas kernels for 19%

profile of v2, /device:TPU:0, one launch (start us, length us, event | category | flops | bytes accessed | tf_op | source)
XLA Modules:
  0.0 88.9 jit_solution(14752902182517442780)
XLA Ops:
  1.8 3.0 %collective-permute-start.2 = (bf16[128,1536]{1,0:T(8,128)(2,1)S(1)}, bf16[128,1536]{1,0:T(8,128)(2,1)S(1)}, u32[]{:S(2)}, u32[]{:S(2)}) collective-permute-start(bf16[128,1536]{1,0:T(8,128)(2,1)S(1)} %fusion.3), channel_id=1, source_target_pairs={{0,16},{8,24},{16,0},{24,8},{1,17},{9,25},{17,1},{25,9},{2,18},{10... | collective-permute-start | bytes 1179656 | tf_op jit(solution)/shard_map/ppermute | solution.py:395
  4.8 1.5 %collective-permute-start.1 = (bf16[128,1536]{1,0:T(8,128)(2,1)S(1)}, bf16[128,1536]{1,0:T(8,128)(2,1)S(1)}, u32[]{:S(2)}, u32[]{:S(2)}) collective-permute-start(bf16[128,1536]{1,0:T(8,128)(2,1)S(1)} %fusion.3), channel_id=1, source_target_pairs={{0,8},{8,0},{16,24},{24,16},{1,9},{9,1},{17,25},{25,17},{2,10},{10... | collective-permute-start | bytes 1179656 | tf_op jit(solution)/shard_map/ppermute | solution.py:395
  7.4 4.9 %collective-permute-start = (bf16[512,256]{1,0:T(8,128)(2,1)S(1)}, bf16[512,256]{1,0:T(8,128)(2,1)S(1)}, u32[]{:S(2)}, u32[]{:S(2)}) collective-permute-start(bf16[512,256]{1,0:T(8,128)(2,1)S(1)} %dynamic-slice_bitcast_fusion), channel_id=1, source_target_pairs={{0,4},{1,5},{2,6},{3,7},{8,12},{9,13},{10,14},{11,15},{16,20},{17,... | collective-permute-start | bytes 786440 | tf_op jit(solution)/shard_map/ppermute | solution.py:18
  12.3 4.7 %collective-permute-done.refs_3_ = bf16[512,256]{1,0:T(8,128)(2,1)S(1)} collective-permute-done((bf16[512,256]{1,0:T(8,128)(2,1)S(1)}, bf16[512,256]{1,0:T(8,128)(2,1)S(1)}, u32[]{:S(2)}, u32[]{:S(2)}) %collective-permute-start) | collective-permute-done | bytes 262176 | tf_op jit(solution)/shard_map/ppermute | solution.py:18
  17.0 6.6 %collective-permute-done.3.refs_10_.refs_12_ = bf16[128,1536]{1,0:T(8,128)(2,1)S(1)} collective-permute-done((bf16[128,1536]{1,0:T(8,128)(2,1)S(1)}, bf16[128,1536]{1,0:T(8,128)(2,1)S(1)}, u32[]{:S(2)}, u32[]{:S(2)}) %collective-permute-start.3) | collective-permute-done | bytes 393248 | tf_op jit(solution)/shard_map/ppermute | solution.py:395
  24.2 2.6 %collective-permute-start.6 = (bf16[512,256]{1,0:T(8,128)(2,1)S(1)}, bf16[512,256]{1,0:T(8,128)(2,1)S(1)}, u32[]{:S(2)}, u32[]{:S(2)}) collective-permute-start(bf16[512,256]{1,0:T(8,128)(2,1)S(1)} %collective-permute-done.refs_3_), channel_id=1, source_target_pairs={{0,24},{8,16},{16,8},{24,0},{1,25},{9,17},{17,9},{25,1},{2,26},{10... | collective-permute-start | bytes 786440 | tf_op jit(solution)/shard_map/ppermute | solution.py:395
  31.4 6.0 %layer_stack.2 = (bf16[4,512,256]{2,1,0:T(8,128)(2,1)}, bf16[4,512,256]{2,1,0:T(8,128)(2,1)S(1)}, bf16[512,256]{1,0:T(8,128)(2,1)S(1)}, f32[256,1536]{1,0:T(8,128)S(1)}) custom-call(bf16[4,512,256]{2,1,0:T(8,128)(2,1)S(1)} %copy-done.4, bf16[4,512,256]{2,1,0:T(8,128)(2,1)S(1)} %copy-done.5, bf16[4,512,256]{2,1,0:T(8,128)(2,1)S(1)} %copy-done.6, ...), custom_call_target="tpu_custom_call" | custom-call | flops 5905580032 | bytes 2097152 | tf_op jit(solution)/shard_map/layer_stack/pallas_call | solution.py:339
  38.6 1.5 %collective-permute-start.10 = (bf16[512,256]{1,0:T(8,128)(2,1)S(1)}, bf16[512,256]{1,0:T(8,128)(2,1)S(1)}, u32[]{:S(2)}, u32[]{:S(2)}) collective-permute-start(bf16[512,256]{1,0:T(8,128)(2,1)S(1)} %get-tuple-element.38), channel_id=1, source_target_pairs={{4,0},{5,1},{6,2},{7,3},{12,8},{13,9},{14,10},{15,11},{20,16},{21,... | collective-permute-start | bytes 786440 | tf_op jit(solution)/shard_map/ppermute | solution.py:18
  40.1 11.1 %layer_stack.3 = (bf16[4,512,256]{2,1,0:T(8,128)(2,1)}, bf16[4,512,256]{2,1,0:T(8,128)(2,1)S(1)}, bf16[128,1536]{1,0:T(8,128)(2,1)S(1)}, f32[128,1536]{1,0:T(8,128)S(1)}) custom-call(bf16[4,512,256]{2,1,0:T(8,128)(2,1)} %refs_0_.3, bf16[4,512,256]{2,1,0:T(8,128)(2,1)} %refs_1_.3, ...), custom_call_target="tpu_custom_call", output_to_operand_aliasing={{0}: (17, {}), {1}: (18, {})} | custom-call | flops 17716740096 | bytes 6291456 | tf_op jit(solution)/shard_map/layer_stack/pallas_call | solution.py:339
  51.2 3.6 %collective-permute-done.10 = bf16[512,256]{1,0:T(8,128)(2,1)S(1)} collective-permute-done((bf16[512,256]{1,0:T(8,128)(2,1)S(1)}, bf16[512,256]{1,0:T(8,128)(2,1)S(1)}, u32[]{:S(2)}, u32[]{:S(2)}) %collective-permute-start.10) | collective-permute-done | bytes 262176 | tf_op jit(solution)/shard_map/ppermute | solution.py:18
  54.8 1.7 %collective-permute-done.14.got = bf16[128,1536]{1,0:T(8,128)(2,1)S(1)} collective-permute-done((bf16[128,1536]{1,0:T(8,128)(2,1)S(1)}, bf16[128,1536]{1,0:T(8,128)(2,1)S(1)}, u32[]{:S(2)}, u32[]{:S(2)}) %collective-permute-start.14) | collective-permute-done | bytes 393248 | tf_op jit(solution)/shard_map/ppermute | solution.py:395
  56.7 1.7 %collective-permute-start.16 = (bf16[32,1536]{1,0:T(8,128)(2,1)S(1)}, bf16[32,1536]{1,0:T(8,128)(2,1)S(1)}, u32[]{:S(2)}, u32[]{:S(2)}) collective-permute-start(bf16[32,1536]{1,0:T(8,128)(2,1)S(1)} %get-tuple-element.44), channel_id=1, source_target_pairs={{0,4},{1,5},{2,6},{3,7},{4,0},{5,1},{6,2},{7,3},{8,12},{9,13},{10,... | collective-permute-start | bytes 294920 | tf_op jit(solution)/shard_map/ppermute | solution.py:395
  58.4 2.7 %collective-permute-start.17 = (bf16[32,1536]{1,0:T(8,128)(2,1)S(1)}, bf16[32,1536]{1,0:T(8,128)(2,1)S(1)}, u32[]{:S(2)}, u32[]{:S(2)}) collective-permute-start(bf16[32,1536]{1,0:T(8,128)(2,1)S(1)} %get-tuple-element.45), channel_id=1, source_target_pairs={{0,6},{1,7},{2,4},{3,5},{4,2},{5,3},{6,0},{7,1},{8,14},{9,15},{10,... | collective-permute-start | bytes 294920 | tf_op jit(solution)/shard_map/ppermute | solution.py:395
  61.1 1.6 %collective-permute-done.15 = bf16[32,1536]{1,0:T(8,128)(2,1)S(1)} collective-permute-done((bf16[32,1536]{1,0:T(8,128)(2,1)S(1)}, bf16[32,1536]{1,0:T(8,128)(2,1)S(1)}, u32[]{:S(2)}, u32[]{:S(2)}) %collective-permute-start.15) | collective-permute-done | bytes 98336 | tf_op jit(solution)/shard_map/ppermute | solution.py:395
  62.7 4.9 %collective-permute-done.16 = bf16[32,1536]{1,0:T(8,128)(2,1)S(1)} collective-permute-done((bf16[32,1536]{1,0:T(8,128)(2,1)S(1)}, bf16[32,1536]{1,0:T(8,128)(2,1)S(1)}, u32[]{:S(2)}, u32[]{:S(2)}) %collective-permute-start.16) | collective-permute-done | bytes 98336 | tf_op jit(solution)/shard_map/ppermute | solution.py:395
  67.6 1.5 %collective-permute-start.20 = (bf16[32,1536]{1,0:T(8,128)(2,1)S(1)}, bf16[32,1536]{1,0:T(8,128)(2,1)S(1)}, u32[]{:S(2)}, u32[]{:S(2)}) collective-permute-start(bf16[32,1536]{1,0:T(8,128)(2,1)S(1)} %add_convert_fusion.1.refs_0_), channel_id=1, source_target_pairs={{0,6},{1,7},{2,4},{3,5},{4,2},{5,3},{6,0},{7,1},{8,14},{9,15},{10,... | collective-permute-start | bytes 294920 | tf_op jit(solution)/shard_map/ppermute | solution.py:395
  69.1 1.9 %collective-permute-start.19 = (bf16[32,1536]{1,0:T(8,128)(2,1)S(1)}, bf16[32,1536]{1,0:T(8,128)(2,1)S(1)}, u32[]{:S(2)}, u32[]{:S(2)}) collective-permute-start(bf16[32,1536]{1,0:T(8,128)(2,1)S(1)} %add_convert_fusion.1.refs_0_), channel_id=1, source_target_pairs={{0,4},{1,5},{2,6},{3,7},{4,0},{5,1},{6,2},{7,3},{8,12},{9,13},{10,... | collective-permute-start | bytes 294920 | tf_op jit(solution)/shard_map/ppermute | solution.py:395
  72.1 1.3 %collective-permute-start.13 = (bf16[512,256]{1,0:T(8,128)(2,1)S(1)}, bf16[512,256]{1,0:T(8,128)(2,1)S(1)}, u32[]{:S(2)}, u32[]{:S(2)}) collective-permute-start(bf16[512,256]{1,0:T(8,128)(2,1)S(1)} %collective-permute-done.10), channel_id=1, source_target_pairs={{24,0},{25,1},{26,2},{27,3},{28,4},{29,5},{30,6},{31,7}} | collective-permute-start | bytes 786440 | tf_op jit(solution)/shard_map/ppermute | solution.py:439
  73.4 1.3 %collective-permute-start.12 = (bf16[512,256]{1,0:T(8,128)(2,1)S(1)}, bf16[512,256]{1,0:T(8,128)(2,1)S(1)}, u32[]{:S(2)}, u32[]{:S(2)}) collective-permute-start(bf16[512,256]{1,0:T(8,128)(2,1)S(1)} %collective-permute-done.10), channel_id=1, source_target_pairs={{16,0},{17,1},{18,2},{19,3},{20,4},{21,5},{22,6},{23,7}} | collective-permute-start | bytes 786440 | tf_op jit(solution)/shard_map/ppermute | solution.py:439
  75.2 1.3 %collective-permute-start.11 = (bf16[512,256]{1,0:T(8,128)(2,1)S(1)}, bf16[512,256]{1,0:T(8,128)(2,1)S(1)}, u32[]{:S(2)}, u32[]{:S(2)}) collective-permute-start(bf16[512,256]{1,0:T(8,128)(2,1)S(1)} %collective-permute-done.10), channel_id=1, source_target_pairs={{8,0},{9,1},{10,2},{11,3},{12,4},{13,5},{14,6},{15,7}} | collective-permute-start | bytes 786440 | tf_op jit(solution)/shard_map/ppermute | solution.py:439
  76.5 2.6 %collective-permute-done.19.refs_2_ = bf16[32,1536]{1,0:T(8,128)(2,1)S(1)} collective-permute-done((bf16[32,1536]{1,0:T(8,128)(2,1)S(1)}, bf16[32,1536]{1,0:T(8,128)(2,1)S(1)}, u32[]{:S(2)}, u32[]{:S(2)}) %collective-permute-start.19) | collective-permute-done | bytes 98336 | tf_op jit(solution)/shard_map/ppermute | solution.py:395
  79.2 2.1 %collective-permute-done.13 = bf16[512,256]{1,0:T(8,128)(2,1)S(1)} collective-permute-done((bf16[512,256]{1,0:T(8,128)(2,1)S(1)}, bf16[512,256]{1,0:T(8,128)(2,1)S(1)}, u32[]{:S(2)}, u32[]{:S(2)}) %collective-permute-start.13) | collective-permute-done | bytes 262176 | tf_op jit(solution)/shard_map/ppermute | solution.py:439
  81.3 5.1 %collective-permute-done.12 = bf16[512,256]{1,0:T(8,128)(2,1)S(1)} collective-permute-done((bf16[512,256]{1,0:T(8,128)(2,1)S(1)}, bf16[512,256]{1,0:T(8,128)(2,1)S(1)}, u32[]{:S(2)}, u32[]{:S(2)}) %collective-permute-start.12) | collective-permute-done | bytes 262176 | tf_op jit(solution)/shard_map/ppermute | solution.py:439
  86.4 1.3 %fusion = bf16[1,4,512,256]{3,2,1,0:T(8,128)(2,1)} fusion(bf16[4,512,256]{2,1,0:T(8,128)(2,1)S(1)} %get-tuple-element.36, bf16[1,512,256]{2,1,0:T(8,128)(2,1)S(1)} %bitcast.25, bf16[1,512,256]{2,1,0:T(8,128)(2,1)S(1)} %bitcast.26, bf16[1,512,256]{2,1,0:T(8,128)(2,1)S(1)} %bitcast.27, bf16[1,512,256]{2,1,0:T(8,128)(2,1)S(1)} %select_bitcast_fusion), kind=kLoop, calls=%fused_computation.1 | loop fusion | flops 3670016 | bytes 3145728 | tf_op jit(solution)/shard_map/broadcast_in_dim | solution.py:445
  (46 shorter events, 11.6 us)
Async XLA Ops:
  0.6 27.0 %copy-start.1 = (bf16[1,256,512]{2,1,0:T(8,128)(2,1)S(1)}, bf16[1,256,512]{2,1,0:T(8,128)(2,1)}, u32[]{:S(2)}) copy-start(bf16[1,256,512]{2,1,0:T(8,128)(2,1)} %refs_9_.1) | copy-start | bytes 786436
  0.6 27.0 %copy-start = (bf16[1,256,512]{2,1,0:T(8,128)(2,1)S(1)}, bf16[1,256,512]{2,1,0:T(8,128)(2,1)}, u32[]{:S(2)}) copy-start(bf16[1,256,512]{2,1,0:T(8,128)(2,1)} %refs_6_.3) | copy-start | bytes 786436
  1.8 15.2 %collective-permute-start.2 = (bf16[128,1536]{1,0:T(8,128)(2,1)S(1)}, bf16[128,1536]{1,0:T(8,128)(2,1)S(1)}, u32[]{:S(2)}, u32[]{:S(2)}) collective-permute-start(bf16[128,1536]{1,0:T(8,128)(2,1)S(1)} %fusion.3), channel_id=1, source_target_pairs={{0,16},{8,24},{16,0},{24,8},{1,17},{9,25},{17,1},{25,9},{2,18},{10... | collective-permute-start | bytes 1179656 | tf_op jit(solution)/shard_map/ppermute | solution.py:395
  4.8 12.2 %collective-permute-start.1 = (bf16[128,1536]{1,0:T(8,128)(2,1)S(1)}, bf16[128,1536]{1,0:T(8,128)(2,1)S(1)}, u32[]{:S(2)}, u32[]{:S(2)}) collective-permute-start(bf16[128,1536]{1,0:T(8,128)(2,1)S(1)} %fusion.3), channel_id=1, source_target_pairs={{0,8},{8,0},{16,24},{24,16},{1,9},{9,1},{17,25},{25,17},{2,10},{10... | collective-permute-start | bytes 1179656 | tf_op jit(solution)/shard_map/ppermute | solution.py:395
  6.3 17.3 %collective-permute-start.3 = (bf16[128,1536]{1,0:T(8,128)(2,1)S(1)}, bf16[128,1536]{1,0:T(8,128)(2,1)S(1)}, u32[]{:S(2)}, u32[]{:S(2)}) collective-permute-start(bf16[128,1536]{1,0:T(8,128)(2,1)S(1)} %fusion.3), channel_id=1, source_target_pairs={{0,24},{8,16},{16,8},{24,0},{1,25},{9,17},{17,9},{25,1},{2,26},{10... | collective-permute-start | bytes 1179656 | tf_op jit(solution)/shard_map/ppermute | solution.py:395
  7.4 9.7 %collective-permute-start = (bf16[512,256]{1,0:T(8,128)(2,1)S(1)}, bf16[512,256]{1,0:T(8,128)(2,1)S(1)}, u32[]{:S(2)}, u32[]{:S(2)}) collective-permute-start(bf16[512,256]{1,0:T(8,128)(2,1)S(1)} %dynamic-slice_bitcast_fusion), channel_id=1, source_target_pairs={{0,4},{1,5},{2,6},{3,7},{8,12},{9,13},{10,14},{11,15},{16,20},{17,... | collective-permute-start | bytes 786440 | tf_op jit(solution)/shard_map/ppermute | solution.py:18
  23.6 3.6 %collective-permute-start.7 = (bf16[128,1536]{1,0:T(8,128)(2,1)S(1)}, bf16[128,1536]{1,0:T(8,128)(2,1)S(1)}, u32[]{:S(2)}, u32[]{:S(2)}) collective-permute-start(bf16[128,1536]{1,0:T(8,128)(2,1)S(1)} %collective-permute-done.1.refs_8_.refs_10_), channel_id=1, source_target_pairs={{0,1},{1,0},{2,3},{3,2},{4,5},{5,4},{6,7},{7,6},{8,9},{9,8},{10,11... | collective-permute-start | bytes 1179656 | tf_op jit(solution)/shard_map/ppermute | solution.py:395
  23.6 4.0 %collective-permute-start.8 = (bf16[128,1536]{1,0:T(8,128)(2,1)S(1)}, bf16[128,1536]{1,0:T(8,128)(2,1)S(1)}, u32[]{:S(2)}, u32[]{:S(2)}) collective-permute-start(bf16[128,1536]{1,0:T(8,128)(2,1)S(1)} %collective-permute-done.2.refs_9_.refs_11_), channel_id=1, source_target_pairs={{0,1},{1,0},{2,3},{3,2},{4,5},{5,4},{6,7},{7,6},{8,9},{9,8},{10,11... | collective-permute-start | bytes 1179656 | tf_op jit(solution)/shard_map/ppermute | solution.py:395
  24.2 3.5 %collective-permute-start.9 = (bf16[128,1536]{1,0:T(8,128)(2,1)S(1)}, bf16[128,1536]{1,0:T(8,128)(2,1)S(1)}, u32[]{:S(2)}, u32[]{:S(2)}) collective-permute-start(bf16[128,1536]{1,0:T(8,128)(2,1)S(1)} %collective-permute-done.3.refs_10_.refs_12_), channel_id=1, source_target_pairs={{0,1},{1,0},{2,3},{3,2},{4,5},{5,4},{6,7},{7,6},{8,9},{9,8},{10,11... | collective-permute-start | bytes 1179656 | tf_op jit(solution)/shard_map/ppermute | solution.py:395
  24.2 15.9 %collective-permute-start.6 = (bf16[512,256]{1,0:T(8,128)(2,1)S(1)}, bf16[512,256]{1,0:T(8,128)(2,1)S(1)}, u32[]{:S(2)}, u32[]{:S(2)}) collective-permute-start(bf16[512,256]{1,0:T(8,128)(2,1)S(1)} %collective-permute-done.refs_3_), channel_id=1, source_target_pairs={{0,24},{8,16},{16,8},{24,0},{1,25},{9,17},{17,9},{25,1},{2,26},{10... | collective-permute-start | bytes 786440 | tf_op jit(solution)/shard_map/ppermute | solution.py:395
  26.8 13.3 %collective-permute-start.5 = (bf16[512,256]{1,0:T(8,128)(2,1)S(1)}, bf16[512,256]{1,0:T(8,128)(2,1)S(1)}, u32[]{:S(2)}, u32[]{:S(2)}) collective-permute-start(bf16[512,256]{1,0:T(8,128)(2,1)S(1)} %collective-permute-done.refs_3_), channel_id=1, source_target_pairs={{0,16},{8,24},{16,0},{24,8},{1,17},{9,25},{17,1},{25,9},{2,18},{10... | collective-permute-start | bytes 786440 | tf_op jit(solution)/shard_map/ppermute | solution.py:395
  27.3 12.8 %collective-permute-start.4 = (bf16[512,256]{1,0:T(8,128)(2,1)S(1)}, bf16[512,256]{1,0:T(8,128)(2,1)S(1)}, u32[]{:S(2)}, u32[]{:S(2)}) collective-permute-start(bf16[512,256]{1,0:T(8,128)(2,1)S(1)} %collective-permute-done.refs_3_), channel_id=1, source_target_pairs={{0,8},{8,0},{16,24},{24,16},{1,9},{9,1},{17,25},{25,17},{2,10},{10... | collective-permute-start | bytes 786440 | tf_op jit(solution)/shard_map/ppermute | solution.py:395
  38.6 16.3 %collective-permute-start.10 = (bf16[512,256]{1,0:T(8,128)(2,1)S(1)}, bf16[512,256]{1,0:T(8,128)(2,1)S(1)}, u32[]{:S(2)}, u32[]{:S(2)}) collective-permute-start(bf16[512,256]{1,0:T(8,128)(2,1)S(1)} %get-tuple-element.38), channel_id=1, source_target_pairs={{4,0},{5,1},{6,2},{7,3},{12,8},{13,9},{14,10},{15,11},{20,16},{21,... | collective-permute-start | bytes 786440 | tf_op jit(solution)/shard_map/ppermute | solution.py:18
  54.8 1.7 %collective-permute-start.14 = (bf16[128,1536]{1,0:T(8,128)(2,1)S(1)}, bf16[128,1536]{1,0:T(8,128)(2,1)S(1)}, u32[]{:S(2)}, u32[]{:S(2)}) collective-permute-start(bf16[128,1536]{1,0:T(8,128)(2,1)S(1)} %get-tuple-element.41), channel_id=1, source_target_pairs={{0,1},{1,0},{2,3},{3,2},{4,5},{5,4},{6,7},{7,6},{8,9},{9,8},{10,11... | collective-permute-start | bytes 1179656 | tf_op jit(solution)/shard_map/ppermute | solution.py:395
  56.6 6.1 %collective-permute-start.15 = (bf16[32,1536]{1,0:T(8,128)(2,1)S(1)}, bf16[32,1536]{1,0:T(8,128)(2,1)S(1)}, u32[]{:S(2)}, u32[]{:S(2)}) collective-permute-start(bf16[32,1536]{1,0:T(8,128)(2,1)S(1)} %get-tuple-element.43), channel_id=1, source_target_pairs={{0,2},{1,3},{2,0},{3,1},{4,6},{5,7},{6,4},{7,5},{8,10},{9,11},{10,... | collective-permute-start | bytes 294920 | tf_op jit(solution)/shard_map/ppermute | solution.py:395
  56.7 10.9 %collective-permute-start.16 = (bf16[32,1536]{1,0:T(8,128)(2,1)S(1)}, bf16[32,1536]{1,0:T(8,128)(2,1)S(1)}, u32[]{:S(2)}, u32[]{:S(2)}) collective-permute-start(bf16[32,1536]{1,0:T(8,128)(2,1)S(1)} %get-tuple-element.44), channel_id=1, source_target_pairs={{0,4},{1,5},{2,6},{3,7},{4,0},{5,1},{6,2},{7,3},{8,12},{9,13},{10,... | collective-permute-start | bytes 294920 | tf_op jit(solution)/shard_map/ppermute | solution.py:395
  58.4 9.2 %collective-permute-start.17 = (bf16[32,1536]{1,0:T(8,128)(2,1)S(1)}, bf16[32,1536]{1,0:T(8,128)(2,1)S(1)}, u32[]{:S(2)}, u32[]{:S(2)}) collective-permute-start(bf16[32,1536]{1,0:T(8,128)(2,1)S(1)} %get-tuple-element.45), channel_id=1, source_target_pairs={{0,6},{1,7},{2,4},{3,5},{4,2},{5,3},{6,0},{7,1},{8,14},{9,15},{10,... | collective-permute-start | bytes 294920 | tf_op jit(solution)/shard_map/ppermute | solution.py:395
  67.6 7.5 %collective-permute-start.20 = (bf16[32,1536]{1,0:T(8,128)(2,1)S(1)}, bf16[32,1536]{1,0:T(8,128)(2,1)S(1)}, u32[]{:S(2)}, u32[]{:S(2)}) collective-permute-start(bf16[32,1536]{1,0:T(8,128)(2,1)S(1)} %add_convert_fusion.1.refs_0_), channel_id=1, source_target_pairs={{0,6},{1,7},{2,4},{3,5},{4,2},{5,3},{6,0},{7,1},{8,14},{9,15},{10,... | collective-permute-start | bytes 294920 | tf_op jit(solution)/shard_map/ppermute | solution.py:395
  69.1 9.9 %collective-permute-start.19 = (bf16[32,1536]{1,0:T(8,128)(2,1)S(1)}, bf16[32,1536]{1,0:T(8,128)(2,1)S(1)}, u32[]{:S(2)}, u32[]{:S(2)}) collective-permute-start(bf16[32,1536]{1,0:T(8,128)(2,1)S(1)} %add_convert_fusion.1.refs_0_), channel_id=1, source_target_pairs={{0,4},{1,5},{2,6},{3,7},{4,0},{5,1},{6,2},{7,3},{8,12},{9,13},{10,... | collective-permute-start | bytes 294920 | tf_op jit(solution)/shard_map/ppermute | solution.py:395
  71.0 8.0 %collective-permute-start.18 = (bf16[32,1536]{1,0:T(8,128)(2,1)S(1)}, bf16[32,1536]{1,0:T(8,128)(2,1)S(1)}, u32[]{:S(2)}, u32[]{:S(2)}) collective-permute-start(bf16[32,1536]{1,0:T(8,128)(2,1)S(1)} %add_convert_fusion.1.refs_0_), channel_id=1, source_target_pairs={{0,2},{1,3},{2,0},{3,1},{4,6},{5,7},{6,4},{7,5},{8,10},{9,11},{10,... | collective-permute-start | bytes 294920 | tf_op jit(solution)/shard_map/ppermute | solution.py:395
  72.1 9.2 %collective-permute-start.13 = (bf16[512,256]{1,0:T(8,128)(2,1)S(1)}, bf16[512,256]{1,0:T(8,128)(2,1)S(1)}, u32[]{:S(2)}, u32[]{:S(2)}) collective-permute-start(bf16[512,256]{1,0:T(8,128)(2,1)S(1)} %collective-permute-done.10), channel_id=1, source_target_pairs={{24,0},{25,1},{26,2},{27,3},{28,4},{29,5},{30,6},{31,7}} | collective-permute-start | bytes 786440 | tf_op jit(solution)/shard_map/ppermute | solution.py:439
  73.4 13.0 %collective-permute-start.12 = (bf16[512,256]{1,0:T(8,128)(2,1)S(1)}, bf16[512,256]{1,0:T(8,128)(2,1)S(1)}, u32[]{:S(2)}, u32[]{:S(2)}) collective-permute-start(bf16[512,256]{1,0:T(8,128)(2,1)S(1)} %collective-permute-done.10), channel_id=1, source_target_pairs={{16,0},{17,1},{18,2},{19,3},{20,4},{21,5},{22,6},{23,7}} | collective-permute-start | bytes 786440 | tf_op jit(solution)/shard_map/ppermute | solution.py:439
  75.2 11.2 %collective-permute-start.11 = (bf16[512,256]{1,0:T(8,128)(2,1)S(1)}, bf16[512,256]{1,0:T(8,128)(2,1)S(1)}, u32[]{:S(2)}, u32[]{:S(2)}) collective-permute-start(bf16[512,256]{1,0:T(8,128)(2,1)S(1)} %collective-permute-done.10), channel_id=1, source_target_pairs={{8,0},{9,1},{10,2},{11,3},{12,4},{13,5},{14,6},{15,7}} | collective-permute-start | bytes 786440 | tf_op jit(solution)/shard_map/ppermute | solution.py:439
  79.1 8.6 %collective-permute-start.21 = (bf16[4,32,1536]{2,1,0:T(8,128)(2,1)S(1)}, bf16[4,32,1536]{2,1,0:T(8,128)(2,1)S(1)}, u32[]{:S(2)}, u32[]{:S(2)}) collective-permute-start(bf16[4,32,1536]{2,1,0:T(8,128)(2,1)S(1)} %pad_maximum_fusion), channel_id=1, source_target_pairs={{0,1},{1,0},{2,3},{3,2},{4,5},{5,4},{6,7},{7,6},{8,9},{9,8},{10,11... | collective-permute-start | bytes 1179656 | tf_op jit(solution)/shard_map/ppermute | solution.py:395
  (6 other events, 58.9 us)

commit v3 on v2

--- a/solution.py
+++ b/solution.py
@@ -183,20 +183,22 @@
 def stack_kernel(layers, last, *refs):
     refs = list(refs)
     take = lambda count: [refs.pop(0) for _ in range(count)]
-    signal, skip_cot, res_cot = take(3)
+    signal, cot, res_cot = take(3)
     taps = take(layers - 1 if last else 1)
-    own = take(4)
-    mine = take(layers - 1)
-    other = take(layers - 1)
     if last:
-        sums_in, _, _ = take(3)
+        weights, sums_in, _, _ = take(4)
         skip_out, grad_out, sent_out, kept_out = take(4)
     else:
-        skip_out, grad_out, back_out, sums = take(4)
-    weights, cot, tapped, h_all, gated_all, dz_all, g_all, tanh_all, sig_all, skip_total = take(10)
-    weights_here, stream_here, tap_here, skip_gone, grad_gone = take(5)
+        own = take(4)
+        mine = take(layers - 1)
+        other = take(layers - 1)
+        skip_out, grad_out, back_out, sums, weights = take(5)
+    tapped, h_all, gated_all, dz_all, g_all, tanh_all, sig_all, skip_total = take(8)
+    stream_here, tap_here, skip_gone, grad_gone = take(4)
     if last:
-        sums, sums_here = take(2)
+        (sums,) = take(1)
+    else:
+        (weights_here,) = take(1)
     section = lax.axis_index("section")
     core = lax.rem(lax.axis_index("tm"), 2)
     _, seqs, seq_rows, channels = h_all.shape
@@ -208,34 +210,28 @@
     low_rows = channels // 2
     these = [jnp.bitwise_xor(section, i + 1) if last else section for i in range(seqs)]
 
-    def start_streams(source, target, there):
-        for i in range(seqs):
-            pltpu.make_async_copy(source.at[these[i]], target.at[i], there).start()
-
-    def wait_streams(target, there):
+    def wait_bytes(target, there):
         pltpu.make_async_copy(target, target, there).wait()
 
-    start_streams(signal, h_all.at[0], stream_here.at[0])
-    for ref, cols in zip(own, (now, res, skip, tap)):
-        pltpu.make_async_copy(ref.at[0], weights.at[section, :, cols], weights_here.at[section]).start()
-    for by in range(1, layers):
-        slot = jnp.bitwise_xor(section, by)
-        for ref, side in ((mine[by - 1], core), (other[by - 1], 1 - core)):
-            rows = pl.ds(pl.multiple_of(side * low_rows, low_rows), low_rows)
-            pltpu.make_async_copy(ref, weights.at[slot, rows], weights_here.at[slot]).start()
+    if not last:
+        for ref, cols in zip(own, (now, res, skip, tap)):
+            pltpu.make_async_copy(ref.at[0], weights.at[section, :, cols], weights_here.at[section]).start()
+        for by in range(1, layers):
+            slot = jnp.bitwise_xor(section, by)
+            for ref, side in ((mine[by - 1], core), (other[by - 1], 1 - core)):
+                rows = pl.ds(pl.multiple_of(side * low_rows, low_rows), low_rows)
+                pltpu.make_async_copy(ref, weights.at[slot, rows], weights_here.at[slot]).start()
+    pltpu.make_async_copy(signal, h_all.at[0], stream_here.at[0]).start()
     for i, ref in enumerate(taps):
         pltpu.make_async_copy(ref, tapped.at[i], tap_here).start()
-    start_streams(skip_cot, cot, stream_here.at[1])
-    start_streams(res_cot, g_all.at[layers], stream_here.at[2])
-    if last:
-        sums_copy = pltpu.make_async_copy(sums_in, sums, sums_here)
-        sums_copy.start()
-
-    wait_streams(h_all.at[0], stream_here.at[0])
+    pltpu.make_async_copy(res_cot, g_all.at[layers], stream_here.at[1]).start()
+
+    wait_bytes(h_all.at[0], stream_here.at[0])
     for k in range(layers):
-        pltpu.make_async_copy(weights.at[k], weights.at[k], weights_here.at[k]).wait()
+        if not last:
+            wait_bytes(weights.at[k], weights_here.at[k])
         if k == 0:
-            pltpu.make_async_copy(tapped, tapped, tap_here).wait()
+            wait_bytes(tapped, tap_here)
         for i in range(seqs):
             pre = narrow_dot(h_all[k, i], weights[k, :, now])
             if k == 0:
@@ -249,8 +245,7 @@
             for i in range(seqs):
                 stream = narrow_dot(gated_all[k, i], weights[k, :, res])
                 h_all[k + 1, i] = (h_all[k, i].astype(jnp.float32) + stream).astype(jnp.bfloat16)
-    wait_streams(cot, stream_here.at[1])
-    wait_streams(g_all.at[layers], stream_here.at[2])
+    wait_bytes(g_all.at[layers], stream_here.at[1])
     for i in range(seqs):
         total = narrow_dot(gated_all[0, i], weights[0, :, skip])
         for k in range(1, layers):
@@ -271,9 +266,7 @@
             g_all[k, i] = (g_all[k + 1, i].astype(jnp.float32) + below).astype(jnp.bfloat16)
     for i in range(seqs):
         pltpu.make_async_copy(g_all.at[section, i], grad_out.at[these[i]], grad_gone).start()
-    if last:
-        sums_copy.wait()
-    else:
+    if not last:
         back_out[...] = turned_dot(dz_all[0, 0], weights[0, :, tap]).astype(jnp.bfloat16)
     for i in range(seqs):
         products = (
@@ -284,32 +277,29 @@
         )
         spots = (slice(0, 2 * half), slice(2 * half, 4 * half), slice(4 * half, 4 * half + channels), slice(4 * half + channels, None))
         for spot, product in zip(spots, products):
-            if i == 0 and not last:
+            if i == 0 and last:
+                sums[:, spot] = sums_in[:, spot] + product
+            elif i == 0:
                 sums[:, spot] = product
             else:
                 sums[:, spot] += product
     if last:
         kept_out[...] = sums[pl.ds(pl.multiple_of(core * low_rows, low_rows), low_rows)]
         sent_out[...] = sums[pl.ds(pl.multiple_of((1 - core) * low_rows, low_rows), low_rows)].astype(jnp.bfloat16)
-    wait_streams(skip_total, skip_gone)
-    wait_streams(cot, grad_gone)
-
-
-def layer_stack(signal, skip_cot, res_cot, taps, own, mine, other, earlier=None):
-    number, seq_rows, channels = signal.shape
-    layers = len(mine) + 1
-    seqs = len(taps)
+    wait_bytes(skip_total, skip_gone)
+    wait_bytes(skip_total, grad_gone)
+
+
+def layer_stack(streams, taps, number, weights, earlier=None):
+    seqs, seq_rows, channels = streams[0].shape
+    layers = number
     last = earlier is not None
     width = 6 * channels
     anywhere = pl.BlockSpec(memory_space=pl.ANY)
-    far = pl.BlockSpec(memory_space=pltpu.HBM)
     near = pl.BlockSpec(memory_space=pltpu.VMEM)
-    stream = jax.ShapeDtypeStruct(signal.shape, jnp.bfloat16)
-    operands = [signal, skip_cot, res_cot, *taps, *own, *mine, *other]
+    stream = jax.ShapeDtypeStruct((number, seq_rows, channels), jnp.bfloat16)
     rows = lambda *shape: pltpu.VMEM((*shape, seqs, seq_rows, channels), jnp.bfloat16)
     scratch = [
-        pltpu.VMEM((layers, channels, width), jnp.bfloat16),
-        rows(),
         rows(),
         rows(layers),
         rows(layers),
@@ -318,35 +308,70 @@
         pltpu.VMEM((layers, seqs, seq_rows, channels), jnp.float32),
         pltpu.VMEM((layers, seqs, seq_rows, channels), jnp.float32),
         rows(),
-        pltpu.SemaphoreType.DMA((layers,)),
-        pltpu.SemaphoreType.DMA((3,)),
+        pltpu.SemaphoreType.DMA((2,)),
         pltpu.SemaphoreType.DMA,
         pltpu.SemaphoreType.DMA,
         pltpu.SemaphoreType.DMA,
     ]
-    in_specs = [far] * 3 + [anywhere] * (len(operands) - 3)
+    operands = [*streams, *taps, *weights]
+    in_specs = [near] * 3 + [anywhere] * len(taps) + [near if last else anywhere] * len(weights)
     aliases = {}
     if last:
         skip_total, grads, sums = earlier
-        in_specs += [anywhere, far, far]
         aliases = {len(operands) + 1: 0, len(operands) + 2: 1}
         operands += [sums, skip_total, grads]
+        in_specs += [near, anywhere, anywhere]
         shapes = [((channels // 2, width), jnp.bfloat16), ((channels // 2, width), jnp.float32)]
-        scratch += [pltpu.VMEM((channels, width), jnp.float32), pltpu.SemaphoreType.DMA]
+        scratch += [pltpu.VMEM((channels, width), jnp.float32)]
     else:
-        shapes = [((seq_rows, channels), jnp.bfloat16), ((channels, width), jnp.float32)]
+        shapes = [((seq_rows, channels), jnp.bfloat16), ((channels, width), jnp.float32), ((layers, channels, width), jnp.bfloat16)]
+        scratch += [pltpu.SemaphoreType.DMA((layers,))]
     flops = 2 * 22 * layers * seqs * seq_rows * channels * channels
     return pl.pallas_call(
         functools.partial(stack_kernel, layers, last),
         in_specs=in_specs,
-        out_specs=[far, far, near, near],
+        out_specs=[anywhere, anywhere] + [near] * len(shapes),
         out_shape=[stream, stream] + [jax.ShapeDtypeStruct(*shape) for shape in shapes],
         scratch_shapes=scratch,
         input_output_aliases=aliases,
-        compiler_params=pltpu.CompilerParams(vmem_limit_bytes=(48 if last else 24) * 2**20),
+        compiler_params=pltpu.CompilerParams(vmem_limit_bytes=(44 if last else 24) * 2**20),
         cost_estimate=pl.CostEstimate(flops=flops, bytes_accessed=16 * seqs * seq_rows * channels, transcendentals=0),
         name="layer_stack",
     )(*operands)
+
+
+def order_kernel(*refs):
+    count = (len(refs) - 1) // 3
+    sources, owns, others, sems = refs[:count], refs[count : 2 * count], refs[2 * count : 3 * count], refs[-1]
+    section = lax.axis_index("section")
+    copies = []
+    for i, source in enumerate(sources):
+        for by in range(source.shape[0]):
+            target = owns[i].at[0] if by == 0 else others[i].at[by - 1]
+            copies.append(pltpu.make_async_copy(source.at[jnp.bitwise_xor(section, by)], target, sems.at[i, by]))
+    for copy in copies:
+        copy.start()
+    for copy in copies:
+        copy.wait()
+
+
+def order_streams(*streams):
+    number, seq_rows, channels = streams[0].shape
+    count = len(streams)
+    anywhere = pl.BlockSpec(memory_space=pl.ANY)
+    near = pl.BlockSpec(memory_space=pltpu.VMEM)
+    shape = lambda seqs: jax.ShapeDtypeStruct((seqs, seq_rows, channels), jnp.bfloat16)
+    ordered = pl.pallas_call(
+        order_kernel,
+        in_specs=[anywhere] * count,
+        out_specs=[near] * 2 * count,
+        out_shape=[shape(1)] * count + [shape(number - 1)] * count,
+        scratch_shapes=[pltpu.SemaphoreType.DMA((count, number))],
+        compiler_params=pltpu.CompilerParams(vmem_limit_bytes=8 * 2**20),
+        cost_estimate=pl.CostEstimate(flops=0, bytes_accessed=2**24, transcendentals=0),
+        name="order_streams",
+    )(*streams)
+    return ordered[:count], ordered[count:]
 
 
 def spread_kernel(places, kept, got, own_out, *outs):
@@ -395,7 +420,11 @@
     return lax.ppermute(x, axis, [(i, i ^ by) for i in range(lax.axis_size(axis))])
 
 
-def sum_over_shards(sent, kept, places, scale):
+def between(x, shards, pairs, reached):
+    return lax.ppermute(x, ("section", "tm"), [(i * shards + t, j * shards + t) for i, j in pairs for t in reached])
+
+
+def sum_over_shards(sent, kept, places, scale, ready):
     rows, width = kept.shape
     piece = (rows // places, width)
     got = swapped(sent, "tm", 1)
@@ -406,11 +435,12 @@
     )
     arrived = [swapped(value, "tm", 2 * (by + 1)) for by, value in enumerate(pieces)]
     total = sum([value.astype(jnp.float32) for value in arrived], own).astype(jnp.bfloat16)
+    total, ready = lax.optimization_barrier((total, ready))
     by_distance = [total] + [swapped(total, "tm", 2 * by) for by in range(1, places)]
     other = swapped(jnp.stack(by_distance), "tm", 1)
     channels = width // 6
     out_shape = [jax.ShapeDtypeStruct((1, 2 * rows, cols), jnp.float32) for cols in (2 * channels, 2 * channels, channels, channels)]
-    return local_call(functools.partial(final_kernel, places, scale), "place_sums", by_distance + [other], out_shape)
+    return local_call(functools.partial(final_kernel, places, scale), "place_sums", by_distance + [other], out_shape), ready
 
 
 def stacked_body(signal, skip_cot, res_cot, w_tap, w_now, w_res, w_skip):
@@ -426,20 +456,21 @@
     half_rows = packed.shape[0] // 2
     own_half = lax.dynamic_slice_in_dim(packed, core * half_rows, half_rows, 0)
     mine = [swapped(own_half, "section", by) for by in range(1, sections)]
-    tap, mine = lax.optimization_barrier((tap, mine))
+    own_streams, other_streams = order_streams(signal, skip_cot, res_cot)
+    tap, mine, own_streams, other_streams = lax.optimization_barrier((tap, mine, own_streams, other_streams))
     other = [swapped(piece, "tm", 1) for piece in mine]
     taps = [tap] + [swapped(tap, "section", by) for by in range(1, sections)]
 
-    own = (w_now, w_res, w_skip, w_tap)
-    streams = (signal, skip_cot, res_cot)
-    skip_total, grads, back, sums = layer_stack(*streams, taps[:1], own, mine, other)
+    pieces = [w_now, w_res, w_skip, w_tap, *mine, *other]
+    skip_total, grads, back, sums, weights = layer_stack(own_streams, taps[:1], number, pieces)
     back = passed_along(back, "tm", -span)
-    skip_total, grads, sent, kept = layer_stack(*streams, taps[1:], own, mine, other, (skip_total, grads, sums))
+    skip_total, grads, sent, kept = layer_stack(other_streams, taps[1:], number, [weights], (skip_total, grads, sums))
     sent, back = lax.optimization_barrier((sent, back))
-    arrived = [lax.ppermute(back, "section", [(by, 0)]) for by in range(1, sections)]
+    reached = range(shards - span)
+    arrived = [between(back, shards, [(by, 0)], reached) for by in range(1, sections)]
+    grad_scale = 1.0 / math.sqrt(number * seq_rows * shards)
+    summed, arrived[::2] = sum_over_shards(sent, kept, shards // 2, grad_scale, arrived[::2])
     first = jnp.where(section == 0, back, jnp.zeros_like(back))
-    grad_scale = 1.0 / math.sqrt(number * seq_rows * shards)
-    summed = sum_over_shards(sent, kept, shards // 2, grad_scale)
     back_total = jnp.stack([first] + arrived).astype(jnp.float32)
     input_grads = (grads.astype(jnp.float32) + back_total).astype(jnp.bfloat16)
     return (skip_total, input_grads[None], *summed)

time: 89.3 us -> 83.5 us (0.935)
  local copies, waits for them, and re-layouts: 5.83 us -> 3.44 us
  waiting for transfers between devices: 33.5 us -> 31.6 us
  Pallas kernels: 18.4 us -> 16.9 us
    ppermute x2, waiting for transfers between devices: 8.38 us -> 3.09 us  [passed_along(): return lax.ppermute(x, axis, pairs)]
    ppermute x17, waiting for transfers between devices: 17.9 us -> 20.6 us  [swapped(): lax.ppermute(x, axis, [(i, i ^ by) for i in range(lax.axis_size(axis))])]
    unnamed x16 -> x14, local copies, waits for them, and re-layouts: 4.86 us -> 2.47 us
    pallas_call x2, Pallas kernels: 17.1 us -> 15.3 us  [layer_stack(): pl.pallas_call(functools.partial(stack_kernel, layers, last), in_specs=in...]
  transfers between devices with their start and end apart: 22 -> 22, of which waited for: 10 -> 12; matrix products, arithmetic and copies ran while one was open for 3% -> 3% of each run, Pallas kernels for 19% -> 19%
where the time goes in v3:
time: 83.5 us; the launch traced here: 83.1 us
  waiting for transfers between devices  31.6 us (38%)
  starting transfers between devices  27.7 us (33%)
  Pallas kernels  16.9 us (20%)
  local copies, waits for them, and re-layouts  3.44 us (4%)
  other arithmetic  2.52 us (3%)
  between operations  0.86 us (1%)
    ppermute x17, waiting for transfers between devices, swapped(): lax.ppermute(x, axis, [(i, i ^ by) for i in range(lax.axis_size(axis))])  20.6 us
    ppermute x17, starting transfers between devices, swapped(): lax.ppermute(x, axis, [(i, i ^ by) for i in range(lax.axis_size(axis))])  17.5 us
    pallas_call x2, Pallas kernels, layer_stack(): pl.pallas_call(functools.partial(stack_kernel, layers, last), in_specs=in...  15.3 us
    ppermute x3, waiting for transfers between devices, between(): lax.ppermute(x, ('section', 'tm'), [(i * shards + t, j * shards + t) for...  7.95 us
    ppermute x2, starting transfers between devices, passed_along(): return lax.ppermute(x, axis, pairs)  6.44 us
    ppermute x3, starting transfers between devices, between(): lax.ppermute(x, ('section', 'tm'), [(i * shards + t, j * shards + t) for...  3.85 us
    ppermute x2, waiting for transfers between devices, passed_along(): return lax.ppermute(x, axis, pairs)  3.09 us
    unnamed x14, local copies, waits for them, and re-layouts  2.47 us
  transfers between devices with their start and end apart: 22, of which 12 were waited for; matrix products, arithmetic and copies ran while one was open for 3% of the time, Pallas kernels for 19%

profile of v3, /device:TPU:0, one launch (start us, length us, event | category | flops | bytes accessed | tf_op | source)
XLA Modules:
  0.0 83.1 jit_solution(10781565715366101701)
XLA Ops:
  1.8 3.0 %collective-permute-start.1 = (bf16[128,1536]{1,0:T(8,128)(2,1)S(1)}, bf16[128,1536]{1,0:T(8,128)(2,1)S(1)}, u32[]{:S(2)}, u32[]{:S(2)}) collective-permute-start(bf16[128,1536]{1,0:T(8,128)(2,1)S(1)} %fusion.3), channel_id=1, source_target_pairs={{0,8},{8,0},{16,24},{24,16},{1,9},{9,1},{17,25},{25,17},{2,10},{10... | collective-permute-start | bytes 1179656 | tf_op jit(solution)/shard_map/ppermute | solution.py:420
  4.9 1.5 %collective-permute-start.2 = (bf16[128,1536]{1,0:T(8,128)(2,1)S(1)}, bf16[128,1536]{1,0:T(8,128)(2,1)S(1)}, u32[]{:S(2)}, u32[]{:S(2)}) collective-permute-start(bf16[128,1536]{1,0:T(8,128)(2,1)S(1)} %fusion.3), channel_id=1, source_target_pairs={{0,16},{8,24},{16,0},{24,8},{1,17},{9,25},{17,1},{25,9},{2,18},{10... | collective-permute-start | bytes 1179656 | tf_op jit(solution)/shard_map/ppermute | solution.py:420
  7.4 5.0 %collective-permute-start = (bf16[512,256]{1,0:T(8,128)(2,1)S(1)}, bf16[512,256]{1,0:T(8,128)(2,1)S(1)}, u32[]{:S(2)}, u32[]{:S(2)}) collective-permute-start(bf16[512,256]{1,0:T(8,128)(2,1)S(1)} %dynamic-slice_bitcast_fusion), channel_id=1, source_target_pairs={{0,4},{1,5},{2,6},{3,7},{8,12},{9,13},{10,14},{11,15},{16,20},{17,... | collective-permute-start | bytes 786440 | tf_op jit(solution)/shard_map/ppermute | solution.py:18
  15.2 1.9 %collective-permute-done.refs_3_ = bf16[512,256]{1,0:T(8,128)(2,1)S(1)} collective-permute-done((bf16[512,256]{1,0:T(8,128)(2,1)S(1)}, bf16[512,256]{1,0:T(8,128)(2,1)S(1)}, u32[]{:S(2)}, u32[]{:S(2)}) %collective-permute-start) | collective-permute-done | bytes 262176 | tf_op jit(solution)/shard_map/ppermute | solution.py:18
  17.1 6.8 %collective-permute-done.2.refs_9_ = bf16[128,1536]{1,0:T(8,128)(2,1)S(1)} collective-permute-done((bf16[128,1536]{1,0:T(8,128)(2,1)S(1)}, bf16[128,1536]{1,0:T(8,128)(2,1)S(1)}, u32[]{:S(2)}, u32[]{:S(2)}) %collective-permute-start.2) | collective-permute-done | bytes 393248 | tf_op jit(solution)/shard_map/ppermute | solution.py:420
  26.4 1.4 %collective-permute-start.6 = (bf16[512,256]{1,0:T(8,128)(2,1)S(1)}, bf16[512,256]{1,0:T(8,128)(2,1)S(1)}, u32[]{:S(2)}, u32[]{:S(2)}) collective-permute-start(bf16[512,256]{1,0:T(8,128)(2,1)S(1)} %collective-permute-done.refs_3_), channel_id=1, source_target_pairs={{0,24},{8,16},{16,8},{24,0},{1,25},{9,17},{17,9},{25,1},{2,26},{10... | collective-permute-start | bytes 786440 | tf_op jit(solution)/shard_map/ppermute | solution.py:420
  27.9 6.0 %layer_stack.2 = (bf16[4,512,256]{2,1,0:T(8,128)(2,1)}, bf16[4,512,256]{2,1,0:T(8,128)(2,1)S(1)}, bf16[512,256]{1,0:T(8,128)(2,1)S(1)}, f32[256,1536]{1,0:T(8,128)S(1)}, bf16[4,256,1536]{2,1,0:T(8,128)(2,1)S(1)}) custom-call(bf16[1,512,256]{2,1,0:T(8,128)(2,1)S(1)} %get-tuple-element.54.refs_0_, bf16[1,512,256]{2,1,0:T(8,128)(2,1)S(1)} %get-tuple-element.55.refs_1_, ...), custom_call_target="tpu_custom_call" | custom-call | flops 5905580032 | bytes 2097152 | tf_op jit(solution)/shard_map/layer_stack/pallas_call | solution.py:330
  33.9 1.5 %collective-permute-start.10 = (bf16[512,256]{1,0:T(8,128)(2,1)S(1)}, bf16[512,256]{1,0:T(8,128)(2,1)S(1)}, u32[]{:S(2)}, u32[]{:S(2)}) collective-permute-start(bf16[512,256]{1,0:T(8,128)(2,1)S(1)} %get-tuple-element.67), channel_id=1, source_target_pairs={{4,0},{5,1},{6,2},{7,3},{12,8},{13,9},{14,10},{15,11},{20,16},{21,... | collective-permute-start | bytes 786440 | tf_op jit(solution)/shard_map/ppermute | solution.py:18
  35.4 2.7 %collective-permute-done.5.refs_4_ = bf16[512,256]{1,0:T(8,128)(2,1)S(1)} collective-permute-done((bf16[512,256]{1,0:T(8,128)(2,1)S(1)}, bf16[512,256]{1,0:T(8,128)(2,1)S(1)}, u32[]{:S(2)}, u32[]{:S(2)}) %collective-permute-start.5) | collective-permute-done | bytes 262176 | tf_op jit(solution)/shard_map/ppermute | solution.py:420
  38.0 1.6 %collective-permute-done.6.refs_5_ = bf16[512,256]{1,0:T(8,128)(2,1)S(1)} collective-permute-done((bf16[512,256]{1,0:T(8,128)(2,1)S(1)}, bf16[512,256]{1,0:T(8,128)(2,1)S(1)}, u32[]{:S(2)}, u32[]{:S(2)}) %collective-permute-start.6) | collective-permute-done | bytes 262176 | tf_op jit(solution)/shard_map/ppermute | solution.py:420
  39.7 9.3 %layer_stack.3 = (bf16[4,512,256]{2,1,0:T(8,128)(2,1)}, bf16[4,512,256]{2,1,0:T(8,128)(2,1)S(1)}, bf16[128,1536]{1,0:T(8,128)(2,1)S(1)}, f32[128,1536]{1,0:T(8,128)S(1)}) custom-call(bf16[3,512,256]{2,1,0:T(8,128)(2,1)S(1)} %get-tuple-element.50.refs_0_, ...), custom_call_target="tpu_custom_call", output_to_operand_aliasing={{0}: (8, {}), {1}: (9, {})} | custom-call | flops 17716740096 | bytes 6291456 | tf_op jit(solution)/shard_map/layer_stack/pallas_call | solution.py:330
  50.2 1.7 %collective-permute-done.11.got = bf16[128,1536]{1,0:T(8,128)(2,1)S(1)} collective-permute-done((bf16[128,1536]{1,0:T(8,128)(2,1)S(1)}, bf16[128,1536]{1,0:T(8,128)(2,1)S(1)}, u32[]{:S(2)}, u32[]{:S(2)}) %collective-permute-start.11) | collective-permute-done | bytes 393248 | tf_op jit(solution)/shard_map/ppermute | solution.py:420
  52.5 2.6 %collective-permute-start.13 = (bf16[32,1536]{1,0:T(8,128)(2,1)S(1)}, bf16[32,1536]{1,0:T(8,128)(2,1)S(1)}, u32[]{:S(2)}, u32[]{:S(2)}) collective-permute-start(bf16[32,1536]{1,0:T(8,128)(2,1)S(1)} %get-tuple-element.73), channel_id=1, source_target_pairs={{0,4},{1,5},{2,6},{3,7},{4,0},{5,1},{6,2},{7,3},{8,12},{9,13},{10,... | collective-permute-start | bytes 294920 | tf_op jit(solution)/shard_map/ppermute | solution.py:420
  55.1 1.3 %collective-permute-start.14 = (bf16[32,1536]{1,0:T(8,128)(2,1)S(1)}, bf16[32,1536]{1,0:T(8,128)(2,1)S(1)}, u32[]{:S(2)}, u32[]{:S(2)}) collective-permute-start(bf16[32,1536]{1,0:T(8,128)(2,1)S(1)} %get-tuple-element.74), channel_id=1, source_target_pairs={{0,6},{1,7},{2,4},{3,5},{4,2},{5,3},{6,0},{7,1},{8,14},{9,15},{10,... | collective-permute-start | bytes 294920 | tf_op jit(solution)/shard_map/ppermute | solution.py:420
  56.4 1.3 %collective-permute-start.15 = (bf16[512,256]{1,0:T(8,128)(2,1)S(1)}, bf16[512,256]{1,0:T(8,128)(2,1)S(1)}, u32[]{:S(2)}, u32[]{:S(2)}) collective-permute-start(bf16[512,256]{1,0:T(8,128)(2,1)S(1)} %collective-permute-done.10), channel_id=1, source_target_pairs={{8,0},{9,1},{10,2},{11,3}} | collective-permute-start | bytes 786440 | tf_op jit(solution)/shard_map/ppermute | solution.py:424
  57.7 1.3 %collective-permute-start.16 = (bf16[512,256]{1,0:T(8,128)(2,1)S(1)}, bf16[512,256]{1,0:T(8,128)(2,1)S(1)}, u32[]{:S(2)}, u32[]{:S(2)}) collective-permute-start(bf16[512,256]{1,0:T(8,128)(2,1)S(1)} %collective-permute-done.10), channel_id=1, source_target_pairs={{24,0},{25,1},{26,2},{27,3}} | collective-permute-start | bytes 786440 | tf_op jit(solution)/shard_map/ppermute | solution.py:424
  59.0 4.2 %collective-permute-done.13 = bf16[32,1536]{1,0:T(8,128)(2,1)S(1)} collective-permute-done((bf16[32,1536]{1,0:T(8,128)(2,1)S(1)}, bf16[32,1536]{1,0:T(8,128)(2,1)S(1)}, u32[]{:S(2)}, u32[]{:S(2)}) %collective-permute-start.13) | collective-permute-done | bytes 98336 | tf_op jit(solution)/shard_map/ppermute | solution.py:420
  63.2 2.6 %collective-permute-done.15 = bf16[512,256]{1,0:T(8,128)(2,1)S(1)} collective-permute-done((bf16[512,256]{1,0:T(8,128)(2,1)S(1)}, bf16[512,256]{1,0:T(8,128)(2,1)S(1)}, u32[]{:S(2)}, u32[]{:S(2)}) %collective-permute-start.15) | collective-permute-done | bytes 262176 | tf_op jit(solution)/shard_map/ppermute | solution.py:424
  65.8 2.2 %collective-permute-done.16 = bf16[512,256]{1,0:T(8,128)(2,1)S(1)} collective-permute-done((bf16[512,256]{1,0:T(8,128)(2,1)S(1)}, bf16[512,256]{1,0:T(8,128)(2,1)S(1)}, u32[]{:S(2)}, u32[]{:S(2)}) %collective-permute-start.16) | collective-permute-done | bytes 262176 | tf_op jit(solution)/shard_map/ppermute | solution.py:424
  68.0 4.4 %collective-permute-start.20 = (bf16[32,1536]{1,0:T(8,128)(2,1)S(1)}, bf16[32,1536]{1,0:T(8,128)(2,1)S(1)}, u32[]{:S(2)}, u32[]{:S(2)}) collective-permute-start(bf16[32,1536]{1,0:T(8,128)(2,1)S(1)} %add_convert_fusion.1.refs_0_), channel_id=1, source_target_pairs={{0,6},{1,7},{2,4},{3,5},{4,2},{5,3},{6,0},{7,1},{8,14},{9,15},{10,... | collective-permute-start | bytes 294920 | tf_op jit(solution)/shard_map/ppermute | solution.py:420
  72.4 1.3 %collective-permute-start.17 = (bf16[512,256]{1,0:T(8,128)(2,1)S(1)}, bf16[512,256]{1,0:T(8,128)(2,1)S(1)}, u32[]{:S(2)}, u32[]{:S(2)}) collective-permute-start(bf16[512,256]{1,0:T(8,128)(2,1)S(1)} %collective-permute-done.10), channel_id=1, source_target_pairs={{16,0},{17,1},{18,2},{19,3}} | collective-permute-start | bytes 786440 | tf_op jit(solution)/shard_map/ppermute | solution.py:424
  74.0 3.3 %collective-permute-done.19.refs_2_ = bf16[32,1536]{1,0:T(8,128)(2,1)S(1)} collective-permute-done((bf16[32,1536]{1,0:T(8,128)(2,1)S(1)}, bf16[32,1536]{1,0:T(8,128)(2,1)S(1)}, u32[]{:S(2)}, u32[]{:S(2)}) %collective-permute-start.19) | collective-permute-done | bytes 98336 | tf_op jit(solution)/shard_map/ppermute | solution.py:420
  77.5 3.2 %collective-permute-done.17 = bf16[512,256]{1,0:T(8,128)(2,1)S(1)} collective-permute-done((bf16[512,256]{1,0:T(8,128)(2,1)S(1)}, bf16[512,256]{1,0:T(8,128)(2,1)S(1)}, u32[]{:S(2)}, u32[]{:S(2)}) %collective-permute-start.17) | collective-permute-done | bytes 262176 | tf_op jit(solution)/shard_map/ppermute | solution.py:424
  81.9 1.3 %place_sums.1 = (f32[1,256,512]{2,1,0:T(8,128)}, f32[1,256,512]{2,1,0:T(8,128)}, f32[1,256,256]{2,1,0:T(8,128)}, f32[1,256,256]{2,1,0:T(8,128)}) custom-call(bf16[32,1536]{1,0:T(8,128)(2,1)S(1)} %add_convert_fusion.1.refs_0_, bf16[32,1536]{1,0:T(8,128)(2,1)S(1)} %collective-permute-done.18.refs_1_, bf16[32,1536]{1,0:T(8,128)(2,1)S(1)} %collective-permute-done.19.refs_2_, ...), custom_call_target="tpu_custom_call" | custom-call | tf_op jit(solution)/shard_map/place_sums/pallas_call | solution.py:409
  (45 shorter events, 11.1 us)
Async XLA Ops:
  0.7 27.2 %copy-start.5 = (bf16[1,256,256]{2,1,0:T(8,128)(2,1)S(1)}, bf16[1,256,256]{2,1,0:T(8,128)(2,1)}, u32[]{:S(2)}) copy-start(bf16[1,256,256]{2,1,0:T(8,128)(2,1)} %refs_5_.1) | copy-start | bytes 393220
  1.8 26.1 %copy-start.3 = (bf16[1,256,512]{2,1,0:T(8,128)(2,1)S(1)}, bf16[1,256,512]{2,1,0:T(8,128)(2,1)}, u32[]{:S(2)}) copy-start(bf16[1,256,512]{2,1,0:T(8,128)(2,1)} %refs_4_.1) | copy-start | bytes 786436
  1.8 15.2 %collective-permute-start.1 = (bf16[128,1536]{1,0:T(8,128)(2,1)S(1)}, bf16[128,1536]{1,0:T(8,128)(2,1)S(1)}, u32[]{:S(2)}, u32[]{:S(2)}) collective-permute-start(bf16[128,1536]{1,0:T(8,128)(2,1)S(1)} %fusion.3), channel_id=1, source_target_pairs={{0,8},{8,0},{16,24},{24,16},{1,9},{9,1},{17,25},{25,17},{2,10},{10... | collective-permute-start | bytes 1179656 | tf_op jit(solution)/shard_map/ppermute | solution.py:420
  4.9 19.0 %collective-permute-start.2 = (bf16[128,1536]{1,0:T(8,128)(2,1)S(1)}, bf16[128,1536]{1,0:T(8,128)(2,1)S(1)}, u32[]{:S(2)}, u32[]{:S(2)}) collective-permute-start(bf16[128,1536]{1,0:T(8,128)(2,1)S(1)} %fusion.3), channel_id=1, source_target_pairs={{0,16},{8,24},{16,0},{24,8},{1,17},{9,25},{17,1},{25,9},{2,18},{10... | collective-permute-start | bytes 1179656 | tf_op jit(solution)/shard_map/ppermute | solution.py:420
  6.4 17.5 %collective-permute-start.3 = (bf16[128,1536]{1,0:T(8,128)(2,1)S(1)}, bf16[128,1536]{1,0:T(8,128)(2,1)S(1)}, u32[]{:S(2)}, u32[]{:S(2)}) collective-permute-start(bf16[128,1536]{1,0:T(8,128)(2,1)S(1)} %fusion.3), channel_id=1, source_target_pairs={{0,24},{8,16},{16,8},{24,0},{1,25},{9,17},{17,9},{25,1},{2,26},{10... | collective-permute-start | bytes 1179656 | tf_op jit(solution)/shard_map/ppermute | solution.py:420
  7.4 9.7 %collective-permute-start = (bf16[512,256]{1,0:T(8,128)(2,1)S(1)}, bf16[512,256]{1,0:T(8,128)(2,1)S(1)}, u32[]{:S(2)}, u32[]{:S(2)}) collective-permute-start(bf16[512,256]{1,0:T(8,128)(2,1)S(1)} %dynamic-slice_bitcast_fusion), channel_id=1, source_target_pairs={{0,4},{1,5},{2,6},{3,7},{8,12},{9,13},{10,14},{11,15},{16,20},{17,... | collective-permute-start | bytes 786440 | tf_op jit(solution)/shard_map/ppermute | solution.py:18
  23.9 2.6 %collective-permute-start.7 = (bf16[128,1536]{1,0:T(8,128)(2,1)S(1)}, bf16[128,1536]{1,0:T(8,128)(2,1)S(1)}, u32[]{:S(2)}, u32[]{:S(2)}) collective-permute-start(bf16[128,1536]{1,0:T(8,128)(2,1)S(1)} %collective-permute-done.1.refs_8_), channel_id=1, source_target_pairs={{0,1},{1,0},{2,3},{3,2},{4,5},{5,4},{6,7},{7,6},{8,9},{9,8},{10,11... | collective-permute-start | bytes 1179656 | tf_op jit(solution)/shard_map/ppermute | solution.py:420
  23.9 4.0 %collective-permute-start.8 = (bf16[128,1536]{1,0:T(8,128)(2,1)S(1)}, bf16[128,1536]{1,0:T(8,128)(2,1)S(1)}, u32[]{:S(2)}, u32[]{:S(2)}) collective-permute-start(bf16[128,1536]{1,0:T(8,128)(2,1)S(1)} %collective-permute-done.2.refs_9_), channel_id=1, source_target_pairs={{0,1},{1,0},{2,3},{3,2},{4,5},{5,4},{6,7},{7,6},{8,9},{9,8},{10,11... | collective-permute-start | bytes 1179656 | tf_op jit(solution)/shard_map/ppermute | solution.py:420
  24.4 3.5 %collective-permute-start.9 = (bf16[128,1536]{1,0:T(8,128)(2,1)S(1)}, bf16[128,1536]{1,0:T(8,128)(2,1)S(1)}, u32[]{:S(2)}, u32[]{:S(2)}) collective-permute-start(bf16[128,1536]{1,0:T(8,128)(2,1)S(1)} %collective-permute-done.3.refs_10_), channel_id=1, source_target_pairs={{0,1},{1,0},{2,3},{3,2},{4,5},{5,4},{6,7},{7,6},{8,9},{9,8},{10,11... | collective-permute-start | bytes 1179656 | tf_op jit(solution)/shard_map/ppermute | solution.py:420
  24.4 11.0 %collective-permute-start.4 = (bf16[512,256]{1,0:T(8,128)(2,1)S(1)}, bf16[512,256]{1,0:T(8,128)(2,1)S(1)}, u32[]{:S(2)}, u32[]{:S(2)}) collective-permute-start(bf16[512,256]{1,0:T(8,128)(2,1)S(1)} %collective-permute-done.refs_3_), channel_id=1, source_target_pairs={{0,8},{8,0},{16,24},{24,16},{1,9},{9,1},{17,25},{25,17},{2,10},{10... | collective-permute-start | bytes 786440 | tf_op jit(solution)/shard_map/ppermute | solution.py:420
  25.6 12.4 %collective-permute-start.5 = (bf16[512,256]{1,0:T(8,128)(2,1)S(1)}, bf16[512,256]{1,0:T(8,128)(2,1)S(1)}, u32[]{:S(2)}, u32[]{:S(2)}) collective-permute-start(bf16[512,256]{1,0:T(8,128)(2,1)S(1)} %collective-permute-done.refs_3_), channel_id=1, source_target_pairs={{0,16},{8,24},{16,0},{24,8},{1,17},{9,25},{17,1},{25,9},{2,18},{10... | collective-permute-start | bytes 786440 | tf_op jit(solution)/shard_map/ppermute | solution.py:420
  26.4 13.2 %collective-permute-start.6 = (bf16[512,256]{1,0:T(8,128)(2,1)S(1)}, bf16[512,256]{1,0:T(8,128)(2,1)S(1)}, u32[]{:S(2)}, u32[]{:S(2)}) collective-permute-start(bf16[512,256]{1,0:T(8,128)(2,1)S(1)} %collective-permute-done.refs_3_), channel_id=1, source_target_pairs={{0,24},{8,16},{16,8},{24,0},{1,25},{9,17},{17,9},{25,1},{2,26},{10... | collective-permute-start | bytes 786440 | tf_op jit(solution)/shard_map/ppermute | solution.py:420
  33.9 16.3 %collective-permute-start.10 = (bf16[512,256]{1,0:T(8,128)(2,1)S(1)}, bf16[512,256]{1,0:T(8,128)(2,1)S(1)}, u32[]{:S(2)}, u32[]{:S(2)}) collective-permute-start(bf16[512,256]{1,0:T(8,128)(2,1)S(1)} %get-tuple-element.67), channel_id=1, source_target_pairs={{4,0},{5,1},{6,2},{7,3},{12,8},{13,9},{14,10},{15,11},{20,16},{21,... | collective-permute-start | bytes 786440 | tf_op jit(solution)/shard_map/ppermute | solution.py:18
  50.2 1.7 %collective-permute-start.11 = (bf16[128,1536]{1,0:T(8,128)(2,1)S(1)}, bf16[128,1536]{1,0:T(8,128)(2,1)S(1)}, u32[]{:S(2)}, u32[]{:S(2)}) collective-permute-start(bf16[128,1536]{1,0:T(8,128)(2,1)S(1)} %get-tuple-element.70), channel_id=1, source_target_pairs={{0,1},{1,0},{2,3},{3,2},{4,5},{5,4},{6,7},{7,6},{8,9},{9,8},{10,11... | collective-permute-start | bytes 1179656 | tf_op jit(solution)/shard_map/ppermute | solution.py:420
  52.0 7.0 %collective-permute-start.12 = (bf16[32,1536]{1,0:T(8,128)(2,1)S(1)}, bf16[32,1536]{1,0:T(8,128)(2,1)S(1)}, u32[]{:S(2)}, u32[]{:S(2)}) collective-permute-start(bf16[32,1536]{1,0:T(8,128)(2,1)S(1)} %get-tuple-element.72), channel_id=1, source_target_pairs={{0,2},{1,3},{2,0},{3,1},{4,6},{5,7},{6,4},{7,5},{8,10},{9,11},{10,... | collective-permute-start | bytes 294920 | tf_op jit(solution)/shard_map/ppermute | solution.py:420
  52.5 10.7 %collective-permute-start.13 = (bf16[32,1536]{1,0:T(8,128)(2,1)S(1)}, bf16[32,1536]{1,0:T(8,128)(2,1)S(1)}, u32[]{:S(2)}, u32[]{:S(2)}) collective-permute-start(bf16[32,1536]{1,0:T(8,128)(2,1)S(1)} %get-tuple-element.73), channel_id=1, source_target_pairs={{0,4},{1,5},{2,6},{3,7},{4,0},{5,1},{6,2},{7,3},{8,12},{9,13},{10,... | collective-permute-start | bytes 294920 | tf_op jit(solution)/shard_map/ppermute | solution.py:420
  55.1 8.1 %collective-permute-start.14 = (bf16[32,1536]{1,0:T(8,128)(2,1)S(1)}, bf16[32,1536]{1,0:T(8,128)(2,1)S(1)}, u32[]{:S(2)}, u32[]{:S(2)}) collective-permute-start(bf16[32,1536]{1,0:T(8,128)(2,1)S(1)} %get-tuple-element.74), channel_id=1, source_target_pairs={{0,6},{1,7},{2,4},{3,5},{4,2},{5,3},{6,0},{7,1},{8,14},{9,15},{10,... | collective-permute-start | bytes 294920 | tf_op jit(solution)/shard_map/ppermute | solution.py:420
  56.4 9.4 %collective-permute-start.15 = (bf16[512,256]{1,0:T(8,128)(2,1)S(1)}, bf16[512,256]{1,0:T(8,128)(2,1)S(1)}, u32[]{:S(2)}, u32[]{:S(2)}) collective-permute-start(bf16[512,256]{1,0:T(8,128)(2,1)S(1)} %collective-permute-done.10), channel_id=1, source_target_pairs={{8,0},{9,1},{10,2},{11,3}} | collective-permute-start | bytes 786440 | tf_op jit(solution)/shard_map/ppermute | solution.py:424
  57.7 10.3 %collective-permute-start.16 = (bf16[512,256]{1,0:T(8,128)(2,1)S(1)}, bf16[512,256]{1,0:T(8,128)(2,1)S(1)}, u32[]{:S(2)}, u32[]{:S(2)}) collective-permute-start(bf16[512,256]{1,0:T(8,128)(2,1)S(1)} %collective-permute-done.10), channel_id=1, source_target_pairs={{24,0},{25,1},{26,2},{27,3}} | collective-permute-start | bytes 786440 | tf_op jit(solution)/shard_map/ppermute | solution.py:424
  68.0 6.0 %collective-permute-start.18 = (bf16[32,1536]{1,0:T(8,128)(2,1)S(1)}, bf16[32,1536]{1,0:T(8,128)(2,1)S(1)}, u32[]{:S(2)}, u32[]{:S(2)}) collective-permute-start(bf16[32,1536]{1,0:T(8,128)(2,1)S(1)} %add_convert_fusion.1.refs_0_), channel_id=1, source_target_pairs={{0,2},{1,3},{2,0},{3,1},{4,6},{5,7},{6,4},{7,5},{8,10},{9,11},{10,... | collective-permute-start | bytes 294920 | tf_op jit(solution)/shard_map/ppermute | solution.py:420
  68.0 9.3 %collective-permute-start.19 = (bf16[32,1536]{1,0:T(8,128)(2,1)S(1)}, bf16[32,1536]{1,0:T(8,128)(2,1)S(1)}, u32[]{:S(2)}, u32[]{:S(2)}) collective-permute-start(bf16[32,1536]{1,0:T(8,128)(2,1)S(1)} %add_convert_fusion.1.refs_0_), channel_id=1, source_target_pairs={{0,4},{1,5},{2,6},{3,7},{4,0},{5,1},{6,2},{7,3},{8,12},{9,13},{10,... | collective-permute-start | bytes 294920 | tf_op jit(solution)/shard_map/ppermute | solution.py:420
  68.0 9.3 %collective-permute-start.20 = (bf16[32,1536]{1,0:T(8,128)(2,1)S(1)}, bf16[32,1536]{1,0:T(8,128)(2,1)S(1)}, u32[]{:S(2)}, u32[]{:S(2)}) collective-permute-start(bf16[32,1536]{1,0:T(8,128)(2,1)S(1)} %add_convert_fusion.1.refs_0_), channel_id=1, source_target_pairs={{0,6},{1,7},{2,4},{3,5},{4,2},{5,3},{6,0},{7,1},{8,14},{9,15},{10,... | collective-permute-start | bytes 294920 | tf_op jit(solution)/shard_map/ppermute | solution.py:420
  72.4 8.3 %collective-permute-start.17 = (bf16[512,256]{1,0:T(8,128)(2,1)S(1)}, bf16[512,256]{1,0:T(8,128)(2,1)S(1)}, u32[]{:S(2)}, u32[]{:S(2)}) collective-permute-start(bf16[512,256]{1,0:T(8,128)(2,1)S(1)} %collective-permute-done.10), channel_id=1, source_target_pairs={{16,0},{17,1},{18,2},{19,3}} | collective-permute-start | bytes 786440 | tf_op jit(solution)/shard_map/ppermute | solution.py:424
  77.3 4.5 %collective-permute-start.21 = (bf16[4,32,1536]{2,1,0:T(8,128)(2,1)S(1)}, bf16[4,32,1536]{2,1,0:T(8,128)(2,1)S(1)}, u32[]{:S(2)}, u32[]{:S(2)}) collective-permute-start(bf16[4,32,1536]{2,1,0:T(8,128)(2,1)S(1)} %pad_maximum_fusion), channel_id=1, source_target_pairs={{0,1},{1,0},{2,3},{3,2},{4,5},{5,4},{6,7},{7,6},{8,9},{9,8},{10,11... | collective-permute-start | bytes 1179656 | tf_op jit(solution)/shard_map/ppermute | solution.py:420
  (5 other events, 53.3 us)

commit v4 on v3

--- a/solution.py
+++ b/solution.py
@@ -404,14 +404,27 @@
                 column += width
 
 
-def local_call(kernel, name, operands, out_shape):
+def add_kernel(grads, *refs):
+    *backs, out = refs
+    own = jnp.where(lax.axis_index("section") == 0, 1.0, 0.0)
+    for i, back in enumerate(backs):
+        term = back[...].astype(jnp.float32)
+        out[i] = (grads[i].astype(jnp.float32) + (term * own if i == 0 else term)).astype(jnp.bfloat16)
+
+
+def add_back(grads, backs):
+    return local_call(add_kernel, "add_back", [grads, *backs], [grads], 2**24)[0]
+
+
+def local_call(kernel, name, operands, out_shape, weight=0):
     near = pl.BlockSpec(memory_space=pltpu.VMEM)
     return pl.pallas_call(
         kernel,
         in_specs=[near] * len(operands),
         out_specs=[near] * len(out_shape),
-        out_shape=out_shape,
+        out_shape=[jax.ShapeDtypeStruct(value.shape, value.dtype) for value in out_shape],
         compiler_params=pltpu.CompilerParams(vmem_limit_bytes=12 * 2**20),
+        cost_estimate=pl.CostEstimate(flops=0, bytes_accessed=weight, transcendentals=0) if weight else None,
         name=name,
     )(*operands)
 
@@ -424,7 +437,7 @@
     return lax.ppermute(x, ("section", "tm"), [(i * shards + t, j * shards + t) for i, j in pairs for t in reached])
 
 
-def sum_over_shards(sent, kept, places, scale, ready):
+def sum_over_shards(sent, kept, places, scale, beside):
     rows, width = kept.shape
     piece = (rows // places, width)
     got = swapped(sent, "tm", 1)
@@ -435,12 +448,12 @@
     )
     arrived = [swapped(value, "tm", 2 * (by + 1)) for by, value in enumerate(pieces)]
     total = sum([value.astype(jnp.float32) for value in arrived], own).astype(jnp.bfloat16)
-    total, ready = lax.optimization_barrier((total, ready))
     by_distance = [total] + [swapped(total, "tm", 2 * by) for by in range(1, places)]
+    by_distance, beside = lax.optimization_barrier((by_distance, beside))
     other = swapped(jnp.stack(by_distance), "tm", 1)
     channels = width // 6
     out_shape = [jax.ShapeDtypeStruct((1, 2 * rows, cols), jnp.float32) for cols in (2 * channels, 2 * channels, channels, channels)]
-    return local_call(functools.partial(final_kernel, places, scale), "place_sums", by_distance + [other], out_shape), ready
+    return local_call(functools.partial(final_kernel, places, scale), "place_sums", by_distance + [other], out_shape), beside
 
 
 def stacked_body(signal, skip_cot, res_cot, w_tap, w_now, w_res, w_skip):
@@ -469,10 +482,8 @@
     reached = range(shards - span)
     arrived = [between(back, shards, [(by, 0)], reached) for by in range(1, sections)]
     grad_scale = 1.0 / math.sqrt(number * seq_rows * shards)
-    summed, arrived[::2] = sum_over_shards(sent, kept, shards // 2, grad_scale, arrived[::2])
-    first = jnp.where(section == 0, back, jnp.zeros_like(back))
-    back_total = jnp.stack([first] + arrived).astype(jnp.float32)
-    input_grads = (grads.astype(jnp.float32) + back_total).astype(jnp.bfloat16)
+    input_grads = add_back(grads, [back, *arrived])
+    summed, input_grads = sum_over_shards(sent, kept, shards // 2, grad_scale, input_grads)
     return (skip_total, input_grads[None], *summed)
 
 

time: 83.5 us -> 78 us (0.934)
  waiting for transfers between devices: 31.6 us -> 24.9 us
  Pallas kernels: 16.9 us -> 18.2 us
  other arithmetic: 2.52 us -> 1.23 us
  local copies, waits for them, and re-layouts: 3.44 us -> 4.65 us
    ppermute x3, waiting for transfers between devices: 7.95 us -> 5.04 us  [between(): lax.ppermute(x, ('section', 'tm'), [(i * shards + t, j * shards + t) for...]
    ppermute x17, waiting for transfers between devices: 20.6 us -> 18 us  [swapped(): lax.ppermute(x, axis, [(i, i ^ by) for i in range(lax.axis_size(axis))])]
    broadcast_in_dim x1 -> x0, other arithmetic: 1.25 us -> none  [stacked_body(): return (skip_total, input_grads[None], *summed)]
    pallas_call x2 -> x3, Pallas kernels: 1.32 us -> 2.55 us  [local_call(): pl.pallas_call(kernel, in_specs=[near] * len(operands), out_specs=[near]...]
    unnamed x14, local copies, waits for them, and re-layouts: 2.47 us -> 3.69 us
    ppermute x2, waiting for transfers between devices: 3.09 us -> 1.88 us  [passed_along(): return lax.ppermute(x, axis, pairs)]
  transfers between devices with their start and end apart: 22 -> 22, of which waited for: 12 -> 10; matrix products, arithmetic and copies ran while one was open for 3% -> 1% of each run, Pallas kernels for 19% -> 22%
where the time goes in v4:
time: 78 us; the launch traced here: 77.6 us
  starting transfers between devices  27.8 us (36%)
  waiting for transfers between devices  24.9 us (32%)
  Pallas kernels  18.2 us (23%)
  local copies, waits for them, and re-layouts  4.65 us (6%)
  other arithmetic  1.23 us (2%)
  between operations  0.84 us (1%)
    ppermute x17, waiting for transfers between devices, swapped(): lax.ppermute(x, axis, [(i, i ^ by) for i in range(lax.axis_size(axis))])  18 us
    ppermute x17, starting transfers between devices, swapped(): lax.ppermute(x, axis, [(i, i ^ by) for i in range(lax.axis_size(axis))])  17.5 us
    pallas_call x2, Pallas kernels, layer_stack(): pl.pallas_call(functools.partial(stack_kernel, layers, last), in_specs=in...  15.3 us
    ppermute x2, starting transfers between devices, passed_along(): return lax.ppermute(x, axis, pairs)  6.44 us
    ppermute x3, waiting for transfers between devices, between(): lax.ppermute(x, ('section', 'tm'), [(i * shards + t, j * shards + t) for...  5.04 us
    ppermute x3, starting transfers between devices, between(): lax.ppermute(x, ('section', 'tm'), [(i * shards + t, j * shards + t) for...  3.86 us
    unnamed x14, local copies, waits for them, and re-layouts  3.69 us
    pallas_call x3, Pallas kernels, local_call(): pl.pallas_call(kernel, in_specs=[near] * len(operands), out_specs=[near]...  2.55 us
  transfers between devices with their start and end apart: 22, of which 10 were waited for; matrix products, arithmetic and copies ran while one was open for 1% of the time, Pallas kernels for 22%

profile of v4, /device:TPU:0, one launch (start us, length us, event | category | flops | bytes accessed | tf_op | source)
XLA Modules:
  0.0 77.6 jit_solution(14395111651714568993)
XLA Ops:
  1.8 3.0 %collective-permute-start.1 = (bf16[128,1536]{1,0:T(8,128)(2,1)S(1)}, bf16[128,1536]{1,0:T(8,128)(2,1)S(1)}, u32[]{:S(2)}, u32[]{:S(2)}) collective-permute-start(bf16[128,1536]{1,0:T(8,128)(2,1)S(1)} %fusion.2), channel_id=1, source_target_pairs={{0,8},{8,0},{16,24},{24,16},{1,9},{9,1},{17,25},{25,17},{2,10},{10... | collective-permute-start | bytes 1179656 | tf_op jit(solution)/shard_map/ppermute | solution.py:433
  4.8 1.5 %collective-permute-start.2 = (bf16[128,1536]{1,0:T(8,128)(2,1)S(1)}, bf16[128,1536]{1,0:T(8,128)(2,1)S(1)}, u32[]{:S(2)}, u32[]{:S(2)}) collective-permute-start(bf16[128,1536]{1,0:T(8,128)(2,1)S(1)} %fusion.2), channel_id=1, source_target_pairs={{0,16},{8,24},{16,0},{24,8},{1,17},{9,25},{17,1},{25,9},{2,18},{10... | collective-permute-start | bytes 1179656 | tf_op jit(solution)/shard_map/ppermute | solution.py:433
  7.3 5.0 %collective-permute-start = (bf16[512,256]{1,0:T(8,128)(2,1)S(1)}, bf16[512,256]{1,0:T(8,128)(2,1)S(1)}, u32[]{:S(2)}, u32[]{:S(2)}) collective-permute-start(bf16[512,256]{1,0:T(8,128)(2,1)S(1)} %dynamic-slice_bitcast_fusion), channel_id=1, source_target_pairs={{0,4},{1,5},{2,6},{3,7},{8,12},{9,13},{10,14},{11,15},{16,20},{17,... | collective-permute-start | bytes 786440 | tf_op jit(solution)/shard_map/ppermute | solution.py:18
  17.0 6.8 %collective-permute-done.2.refs_9_ = bf16[128,1536]{1,0:T(8,128)(2,1)S(1)} collective-permute-done((bf16[128,1536]{1,0:T(8,128)(2,1)S(1)}, bf16[128,1536]{1,0:T(8,128)(2,1)S(1)}, u32[]{:S(2)}, u32[]{:S(2)}) %collective-permute-start.2) | collective-permute-done | bytes 393248 | tf_op jit(solution)/shard_map/ppermute | solution.py:433
  26.4 1.4 %collective-permute-start.6 = (bf16[512,256]{1,0:T(8,128)(2,1)S(1)}, bf16[512,256]{1,0:T(8,128)(2,1)S(1)}, u32[]{:S(2)}, u32[]{:S(2)}) collective-permute-start(bf16[512,256]{1,0:T(8,128)(2,1)S(1)} %collective-permute-done.refs_3_), channel_id=1, source_target_pairs={{0,24},{8,16},{16,8},{24,0},{1,25},{9,17},{17,9},{25,1},{2,26},{10... | collective-permute-start | bytes 786440 | tf_op jit(solution)/shard_map/ppermute | solution.py:433
  27.9 6.0 %layer_stack.2 = (bf16[4,512,256]{2,1,0:T(8,128)(2,1)}, bf16[4,512,256]{2,1,0:T(8,128)(2,1)S(1)}, bf16[512,256]{1,0:T(8,128)(2,1)S(1)}, f32[256,1536]{1,0:T(8,128)S(1)}, bf16[4,256,1536]{2,1,0:T(8,128)(2,1)S(1)}) custom-call(bf16[1,512,256]{2,1,0:T(8,128)(2,1)S(1)} %get-tuple-element.56.refs_0_, bf16[1,512,256]{2,1,0:T(8,128)(2,1)S(1)} %get-tuple-element.57.refs_1_, ...), custom_call_target="tpu_custom_call" | custom-call | flops 5905580032 | bytes 2097152 | tf_op jit(solution)/shard_map/layer_stack/pallas_call | solution.py:330
  33.8 1.5 %collective-permute-start.10 = (bf16[512,256]{1,0:T(8,128)(2,1)S(1)}, bf16[512,256]{1,0:T(8,128)(2,1)S(1)}, u32[]{:S(2)}, u32[]{:S(2)}) collective-permute-start(bf16[512,256]{1,0:T(8,128)(2,1)S(1)} %get-tuple-element.69), channel_id=1, source_target_pairs={{4,0},{5,1},{6,2},{7,3},{12,8},{13,9},{14,10},{15,11},{20,16},{21,... | collective-permute-start | bytes 786440 | tf_op jit(solution)/shard_map/ppermute | solution.py:18
  35.3 2.7 %collective-permute-done.5.refs_4_ = bf16[512,256]{1,0:T(8,128)(2,1)S(1)} collective-permute-done((bf16[512,256]{1,0:T(8,128)(2,1)S(1)}, bf16[512,256]{1,0:T(8,128)(2,1)S(1)}, u32[]{:S(2)}, u32[]{:S(2)}) %collective-permute-start.5) | collective-permute-done | bytes 262176 | tf_op jit(solution)/shard_map/ppermute | solution.py:433
  38.0 1.6 %collective-permute-done.6.refs_5_ = bf16[512,256]{1,0:T(8,128)(2,1)S(1)} collective-permute-done((bf16[512,256]{1,0:T(8,128)(2,1)S(1)}, bf16[512,256]{1,0:T(8,128)(2,1)S(1)}, u32[]{:S(2)}, u32[]{:S(2)}) %collective-permute-start.6) | collective-permute-done | bytes 262176 | tf_op jit(solution)/shard_map/ppermute | solution.py:433
  39.6 9.3 %layer_stack.3 = (bf16[4,512,256]{2,1,0:T(8,128)(2,1)}, bf16[4,512,256]{2,1,0:T(8,128)(2,1)S(1)}, bf16[128,1536]{1,0:T(8,128)(2,1)S(1)}, f32[128,1536]{1,0:T(8,128)S(1)}) custom-call(bf16[3,512,256]{2,1,0:T(8,128)(2,1)S(1)} %get-tuple-element.52.refs_0_, ...), custom_call_target="tpu_custom_call", output_to_operand_aliasing={{0}: (8, {}), {1}: (9, {})} | custom-call | flops 17716740096 | bytes 6291456 | tf_op jit(solution)/shard_map/layer_stack/pallas_call | solution.py:330
  50.1 1.7 %collective-permute-done.11.got = bf16[128,1536]{1,0:T(8,128)(2,1)S(1)} collective-permute-done((bf16[128,1536]{1,0:T(8,128)(2,1)S(1)}, bf16[128,1536]{1,0:T(8,128)(2,1)S(1)}, u32[]{:S(2)}, u32[]{:S(2)}) %collective-permute-start.11) | collective-permute-done | bytes 393248 | tf_op jit(solution)/shard_map/ppermute | solution.py:433
  52.5 2.6 %collective-permute-start.13 = (bf16[32,1536]{1,0:T(8,128)(2,1)S(1)}, bf16[32,1536]{1,0:T(8,128)(2,1)S(1)}, u32[]{:S(2)}, u32[]{:S(2)}) collective-permute-start(bf16[32,1536]{1,0:T(8,128)(2,1)S(1)} %get-tuple-element.73), channel_id=1, source_target_pairs={{0,4},{1,5},{2,6},{3,7},{4,0},{5,1},{6,2},{7,3},{8,12},{9,13},{10,... | collective-permute-start | bytes 294920 | tf_op jit(solution)/shard_map/ppermute | solution.py:433
  55.1 1.3 %collective-permute-start.14 = (bf16[32,1536]{1,0:T(8,128)(2,1)S(1)}, bf16[32,1536]{1,0:T(8,128)(2,1)S(1)}, u32[]{:S(2)}, u32[]{:S(2)}) collective-permute-start(bf16[32,1536]{1,0:T(8,128)(2,1)S(1)} %get-tuple-element.74), channel_id=1, source_target_pairs={{0,6},{1,7},{2,4},{3,5},{4,2},{5,3},{6,0},{7,1},{8,14},{9,15},{10,... | collective-permute-start | bytes 294920 | tf_op jit(solution)/shard_map/ppermute | solution.py:433
  56.4 1.3 %collective-permute-start.18 = (bf16[512,256]{1,0:T(8,128)(2,1)S(1)}, bf16[512,256]{1,0:T(8,128)(2,1)S(1)}, u32[]{:S(2)}, u32[]{:S(2)}) collective-permute-start(bf16[512,256]{1,0:T(8,128)(2,1)S(1)} %collective-permute-done.10.refs_0_), channel_id=1, source_target_pairs={{8,0},{9,1},{10,2},{11,3}} | collective-permute-start | bytes 786440 | tf_op jit(solution)/shard_map/ppermute | solution.py:437
  57.7 1.3 %collective-permute-start.19 = (bf16[512,256]{1,0:T(8,128)(2,1)S(1)}, bf16[512,256]{1,0:T(8,128)(2,1)S(1)}, u32[]{:S(2)}, u32[]{:S(2)}) collective-permute-start(bf16[512,256]{1,0:T(8,128)(2,1)S(1)} %collective-permute-done.10.refs_0_), channel_id=1, source_target_pairs={{16,0},{17,1},{18,2},{19,3}} | collective-permute-start | bytes 786440 | tf_op jit(solution)/shard_map/ppermute | solution.py:437
  59.0 1.3 %collective-permute-start.20 = (bf16[512,256]{1,0:T(8,128)(2,1)S(1)}, bf16[512,256]{1,0:T(8,128)(2,1)S(1)}, u32[]{:S(2)}, u32[]{:S(2)}) collective-permute-start(bf16[512,256]{1,0:T(8,128)(2,1)S(1)} %collective-permute-done.10.refs_0_), channel_id=1, source_target_pairs={{24,0},{25,1},{26,2},{27,3}} | collective-permute-start | bytes 786440 | tf_op jit(solution)/shard_map/ppermute | solution.py:437
  60.3 2.9 %collective-permute-done.13 = bf16[32,1536]{1,0:T(8,128)(2,1)S(1)} collective-permute-done((bf16[32,1536]{1,0:T(8,128)(2,1)S(1)}, bf16[32,1536]{1,0:T(8,128)(2,1)S(1)}, u32[]{:S(2)}, u32[]{:S(2)}) %collective-permute-start.13) | collective-permute-done | bytes 98336 | tf_op jit(solution)/shard_map/ppermute | solution.py:433
  63.2 1.8 %collective-permute-start.15 = (bf16[32,1536]{1,0:T(8,128)(2,1)S(1)}, bf16[32,1536]{1,0:T(8,128)(2,1)S(1)}, u32[]{:S(2)}, u32[]{:S(2)}) collective-permute-start(bf16[32,1536]{1,0:T(8,128)(2,1)S(1)} %add_convert_fusion.refs_0_), channel_id=1, source_target_pairs={{0,2},{1,3},{2,0},{3,1},{4,6},{5,7},{6,4},{7,5},{8,10},{9,11},{10,... | collective-permute-start | bytes 294920 | tf_op jit(solution)/shard_map/ppermute | solution.py:433
  65.0 1.4 %collective-permute-start.16 = (bf16[32,1536]{1,0:T(8,128)(2,1)S(1)}, bf16[32,1536]{1,0:T(8,128)(2,1)S(1)}, u32[]{:S(2)}, u32[]{:S(2)}) collective-permute-start(bf16[32,1536]{1,0:T(8,128)(2,1)S(1)} %add_convert_fusion.refs_0_), channel_id=1, source_target_pairs={{0,4},{1,5},{2,6},{3,7},{4,0},{5,1},{6,2},{7,3},{8,12},{9,13},{10,... | collective-permute-start | bytes 294920 | tf_op jit(solution)/shard_map/ppermute | solution.py:433
  66.4 1.2 %collective-permute-start.17 = (bf16[32,1536]{1,0:T(8,128)(2,1)S(1)}, bf16[32,1536]{1,0:T(8,128)(2,1)S(1)}, u32[]{:S(2)}, u32[]{:S(2)}) collective-permute-start(bf16[32,1536]{1,0:T(8,128)(2,1)S(1)} %add_convert_fusion.refs_0_), channel_id=1, source_target_pairs={{0,6},{1,7},{2,4},{3,5},{4,2},{5,3},{6,0},{7,1},{8,14},{9,15},{10,... | collective-permute-start | bytes 294920 | tf_op jit(solution)/shard_map/ppermute | solution.py:433
  67.7 5.0 %collective-permute-done.19.refs_2_ = bf16[512,256]{1,0:T(8,128)(2,1)S(1)} collective-permute-done((bf16[512,256]{1,0:T(8,128)(2,1)S(1)}, bf16[512,256]{1,0:T(8,128)(2,1)S(1)}, u32[]{:S(2)}, u32[]{:S(2)}) %collective-permute-start.19) | collective-permute-done | bytes 262176 | tf_op jit(solution)/shard_map/ppermute | solution.py:437
  72.7 1.2 %add_back.1 = bf16[4,512,256]{2,1,0:T(8,128)(2,1)} custom-call(bf16[4,512,256]{2,1,0:T(8,128)(2,1)S(1)} %get-tuple-element.75.grads, bf16[512,256]{1,0:T(8,128)(2,1)S(1)} %collective-permute-done.10.refs_0_, bf16[512,256]{1,0:T(8,128)(2,1)S(1)} %collective-permute-done.18.refs_1_, bf16[512,256]{1,0:T(8,128)(2,1)S(1)} %collective-permute-done.19.refs_2_, ...), custom_call_target="tpu_custom_call" | custom-call | bytes 16777216 | tf_op jit(solution)/shard_map/add_back/pallas_call | solution.py:421
  74.6 1.7 %collective-permute-done.21.refs_4_ = bf16[4,32,1536]{2,1,0:T(8,128)(2,1)S(1)} collective-permute-done((bf16[4,32,1536]{2,1,0:T(8,128)(2,1)S(1)}, bf16[4,32,1536]{2,1,0:T(8,128)(2,1)S(1)}, u32[]{:S(2)}, u32[]{:S(2)}) %collective-permute-start.21) | collective-permute-done | bytes 393248 | tf_op jit(solution)/shard_map/ppermute | solution.py:433
  76.3 1.3 %place_sums.1 = (f32[1,256,512]{2,1,0:T(8,128)}, f32[1,256,512]{2,1,0:T(8,128)}, f32[1,256,256]{2,1,0:T(8,128)}, f32[1,256,256]{2,1,0:T(8,128)}) custom-call(bf16[32,1536]{1,0:T(8,128)(2,1)S(1)} %add_convert_fusion.refs_0_, bf16[32,1536]{1,0:T(8,128)(2,1)S(1)} %collective-permute-done.15.refs_1_, bf16[32,1536]{1,0:T(8,128)(2,1)S(1)} %collective-permute-done.16.refs_2_, ...), custom_call_target="tpu_custom_call" | custom-call | tf_op jit(solution)/shard_map/place_sums/pallas_call | solution.py:421
  (44 shorter events, 12.0 us)
Async XLA Ops:
  0.6 27.2 %copy-start.3 = (bf16[1,256,512]{2,1,0:T(8,128)(2,1)S(1)}, bf16[1,256,512]{2,1,0:T(8,128)(2,1)}, u32[]{:S(2)}) copy-start(bf16[1,256,512]{2,1,0:T(8,128)(2,1)} %refs_4_.1) | copy-start | bytes 786436
  0.6 27.2 %copy-start.5 = (bf16[1,256,256]{2,1,0:T(8,128)(2,1)S(1)}, bf16[1,256,256]{2,1,0:T(8,128)(2,1)}, u32[]{:S(2)}) copy-start(bf16[1,256,256]{2,1,0:T(8,128)(2,1)} %refs_5_.1) | copy-start | bytes 393220
  1.8 15.2 %collective-permute-start.1 = (bf16[128,1536]{1,0:T(8,128)(2,1)S(1)}, bf16[128,1536]{1,0:T(8,128)(2,1)S(1)}, u32[]{:S(2)}, u32[]{:S(2)}) collective-permute-start(bf16[128,1536]{1,0:T(8,128)(2,1)S(1)} %fusion.2), channel_id=1, source_target_pairs={{0,8},{8,0},{16,24},{24,16},{1,9},{9,1},{17,25},{25,17},{2,10},{10... | collective-permute-start | bytes 1179656 | tf_op jit(solution)/shard_map/ppermute | solution.py:433
  4.8 19.0 %collective-permute-start.2 = (bf16[128,1536]{1,0:T(8,128)(2,1)S(1)}, bf16[128,1536]{1,0:T(8,128)(2,1)S(1)}, u32[]{:S(2)}, u32[]{:S(2)}) collective-permute-start(bf16[128,1536]{1,0:T(8,128)(2,1)S(1)} %fusion.2), channel_id=1, source_target_pairs={{0,16},{8,24},{16,0},{24,8},{1,17},{9,25},{17,1},{25,9},{2,18},{10... | collective-permute-start | bytes 1179656 | tf_op jit(solution)/shard_map/ppermute | solution.py:433
  6.3 17.5 %collective-permute-start.3 = (bf16[128,1536]{1,0:T(8,128)(2,1)S(1)}, bf16[128,1536]{1,0:T(8,128)(2,1)S(1)}, u32[]{:S(2)}, u32[]{:S(2)}) collective-permute-start(bf16[128,1536]{1,0:T(8,128)(2,1)S(1)} %fusion.2), channel_id=1, source_target_pairs={{0,24},{8,16},{16,8},{24,0},{1,25},{9,17},{17,9},{25,1},{2,26},{10... | collective-permute-start | bytes 1179656 | tf_op jit(solution)/shard_map/ppermute | solution.py:433
  7.3 9.7 %collective-permute-start = (bf16[512,256]{1,0:T(8,128)(2,1)S(1)}, bf16[512,256]{1,0:T(8,128)(2,1)S(1)}, u32[]{:S(2)}, u32[]{:S(2)}) collective-permute-start(bf16[512,256]{1,0:T(8,128)(2,1)S(1)} %dynamic-slice_bitcast_fusion), channel_id=1, source_target_pairs={{0,4},{1,5},{2,6},{3,7},{8,12},{9,13},{10,14},{11,15},{16,20},{17,... | collective-permute-start | bytes 786440 | tf_op jit(solution)/shard_map/ppermute | solution.py:18
  23.8 2.6 %collective-permute-start.7 = (bf16[128,1536]{1,0:T(8,128)(2,1)S(1)}, bf16[128,1536]{1,0:T(8,128)(2,1)S(1)}, u32[]{:S(2)}, u32[]{:S(2)}) collective-permute-start(bf16[128,1536]{1,0:T(8,128)(2,1)S(1)} %collective-permute-done.1.refs_8_), channel_id=1, source_target_pairs={{0,1},{1,0},{2,3},{3,2},{4,5},{5,4},{6,7},{7,6},{8,9},{9,8},{10,11... | collective-permute-start | bytes 1179656 | tf_op jit(solution)/shard_map/ppermute | solution.py:433
  23.8 4.0 %collective-permute-start.8 = (bf16[128,1536]{1,0:T(8,128)(2,1)S(1)}, bf16[128,1536]{1,0:T(8,128)(2,1)S(1)}, u32[]{:S(2)}, u32[]{:S(2)}) collective-permute-start(bf16[128,1536]{1,0:T(8,128)(2,1)S(1)} %collective-permute-done.2.refs_9_), channel_id=1, source_target_pairs={{0,1},{1,0},{2,3},{3,2},{4,5},{5,4},{6,7},{7,6},{8,9},{9,8},{10,11... | collective-permute-start | bytes 1179656 | tf_op jit(solution)/shard_map/ppermute | solution.py:433
  24.3 3.5 %collective-permute-start.9 = (bf16[128,1536]{1,0:T(8,128)(2,1)S(1)}, bf16[128,1536]{1,0:T(8,128)(2,1)S(1)}, u32[]{:S(2)}, u32[]{:S(2)}) collective-permute-start(bf16[128,1536]{1,0:T(8,128)(2,1)S(1)} %collective-permute-done.3.refs_10_), channel_id=1, source_target_pairs={{0,1},{1,0},{2,3},{3,2},{4,5},{5,4},{6,7},{7,6},{8,9},{9,8},{10,11... | collective-permute-start | bytes 1179656 | tf_op jit(solution)/shard_map/ppermute | solution.py:433
  24.3 11.0 %collective-permute-start.4 = (bf16[512,256]{1,0:T(8,128)(2,1)S(1)}, bf16[512,256]{1,0:T(8,128)(2,1)S(1)}, u32[]{:S(2)}, u32[]{:S(2)}) collective-permute-start(bf16[512,256]{1,0:T(8,128)(2,1)S(1)} %collective-permute-done.refs_3_), channel_id=1, source_target_pairs={{0,8},{8,0},{16,24},{24,16},{1,9},{9,1},{17,25},{25,17},{2,10},{10... | collective-permute-start | bytes 786440 | tf_op jit(solution)/shard_map/ppermute | solution.py:433
  25.6 12.4 %collective-permute-start.5 = (bf16[512,256]{1,0:T(8,128)(2,1)S(1)}, bf16[512,256]{1,0:T(8,128)(2,1)S(1)}, u32[]{:S(2)}, u32[]{:S(2)}) collective-permute-start(bf16[512,256]{1,0:T(8,128)(2,1)S(1)} %collective-permute-done.refs_3_), channel_id=1, source_target_pairs={{0,16},{8,24},{16,0},{24,8},{1,17},{9,25},{17,1},{25,9},{2,18},{10... | collective-permute-start | bytes 786440 | tf_op jit(solution)/shard_map/ppermute | solution.py:433
  26.4 13.2 %collective-permute-start.6 = (bf16[512,256]{1,0:T(8,128)(2,1)S(1)}, bf16[512,256]{1,0:T(8,128)(2,1)S(1)}, u32[]{:S(2)}, u32[]{:S(2)}) collective-permute-start(bf16[512,256]{1,0:T(8,128)(2,1)S(1)} %collective-permute-done.refs_3_), channel_id=1, source_target_pairs={{0,24},{8,16},{16,8},{24,0},{1,25},{9,17},{17,9},{25,1},{2,26},{10... | collective-permute-start | bytes 786440 | tf_op jit(solution)/shard_map/ppermute | solution.py:433
  33.8 16.3 %collective-permute-start.10 = (bf16[512,256]{1,0:T(8,128)(2,1)S(1)}, bf16[512,256]{1,0:T(8,128)(2,1)S(1)}, u32[]{:S(2)}, u32[]{:S(2)}) collective-permute-start(bf16[512,256]{1,0:T(8,128)(2,1)S(1)} %get-tuple-element.69), channel_id=1, source_target_pairs={{4,0},{5,1},{6,2},{7,3},{12,8},{13,9},{14,10},{15,11},{20,16},{21,... | collective-permute-start | bytes 786440 | tf_op jit(solution)/shard_map/ppermute | solution.py:18
  50.1 1.7 %collective-permute-start.11 = (bf16[128,1536]{1,0:T(8,128)(2,1)S(1)}, bf16[128,1536]{1,0:T(8,128)(2,1)S(1)}, u32[]{:S(2)}, u32[]{:S(2)}) collective-permute-start(bf16[128,1536]{1,0:T(8,128)(2,1)S(1)} %get-tuple-element.70), channel_id=1, source_target_pairs={{0,1},{1,0},{2,3},{3,2},{4,5},{5,4},{6,7},{7,6},{8,9},{9,8},{10,11... | collective-permute-start | bytes 1179656 | tf_op jit(solution)/shard_map/ppermute | solution.py:433
  51.9 7.0 %collective-permute-start.12 = (bf16[32,1536]{1,0:T(8,128)(2,1)S(1)}, bf16[32,1536]{1,0:T(8,128)(2,1)S(1)}, u32[]{:S(2)}, u32[]{:S(2)}) collective-permute-start(bf16[32,1536]{1,0:T(8,128)(2,1)S(1)} %get-tuple-element.72), channel_id=1, source_target_pairs={{0,2},{1,3},{2,0},{3,1},{4,6},{5,7},{6,4},{7,5},{8,10},{9,11},{10,... | collective-permute-start | bytes 294920 | tf_op jit(solution)/shard_map/ppermute | solution.py:433
  52.5 10.7 %collective-permute-start.13 = (bf16[32,1536]{1,0:T(8,128)(2,1)S(1)}, bf16[32,1536]{1,0:T(8,128)(2,1)S(1)}, u32[]{:S(2)}, u32[]{:S(2)}) collective-permute-start(bf16[32,1536]{1,0:T(8,128)(2,1)S(1)} %get-tuple-element.73), channel_id=1, source_target_pairs={{0,4},{1,5},{2,6},{3,7},{4,0},{5,1},{6,2},{7,3},{8,12},{9,13},{10,... | collective-permute-start | bytes 294920 | tf_op jit(solution)/shard_map/ppermute | solution.py:433
  55.1 8.1 %collective-permute-start.14 = (bf16[32,1536]{1,0:T(8,128)(2,1)S(1)}, bf16[32,1536]{1,0:T(8,128)(2,1)S(1)}, u32[]{:S(2)}, u32[]{:S(2)}) collective-permute-start(bf16[32,1536]{1,0:T(8,128)(2,1)S(1)} %get-tuple-element.74), channel_id=1, source_target_pairs={{0,6},{1,7},{2,4},{3,5},{4,2},{5,3},{6,0},{7,1},{8,14},{9,15},{10,... | collective-permute-start | bytes 294920 | tf_op jit(solution)/shard_map/ppermute | solution.py:433
  56.4 10.0 %collective-permute-start.18 = (bf16[512,256]{1,0:T(8,128)(2,1)S(1)}, bf16[512,256]{1,0:T(8,128)(2,1)S(1)}, u32[]{:S(2)}, u32[]{:S(2)}) collective-permute-start(bf16[512,256]{1,0:T(8,128)(2,1)S(1)} %collective-permute-done.10.refs_0_), channel_id=1, source_target_pairs={{8,0},{9,1},{10,2},{11,3}} | collective-permute-start | bytes 786440 | tf_op jit(solution)/shard_map/ppermute | solution.py:437
  57.7 15.0 %collective-permute-start.19 = (bf16[512,256]{1,0:T(8,128)(2,1)S(1)}, bf16[512,256]{1,0:T(8,128)(2,1)S(1)}, u32[]{:S(2)}, u32[]{:S(2)}) collective-permute-start(bf16[512,256]{1,0:T(8,128)(2,1)S(1)} %collective-permute-done.10.refs_0_), channel_id=1, source_target_pairs={{16,0},{17,1},{18,2},{19,3}} | collective-permute-start | bytes 786440 | tf_op jit(solution)/shard_map/ppermute | solution.py:437
  59.0 13.7 %collective-permute-start.20 = (bf16[512,256]{1,0:T(8,128)(2,1)S(1)}, bf16[512,256]{1,0:T(8,128)(2,1)S(1)}, u32[]{:S(2)}, u32[]{:S(2)}) collective-permute-start(bf16[512,256]{1,0:T(8,128)(2,1)S(1)} %collective-permute-done.10.refs_0_), channel_id=1, source_target_pairs={{24,0},{25,1},{26,2},{27,3}} | collective-permute-start | bytes 786440 | tf_op jit(solution)/shard_map/ppermute | solution.py:437
  63.2 10.7 %collective-permute-start.15 = (bf16[32,1536]{1,0:T(8,128)(2,1)S(1)}, bf16[32,1536]{1,0:T(8,128)(2,1)S(1)}, u32[]{:S(2)}, u32[]{:S(2)}) collective-permute-start(bf16[32,1536]{1,0:T(8,128)(2,1)S(1)} %add_convert_fusion.refs_0_), channel_id=1, source_target_pairs={{0,2},{1,3},{2,0},{3,1},{4,6},{5,7},{6,4},{7,5},{8,10},{9,11},{10,... | collective-permute-start | bytes 294920 | tf_op jit(solution)/shard_map/ppermute | solution.py:433
  65.0 9.5 %collective-permute-start.16 = (bf16[32,1536]{1,0:T(8,128)(2,1)S(1)}, bf16[32,1536]{1,0:T(8,128)(2,1)S(1)}, u32[]{:S(2)}, u32[]{:S(2)}) collective-permute-start(bf16[32,1536]{1,0:T(8,128)(2,1)S(1)} %add_convert_fusion.refs_0_), channel_id=1, source_target_pairs={{0,4},{1,5},{2,6},{3,7},{4,0},{5,1},{6,2},{7,3},{8,12},{9,13},{10,... | collective-permute-start | bytes 294920 | tf_op jit(solution)/shard_map/ppermute | solution.py:433
  66.4 8.1 %collective-permute-start.17 = (bf16[32,1536]{1,0:T(8,128)(2,1)S(1)}, bf16[32,1536]{1,0:T(8,128)(2,1)S(1)}, u32[]{:S(2)}, u32[]{:S(2)}) collective-permute-start(bf16[32,1536]{1,0:T(8,128)(2,1)S(1)} %add_convert_fusion.refs_0_), channel_id=1, source_target_pairs={{0,6},{1,7},{2,4},{3,5},{4,2},{5,3},{6,0},{7,1},{8,14},{9,15},{10,... | collective-permute-start | bytes 294920 | tf_op jit(solution)/shard_map/ppermute | solution.py:433
  74.6 1.8 %collective-permute-start.21 = (bf16[4,32,1536]{2,1,0:T(8,128)(2,1)S(1)}, bf16[4,32,1536]{2,1,0:T(8,128)(2,1)S(1)}, u32[]{:S(2)}, u32[]{:S(2)}) collective-permute-start(bf16[4,32,1536]{2,1,0:T(8,128)(2,1)S(1)} %pad_maximum_fusion), channel_id=1, source_target_pairs={{0,1},{1,0},{2,3},{3,2},{4,5},{5,4},{6,7},{7,6},{8,9},{9,8},{10,11... | collective-permute-start | bytes 1179656 | tf_op jit(solution)/shard_map/ppermute | solution.py:433
  (5 other events, 58.1 us)

commit v5 on v4

--- a/solution.py
+++ b/solution.py
@@ -180,25 +180,56 @@
     return lax.dot_general(left, right, (((1,), (1,)), ((), ())), preferred_element_type=jnp.float32)
 
 
+def skip_sum(gated, weights, columns):
+    total = narrow_dot(gated[0], weights[0, :, columns])
+    for k in range(1, len(gated)):
+        total = total + narrow_dot(gated[k], weights[k, :, columns])
+    return total.astype(jnp.bfloat16)
+
+
+def finish_kernel(own_skip, gated_all, dz_all, g_all, weights, skip_out, base_out):
+    section = lax.axis_index("section")
+    layers, seqs, _, channels = gated_all.shape
+    skip_out[section] = own_skip[...]
+    above = jnp.maximum(section, 1)
+    lowest = section == 0
+    for i in range(seqs):
+        at = jnp.bitwise_xor(section, i + 1)
+        skip_out[at] = skip_sum([gated_all[k, i] for k in range(layers)], weights, slice(3 * channels, 4 * channels))
+        below = turned_dot(dz_all[0, i], weights[0, :, : 2 * channels])
+        base_out[i] = g_all[above, i].astype(jnp.float32) + jnp.where(lowest, below, 0.0)
+
+
+def finish(own_skip, gated_all, dz_all, g_all, weights):
+    layers, seqs, seq_rows, channels = gated_all.shape
+    out_shape = [
+        jax.ShapeDtypeStruct((layers, seq_rows, channels), jnp.bfloat16),
+        jax.ShapeDtypeStruct((seqs, seq_rows, channels), jnp.float32),
+    ]
+    return local_call(finish_kernel, "finish", [own_skip, gated_all, dz_all, g_all, weights], out_shape)
+
+
 def stack_kernel(layers, last, *refs):
     refs = list(refs)
     take = lambda count: [refs.pop(0) for _ in range(count)]
     signal, cot, res_cot = take(3)
     taps = take(layers - 1 if last else 1)
     if last:
-        weights, sums_in, _, _ = take(4)
-        skip_out, grad_out, sent_out, kept_out = take(4)
+        weights, sums_in, ahead_pre, ahead_du = take(4)
+        gated_all, dz_all, g_all, *sent_outs, kept_out = take(6)
     else:
         own = take(4)
         mine = take(layers - 1)
         other = take(layers - 1)
-        skip_out, grad_out, back_out, sums, weights = take(5)
-    tapped, h_all, gated_all, dz_all, g_all, tanh_all, sig_all, skip_total = take(8)
-    stream_here, tap_here, skip_gone, grad_gone = take(4)
+        next_signal, next_cot = take(2)
+        skip_out, grad_out, back_out, sums, weights, ahead_pre, ahead_du = take(7)
+    early = layers - ahead_du.shape[0]
+    tapped, h_all, tanh_all, sig_all = take(4)
+    stream_here, tap_here = take(2)
     if last:
         (sums,) = take(1)
     else:
-        (weights_here,) = take(1)
+        gated_all, dz_all, g_all, weights_here = take(4)
     section = lax.axis_index("section")
     core = lax.rem(lax.axis_index("tm"), 2)
     _, seqs, seq_rows, channels = h_all.shape
@@ -208,8 +239,6 @@
     skip = slice(2 * half + channels, 2 * half + 2 * channels)
     tap = slice(2 * half + 2 * channels, 4 * half + 2 * channels)
     low_rows = channels // 2
-    these = [jnp.bitwise_xor(section, i + 1) if last else section for i in range(seqs)]
-
     def wait_bytes(target, there):
         pltpu.make_async_copy(target, target, there).wait()
 
@@ -233,40 +262,47 @@
         if k == 0:
             wait_bytes(tapped, tap_here)
         for i in range(seqs):
-            pre = narrow_dot(h_all[k, i], weights[k, :, now])
-            if k == 0:
-                pre = pre + narrow_dot(tapped[i], weights[0, :, tap])
+            if k == 0 and last:
+                pre = ahead_pre[i] + narrow_dot(tapped[i], weights[0, :, tap])
+            else:
+                pre = narrow_dot(h_all[k, i], weights[k, :, now])
+                if k == 0:
+                    pre = pre + narrow_dot(tapped[i], weights[0, :, tap])
             tanh_part = jnp.tanh(pre[:, :half])
             sig_part = 0.5 * jnp.tanh(0.5 * pre[:, half:]) + 0.5
             tanh_all[k, i] = tanh_part
             sig_all[k, i] = sig_part
             gated_all[k, i] = (tanh_part * sig_part).astype(jnp.bfloat16)
+        if k == 0 and not last:
+            for i in range(layers - 1):
+                ahead_pre[i] = narrow_dot(next_signal[i], weights[0, :, now])
         if k + 1 < layers:
             for i in range(seqs):
                 stream = narrow_dot(gated_all[k, i], weights[k, :, res])
                 h_all[k + 1, i] = (h_all[k, i].astype(jnp.float32) + stream).astype(jnp.bfloat16)
     wait_bytes(g_all.at[layers], stream_here.at[1])
-    for i in range(seqs):
-        total = narrow_dot(gated_all[0, i], weights[0, :, skip])
-        for k in range(1, layers):
-            total = total + narrow_dot(gated_all[k, i], weights[k, :, skip])
-        skip_total[i] = total.astype(jnp.bfloat16)
-    for i in range(seqs):
-        pltpu.make_async_copy(skip_total.at[i], skip_out.at[these[i]], skip_gone).start()
+    if not last:
+        skip_out[...] = skip_sum([gated_all[k, 0] for k in range(layers)], weights, skip)
     for k in reversed(range(layers)):
         for i in range(seqs):
-            du = turned_dot(g_all[k + 1, i], weights[k, :, res]) + turned_dot(cot[i], weights[k, :, skip])
+            du = turned_dot(g_all[k + 1, i], weights[k, :, res])
+            if last and k >= early:
+                du = du + ahead_du[k - early, i]
+            else:
+                du = du + turned_dot(cot[i], weights[k, :, skip])
             tanh_part = tanh_all[k, i]
             sig_part = sig_all[k, i]
             scaled = du * sig_part
             dz_all[k, i, :, :half] = (scaled * (1.0 - tanh_part * tanh_part)).astype(jnp.bfloat16)
             dz_all[k, i, :, half:] = (scaled * (tanh_part * (1.0 - sig_part))).astype(jnp.bfloat16)
-        for i in range(seqs):
+        if k >= early and not last:
+            for i in range(layers - 1):
+                ahead_du[k - early, i] = turned_dot(next_cot[i], weights[k, :, skip])
+        for i in range(seqs if k or not last else 0):
             below = turned_dot(dz_all[k, i], weights[k, :, now])
             g_all[k, i] = (g_all[k + 1, i].astype(jnp.float32) + below).astype(jnp.bfloat16)
-    for i in range(seqs):
-        pltpu.make_async_copy(g_all.at[section, i], grad_out.at[these[i]], grad_gone).start()
     if not last:
+        grad_out[...] = g_all[section, 0]
         back_out[...] = turned_dot(dz_all[0, 0], weights[0, :, tap]).astype(jnp.bfloat16)
     for i in range(seqs):
         products = (
@@ -285,56 +321,52 @@
                 sums[:, spot] += product
     if last:
         kept_out[...] = sums[pl.ds(pl.multiple_of(core * low_rows, low_rows), low_rows)]
-        sent_out[...] = sums[pl.ds(pl.multiple_of((1 - core) * low_rows, low_rows), low_rows)].astype(jnp.bfloat16)
-    wait_bytes(skip_total, skip_gone)
-    wait_bytes(skip_total, grad_gone)
-
-
-def layer_stack(streams, taps, number, weights, earlier=None):
+        sent_rows = low_rows // len(sent_outs)
+        for i, sent_out in enumerate(sent_outs):
+            start = pl.multiple_of((1 - core) * low_rows + i * sent_rows, sent_rows)
+            sent_out[...] = sums[pl.ds(start, sent_rows)].astype(jnp.bfloat16)
+
+
+def layer_stack(streams, taps, number, weights, following=(), earlier=None):
     seqs, seq_rows, channels = streams[0].shape
     layers = number
     last = earlier is not None
     width = 6 * channels
     anywhere = pl.BlockSpec(memory_space=pl.ANY)
     near = pl.BlockSpec(memory_space=pltpu.VMEM)
-    stream = jax.ShapeDtypeStruct((number, seq_rows, channels), jnp.bfloat16)
-    rows = lambda *shape: pltpu.VMEM((*shape, seqs, seq_rows, channels), jnp.bfloat16)
+    rows = lambda count, wide=1: ((count, seqs, seq_rows, wide * channels), jnp.bfloat16)
+    kept = [rows(layers), rows(layers, 2), rows(layers + 1)]
     scratch = [
-        rows(),
-        rows(layers),
-        rows(layers),
-        pltpu.VMEM((layers, seqs, seq_rows, 2 * channels), jnp.bfloat16),
-        rows(layers + 1),
+        pltpu.VMEM((seqs, seq_rows, channels), jnp.bfloat16),
+        pltpu.VMEM(*rows(layers)),
         pltpu.VMEM((layers, seqs, seq_rows, channels), jnp.float32),
         pltpu.VMEM((layers, seqs, seq_rows, channels), jnp.float32),
-        rows(),
         pltpu.SemaphoreType.DMA((2,)),
-        pltpu.SemaphoreType.DMA,
-        pltpu.SemaphoreType.DMA,
         pltpu.SemaphoreType.DMA,
     ]
     operands = [*streams, *taps, *weights]
     in_specs = [near] * 3 + [anywhere] * len(taps) + [near if last else anywhere] * len(weights)
-    aliases = {}
     if last:
-        skip_total, grads, sums = earlier
-        aliases = {len(operands) + 1: 0, len(operands) + 2: 1}
-        operands += [sums, skip_total, grads]
-        in_specs += [near, anywhere, anywhere]
-        shapes = [((channels // 2, width), jnp.bfloat16), ((channels // 2, width), jnp.float32)]
+        operands += [*earlier]
+        in_specs += [near] * len(earlier)
+        shapes = kept + [((channels // 4, width), jnp.bfloat16)] * 2 + [((channels // 2, width), jnp.float32)]
         scratch += [pltpu.VMEM((channels, width), jnp.float32)]
     else:
-        shapes = [((seq_rows, channels), jnp.bfloat16), ((channels, width), jnp.float32), ((layers, channels, width), jnp.bfloat16)]
-        scratch += [pltpu.SemaphoreType.DMA((layers,))]
+        shapes = [((seq_rows, channels), jnp.bfloat16)] * 3
+        shapes += [((channels, width), jnp.float32), ((layers, channels, width), jnp.bfloat16)]
+        shapes += [((layers - 1, seq_rows, 2 * channels), jnp.float32)]
+        shapes += [((2, layers - 1, seq_rows, channels), jnp.float32)]
+        operands += [*following]
+        in_specs += [near] * len(following)
+        scratch += [pltpu.VMEM(*shape) for shape in kept] + [pltpu.SemaphoreType.DMA((layers,))]
     flops = 2 * 22 * layers * seqs * seq_rows * channels * channels
     return pl.pallas_call(
         functools.partial(stack_kernel, layers, last),
         in_specs=in_specs,
-        out_specs=[anywhere, anywhere] + [near] * len(shapes),
-        out_shape=[stream, stream] + [jax.ShapeDtypeStruct(*shape) for shape in shapes],
+        out_specs=[near] * len(shapes),
+        out_shape=[jax.ShapeDtypeStruct(*shape) for shape in shapes],
         scratch_shapes=scratch,
-        input_output_aliases=aliases,
-        compiler_params=pltpu.CompilerParams(vmem_limit_bytes=(44 if last else 24) * 2**20),
+        compiler_params=pltpu.CompilerParams(vmem_limit_bytes=(24 if last else 20) * 2**20),
         cost_estimate=pl.CostEstimate(flops=flops, bytes_accessed=16 * seqs * seq_rows * channels, transcendentals=0),
         name="layer_stack",
     )(*operands)
@@ -374,12 +406,14 @@
     return ordered[:count], ordered[count:]
 
 
-def spread_kernel(places, kept, got, own_out, *outs):
+def spread_kernel(places, kept, got_low, got_high, own_out, *outs):
     place = lax.axis_index("tm") // 2
     piece_rows = own_out.shape[0]
     for by in range(places):
         rows = pl.ds(pl.multiple_of(jnp.bitwise_xor(place, by) * piece_rows, piece_rows), piece_rows)
-        total = kept[rows] + got[rows].astype(jnp.float32)
+        here = pl.ds(pl.multiple_of(lax.rem(jnp.bitwise_xor(place, by) * piece_rows, got_low.shape[0]), piece_rows), piece_rows)
+        got = jnp.where(jnp.bitwise_xor(place, by) * piece_rows < got_low.shape[0], got_low[here], got_high[here])
+        total = kept[rows] + got.astype(jnp.float32)
         if by == 0:
             own_out[...] = total
         else:
@@ -404,16 +438,19 @@
                 column += width
 
 
-def add_kernel(grads, *refs):
+def add_kernel(own_base, base, *refs):
     *backs, out = refs
-    own = jnp.where(lax.axis_index("section") == 0, 1.0, 0.0)
+    section = lax.axis_index("section")
+    own = jnp.where(section == 0, 1.0, 0.0)
     for i, back in enumerate(backs):
         term = back[...].astype(jnp.float32)
-        out[i] = (grads[i].astype(jnp.float32) + (term * own if i == 0 else term)).astype(jnp.bfloat16)
-
-
-def add_back(grads, backs):
-    return local_call(add_kernel, "add_back", [grads, *backs], [grads], 2**24)[0]
+        total = base[i - 1] + term if i else own_base[...].astype(jnp.float32) + term * own
+        out[0, jnp.bitwise_xor(section, i)] = total.astype(jnp.bfloat16)
+
+
+def add_back(own_base, base, backs):
+    shape = (1, len(backs), *own_base.shape)
+    return local_call(add_kernel, "add_back", [own_base, base, *backs], [jax.ShapeDtypeStruct(shape, jnp.bfloat16)], 2**24)[0]
 
 
 def local_call(kernel, name, operands, out_shape, weight=0):
@@ -437,22 +474,27 @@
     return lax.ppermute(x, ("section", "tm"), [(i * shards + t, j * shards + t) for i, j in pairs for t in reached])
 
 
-def sum_over_shards(sent, kept, places, scale, beside):
+def spread(got, kept, places):
     rows, width = kept.shape
     piece = (rows // places, width)
-    got = swapped(sent, "tm", 1)
     narrow = jax.ShapeDtypeStruct(piece, jnp.bfloat16)
     own, *pieces = local_call(
-        functools.partial(spread_kernel, places), "spread", [kept, got],
+        functools.partial(spread_kernel, places), "spread", [kept, *got],
         [jax.ShapeDtypeStruct(piece, jnp.float32)] + [narrow] * (places - 1),
     )
+    return own, pieces
+
+
+def sum_over_chips(own, pieces, scale, beside):
+    rows, width = own.shape
+    places = len(pieces) + 1
     arrived = [swapped(value, "tm", 2 * (by + 1)) for by, value in enumerate(pieces)]
     total = sum([value.astype(jnp.float32) for value in arrived], own).astype(jnp.bfloat16)
     by_distance = [total] + [swapped(total, "tm", 2 * by) for by in range(1, places)]
     by_distance, beside = lax.optimization_barrier((by_distance, beside))
     other = swapped(jnp.stack(by_distance), "tm", 1)
     channels = width // 6
-    out_shape = [jax.ShapeDtypeStruct((1, 2 * rows, cols), jnp.float32) for cols in (2 * channels, 2 * channels, channels, channels)]
+    out_shape = [jax.ShapeDtypeStruct((1, 2 * places * rows, cols), jnp.float32) for cols in (2 * channels, 2 * channels, channels, channels)]
     return local_call(functools.partial(final_kernel, places, scale), "place_sums", by_distance + [other], out_shape), beside
 
 
@@ -475,16 +517,20 @@
     taps = [tap] + [swapped(tap, "section", by) for by in range(1, sections)]
 
     pieces = [w_now, w_res, w_skip, w_tap, *mine, *other]
-    skip_total, grads, back, sums, weights = layer_stack(own_streams, taps[:1], number, pieces)
+    following = other_streams[:2]
+    own_skip, own_base, back, sums, weights, *ahead = layer_stack(own_streams, taps[:1], number, pieces, following)
     back = passed_along(back, "tm", -span)
-    skip_total, grads, sent, kept = layer_stack(other_streams, taps[1:], number, [weights], (skip_total, grads, sums))
-    sent, back = lax.optimization_barrier((sent, back))
+    gated, dz, g, *sent, kept = layer_stack(other_streams, taps[1:], number, [weights], earlier=(sums, *ahead))
+    got = [swapped(value, "tm", 1) for value in sent]
+    own_piece, pieces = spread(got, kept, shards // 2)
+    pieces, back = lax.optimization_barrier((pieces, back))
     reached = range(shards - span)
     arrived = [between(back, shards, [(by, 0)], reached) for by in range(1, sections)]
     grad_scale = 1.0 / math.sqrt(number * seq_rows * shards)
-    input_grads = add_back(grads, [back, *arrived])
-    summed, input_grads = sum_over_shards(sent, kept, shards // 2, grad_scale, input_grads)
-    return (skip_total, input_grads[None], *summed)
+    skip_total, base = finish(own_skip, gated, dz, g, weights)
+    input_grads = add_back(own_base, base, [back, *arrived])
+    summed, input_grads = sum_over_chips(own_piece, pieces, grad_scale, input_grads)
+    return (skip_total, input_grads, *summed)
 
 
 def body(signal, skip_cot, res_cot, w_tap, w_now, w_res, w_skip):

time: 78 us -> 76.2 us (0.977)
  waiting for transfers between devices: 24.9 us -> 21.6 us
  Pallas kernels: 18.2 us -> 19.1 us
    ppermute x3, waiting for transfers between devices: 5.04 us -> 1.29 us  [between(): lax.ppermute(x, ('section', 'tm'), [(i * shards + t, j * shards + t) for...]
    pallas_call x3 -> x4, Pallas kernels: 2.55 us -> 4.88 us  [local_call(): pl.pallas_call(kernel, in_specs=[near] * len(operands), out_specs=[near]...]
    pallas_call x2, Pallas kernels: 15.3 us -> 13.9 us  [layer_stack(): pl.pallas_call(functools.partial(stack_kernel, layers, last), in_specs=in...]
    ppermute x17 -> x18, starting transfers between devices: 17.5 us -> 18.1 us  [swapped(): lax.ppermute(x, axis, [(i, i ^ by) for i in range(lax.axis_size(axis))])]
    ppermute x17 -> x18, waiting for transfers between devices: 18 us -> 18.4 us  [swapped(): lax.ppermute(x, axis, [(i, i ^ by) for i in range(lax.axis_size(axis))])]
  transfers between devices with their start and end apart: 22 -> 23, of which waited for: 10 -> 11; matrix products, arithmetic and copies ran while one was open for 1% -> 1% of each run, Pallas kernels for 22% -> 24%
where the time goes in v5:
time: 76.2 us; the launch traced here: 75.8 us
  starting transfers between devices  28.3 us (37%)
  waiting for transfers between devices  21.6 us (28%)
  Pallas kernels  19.1 us (25%)
  local copies, waits for them, and re-layouts  4.65 us (6%)
  other arithmetic  1.22 us (2%)
  between operations  0.85 us (1%)
    ppermute x18, waiting for transfers between devices, swapped(): lax.ppermute(x, axis, [(i, i ^ by) for i in range(lax.axis_size(axis))])  18.4 us
    ppermute x18, starting transfers between devices, swapped(): lax.ppermute(x, axis, [(i, i ^ by) for i in range(lax.axis_size(axis))])  18.1 us
    pallas_call x2, Pallas kernels, layer_stack(): pl.pallas_call(functools.partial(stack_kernel, layers, last), in_specs=in...  13.9 us
    ppermute x2, starting transfers between devices, passed_along(): return lax.ppermute(x, axis, pairs)  6.41 us
    pallas_call x4, Pallas kernels, local_call(): pl.pallas_call(kernel, in_specs=[near] * len(operands), out_specs=[near]...  4.88 us
    ppermute x3, starting transfers between devices, between(): lax.ppermute(x, ('section', 'tm'), [(i * shards + t, j * shards + t) for...  3.86 us
    unnamed x14, local copies, waits for them, and re-layouts  3.69 us
    ppermute x2, waiting for transfers between devices, passed_along(): return lax.ppermute(x, axis, pairs)  1.94 us
  transfers between devices with their start and end apart: 23, of which 11 were waited for; matrix products, arithmetic and copies ran while one was open for 1% of the time, Pallas kernels for 24%

profile of v5, /device:TPU:0, one launch (start us, length us, event | category | flops | bytes accessed | tf_op | source)
XLA Modules:
  0.0 75.8 jit_solution(15264664709014475120)
XLA Ops:
  1.8 3.0 %collective-permute-start.2 = (bf16[128,1536]{1,0:T(8,128)(2,1)S(1)}, bf16[128,1536]{1,0:T(8,128)(2,1)S(1)}, u32[]{:S(2)}, u32[]{:S(2)}) collective-permute-start(bf16[128,1536]{1,0:T(8,128)(2,1)S(1)} %fusion.2), channel_id=1, source_target_pairs={{0,16},{8,24},{16,0},{24,8},{1,17},{9,25},{17,1},{25,9},{2,18},{10... | collective-permute-start | bytes 1179656 | tf_op jit(solution)/shard_map/ppermute | solution.py:470
  4.8 1.5 %collective-permute-start.1 = (bf16[128,1536]{1,0:T(8,128)(2,1)S(1)}, bf16[128,1536]{1,0:T(8,128)(2,1)S(1)}, u32[]{:S(2)}, u32[]{:S(2)}) collective-permute-start(bf16[128,1536]{1,0:T(8,128)(2,1)S(1)} %fusion.2), channel_id=1, source_target_pairs={{0,8},{8,0},{16,24},{24,16},{1,9},{9,1},{17,25},{25,17},{2,10},{10... | collective-permute-start | bytes 1179656 | tf_op jit(solution)/shard_map/ppermute | solution.py:470
  7.4 4.9 %collective-permute-start = (bf16[512,256]{1,0:T(8,128)(2,1)S(1)}, bf16[512,256]{1,0:T(8,128)(2,1)S(1)}, u32[]{:S(2)}, u32[]{:S(2)}) collective-permute-start(bf16[512,256]{1,0:T(8,128)(2,1)S(1)} %dynamic-slice_bitcast_fusion), channel_id=1, source_target_pairs={{0,4},{1,5},{2,6},{3,7},{8,12},{9,13},{10,14},{11,15},{16,20},{17,... | collective-permute-start | bytes 786440 | tf_op jit(solution)/shard_map/ppermute | solution.py:18
  13.5 1.2 %copy-done.1 = bf16[4,512,256]{2,1,0:T(8,128)(2,1)S(1)} copy-done((bf16[4,512,256]{2,1,0:T(8,128)(2,1)S(1)}, bf16[4,512,256]{2,1,0:T(8,128)(2,1)}, u32[]{:S(2)}) %copy-start.1) | copy-done | bytes 1048600
  14.8 1.2 %copy-done.2 = bf16[4,512,256]{2,1,0:T(8,128)(2,1)S(1)} copy-done((bf16[4,512,256]{2,1,0:T(8,128)(2,1)S(1)}, bf16[4,512,256]{2,1,0:T(8,128)(2,1)}, u32[]{:S(2)}) %copy-start.2) | copy-done | bytes 1048600
  17.0 6.6 %collective-permute-done.3.refs_10_ = bf16[128,1536]{1,0:T(8,128)(2,1)S(1)} collective-permute-done((bf16[128,1536]{1,0:T(8,128)(2,1)S(1)}, bf16[128,1536]{1,0:T(8,128)(2,1)S(1)}, u32[]{:S(2)}, u32[]{:S(2)}) %collective-permute-start.3) | collective-permute-done | bytes 393248 | tf_op jit(solution)/shard_map/ppermute | solution.py:470
  24.2 2.6 %collective-permute-start.9 = (bf16[512,256]{1,0:T(8,128)(2,1)S(1)}, bf16[512,256]{1,0:T(8,128)(2,1)S(1)}, u32[]{:S(2)}, u32[]{:S(2)}) collective-permute-start(bf16[512,256]{1,0:T(8,128)(2,1)S(1)} %collective-permute-done.refs_3_), channel_id=1, source_target_pairs={{0,24},{8,16},{16,8},{24,0},{1,25},{9,17},{17,9},{25,1},{2,26},{10... | collective-permute-start | bytes 786440 | tf_op jit(solution)/shard_map/ppermute | solution.py:470
  27.7 6.3 %layer_stack.2 = (bf16[512,256]{1,0:T(8,128)(2,1)S(1)}, bf16[512,256]{1,0:T(8,128)(2,1)S(1)}, bf16[512,256]{1,0:T(8,128)(2,1)S(1)}, f32[256,1536]{1,0:T(8,128)S(...) custom-call(bf16[1,512,256]{2,1,0:T(8,128)(2,1)S(1)} %get-tuple-element.60.refs_0_, ...), custom_call_target="tpu_custom_call" | custom-call | flops 5905580032 | bytes 2097152 | tf_op jit(solution)/shard_map/layer_stack/pallas_call | solution.py:363
  34.0 1.5 %collective-permute-start.12 = (bf16[512,256]{1,0:T(8,128)(2,1)S(1)}, bf16[512,256]{1,0:T(8,128)(2,1)S(1)}, u32[]{:S(2)}, u32[]{:S(2)}) collective-permute-start(bf16[512,256]{1,0:T(8,128)(2,1)S(1)} %get-tuple-element.86), channel_id=1, source_target_pairs={{4,0},{5,1},{6,2},{7,3},{12,8},{13,9},{14,10},{15,11},{20,16},{21,... | collective-permute-start | bytes 786440 | tf_op jit(solution)/shard_map/ppermute | solution.py:18
  35.5 3.9 %collective-permute-done.8.refs_4_ = bf16[512,256]{1,0:T(8,128)(2,1)S(1)} collective-permute-done((bf16[512,256]{1,0:T(8,128)(2,1)S(1)}, bf16[512,256]{1,0:T(8,128)(2,1)S(1)}, u32[]{:S(2)}, u32[]{:S(2)}) %collective-permute-start.8) | collective-permute-done | bytes 262176 | tf_op jit(solution)/shard_map/ppermute | solution.py:470
  39.6 7.6 %layer_stack.3 = (bf16[4,3,512,256]{3,2,1,0:T(8,128)(2,1)S(1)}, bf16[4,3,512,512]{3,2,1,0:T(8,128)(2,1)S(1)}, bf16[5,3,512,256]{3,2,1,0:T(8,128)(2,1)S(1)}, bf16...) custom-call(bf16[3,512,256]{2,1,0:T(8,128)(2,1)S(1)} %get-tuple-element.67.refs_14_.refs_0_, ...), custom_call_target="tpu_custom_call" | custom-call | flops 17716740096 | bytes 6291456 | tf_op jit(solution)/shard_map/layer_stack/pallas_call | solution.py:363
  49.1 1.2 %collective-permute-done.12.refs_0_ = bf16[512,256]{1,0:T(8,128)(2,1)S(1)} collective-permute-done((bf16[512,256]{1,0:T(8,128)(2,1)S(1)}, bf16[512,256]{1,0:T(8,128)(2,1)S(1)}, u32[]{:S(2)}, u32[]{:S(2)}) %collective-permute-start.12) | collective-permute-done | bytes 262176 | tf_op jit(solution)/shard_map/ppermute | solution.py:18
  50.7 2.6 %collective-permute-start.14 = (bf16[32,1536]{1,0:T(8,128)(2,1)S(1)}, bf16[32,1536]{1,0:T(8,128)(2,1)S(1)}, u32[]{:S(2)}, u32[]{:S(2)}) collective-permute-start(bf16[32,1536]{1,0:T(8,128)(2,1)S(1)} %get-tuple-element.88), channel_id=1, source_target_pairs={{0,4},{1,5},{2,6},{3,7},{4,0},{5,1},{6,2},{7,3},{8,12},{9,13},{10,... | collective-permute-start | bytes 294920 | tf_op jit(solution)/shard_map/ppermute | solution.py:470
  53.3 1.4 %collective-permute-start.15 = (bf16[32,1536]{1,0:T(8,128)(2,1)S(1)}, bf16[32,1536]{1,0:T(8,128)(2,1)S(1)}, u32[]{:S(2)}, u32[]{:S(2)}) collective-permute-start(bf16[32,1536]{1,0:T(8,128)(2,1)S(1)} %get-tuple-element.89), channel_id=1, source_target_pairs={{0,6},{1,7},{2,4},{3,5},{4,2},{5,3},{6,0},{7,1},{8,14},{9,15},{10,... | collective-permute-start | bytes 294920 | tf_op jit(solution)/shard_map/ppermute | solution.py:470
  54.7 1.3 %collective-permute-start.21 = (bf16[512,256]{1,0:T(8,128)(2,1)S(1)}, bf16[512,256]{1,0:T(8,128)(2,1)S(1)}, u32[]{:S(2)}, u32[]{:S(2)}) collective-permute-start(bf16[512,256]{1,0:T(8,128)(2,1)S(1)} %collective-permute-done.12.refs_0_), channel_id=1, source_target_pairs={{24,0},{25,1},{26,2},{27,3}} | collective-permute-start | bytes 786440 | tf_op jit(solution)/shard_map/ppermute | solution.py:474
  56.0 1.3 %collective-permute-start.20 = (bf16[512,256]{1,0:T(8,128)(2,1)S(1)}, bf16[512,256]{1,0:T(8,128)(2,1)S(1)}, u32[]{:S(2)}, u32[]{:S(2)}) collective-permute-start(bf16[512,256]{1,0:T(8,128)(2,1)S(1)} %collective-permute-done.12.refs_0_), channel_id=1, source_target_pairs={{16,0},{17,1},{18,2},{19,3}} | collective-permute-start | bytes 786440 | tf_op jit(solution)/shard_map/ppermute | solution.py:474
  57.3 1.3 %collective-permute-start.19 = (bf16[512,256]{1,0:T(8,128)(2,1)S(1)}, bf16[512,256]{1,0:T(8,128)(2,1)S(1)}, u32[]{:S(2)}, u32[]{:S(2)}) collective-permute-start(bf16[512,256]{1,0:T(8,128)(2,1)S(1)} %collective-permute-done.12.refs_0_), channel_id=1, source_target_pairs={{8,0},{9,1},{10,2},{11,3}} | collective-permute-start | bytes 786440 | tf_op jit(solution)/shard_map/ppermute | solution.py:474
  58.6 2.8 %collective-permute-done.14 = bf16[32,1536]{1,0:T(8,128)(2,1)S(1)} collective-permute-done((bf16[32,1536]{1,0:T(8,128)(2,1)S(1)}, bf16[32,1536]{1,0:T(8,128)(2,1)S(1)}, u32[]{:S(2)}, u32[]{:S(2)}) %collective-permute-start.14) | collective-permute-done | bytes 98336 | tf_op jit(solution)/shard_map/ppermute | solution.py:470
  61.5 2.6 %collective-permute-start.18 = (bf16[32,1536]{1,0:T(8,128)(2,1)S(1)}, bf16[32,1536]{1,0:T(8,128)(2,1)S(1)}, u32[]{:S(2)}, u32[]{:S(2)}) collective-permute-start(bf16[32,1536]{1,0:T(8,128)(2,1)S(1)} %add_convert_fusion.refs_0_), channel_id=1, source_target_pairs={{0,6},{1,7},{2,4},{3,5},{4,2},{5,3},{6,0},{7,1},{8,14},{9,15},{10,... | collective-permute-start | bytes 294920 | tf_op jit(solution)/shard_map/ppermute | solution.py:470
  65.9 2.4 %finish.1 = (bf16[4,512,256]{2,1,0:T(8,128)(2,1)}, f32[3,512,256]{2,1,0:T(8,128)S(1)}) custom-call(bf16[512,256]{1,0:T(8,128)(2,1)S(1)} %get-tuple-element.69.own_skip, bf16[4,3,512,256]{3,2,1,0:T(8,128)(2,1)S(1)} %get-tuple-element.75.gated_all, bf16[4,3,512,512]{3,2,1,0:T(8,128)(2,1)S(1)} %get-tuple-element.76.dz_all, ...), custom_call_target="tpu_custom_call" | custom-call | tf_op jit(solution)/shard_map/finish/pallas_call | solution.py:458
  68.3 1.3 %collective-permute-done.20.refs_2_ = bf16[512,256]{1,0:T(8,128)(2,1)S(1)} collective-permute-done((bf16[512,256]{1,0:T(8,128)(2,1)S(1)}, bf16[512,256]{1,0:T(8,128)(2,1)S(1)}, u32[]{:S(2)}, u32[]{:S(2)}) %collective-permute-start.20) | collective-permute-done | bytes 262176 | tf_op jit(solution)/shard_map/ppermute | solution.py:474
  70.8 1.9 %collective-permute-done.17.refs_2_ = bf16[32,1536]{1,0:T(8,128)(2,1)S(1)} collective-permute-done((bf16[32,1536]{1,0:T(8,128)(2,1)S(1)}, bf16[32,1536]{1,0:T(8,128)(2,1)S(1)}, u32[]{:S(2)}, u32[]{:S(2)}) %collective-permute-start.17) | collective-permute-done | bytes 98336 | tf_op jit(solution)/shard_map/ppermute | solution.py:470
  72.8 1.7 %collective-permute-done.22.refs_4_ = bf16[4,32,1536]{2,1,0:T(8,128)(2,1)S(1)} collective-permute-done((bf16[4,32,1536]{2,1,0:T(8,128)(2,1)S(1)}, bf16[4,32,1536]{2,1,0:T(8,128)(2,1)S(1)}, u32[]{:S(2)}, u32[]{:S(2)}) %collective-permute-start.22) | collective-permute-done | bytes 393248 | tf_op jit(solution)/shard_map/ppermute | solution.py:470
  74.5 1.3 %place_sums.1 = (f32[1,256,512]{2,1,0:T(8,128)}, f32[1,256,512]{2,1,0:T(8,128)}, f32[1,256,256]{2,1,0:T(8,128)}, f32[1,256,256]{2,1,0:T(8,128)}) custom-call(bf16[32,1536]{1,0:T(8,128)(2,1)S(1)} %add_convert_fusion.refs_0_, bf16[32,1536]{1,0:T(8,128)(2,1)S(1)} %collective-permute-done.16.refs_1_, bf16[32,1536]{1,0:T(8,128)(2,1)S(1)} %collective-permute-done.17.refs_2_, ...), custom_call_target="tpu_custom_call" | custom-call | tf_op jit(solution)/shard_map/place_sums/pallas_call | solution.py:458
  (47 shorter events, 11.6 us)
Async XLA Ops:
  0.6 27.0 %copy-start.4 = (bf16[1,256,512]{2,1,0:T(8,128)(2,1)S(1)}, bf16[1,256,512]{2,1,0:T(8,128)(2,1)}, u32[]{:S(2)}) copy-start(bf16[1,256,512]{2,1,0:T(8,128)(2,1)} %refs_7_.1) | copy-start | bytes 786436
  1.8 15.2 %collective-permute-start.2 = (bf16[128,1536]{1,0:T(8,128)(2,1)S(1)}, bf16[128,1536]{1,0:T(8,128)(2,1)S(1)}, u32[]{:S(2)}, u32[]{:S(2)}) collective-permute-start(bf16[128,1536]{1,0:T(8,128)(2,1)S(1)} %fusion.2), channel_id=1, source_target_pairs={{0,16},{8,24},{16,0},{24,8},{1,17},{9,25},{17,1},{25,9},{2,18},{10... | collective-permute-start | bytes 1179656 | tf_op jit(solution)/shard_map/ppermute | solution.py:470
  4.8 12.2 %collective-permute-start.1 = (bf16[128,1536]{1,0:T(8,128)(2,1)S(1)}, bf16[128,1536]{1,0:T(8,128)(2,1)S(1)}, u32[]{:S(2)}, u32[]{:S(2)}) collective-permute-start(bf16[128,1536]{1,0:T(8,128)(2,1)S(1)} %fusion.2), channel_id=1, source_target_pairs={{0,8},{8,0},{16,24},{24,16},{1,9},{9,1},{17,25},{25,17},{2,10},{10... | collective-permute-start | bytes 1179656 | tf_op jit(solution)/shard_map/ppermute | solution.py:470
  6.3 17.3 %collective-permute-start.3 = (bf16[128,1536]{1,0:T(8,128)(2,1)S(1)}, bf16[128,1536]{1,0:T(8,128)(2,1)S(1)}, u32[]{:S(2)}, u32[]{:S(2)}) collective-permute-start(bf16[128,1536]{1,0:T(8,128)(2,1)S(1)} %fusion.2), channel_id=1, source_target_pairs={{0,24},{8,16},{16,8},{24,0},{1,25},{9,17},{17,9},{25,1},{2,26},{10... | collective-permute-start | bytes 1179656 | tf_op jit(solution)/shard_map/ppermute | solution.py:470
  7.4 9.7 %collective-permute-start = (bf16[512,256]{1,0:T(8,128)(2,1)S(1)}, bf16[512,256]{1,0:T(8,128)(2,1)S(1)}, u32[]{:S(2)}, u32[]{:S(2)}) collective-permute-start(bf16[512,256]{1,0:T(8,128)(2,1)S(1)} %dynamic-slice_bitcast_fusion), channel_id=1, source_target_pairs={{0,4},{1,5},{2,6},{3,7},{8,12},{9,13},{10,14},{11,15},{16,20},{17,... | collective-permute-start | bytes 786440 | tf_op jit(solution)/shard_map/ppermute | solution.py:18
  23.6 3.6 %collective-permute-start.4 = (bf16[128,1536]{1,0:T(8,128)(2,1)S(1)}, bf16[128,1536]{1,0:T(8,128)(2,1)S(1)}, u32[]{:S(2)}, u32[]{:S(2)}) collective-permute-start(bf16[128,1536]{1,0:T(8,128)(2,1)S(1)} %collective-permute-done.1.refs_8_), channel_id=1, source_target_pairs={{0,1},{1,0},{2,3},{3,2},{4,5},{5,4},{6,7},{7,6},{8,9},{9,8},{10,11... | collective-permute-start | bytes 1179656 | tf_op jit(solution)/shard_map/ppermute | solution.py:470
  23.6 4.0 %collective-permute-start.5 = (bf16[128,1536]{1,0:T(8,128)(2,1)S(1)}, bf16[128,1536]{1,0:T(8,128)(2,1)S(1)}, u32[]{:S(2)}, u32[]{:S(2)}) collective-permute-start(bf16[128,1536]{1,0:T(8,128)(2,1)S(1)} %collective-permute-done.2.refs_9_), channel_id=1, source_target_pairs={{0,1},{1,0},{2,3},{3,2},{4,5},{5,4},{6,7},{7,6},{8,9},{9,8},{10,11... | collective-permute-start | bytes 1179656 | tf_op jit(solution)/shard_map/ppermute | solution.py:470
  24.2 3.5 %collective-permute-start.6 = (bf16[128,1536]{1,0:T(8,128)(2,1)S(1)}, bf16[128,1536]{1,0:T(8,128)(2,1)S(1)}, u32[]{:S(2)}, u32[]{:S(2)}) collective-permute-start(bf16[128,1536]{1,0:T(8,128)(2,1)S(1)} %collective-permute-done.3.refs_10_), channel_id=1, source_target_pairs={{0,1},{1,0},{2,3},{3,2},{4,5},{5,4},{6,7},{7,6},{8,9},{9,8},{10,11... | collective-permute-start | bytes 1179656 | tf_op jit(solution)/shard_map/ppermute | solution.py:470
  24.2 11.4 %collective-permute-start.9 = (bf16[512,256]{1,0:T(8,128)(2,1)S(1)}, bf16[512,256]{1,0:T(8,128)(2,1)S(1)}, u32[]{:S(2)}, u32[]{:S(2)}) collective-permute-start(bf16[512,256]{1,0:T(8,128)(2,1)S(1)} %collective-permute-done.refs_3_), channel_id=1, source_target_pairs={{0,24},{8,16},{16,8},{24,0},{1,25},{9,17},{17,9},{25,1},{2,26},{10... | collective-permute-start | bytes 786440 | tf_op jit(solution)/shard_map/ppermute | solution.py:470
  26.8 12.6 %collective-permute-start.8 = (bf16[512,256]{1,0:T(8,128)(2,1)S(1)}, bf16[512,256]{1,0:T(8,128)(2,1)S(1)}, u32[]{:S(2)}, u32[]{:S(2)}) collective-permute-start(bf16[512,256]{1,0:T(8,128)(2,1)S(1)} %collective-permute-done.refs_3_), channel_id=1, source_target_pairs={{0,16},{8,24},{16,0},{24,8},{1,17},{9,25},{17,1},{25,9},{2,18},{10... | collective-permute-start | bytes 786440 | tf_op jit(solution)/shard_map/ppermute | solution.py:470
  27.3 12.4 %collective-permute-start.7 = (bf16[512,256]{1,0:T(8,128)(2,1)S(1)}, bf16[512,256]{1,0:T(8,128)(2,1)S(1)}, u32[]{:S(2)}, u32[]{:S(2)}) collective-permute-start(bf16[512,256]{1,0:T(8,128)(2,1)S(1)} %collective-permute-done.refs_3_), channel_id=1, source_target_pairs={{0,8},{8,0},{16,24},{24,16},{1,9},{9,1},{17,25},{25,17},{2,10},{10... | collective-permute-start | bytes 786440 | tf_op jit(solution)/shard_map/ppermute | solution.py:470
  34.0 16.3 %collective-permute-start.12 = (bf16[512,256]{1,0:T(8,128)(2,1)S(1)}, bf16[512,256]{1,0:T(8,128)(2,1)S(1)}, u32[]{:S(2)}, u32[]{:S(2)}) collective-permute-start(bf16[512,256]{1,0:T(8,128)(2,1)S(1)} %get-tuple-element.86), channel_id=1, source_target_pairs={{4,0},{5,1},{6,2},{7,3},{12,8},{13,9},{14,10},{15,11},{20,16},{21,... | collective-permute-start | bytes 786440 | tf_op jit(solution)/shard_map/ppermute | solution.py:18
  47.2 1.5 %collective-permute-start.10 = (bf16[64,1536]{1,0:T(8,128)(2,1)S(1)}, bf16[64,1536]{1,0:T(8,128)(2,1)S(1)}, u32[]{:S(2)}, u32[]{:S(2)}) collective-permute-start(bf16[64,1536]{1,0:T(8,128)(2,1)S(1)} %get-tuple-element.80), channel_id=1, source_target_pairs={{0,1},{1,0},{2,3},{3,2},{4,5},{5,4},{6,7},{7,6},{8,9},{9,8},{10,11... | collective-permute-start | bytes 589832 | tf_op jit(solution)/shard_map/ppermute | solution.py:470
  47.3 1.7 %collective-permute-start.11 = (bf16[64,1536]{1,0:T(8,128)(2,1)S(1)}, bf16[64,1536]{1,0:T(8,128)(2,1)S(1)}, u32[]{:S(2)}, u32[]{:S(2)}) collective-permute-start(bf16[64,1536]{1,0:T(8,128)(2,1)S(1)} %get-tuple-element.81), channel_id=1, source_target_pairs={{0,1},{1,0},{2,3},{3,2},{4,5},{5,4},{6,7},{7,6},{8,9},{9,8},{10,11... | collective-permute-start | bytes 589832 | tf_op jit(solution)/shard_map/ppermute | solution.py:470
  50.3 7.0 %collective-permute-start.13 = (bf16[32,1536]{1,0:T(8,128)(2,1)S(1)}, bf16[32,1536]{1,0:T(8,128)(2,1)S(1)}, u32[]{:S(2)}, u32[]{:S(2)}) collective-permute-start(bf16[32,1536]{1,0:T(8,128)(2,1)S(1)} %get-tuple-element.87), channel_id=1, source_target_pairs={{0,2},{1,3},{2,0},{3,1},{4,6},{5,7},{6,4},{7,5},{8,10},{9,11},{10,... | collective-permute-start | bytes 294920 | tf_op jit(solution)/shard_map/ppermute | solution.py:470
  50.7 10.7 %collective-permute-start.14 = (bf16[32,1536]{1,0:T(8,128)(2,1)S(1)}, bf16[32,1536]{1,0:T(8,128)(2,1)S(1)}, u32[]{:S(2)}, u32[]{:S(2)}) collective-permute-start(bf16[32,1536]{1,0:T(8,128)(2,1)S(1)} %get-tuple-element.88), channel_id=1, source_target_pairs={{0,4},{1,5},{2,6},{3,7},{4,0},{5,1},{6,2},{7,3},{8,12},{9,13},{10,... | collective-permute-start | bytes 294920 | tf_op jit(solution)/shard_map/ppermute | solution.py:470
  53.3 8.1 %collective-permute-start.15 = (bf16[32,1536]{1,0:T(8,128)(2,1)S(1)}, bf16[32,1536]{1,0:T(8,128)(2,1)S(1)}, u32[]{:S(2)}, u32[]{:S(2)}) collective-permute-start(bf16[32,1536]{1,0:T(8,128)(2,1)S(1)} %get-tuple-element.89), channel_id=1, source_target_pairs={{0,6},{1,7},{2,4},{3,5},{4,2},{5,3},{6,0},{7,1},{8,14},{9,15},{10,... | collective-permute-start | bytes 294920 | tf_op jit(solution)/shard_map/ppermute | solution.py:470
  54.7 10.1 %collective-permute-start.21 = (bf16[512,256]{1,0:T(8,128)(2,1)S(1)}, bf16[512,256]{1,0:T(8,128)(2,1)S(1)}, u32[]{:S(2)}, u32[]{:S(2)}) collective-permute-start(bf16[512,256]{1,0:T(8,128)(2,1)S(1)} %collective-permute-done.12.refs_0_), channel_id=1, source_target_pairs={{24,0},{25,1},{26,2},{27,3}} | collective-permute-start | bytes 786440 | tf_op jit(solution)/shard_map/ppermute | solution.py:474
  56.0 13.6 %collective-permute-start.20 = (bf16[512,256]{1,0:T(8,128)(2,1)S(1)}, bf16[512,256]{1,0:T(8,128)(2,1)S(1)}, u32[]{:S(2)}, u32[]{:S(2)}) collective-permute-start(bf16[512,256]{1,0:T(8,128)(2,1)S(1)} %collective-permute-done.12.refs_0_), channel_id=1, source_target_pairs={{16,0},{17,1},{18,2},{19,3}} | collective-permute-start | bytes 786440 | tf_op jit(solution)/shard_map/ppermute | solution.py:474
  57.3 12.3 %collective-permute-start.19 = (bf16[512,256]{1,0:T(8,128)(2,1)S(1)}, bf16[512,256]{1,0:T(8,128)(2,1)S(1)}, u32[]{:S(2)}, u32[]{:S(2)}) collective-permute-start(bf16[512,256]{1,0:T(8,128)(2,1)S(1)} %collective-permute-done.12.refs_0_), channel_id=1, source_target_pairs={{8,0},{9,1},{10,2},{11,3}} | collective-permute-start | bytes 786440 | tf_op jit(solution)/shard_map/ppermute | solution.py:474
  61.5 9.3 %collective-permute-start.18 = (bf16[32,1536]{1,0:T(8,128)(2,1)S(1)}, bf16[32,1536]{1,0:T(8,128)(2,1)S(1)}, u32[]{:S(2)}, u32[]{:S(2)}) collective-permute-start(bf16[32,1536]{1,0:T(8,128)(2,1)S(1)} %add_convert_fusion.refs_0_), channel_id=1, source_target_pairs={{0,6},{1,7},{2,4},{3,5},{4,2},{5,3},{6,0},{7,1},{8,14},{9,15},{10,... | collective-permute-start | bytes 294920 | tf_op jit(solution)/shard_map/ppermute | solution.py:470
  64.1 8.6 %collective-permute-start.17 = (bf16[32,1536]{1,0:T(8,128)(2,1)S(1)}, bf16[32,1536]{1,0:T(8,128)(2,1)S(1)}, u32[]{:S(2)}, u32[]{:S(2)}) collective-permute-start(bf16[32,1536]{1,0:T(8,128)(2,1)S(1)} %add_convert_fusion.refs_0_), channel_id=1, source_target_pairs={{0,4},{1,5},{2,6},{3,7},{4,0},{5,1},{6,2},{7,3},{8,12},{9,13},{10,... | collective-permute-start | bytes 294920 | tf_op jit(solution)/shard_map/ppermute | solution.py:470
  64.8 7.9 %collective-permute-start.16 = (bf16[32,1536]{1,0:T(8,128)(2,1)S(1)}, bf16[32,1536]{1,0:T(8,128)(2,1)S(1)}, u32[]{:S(2)}, u32[]{:S(2)}) collective-permute-start(bf16[32,1536]{1,0:T(8,128)(2,1)S(1)} %add_convert_fusion.refs_0_), channel_id=1, source_target_pairs={{0,2},{1,3},{2,0},{3,1},{4,6},{5,7},{6,4},{7,5},{8,10},{9,11},{10,... | collective-permute-start | bytes 294920 | tf_op jit(solution)/shard_map/ppermute | solution.py:470
  72.8 1.8 %collective-permute-start.22 = (bf16[4,32,1536]{2,1,0:T(8,128)(2,1)S(1)}, bf16[4,32,1536]{2,1,0:T(8,128)(2,1)S(1)}, u32[]{:S(2)}, u32[]{:S(2)}) collective-permute-start(bf16[4,32,1536]{2,1,0:T(8,128)(2,1)S(1)} %pad_maximum_fusion), channel_id=1, source_target_pairs={{0,1},{1,0},{2,3},{3,2},{4,5},{5,4},{6,7},{7,6},{8,9},{9,8},{10,11... | collective-permute-start | bytes 1179656 | tf_op jit(solution)/shard_map/ppermute | solution.py:470
  (6 other events, 84.7 us)

commit v6 on v5

--- a/solution.py
+++ b/solution.py
@@ -221,7 +221,7 @@
         own = take(4)
         mine = take(layers - 1)
         other = take(layers - 1)
-        next_signal, next_cot = take(2)
+        next_signal, next_cot, next_res = take(3)
         skip_out, grad_out, back_out, sums, weights, ahead_pre, ahead_du = take(7)
     early = layers - ahead_du.shape[0]
     tapped, h_all, tanh_all, sig_all = take(4)
@@ -285,11 +285,14 @@
         skip_out[...] = skip_sum([gated_all[k, 0] for k in range(layers)], weights, skip)
     for k in reversed(range(layers)):
         for i in range(seqs):
-            du = turned_dot(g_all[k + 1, i], weights[k, :, res])
-            if last and k >= early:
-                du = du + ahead_du[k - early, i]
+            if last and k == layers - 1:
+                du = ahead_du[k - early, i]
             else:
-                du = du + turned_dot(cot[i], weights[k, :, skip])
+                du = turned_dot(g_all[k + 1, i], weights[k, :, res])
+                if last and k >= early:
+                    du = du + ahead_du[k - early, i]
+                else:
+                    du = du + turned_dot(cot[i], weights[k, :, skip])
             tanh_part = tanh_all[k, i]
             sig_part = sig_all[k, i]
             scaled = du * sig_part
@@ -297,7 +300,10 @@
             dz_all[k, i, :, half:] = (scaled * (tanh_part * (1.0 - sig_part))).astype(jnp.bfloat16)
         if k >= early and not last:
             for i in range(layers - 1):
-                ahead_du[k - early, i] = turned_dot(next_cot[i], weights[k, :, skip])
+                du = turned_dot(next_cot[i], weights[k, :, skip])
+                if k == layers - 1:
+                    du = du + turned_dot(next_res[i], weights[k, :, res])
+                ahead_du[k - early, i] = du
         for i in range(seqs if k or not last else 0):
             below = turned_dot(dz_all[k, i], weights[k, :, now])
             g_all[k, i] = (g_all[k + 1, i].astype(jnp.float32) + below).astype(jnp.bfloat16)
@@ -488,7 +494,7 @@
 def sum_over_chips(own, pieces, scale, beside):
     rows, width = own.shape
     places = len(pieces) + 1
-    arrived = [swapped(value, "tm", 2 * (by + 1)) for by, value in enumerate(pieces)]
+    arrived = [swapped(value, "tm", 2 * (by + 1)) for by, value in reversed(list(enumerate(pieces)))]
     total = sum([value.astype(jnp.float32) for value in arrived], own).astype(jnp.bfloat16)
     by_distance = [total] + [swapped(total, "tm", 2 * by) for by in range(1, places)]
     by_distance, beside = lax.optimization_barrier((by_distance, beside))
@@ -517,8 +523,7 @@
     taps = [tap] + [swapped(tap, "section", by) for by in range(1, sections)]
 
     pieces = [w_now, w_res, w_skip, w_tap, *mine, *other]
-    following = other_streams[:2]
-    own_skip, own_base, back, sums, weights, *ahead = layer_stack(own_streams, taps[:1], number, pieces, following)
+    own_skip, own_base, back, sums, weights, *ahead = layer_stack(own_streams, taps[:1], number, pieces, other_streams)
     back = passed_along(back, "tm", -span)
     gated, dz, g, *sent, kept = layer_stack(other_streams, taps[1:], number, [weights], earlier=(sums, *ahead))
     got = [swapped(value, "tm", 1) for value in sent]

time: 76.2 us -> 75.7 us (level)
    ppermute x18, waiting for transfers between devices: 18.4 us -> 17.1 us  [swapped(): lax.ppermute(x, axis, [(i, i ^ by) for i in range(lax.axis_size(axis))])]
  transfers between devices with their start and end apart: 23 -> 23, of which waited for: 11 -> 12; matrix products, arithmetic and copies ran while one was open for 1% -> 1% of each run, Pallas kernels for 24% -> 24%
where the time goes in v6:
time: 75.7 us; the launch traced here: 75.3 us
  starting transfers between devices  27.9 us (37%)
  waiting for transfers between devices  21.5 us (28%)
  Pallas kernels  19.2 us (25%)
  local copies, waits for them, and re-layouts  4.65 us (6%)
  other arithmetic  1.22 us (2%)
  between operations  0.85 us (1%)
    ppermute x18, starting transfers between devices, swapped(): lax.ppermute(x, axis, [(i, i ^ by) for i in range(lax.axis_size(axis))])  17.6 us
    ppermute x18, waiting for transfers between devices, swapped(): lax.ppermute(x, axis, [(i, i ^ by) for i in range(lax.axis_size(axis))])  17.1 us
    pallas_call x2, Pallas kernels, layer_stack(): pl.pallas_call(functools.partial(stack_kernel, layers, last), in_specs=in...  14 us
    ppermute x2, starting transfers between devices, passed_along(): return lax.ppermute(x, axis, pairs)  6.41 us
    pallas_call x4, Pallas kernels, local_call(): pl.pallas_call(kernel, in_specs=[near] * len(operands), out_specs=[near]...  4.88 us
    ppermute x3, starting transfers between devices, between(): lax.ppermute(x, ('section', 'tm'), [(i * shards + t, j * shards + t) for...  3.86 us
    unnamed x14, local copies, waits for them, and re-layouts  3.69 us
    ppermute x2, waiting for transfers between devices, passed_along(): return lax.ppermute(x, axis, pairs)  2.46 us
  transfers between devices with their start and end apart: 23, of which 12 were waited for; matrix products, arithmetic and copies ran while one was open for 1% of the time, Pallas kernels for 24%

profile of v6, /device:TPU:0, one launch (start us, length us, event | category | flops | bytes accessed | tf_op | source)
XLA Modules:
  0.0 75.3 jit_solution(41654650983553429)
XLA Ops:
  1.8 3.0 %collective-permute-start.2 = (bf16[128,1536]{1,0:T(8,128)(2,1)S(1)}, bf16[128,1536]{1,0:T(8,128)(2,1)S(1)}, u32[]{:S(2)}, u32[]{:S(2)}) collective-permute-start(bf16[128,1536]{1,0:T(8,128)(2,1)S(1)} %fusion.2), channel_id=1, source_target_pairs={{0,16},{8,24},{16,0},{24,8},{1,17},{9,25},{17,1},{25,9},{2,18},{10... | collective-permute-start | bytes 1179656 | tf_op jit(solution)/shard_map/ppermute | solution.py:476
  4.8 1.5 %collective-permute-start.1 = (bf16[128,1536]{1,0:T(8,128)(2,1)S(1)}, bf16[128,1536]{1,0:T(8,128)(2,1)S(1)}, u32[]{:S(2)}, u32[]{:S(2)}) collective-permute-start(bf16[128,1536]{1,0:T(8,128)(2,1)S(1)} %fusion.2), channel_id=1, source_target_pairs={{0,8},{8,0},{16,24},{24,16},{1,9},{9,1},{17,25},{25,17},{2,10},{10... | collective-permute-start | bytes 1179656 | tf_op jit(solution)/shard_map/ppermute | solution.py:476
  7.4 4.9 %collective-permute-start = (bf16[512,256]{1,0:T(8,128)(2,1)S(1)}, bf16[512,256]{1,0:T(8,128)(2,1)S(1)}, u32[]{:S(2)}, u32[]{:S(2)}) collective-permute-start(bf16[512,256]{1,0:T(8,128)(2,1)S(1)} %dynamic-slice_bitcast_fusion), channel_id=1, source_target_pairs={{0,4},{1,5},{2,6},{3,7},{8,12},{9,13},{10,14},{11,15},{16,20},{17,... | collective-permute-start | bytes 786440 | tf_op jit(solution)/shard_map/ppermute | solution.py:18
  13.5 1.2 %copy-done.1 = bf16[4,512,256]{2,1,0:T(8,128)(2,1)S(1)} copy-done((bf16[4,512,256]{2,1,0:T(8,128)(2,1)S(1)}, bf16[4,512,256]{2,1,0:T(8,128)(2,1)}, u32[]{:S(2)}) %copy-start.1) | copy-done | bytes 1048600
  17.0 6.6 %collective-permute-done.3.refs_10_ = bf16[128,1536]{1,0:T(8,128)(2,1)S(1)} collective-permute-done((bf16[128,1536]{1,0:T(8,128)(2,1)S(1)}, bf16[128,1536]{1,0:T(8,128)(2,1)S(1)}, u32[]{:S(2)}, u32[]{:S(2)}) %collective-permute-start.3) | collective-permute-done | bytes 393248 | tf_op jit(solution)/shard_map/ppermute | solution.py:476
  24.2 2.6 %collective-permute-start.9 = (bf16[512,256]{1,0:T(8,128)(2,1)S(1)}, bf16[512,256]{1,0:T(8,128)(2,1)S(1)}, u32[]{:S(2)}, u32[]{:S(2)}) collective-permute-start(bf16[512,256]{1,0:T(8,128)(2,1)S(1)} %collective-permute-done.refs_3_), channel_id=1, source_target_pairs={{0,24},{8,16},{16,8},{24,0},{1,25},{9,17},{17,9},{25,1},{2,26},{10... | collective-permute-start | bytes 786440 | tf_op jit(solution)/shard_map/ppermute | solution.py:476
  27.7 6.6 %layer_stack.2 = (bf16[512,256]{1,0:T(8,128)(2,1)S(1)}, bf16[512,256]{1,0:T(8,128)(2,1)S(1)}, bf16[512,256]{1,0:T(8,128)(2,1)S(1)}, f32[256,1536]{1,0:T(8,128)S(...) custom-call(bf16[1,512,256]{2,1,0:T(8,128)(2,1)S(1)} %get-tuple-element.60.refs_0_, ...), custom_call_target="tpu_custom_call" | custom-call | flops 5905580032 | bytes 2097152 | tf_op jit(solution)/shard_map/layer_stack/pallas_call | solution.py:369
  34.3 1.5 %collective-permute-start.12 = (bf16[512,256]{1,0:T(8,128)(2,1)S(1)}, bf16[512,256]{1,0:T(8,128)(2,1)S(1)}, u32[]{:S(2)}, u32[]{:S(2)}) collective-permute-start(bf16[512,256]{1,0:T(8,128)(2,1)S(1)} %get-tuple-element.86), channel_id=1, source_target_pairs={{4,0},{5,1},{6,2},{7,3},{12,8},{13,9},{14,10},{15,11},{20,16},{21,... | collective-permute-start | bytes 786440 | tf_op jit(solution)/shard_map/ppermute | solution.py:18
  35.8 3.6 %collective-permute-done.8.refs_4_ = bf16[512,256]{1,0:T(8,128)(2,1)S(1)} collective-permute-done((bf16[512,256]{1,0:T(8,128)(2,1)S(1)}, bf16[512,256]{1,0:T(8,128)(2,1)S(1)}, u32[]{:S(2)}, u32[]{:S(2)}) %collective-permute-start.8) | collective-permute-done | bytes 262176 | tf_op jit(solution)/shard_map/ppermute | solution.py:476
  39.6 7.3 %layer_stack.3 = (bf16[4,3,512,256]{3,2,1,0:T(8,128)(2,1)S(1)}, bf16[4,3,512,512]{3,2,1,0:T(8,128)(2,1)S(1)}, bf16[5,3,512,256]{3,2,1,0:T(8,128)(2,1)S(1)}, bf16...) custom-call(bf16[3,512,256]{2,1,0:T(8,128)(2,1)S(1)} %get-tuple-element.67.refs_14_.refs_0_, ...), custom_call_target="tpu_custom_call" | custom-call | flops 17716740096 | bytes 6291456 | tf_op jit(solution)/shard_map/layer_stack/pallas_call | solution.py:369
  48.9 1.8 %collective-permute-done.12.refs_0_ = bf16[512,256]{1,0:T(8,128)(2,1)S(1)} collective-permute-done((bf16[512,256]{1,0:T(8,128)(2,1)S(1)}, bf16[512,256]{1,0:T(8,128)(2,1)S(1)}, u32[]{:S(2)}, u32[]{:S(2)}) %collective-permute-start.12) | collective-permute-done | bytes 262176 | tf_op jit(solution)/shard_map/ppermute | solution.py:18
  50.6 1.9 %collective-permute-start.13 = (bf16[32,1536]{1,0:T(8,128)(2,1)S(1)}, bf16[32,1536]{1,0:T(8,128)(2,1)S(1)}, u32[]{:S(2)}, u32[]{:S(2)}) collective-permute-start(bf16[32,1536]{1,0:T(8,128)(2,1)S(1)} %get-tuple-element.87), channel_id=1, source_target_pairs={{0,6},{1,7},{2,4},{3,5},{4,2},{5,3},{6,0},{7,1},{8,14},{9,15},{10,... | collective-permute-start | bytes 294920 | tf_op jit(solution)/shard_map/ppermute | solution.py:476
  52.5 2.5 %collective-permute-start.15 = (bf16[32,1536]{1,0:T(8,128)(2,1)S(1)}, bf16[32,1536]{1,0:T(8,128)(2,1)S(1)}, u32[]{:S(2)}, u32[]{:S(2)}) collective-permute-start(bf16[32,1536]{1,0:T(8,128)(2,1)S(1)} %get-tuple-element.89), channel_id=1, source_target_pairs={{0,2},{1,3},{2,0},{3,1},{4,6},{5,7},{6,4},{7,5},{8,10},{9,11},{10,... | collective-permute-start | bytes 294920 | tf_op jit(solution)/shard_map/ppermute | solution.py:476
  55.0 1.3 %collective-permute-start.21 = (bf16[512,256]{1,0:T(8,128)(2,1)S(1)}, bf16[512,256]{1,0:T(8,128)(2,1)S(1)}, u32[]{:S(2)}, u32[]{:S(2)}) collective-permute-start(bf16[512,256]{1,0:T(8,128)(2,1)S(1)} %collective-permute-done.12.refs_0_), channel_id=1, source_target_pairs={{24,0},{25,1},{26,2},{27,3}} | collective-permute-start | bytes 786440 | tf_op jit(solution)/shard_map/ppermute | solution.py:480
  56.3 1.3 %collective-permute-start.20 = (bf16[512,256]{1,0:T(8,128)(2,1)S(1)}, bf16[512,256]{1,0:T(8,128)(2,1)S(1)}, u32[]{:S(2)}, u32[]{:S(2)}) collective-permute-start(bf16[512,256]{1,0:T(8,128)(2,1)S(1)} %collective-permute-done.12.refs_0_), channel_id=1, source_target_pairs={{16,0},{17,1},{18,2},{19,3}} | collective-permute-start | bytes 786440 | tf_op jit(solution)/shard_map/ppermute | solution.py:480
  57.6 1.3 %collective-permute-start.19 = (bf16[512,256]{1,0:T(8,128)(2,1)S(1)}, bf16[512,256]{1,0:T(8,128)(2,1)S(1)}, u32[]{:S(2)}, u32[]{:S(2)}) collective-permute-start(bf16[512,256]{1,0:T(8,128)(2,1)S(1)} %collective-permute-done.12.refs_0_), channel_id=1, source_target_pairs={{8,0},{9,1},{10,2},{11,3}} | collective-permute-start | bytes 786440 | tf_op jit(solution)/shard_map/ppermute | solution.py:480
  58.9 2.3 %collective-permute-done.14 = bf16[32,1536]{1,0:T(8,128)(2,1)S(1)} collective-permute-done((bf16[32,1536]{1,0:T(8,128)(2,1)S(1)}, bf16[32,1536]{1,0:T(8,128)(2,1)S(1)}, u32[]{:S(2)}, u32[]{:S(2)}) %collective-permute-start.14) | collective-permute-done | bytes 98336 | tf_op jit(solution)/shard_map/ppermute | solution.py:476
  61.3 2.5 %collective-permute-start.18 = (bf16[32,1536]{1,0:T(8,128)(2,1)S(1)}, bf16[32,1536]{1,0:T(8,128)(2,1)S(1)}, u32[]{:S(2)}, u32[]{:S(2)}) collective-permute-start(bf16[32,1536]{1,0:T(8,128)(2,1)S(1)} %add_convert_fusion.refs_0_), channel_id=1, source_target_pairs={{0,6},{1,7},{2,4},{3,5},{4,2},{5,3},{6,0},{7,1},{8,14},{9,15},{10,... | collective-permute-start | bytes 294920 | tf_op jit(solution)/shard_map/ppermute | solution.py:476
  64.2 1.5 %collective-permute-start.16 = (bf16[32,1536]{1,0:T(8,128)(2,1)S(1)}, bf16[32,1536]{1,0:T(8,128)(2,1)S(1)}, u32[]{:S(2)}, u32[]{:S(2)}) collective-permute-start(bf16[32,1536]{1,0:T(8,128)(2,1)S(1)} %add_convert_fusion.refs_0_), channel_id=1, source_target_pairs={{0,2},{1,3},{2,0},{3,1},{4,6},{5,7},{6,4},{7,5},{8,10},{9,11},{10,... | collective-permute-start | bytes 294920 | tf_op jit(solution)/shard_map/ppermute | solution.py:476
  65.7 2.4 %finish.1 = (bf16[4,512,256]{2,1,0:T(8,128)(2,1)}, f32[3,512,256]{2,1,0:T(8,128)S(1)}) custom-call(bf16[512,256]{1,0:T(8,128)(2,1)S(1)} %get-tuple-element.70.own_skip, bf16[4,3,512,256]{3,2,1,0:T(8,128)(2,1)S(1)} %get-tuple-element.75.gated_all, bf16[4,3,512,512]{3,2,1,0:T(8,128)(2,1)S(1)} %get-tuple-element.76.dz_all, ...), custom_call_target="tpu_custom_call" | custom-call | tf_op jit(solution)/shard_map/finish/pallas_call | solution.py:464
  68.1 1.5 %collective-permute-done.20.refs_2_ = bf16[512,256]{1,0:T(8,128)(2,1)S(1)} collective-permute-done((bf16[512,256]{1,0:T(8,128)(2,1)S(1)}, bf16[512,256]{1,0:T(8,128)(2,1)S(1)}, u32[]{:S(2)}, u32[]{:S(2)}) %collective-permute-start.20) | collective-permute-done | bytes 262176 | tf_op jit(solution)/shard_map/ppermute | solution.py:480
  70.8 1.4 %collective-permute-done.17.refs_2_ = bf16[32,1536]{1,0:T(8,128)(2,1)S(1)} collective-permute-done((bf16[32,1536]{1,0:T(8,128)(2,1)S(1)}, bf16[32,1536]{1,0:T(8,128)(2,1)S(1)}, u32[]{:S(2)}, u32[]{:S(2)}) %collective-permute-start.17) | collective-permute-done | bytes 98336 | tf_op jit(solution)/shard_map/ppermute | solution.py:476
  72.3 1.7 %collective-permute-done.22.refs_4_ = bf16[4,32,1536]{2,1,0:T(8,128)(2,1)S(1)} collective-permute-done((bf16[4,32,1536]{2,1,0:T(8,128)(2,1)S(1)}, bf16[4,32,1536]{2,1,0:T(8,128)(2,1)S(1)}, u32[]{:S(2)}, u32[]{:S(2)}) %collective-permute-start.22) | collective-permute-done | bytes 393248 | tf_op jit(solution)/shard_map/ppermute | solution.py:476
  74.1 1.3 %place_sums.1 = (f32[1,256,512]{2,1,0:T(8,128)}, f32[1,256,512]{2,1,0:T(8,128)}, f32[1,256,256]{2,1,0:T(8,128)}, f32[1,256,256]{2,1,0:T(8,128)}) custom-call(bf16[32,1536]{1,0:T(8,128)(2,1)S(1)} %add_convert_fusion.refs_0_, bf16[32,1536]{1,0:T(8,128)(2,1)S(1)} %collective-permute-done.16.refs_1_, bf16[32,1536]{1,0:T(8,128)(2,1)S(1)} %collective-permute-done.17.refs_2_, ...), custom_call_target="tpu_custom_call" | custom-call | tf_op jit(solution)/shard_map/place_sums/pallas_call | solution.py:464
  (47 shorter events, 11.0 us)
Async XLA Ops:
  0.6 27.0 %copy-start.4 = (bf16[1,256,512]{2,1,0:T(8,128)(2,1)S(1)}, bf16[1,256,512]{2,1,0:T(8,128)(2,1)}, u32[]{:S(2)}) copy-start(bf16[1,256,512]{2,1,0:T(8,128)(2,1)} %refs_7_.1) | copy-start | bytes 786436
  1.8 15.2 %collective-permute-start.2 = (bf16[128,1536]{1,0:T(8,128)(2,1)S(1)}, bf16[128,1536]{1,0:T(8,128)(2,1)S(1)}, u32[]{:S(2)}, u32[]{:S(2)}) collective-permute-start(bf16[128,1536]{1,0:T(8,128)(2,1)S(1)} %fusion.2), channel_id=1, source_target_pairs={{0,16},{8,24},{16,0},{24,8},{1,17},{9,25},{17,1},{25,9},{2,18},{10... | collective-permute-start | bytes 1179656 | tf_op jit(solution)/shard_map/ppermute | solution.py:476
  4.8 12.2 %collective-permute-start.1 = (bf16[128,1536]{1,0:T(8,128)(2,1)S(1)}, bf16[128,1536]{1,0:T(8,128)(2,1)S(1)}, u32[]{:S(2)}, u32[]{:S(2)}) collective-permute-start(bf16[128,1536]{1,0:T(8,128)(2,1)S(1)} %fusion.2), channel_id=1, source_target_pairs={{0,8},{8,0},{16,24},{24,16},{1,9},{9,1},{17,25},{25,17},{2,10},{10... | collective-permute-start | bytes 1179656 | tf_op jit(solution)/shard_map/ppermute | solution.py:476
  6.3 17.3 %collective-permute-start.3 = (bf16[128,1536]{1,0:T(8,128)(2,1)S(1)}, bf16[128,1536]{1,0:T(8,128)(2,1)S(1)}, u32[]{:S(2)}, u32[]{:S(2)}) collective-permute-start(bf16[128,1536]{1,0:T(8,128)(2,1)S(1)} %fusion.2), channel_id=1, source_target_pairs={{0,24},{8,16},{16,8},{24,0},{1,25},{9,17},{17,9},{25,1},{2,26},{10... | collective-permute-start | bytes 1179656 | tf_op jit(solution)/shard_map/ppermute | solution.py:476
  7.4 9.7 %collective-permute-start = (bf16[512,256]{1,0:T(8,128)(2,1)S(1)}, bf16[512,256]{1,0:T(8,128)(2,1)S(1)}, u32[]{:S(2)}, u32[]{:S(2)}) collective-permute-start(bf16[512,256]{1,0:T(8,128)(2,1)S(1)} %dynamic-slice_bitcast_fusion), channel_id=1, source_target_pairs={{0,4},{1,5},{2,6},{3,7},{8,12},{9,13},{10,14},{11,15},{16,20},{17,... | collective-permute-start | bytes 786440 | tf_op jit(solution)/shard_map/ppermute | solution.py:18
  23.6 3.6 %collective-permute-start.4 = (bf16[128,1536]{1,0:T(8,128)(2,1)S(1)}, bf16[128,1536]{1,0:T(8,128)(2,1)S(1)}, u32[]{:S(2)}, u32[]{:S(2)}) collective-permute-start(bf16[128,1536]{1,0:T(8,128)(2,1)S(1)} %collective-permute-done.1.refs_8_), channel_id=1, source_target_pairs={{0,1},{1,0},{2,3},{3,2},{4,5},{5,4},{6,7},{7,6},{8,9},{9,8},{10,11... | collective-permute-start | bytes 1179656 | tf_op jit(solution)/shard_map/ppermute | solution.py:476
  23.6 4.0 %collective-permute-start.5 = (bf16[128,1536]{1,0:T(8,128)(2,1)S(1)}, bf16[128,1536]{1,0:T(8,128)(2,1)S(1)}, u32[]{:S(2)}, u32[]{:S(2)}) collective-permute-start(bf16[128,1536]{1,0:T(8,128)(2,1)S(1)} %collective-permute-done.2.refs_9_), channel_id=1, source_target_pairs={{0,1},{1,0},{2,3},{3,2},{4,5},{5,4},{6,7},{7,6},{8,9},{9,8},{10,11... | collective-permute-start | bytes 1179656 | tf_op jit(solution)/shard_map/ppermute | solution.py:476
  24.2 3.5 %collective-permute-start.6 = (bf16[128,1536]{1,0:T(8,128)(2,1)S(1)}, bf16[128,1536]{1,0:T(8,128)(2,1)S(1)}, u32[]{:S(2)}, u32[]{:S(2)}) collective-permute-start(bf16[128,1536]{1,0:T(8,128)(2,1)S(1)} %collective-permute-done.3.refs_10_), channel_id=1, source_target_pairs={{0,1},{1,0},{2,3},{3,2},{4,5},{5,4},{6,7},{7,6},{8,9},{9,8},{10,11... | collective-permute-start | bytes 1179656 | tf_op jit(solution)/shard_map/ppermute | solution.py:476
  24.2 11.6 %collective-permute-start.9 = (bf16[512,256]{1,0:T(8,128)(2,1)S(1)}, bf16[512,256]{1,0:T(8,128)(2,1)S(1)}, u32[]{:S(2)}, u32[]{:S(2)}) collective-permute-start(bf16[512,256]{1,0:T(8,128)(2,1)S(1)} %collective-permute-done.refs_3_), channel_id=1, source_target_pairs={{0,24},{8,16},{16,8},{24,0},{1,25},{9,17},{17,9},{25,1},{2,26},{10... | collective-permute-start | bytes 786440 | tf_op jit(solution)/shard_map/ppermute | solution.py:476
  26.8 12.6 %collective-permute-start.8 = (bf16[512,256]{1,0:T(8,128)(2,1)S(1)}, bf16[512,256]{1,0:T(8,128)(2,1)S(1)}, u32[]{:S(2)}, u32[]{:S(2)}) collective-permute-start(bf16[512,256]{1,0:T(8,128)(2,1)S(1)} %collective-permute-done.refs_3_), channel_id=1, source_target_pairs={{0,16},{8,24},{16,0},{24,8},{1,17},{9,25},{17,1},{25,9},{2,18},{10... | collective-permute-start | bytes 786440 | tf_op jit(solution)/shard_map/ppermute | solution.py:476
  27.3 12.4 %collective-permute-start.7 = (bf16[512,256]{1,0:T(8,128)(2,1)S(1)}, bf16[512,256]{1,0:T(8,128)(2,1)S(1)}, u32[]{:S(2)}, u32[]{:S(2)}) collective-permute-start(bf16[512,256]{1,0:T(8,128)(2,1)S(1)} %collective-permute-done.refs_3_), channel_id=1, source_target_pairs={{0,8},{8,0},{16,24},{24,16},{1,9},{9,1},{17,25},{25,17},{2,10},{10... | collective-permute-start | bytes 786440 | tf_op jit(solution)/shard_map/ppermute | solution.py:476
  34.3 16.3 %collective-permute-start.12 = (bf16[512,256]{1,0:T(8,128)(2,1)S(1)}, bf16[512,256]{1,0:T(8,128)(2,1)S(1)}, u32[]{:S(2)}, u32[]{:S(2)}) collective-permute-start(bf16[512,256]{1,0:T(8,128)(2,1)S(1)} %get-tuple-element.86), channel_id=1, source_target_pairs={{4,0},{5,1},{6,2},{7,3},{12,8},{13,9},{14,10},{15,11},{20,16},{21,... | collective-permute-start | bytes 786440 | tf_op jit(solution)/shard_map/ppermute | solution.py:18
  47.0 1.5 %collective-permute-start.10 = (bf16[64,1536]{1,0:T(8,128)(2,1)S(1)}, bf16[64,1536]{1,0:T(8,128)(2,1)S(1)}, u32[]{:S(2)}, u32[]{:S(2)}) collective-permute-start(bf16[64,1536]{1,0:T(8,128)(2,1)S(1)} %get-tuple-element.80), channel_id=1, source_target_pairs={{0,1},{1,0},{2,3},{3,2},{4,5},{5,4},{6,7},{7,6},{8,9},{9,8},{10,11... | collective-permute-start | bytes 589832 | tf_op jit(solution)/shard_map/ppermute | solution.py:476
  47.1 1.7 %collective-permute-start.11 = (bf16[64,1536]{1,0:T(8,128)(2,1)S(1)}, bf16[64,1536]{1,0:T(8,128)(2,1)S(1)}, u32[]{:S(2)}, u32[]{:S(2)}) collective-permute-start(bf16[64,1536]{1,0:T(8,128)(2,1)S(1)} %get-tuple-element.81), channel_id=1, source_target_pairs={{0,1},{1,0},{2,3},{3,2},{4,5},{5,4},{6,7},{7,6},{8,9},{9,8},{10,11... | collective-permute-start | bytes 589832 | tf_op jit(solution)/shard_map/ppermute | solution.py:476
  50.6 7.0 %collective-permute-start.13 = (bf16[32,1536]{1,0:T(8,128)(2,1)S(1)}, bf16[32,1536]{1,0:T(8,128)(2,1)S(1)}, u32[]{:S(2)}, u32[]{:S(2)}) collective-permute-start(bf16[32,1536]{1,0:T(8,128)(2,1)S(1)} %get-tuple-element.87), channel_id=1, source_target_pairs={{0,6},{1,7},{2,4},{3,5},{4,2},{5,3},{6,0},{7,1},{8,14},{9,15},{10,... | collective-permute-start | bytes 294920 | tf_op jit(solution)/shard_map/ppermute | solution.py:476
  52.5 8.7 %collective-permute-start.14 = (bf16[32,1536]{1,0:T(8,128)(2,1)S(1)}, bf16[32,1536]{1,0:T(8,128)(2,1)S(1)}, u32[]{:S(2)}, u32[]{:S(2)}) collective-permute-start(bf16[32,1536]{1,0:T(8,128)(2,1)S(1)} %get-tuple-element.88), channel_id=1, source_target_pairs={{0,4},{1,5},{2,6},{3,7},{4,0},{5,1},{6,2},{7,3},{8,12},{9,13},{10,... | collective-permute-start | bytes 294920 | tf_op jit(solution)/shard_map/ppermute | solution.py:476
  52.5 8.7 %collective-permute-start.15 = (bf16[32,1536]{1,0:T(8,128)(2,1)S(1)}, bf16[32,1536]{1,0:T(8,128)(2,1)S(1)}, u32[]{:S(2)}, u32[]{:S(2)}) collective-permute-start(bf16[32,1536]{1,0:T(8,128)(2,1)S(1)} %get-tuple-element.89), channel_id=1, source_target_pairs={{0,2},{1,3},{2,0},{3,1},{4,6},{5,7},{6,4},{7,5},{8,10},{9,11},{10,... | collective-permute-start | bytes 294920 | tf_op jit(solution)/shard_map/ppermute | solution.py:476
  55.0 9.2 %collective-permute-start.21 = (bf16[512,256]{1,0:T(8,128)(2,1)S(1)}, bf16[512,256]{1,0:T(8,128)(2,1)S(1)}, u32[]{:S(2)}, u32[]{:S(2)}) collective-permute-start(bf16[512,256]{1,0:T(8,128)(2,1)S(1)} %collective-permute-done.12.refs_0_), channel_id=1, source_target_pairs={{24,0},{25,1},{26,2},{27,3}} | collective-permute-start | bytes 786440 | tf_op jit(solution)/shard_map/ppermute | solution.py:480
  56.3 13.3 %collective-permute-start.20 = (bf16[512,256]{1,0:T(8,128)(2,1)S(1)}, bf16[512,256]{1,0:T(8,128)(2,1)S(1)}, u32[]{:S(2)}, u32[]{:S(2)}) collective-permute-start(bf16[512,256]{1,0:T(8,128)(2,1)S(1)} %collective-permute-done.12.refs_0_), channel_id=1, source_target_pairs={{16,0},{17,1},{18,2},{19,3}} | collective-permute-start | bytes 786440 | tf_op jit(solution)/shard_map/ppermute | solution.py:480
  57.6 12.0 %collective-permute-start.19 = (bf16[512,256]{1,0:T(8,128)(2,1)S(1)}, bf16[512,256]{1,0:T(8,128)(2,1)S(1)}, u32[]{:S(2)}, u32[]{:S(2)}) collective-permute-start(bf16[512,256]{1,0:T(8,128)(2,1)S(1)} %collective-permute-done.12.refs_0_), channel_id=1, source_target_pairs={{8,0},{9,1},{10,2},{11,3}} | collective-permute-start | bytes 786440 | tf_op jit(solution)/shard_map/ppermute | solution.py:480
  61.3 9.5 %collective-permute-start.18 = (bf16[32,1536]{1,0:T(8,128)(2,1)S(1)}, bf16[32,1536]{1,0:T(8,128)(2,1)S(1)}, u32[]{:S(2)}, u32[]{:S(2)}) collective-permute-start(bf16[32,1536]{1,0:T(8,128)(2,1)S(1)} %add_convert_fusion.refs_0_), channel_id=1, source_target_pairs={{0,6},{1,7},{2,4},{3,5},{4,2},{5,3},{6,0},{7,1},{8,14},{9,15},{10,... | collective-permute-start | bytes 294920 | tf_op jit(solution)/shard_map/ppermute | solution.py:476
  63.8 8.4 %collective-permute-start.17 = (bf16[32,1536]{1,0:T(8,128)(2,1)S(1)}, bf16[32,1536]{1,0:T(8,128)(2,1)S(1)}, u32[]{:S(2)}, u32[]{:S(2)}) collective-permute-start(bf16[32,1536]{1,0:T(8,128)(2,1)S(1)} %add_convert_fusion.refs_0_), channel_id=1, source_target_pairs={{0,4},{1,5},{2,6},{3,7},{4,0},{5,1},{6,2},{7,3},{8,12},{9,13},{10,... | collective-permute-start | bytes 294920 | tf_op jit(solution)/shard_map/ppermute | solution.py:476
  64.2 8.0 %collective-permute-start.16 = (bf16[32,1536]{1,0:T(8,128)(2,1)S(1)}, bf16[32,1536]{1,0:T(8,128)(2,1)S(1)}, u32[]{:S(2)}, u32[]{:S(2)}) collective-permute-start(bf16[32,1536]{1,0:T(8,128)(2,1)S(1)} %add_convert_fusion.refs_0_), channel_id=1, source_target_pairs={{0,2},{1,3},{2,0},{3,1},{4,6},{5,7},{6,4},{7,5},{8,10},{9,11},{10,... | collective-permute-start | bytes 294920 | tf_op jit(solution)/shard_map/ppermute | solution.py:476
  72.3 1.8 %collective-permute-start.22 = (bf16[4,32,1536]{2,1,0:T(8,128)(2,1)S(1)}, bf16[4,32,1536]{2,1,0:T(8,128)(2,1)S(1)}, u32[]{:S(2)}, u32[]{:S(2)}) collective-permute-start(bf16[4,32,1536]{2,1,0:T(8,128)(2,1)S(1)} %pad_maximum_fusion), channel_id=1, source_target_pairs={{0,1},{1,0},{2,3},{3,2},{4,5},{5,4},{6,7},{7,6},{8,9},{9,8},{10,11... | collective-permute-start | bytes 1179656 | tf_op jit(solution)/shard_map/ppermute | solution.py:476
  (6 other events, 84.7 us)

commit v7 on v6

--- a/solution.py
+++ b/solution.py
@@ -209,6 +209,48 @@
     return local_call(finish_kernel, "finish", [own_skip, gated_all, dz_all, g_all, weights], out_shape)
 
 
+def add_products(section, sums, sums_in, tapped, h_all, gated_all, dz_all, g_all, cot):
+    channels = tapped.shape[-1]
+    for i in range(tapped.shape[0]):
+        products = (
+            rows_dot(tapped[i], dz_all[section, i]),
+            rows_dot(h_all[section, i], dz_all[section, i]),
+            rows_dot(gated_all[section, i], g_all[section + 1, i]),
+            rows_dot(gated_all[section, i], cot[i]),
+        )
+        column = 0
+        for product in products:
+            spot = slice(column, column + product.shape[1])
+            column += product.shape[1]
+            if i:
+                sums[:, spot] += product
+            else:
+                sums[:, spot] = sums_in[:, spot] + product if sums_in is not None else product
+
+
+def ahead_kernel(tapped, cot, h_all, gated_all, dz_all, g_all, weights, next_signal, next_cot, next_res, sums, ahead_pre, ahead_du):
+    layers, _, _, channels = gated_all.shape
+    half = channels
+    early = layers - ahead_du.shape[0]
+    section = lax.axis_index("section")
+    add_products(section, sums, None, tapped, h_all, gated_all, dz_all, g_all, cot)
+    for i in range(layers - 1):
+        ahead_pre[i] = narrow_dot(next_signal[i], weights[0, :, : 2 * half])
+        for k in range(early, layers):
+            du = turned_dot(next_cot[i], weights[k, :, 3 * half : 4 * half])
+            if k == layers - 1:
+                du = du + turned_dot(next_res[i], weights[k, :, 2 * half : 3 * half])
+            ahead_du[k - early, i] = du
+
+
+def ahead(tap, cot, kept, weights, following):
+    layers, channels, width = weights.shape
+    _, seq_rows, _ = cot.shape
+    shapes = [(channels, width), (layers - 1, seq_rows, 2 * channels), (4, layers - 1, seq_rows, channels)]
+    out_shape = [jax.ShapeDtypeStruct(shape, jnp.float32) for shape in shapes]
+    return local_call(ahead_kernel, "ahead", [tap[None], cot, *kept, weights, *following], out_shape)
+
+
 def stack_kernel(layers, last, *refs):
     refs = list(refs)
     take = lambda count: [refs.pop(0) for _ in range(count)]
@@ -221,15 +263,16 @@
         own = take(4)
         mine = take(layers - 1)
         other = take(layers - 1)
-        next_signal, next_cot, next_res = take(3)
-        skip_out, grad_out, back_out, sums, weights, ahead_pre, ahead_du = take(7)
-    early = layers - ahead_du.shape[0]
-    tapped, h_all, tanh_all, sig_all = take(4)
+        skip_out, grad_out, back_out, weights, h_all, gated_all, dz_all, g_all = take(8)
+    early = layers - ahead_du.shape[0] if last else layers
+    if last:
+        (h_all,) = take(1)
+    tapped, tanh_all, sig_all = take(3)
     stream_here, tap_here = take(2)
     if last:
         (sums,) = take(1)
     else:
-        gated_all, dz_all, g_all, weights_here = take(4)
+        (weights_here,) = take(1)
     section = lax.axis_index("section")
     core = lax.rem(lax.axis_index("tm"), 2)
     _, seqs, seq_rows, channels = h_all.shape
@@ -255,32 +298,27 @@
         pltpu.make_async_copy(ref, tapped.at[i], tap_here).start()
     pltpu.make_async_copy(res_cot, g_all.at[layers], stream_here.at[1]).start()
 
-    wait_bytes(h_all.at[0], stream_here.at[0])
+    layer_in = lambda k, i: h_all[k, i] if k else signal[i]
+    grad_out_of = lambda k, i: g_all[k + 1, i] if k + 1 < layers else res_cot[i]
     for k in range(layers):
         if not last:
             wait_bytes(weights.at[k], weights_here.at[k])
-        if k == 0:
-            wait_bytes(tapped, tap_here)
         for i in range(seqs):
             if k == 0 and last:
-                pre = ahead_pre[i] + narrow_dot(tapped[i], weights[0, :, tap])
+                pre = ahead_pre[i] + narrow_dot(taps[i][...], weights[0, :, tap])
             else:
-                pre = narrow_dot(h_all[k, i], weights[k, :, now])
+                pre = narrow_dot(layer_in(k, i), weights[k, :, now])
                 if k == 0:
-                    pre = pre + narrow_dot(tapped[i], weights[0, :, tap])
+                    pre = pre + narrow_dot(taps[i][...], weights[0, :, tap])
             tanh_part = jnp.tanh(pre[:, :half])
             sig_part = 0.5 * jnp.tanh(0.5 * pre[:, half:]) + 0.5
             tanh_all[k, i] = tanh_part
             sig_all[k, i] = sig_part
             gated_all[k, i] = (tanh_part * sig_part).astype(jnp.bfloat16)
-        if k == 0 and not last:
-            for i in range(layers - 1):
-                ahead_pre[i] = narrow_dot(next_signal[i], weights[0, :, now])
         if k + 1 < layers:
             for i in range(seqs):
                 stream = narrow_dot(gated_all[k, i], weights[k, :, res])
-                h_all[k + 1, i] = (h_all[k, i].astype(jnp.float32) + stream).astype(jnp.bfloat16)
-    wait_bytes(g_all.at[layers], stream_here.at[1])
+                h_all[k + 1, i] = (layer_in(k, i).astype(jnp.float32) + stream).astype(jnp.bfloat16)
     if not last:
         skip_out[...] = skip_sum([gated_all[k, 0] for k in range(layers)], weights, skip)
     for k in reversed(range(layers)):
@@ -288,7 +326,7 @@
             if last and k == layers - 1:
                 du = ahead_du[k - early, i]
             else:
-                du = turned_dot(g_all[k + 1, i], weights[k, :, res])
+                du = turned_dot(grad_out_of(k, i), weights[k, :, res])
                 if last and k >= early:
                     du = du + ahead_du[k - early, i]
                 else:
@@ -298,33 +336,17 @@
             scaled = du * sig_part
             dz_all[k, i, :, :half] = (scaled * (1.0 - tanh_part * tanh_part)).astype(jnp.bfloat16)
             dz_all[k, i, :, half:] = (scaled * (tanh_part * (1.0 - sig_part))).astype(jnp.bfloat16)
-        if k >= early and not last:
-            for i in range(layers - 1):
-                du = turned_dot(next_cot[i], weights[k, :, skip])
-                if k == layers - 1:
-                    du = du + turned_dot(next_res[i], weights[k, :, res])
-                ahead_du[k - early, i] = du
         for i in range(seqs if k or not last else 0):
             below = turned_dot(dz_all[k, i], weights[k, :, now])
-            g_all[k, i] = (g_all[k + 1, i].astype(jnp.float32) + below).astype(jnp.bfloat16)
+            g_all[k, i] = (grad_out_of(k, i).astype(jnp.float32) + below).astype(jnp.bfloat16)
+    wait_bytes(h_all.at[0], stream_here.at[0])
+    wait_bytes(tapped, tap_here)
+    wait_bytes(g_all.at[layers], stream_here.at[1])
     if not last:
         grad_out[...] = g_all[section, 0]
         back_out[...] = turned_dot(dz_all[0, 0], weights[0, :, tap]).astype(jnp.bfloat16)
-    for i in range(seqs):
-        products = (
-            rows_dot(tapped[i], dz_all[section, i]),
-            rows_dot(h_all[section, i], dz_all[section, i]),
-            rows_dot(gated_all[section, i], g_all[section + 1, i]),
-            rows_dot(gated_all[section, i], cot[i]),
-        )
-        spots = (slice(0, 2 * half), slice(2 * half, 4 * half), slice(4 * half, 4 * half + channels), slice(4 * half + channels, None))
-        for spot, product in zip(spots, products):
-            if i == 0 and last:
-                sums[:, spot] = sums_in[:, spot] + product
-            elif i == 0:
-                sums[:, spot] = product
-            else:
-                sums[:, spot] += product
+    if last:
+        add_products(section, sums, sums_in, tapped, h_all, gated_all, dz_all, g_all, cot)
     if last:
         kept_out[...] = sums[pl.ds(pl.multiple_of(core * low_rows, low_rows), low_rows)]
         sent_rows = low_rows // len(sent_outs)
@@ -333,7 +355,7 @@
             sent_out[...] = sums[pl.ds(start, sent_rows)].astype(jnp.bfloat16)
 
 
-def layer_stack(streams, taps, number, weights, following=(), earlier=None):
+def layer_stack(streams, taps, number, weights, earlier=None):
     seqs, seq_rows, channels = streams[0].shape
     layers = number
     last = earlier is not None
@@ -342,29 +364,24 @@
     near = pl.BlockSpec(memory_space=pltpu.VMEM)
     rows = lambda count, wide=1: ((count, seqs, seq_rows, wide * channels), jnp.bfloat16)
     kept = [rows(layers), rows(layers, 2), rows(layers + 1)]
-    scratch = [
+    scratch = [pltpu.VMEM(*rows(layers))] if last else []
+    scratch += [
         pltpu.VMEM((seqs, seq_rows, channels), jnp.bfloat16),
-        pltpu.VMEM(*rows(layers)),
         pltpu.VMEM((layers, seqs, seq_rows, channels), jnp.float32),
         pltpu.VMEM((layers, seqs, seq_rows, channels), jnp.float32),
         pltpu.SemaphoreType.DMA((2,)),
         pltpu.SemaphoreType.DMA,
     ]
     operands = [*streams, *taps, *weights]
-    in_specs = [near] * 3 + [anywhere] * len(taps) + [near if last else anywhere] * len(weights)
+    in_specs = [near] * (3 + len(taps)) + [near if last else anywhere] * len(weights)
     if last:
         operands += [*earlier]
         in_specs += [near] * len(earlier)
         shapes = kept + [((channels // 4, width), jnp.bfloat16)] * 2 + [((channels // 2, width), jnp.float32)]
         scratch += [pltpu.VMEM((channels, width), jnp.float32)]
     else:
-        shapes = [((seq_rows, channels), jnp.bfloat16)] * 3
-        shapes += [((channels, width), jnp.float32), ((layers, channels, width), jnp.bfloat16)]
-        shapes += [((layers - 1, seq_rows, 2 * channels), jnp.float32)]
-        shapes += [((2, layers - 1, seq_rows, channels), jnp.float32)]
-        operands += [*following]
-        in_specs += [near] * len(following)
-        scratch += [pltpu.VMEM(*shape) for shape in kept] + [pltpu.SemaphoreType.DMA((layers,))]
+        shapes = [((seq_rows, channels), jnp.bfloat16)] * 3 + [((layers, channels, width), jnp.bfloat16), rows(layers)] + kept
+        scratch += [pltpu.SemaphoreType.DMA((layers,))]
     flops = 2 * 22 * layers * seqs * seq_rows * channels * channels
     return pl.pallas_call(
         functools.partial(stack_kernel, layers, last),
@@ -372,7 +389,7 @@
         out_specs=[near] * len(shapes),
         out_shape=[jax.ShapeDtypeStruct(*shape) for shape in shapes],
         scratch_shapes=scratch,
-        compiler_params=pltpu.CompilerParams(vmem_limit_bytes=(24 if last else 20) * 2**20),
+        compiler_params=pltpu.CompilerParams(vmem_limit_bytes=(21 if last else 18) * 2**20),
         cost_estimate=pl.CostEstimate(flops=flops, bytes_accessed=16 * seqs * seq_rows * channels, transcendentals=0),
         name="layer_stack",
     )(*operands)
@@ -523,9 +540,10 @@
     taps = [tap] + [swapped(tap, "section", by) for by in range(1, sections)]
 
     pieces = [w_now, w_res, w_skip, w_tap, *mine, *other]
-    own_skip, own_base, back, sums, weights, *ahead = layer_stack(own_streams, taps[:1], number, pieces, other_streams)
+    own_skip, own_base, back, weights, *kept_own = layer_stack(own_streams, taps[:1], number, pieces)
+    ahead_terms = ahead(taps[0], own_streams[1], kept_own, weights, other_streams)
     back = passed_along(back, "tm", -span)
-    gated, dz, g, *sent, kept = layer_stack(other_streams, taps[1:], number, [weights], earlier=(sums, *ahead))
+    gated, dz, g, *sent, kept = layer_stack(other_streams, taps[1:], number, [weights], earlier=ahead_terms)
     got = [swapped(value, "tm", 1) for value in sent]
     own_piece, pieces = spread(got, kept, shards // 2)
     pieces, back = lax.optimization_barrier((pieces, back))

time: 75.7 us -> 75.4 us (level)
  waiting for transfers between devices: 21.5 us -> 20.3 us
    pallas_call x4 -> x5, Pallas kernels: 4.88 us -> 6.94 us  [local_call(): pl.pallas_call(kernel, in_specs=[near] * len(operands), out_specs=[near]...]
    pallas_call x2, Pallas kernels: 14 us -> 12.6 us  [layer_stack(): pl.pallas_call(functools.partial(stack_kernel, layers, last), in_specs=in...]
    ppermute x2, waiting for transfers between devices: 2.46 us -> 1.58 us  [passed_along(): return lax.ppermute(x, axis, pairs)]
  transfers between devices with their start and end apart: 23 -> 23, of which waited for: 12 -> 13; matrix products, arithmetic and copies ran while one was open for 1% -> 1% of each run, Pallas kernels for 24% -> 25%
where the time goes in v7:
time: 75.4 us; the launch traced here: 75 us
  starting transfers between devices  28.2 us (37%)
  waiting for transfers between devices  20.3 us (27%)
  Pallas kernels  19.8 us (26%)
  local copies, waits for them, and re-layouts  4.65 us (6%)
  other arithmetic  1.22 us (2%)
  between operations  0.85 us (1%)
    ppermute x18, starting transfers between devices, swapped(): lax.ppermute(x, axis, [(i, i ^ by) for i in range(lax.axis_size(axis))])  17.9 us
    ppermute x18, waiting for transfers between devices, swapped(): lax.ppermute(x, axis, [(i, i ^ by) for i in range(lax.axis_size(axis))])  17.2 us
    pallas_call x2, Pallas kernels, layer_stack(): pl.pallas_call(functools.partial(stack_kernel, layers, last), in_specs=in...  12.6 us
    pallas_call x5, Pallas kernels, local_call(): pl.pallas_call(kernel, in_specs=[near] * len(operands), out_specs=[near]...  6.94 us
    ppermute x2, starting transfers between devices, passed_along(): return lax.ppermute(x, axis, pairs)  6.41 us
    ppermute x3, starting transfers between devices, between(): lax.ppermute(x, ('section', 'tm'), [(i * shards + t, j * shards + t) for...  3.85 us
    unnamed x14, local copies, waits for them, and re-layouts  3.69 us
    ppermute x2, waiting for transfers between devices, passed_along(): return lax.ppermute(x, axis, pairs)  1.58 us
  transfers between devices with their start and end apart: 23, of which 13 were waited for; matrix products, arithmetic and copies ran while one was open for 1% of the time, Pallas kernels for 25%

profile of v7, /device:TPU:0, one launch (start us, length us, event | category | flops | bytes accessed | tf_op | source)
XLA Modules:
  0.0 75.0 jit_solution(2209240333859794584)
XLA Ops:
  1.8 3.0 %collective-permute-start.2 = (bf16[128,1536]{1,0:T(8,128)(2,1)S(1)}, bf16[128,1536]{1,0:T(8,128)(2,1)S(1)}, u32[]{:S(2)}, u32[]{:S(2)}) collective-permute-start(bf16[128,1536]{1,0:T(8,128)(2,1)S(1)} %fusion.2), channel_id=1, source_target_pairs={{0,16},{8,24},{16,0},{24,8},{1,17},{9,25},{17,1},{25,9},{2,18},{10... | collective-permute-start | bytes 1179656 | tf_op jit(solution)/shard_map/ppermute | solution.py:493
  4.8 1.5 %collective-permute-start.1 = (bf16[128,1536]{1,0:T(8,128)(2,1)S(1)}, bf16[128,1536]{1,0:T(8,128)(2,1)S(1)}, u32[]{:S(2)}, u32[]{:S(2)}) collective-permute-start(bf16[128,1536]{1,0:T(8,128)(2,1)S(1)} %fusion.2), channel_id=1, source_target_pairs={{0,8},{8,0},{16,24},{24,16},{1,9},{9,1},{17,25},{25,17},{2,10},{10... | collective-permute-start | bytes 1179656 | tf_op jit(solution)/shard_map/ppermute | solution.py:493
  7.4 4.9 %collective-permute-start = (bf16[512,256]{1,0:T(8,128)(2,1)S(1)}, bf16[512,256]{1,0:T(8,128)(2,1)S(1)}, u32[]{:S(2)}, u32[]{:S(2)}) collective-permute-start(bf16[512,256]{1,0:T(8,128)(2,1)S(1)} %dynamic-slice_bitcast_fusion), channel_id=1, source_target_pairs={{0,4},{1,5},{2,6},{3,7},{8,12},{9,13},{10,14},{11,15},{16,20},{17,... | collective-permute-start | bytes 786440 | tf_op jit(solution)/shard_map/ppermute | solution.py:18
  13.5 1.2 %copy-done.1 = bf16[4,512,256]{2,1,0:T(8,128)(2,1)S(1)} copy-done((bf16[4,512,256]{2,1,0:T(8,128)(2,1)S(1)}, bf16[4,512,256]{2,1,0:T(8,128)(2,1)}, u32[]{:S(2)}) %copy-start.1) | copy-done | bytes 1048600
  17.0 6.6 %collective-permute-done.3.refs_10_ = bf16[128,1536]{1,0:T(8,128)(2,1)S(1)} collective-permute-done((bf16[128,1536]{1,0:T(8,128)(2,1)S(1)}, bf16[128,1536]{1,0:T(8,128)(2,1)S(1)}, u32[]{:S(2)}, u32[]{:S(2)}) %collective-permute-start.3) | collective-permute-done | bytes 393248 | tf_op jit(solution)/shard_map/ppermute | solution.py:493
  24.2 2.6 %collective-permute-start.9 = (bf16[512,256]{1,0:T(8,128)(2,1)S(1)}, bf16[512,256]{1,0:T(8,128)(2,1)S(1)}, u32[]{:S(2)}, u32[]{:S(2)}) collective-permute-start(bf16[512,256]{1,0:T(8,128)(2,1)S(1)} %collective-permute-done.refs_3_), channel_id=1, source_target_pairs={{0,24},{8,16},{16,8},{24,0},{1,25},{9,17},{17,9},{25,1},{2,26},{10... | collective-permute-start | bytes 786440 | tf_op jit(solution)/shard_map/ppermute | solution.py:493
  27.7 5.5 %layer_stack.2 = (bf16[512,256]{1,0:T(8,128)(2,1)S(1)}, bf16[512,256]{1,0:T(8,128)(2,1)S(1)}, bf16[512,256]{1,0:T(8,128)(2,1)S(1)}, bf16[4,256,1536]{2,1,0:T(8,1...) custom-call(bf16[1,512,256]{2,1,0:T(8,128)(2,1)S(1)} %get-tuple-elem, ...), custom_call_target="tpu_custom_call" | custom-call | flops 5905580032 | bytes 2097152 | tf_op jit(solution)/shard_map/layer_stack/pallas_call | solution.py:386
  33.2 1.5 %collective-permute-start.12 = (bf16[512,256]{1,0:T(8,128)(2,1)S(1)}, bf16[512,256]{1,0:T(8,128)(2,1)S(1)}, u32[]{:S(2)}, u32[]{:S(2)}) collective-permute-start(bf16[512,256]{1,0:T(8,128)(2,1)S(1)} %get-tuple-element.94), channel_id=1, source_target_pairs={{4,0},{5,1},{6,2},{7,3},{12,8},{13,9},{14,10},{15,11},{20,16},{21,... | collective-permute-start | bytes 786440 | tf_op jit(solution)/shard_map/ppermute | solution.py:18
  34.7 2.1 %ahead.1 = (f32[256,1536]{1,0:T(8,128)S(1)}, f32[3,512,512]{2,1,0:T(8,128)S(1)}, f32[4,3,512,256]{3,2,1,0:T(8,128)S(1)}) custom-call(bf16[1,512,256]{2,1,0:T(8,128)(2,1)S(1)} %bitcast.15, bf16[1,512,256]{2,1,0:T(8,128)(2,1)S(1)} %get-tuple-element.65.refs_1_.cot, bf16[4,1,512,256]{3,2,1,0:T(8,128)(2,1)S(1)} %get-tuple-element.76.h_all, ...), custom_call_target="tpu_custom_call" | custom-call | tf_op jit(solution)/shard_map/ahead/pallas_call | solution.py:481
  36.7 2.7 %collective-permute-done.8.refs_4_ = bf16[512,256]{1,0:T(8,128)(2,1)S(1)} collective-permute-done((bf16[512,256]{1,0:T(8,128)(2,1)S(1)}, bf16[512,256]{1,0:T(8,128)(2,1)S(1)}, u32[]{:S(2)}, u32[]{:S(2)}) %collective-permute-start.8) | collective-permute-done | bytes 262176 | tf_op jit(solution)/shard_map/ppermute | solution.py:493
  39.6 7.1 %layer_stack.3 = (bf16[4,3,512,256]{3,2,1,0:T(8,128)(2,1)S(1)}, bf16[4,3,512,512]{3,2,1,0:T(8,128)(2,1)S(1)}, bf16[5,3,512,256]{3,2,1,0:T(8,128)(2,1)S(1)}, bf16...) custom-call(bf16[3,512,256]{2,1,0:T(8,128)(2,1)S(1)} %get-tuple-element.72.next_signal.refs_0_, ...), custom_call_target="tpu_custom_call" | custom-call | flops 17716740096 | bytes 6291456 | tf_op jit(solution)/shard_map/layer_stack/pallas_call | solution.py:386
  49.5 2.8 %collective-permute-start.13 = (bf16[32,1536]{1,0:T(8,128)(2,1)S(1)}, bf16[32,1536]{1,0:T(8,128)(2,1)S(1)}, u32[]{:S(2)}, u32[]{:S(2)}) collective-permute-start(bf16[32,1536]{1,0:T(8,128)(2,1)S(1)} %get-tuple-element.95), channel_id=1, source_target_pairs={{0,6},{1,7},{2,4},{3,5},{4,2},{5,3},{6,0},{7,1},{8,14},{9,15},{10,... | collective-permute-start | bytes 294920 | tf_op jit(solution)/shard_map/ppermute | solution.py:493
  52.3 1.6 %collective-permute-start.15 = (bf16[32,1536]{1,0:T(8,128)(2,1)S(1)}, bf16[32,1536]{1,0:T(8,128)(2,1)S(1)}, u32[]{:S(2)}, u32[]{:S(2)}) collective-permute-start(bf16[32,1536]{1,0:T(8,128)(2,1)S(1)} %get-tuple-element.97), channel_id=1, source_target_pairs={{0,2},{1,3},{2,0},{3,1},{4,6},{5,7},{6,4},{7,5},{8,10},{9,11},{10,... | collective-permute-start | bytes 294920 | tf_op jit(solution)/shard_map/ppermute | solution.py:493
  53.9 1.3 %collective-permute-start.21 = (bf16[512,256]{1,0:T(8,128)(2,1)S(1)}, bf16[512,256]{1,0:T(8,128)(2,1)S(1)}, u32[]{:S(2)}, u32[]{:S(2)}) collective-permute-start(bf16[512,256]{1,0:T(8,128)(2,1)S(1)} %collective-permute-done.12.refs_0_), channel_id=1, source_target_pairs={{24,0},{25,1},{26,2},{27,3}} | collective-permute-start | bytes 786440 | tf_op jit(solution)/shard_map/ppermute | solution.py:497
  55.2 1.3 %collective-permute-start.20 = (bf16[512,256]{1,0:T(8,128)(2,1)S(1)}, bf16[512,256]{1,0:T(8,128)(2,1)S(1)}, u32[]{:S(2)}, u32[]{:S(2)}) collective-permute-start(bf16[512,256]{1,0:T(8,128)(2,1)S(1)} %collective-permute-done.12.refs_0_), channel_id=1, source_target_pairs={{16,0},{17,1},{18,2},{19,3}} | collective-permute-start | bytes 786440 | tf_op jit(solution)/shard_map/ppermute | solution.py:497
  57.0 1.3 %collective-permute-start.19 = (bf16[512,256]{1,0:T(8,128)(2,1)S(1)}, bf16[512,256]{1,0:T(8,128)(2,1)S(1)}, u32[]{:S(2)}, u32[]{:S(2)}) collective-permute-start(bf16[512,256]{1,0:T(8,128)(2,1)S(1)} %collective-permute-done.12.refs_0_), channel_id=1, source_target_pairs={{8,0},{9,1},{10,2},{11,3}} | collective-permute-start | bytes 786440 | tf_op jit(solution)/shard_map/ppermute | solution.py:497
  58.3 2.7 %collective-permute-done.14 = bf16[32,1536]{1,0:T(8,128)(2,1)S(1)} collective-permute-done((bf16[32,1536]{1,0:T(8,128)(2,1)S(1)}, bf16[32,1536]{1,0:T(8,128)(2,1)S(1)}, u32[]{:S(2)}, u32[]{:S(2)}) %collective-permute-start.14) | collective-permute-done | bytes 98336 | tf_op jit(solution)/shard_map/ppermute | solution.py:493
  61.0 2.5 %collective-permute-start.18 = (bf16[32,1536]{1,0:T(8,128)(2,1)S(1)}, bf16[32,1536]{1,0:T(8,128)(2,1)S(1)}, u32[]{:S(2)}, u32[]{:S(2)}) collective-permute-start(bf16[32,1536]{1,0:T(8,128)(2,1)S(1)} %add_convert_fusion.refs_0_), channel_id=1, source_target_pairs={{0,6},{1,7},{2,4},{3,5},{4,2},{5,3},{6,0},{7,1},{8,14},{9,15},{10,... | collective-permute-start | bytes 294920 | tf_op jit(solution)/shard_map/ppermute | solution.py:493
  63.7 1.8 %collective-permute-start.16 = (bf16[32,1536]{1,0:T(8,128)(2,1)S(1)}, bf16[32,1536]{1,0:T(8,128)(2,1)S(1)}, u32[]{:S(2)}, u32[]{:S(2)}) collective-permute-start(bf16[32,1536]{1,0:T(8,128)(2,1)S(1)} %add_convert_fusion.refs_0_), channel_id=1, source_target_pairs={{0,2},{1,3},{2,0},{3,1},{4,6},{5,7},{6,4},{7,5},{8,10},{9,11},{10,... | collective-permute-start | bytes 294920 | tf_op jit(solution)/shard_map/ppermute | solution.py:493
  65.4 2.4 %finish.1 = (bf16[4,512,256]{2,1,0:T(8,128)(2,1)}, f32[3,512,256]{2,1,0:T(8,128)S(1)}) custom-call(bf16[512,256]{1,0:T(8,128)(2,1)S(1)} %get-tuple-element.71.own_skip, bf16[4,3,512,256]{3,2,1,0:T(8,128)(2,1)S(1)} %get-tuple-element.83.gated_all, bf16[4,3,512,512]{3,2,1,0:T(8,128)(2,1)S(1)} %get-tuple-element.84.dz_all, ...), custom_call_target="tpu_custom_call" | custom-call | tf_op jit(solution)/shard_map/finish/pallas_call | solution.py:481
  67.8 1.4 %collective-permute-done.20.refs_2_ = bf16[512,256]{1,0:T(8,128)(2,1)S(1)} collective-permute-done((bf16[512,256]{1,0:T(8,128)(2,1)S(1)}, bf16[512,256]{1,0:T(8,128)(2,1)S(1)}, u32[]{:S(2)}, u32[]{:S(2)}) %collective-permute-start.20) | collective-permute-done | bytes 262176 | tf_op jit(solution)/shard_map/ppermute | solution.py:497
  70.4 1.6 %collective-permute-done.17.refs_2_ = bf16[32,1536]{1,0:T(8,128)(2,1)S(1)} collective-permute-done((bf16[32,1536]{1,0:T(8,128)(2,1)S(1)}, bf16[32,1536]{1,0:T(8,128)(2,1)S(1)}, u32[]{:S(2)}, u32[]{:S(2)}) %collective-permute-start.17) | collective-permute-done | bytes 98336 | tf_op jit(solution)/shard_map/ppermute | solution.py:493
  72.1 1.7 %collective-permute-done.22.refs_4_ = bf16[4,32,1536]{2,1,0:T(8,128)(2,1)S(1)} collective-permute-done((bf16[4,32,1536]{2,1,0:T(8,128)(2,1)S(1)}, bf16[4,32,1536]{2,1,0:T(8,128)(2,1)S(1)}, u32[]{:S(2)}, u32[]{:S(2)}) %collective-permute-start.22) | collective-permute-done | bytes 393248 | tf_op jit(solution)/shard_map/ppermute | solution.py:493
  73.8 1.3 %place_sums.1 = (f32[1,256,512]{2,1,0:T(8,128)}, f32[1,256,512]{2,1,0:T(8,128)}, f32[1,256,256]{2,1,0:T(8,128)}, f32[1,256,256]{2,1,0:T(8,128)}) custom-call(bf16[32,1536]{1,0:T(8,128)(2,1)S(1)} %add_convert_fusion.refs_0_, bf16[32,1536]{1,0:T(8,128)(2,1)S(1)} %collective-permute-done.16.refs_1_, bf16[32,1536]{1,0:T(8,128)(2,1)S(1)} %collective-permute-done.17.refs_2_, ...), custom_call_target="tpu_custom_call" | custom-call | tf_op jit(solution)/shard_map/place_sums/pallas_call | solution.py:481
  (48 shorter events, 12.1 us)
Async XLA Ops:
  0.6 27.0 %copy-start.4 = (bf16[1,256,512]{2,1,0:T(8,128)(2,1)S(1)}, bf16[1,256,512]{2,1,0:T(8,128)(2,1)}, u32[]{:S(2)}) copy-start(bf16[1,256,512]{2,1,0:T(8,128)(2,1)} %refs_7_.1) | copy-start | bytes 786436
  1.8 15.2 %collective-permute-start.2 = (bf16[128,1536]{1,0:T(8,128)(2,1)S(1)}, bf16[128,1536]{1,0:T(8,128)(2,1)S(1)}, u32[]{:S(2)}, u32[]{:S(2)}) collective-permute-start(bf16[128,1536]{1,0:T(8,128)(2,1)S(1)} %fusion.2), channel_id=1, source_target_pairs={{0,16},{8,24},{16,0},{24,8},{1,17},{9,25},{17,1},{25,9},{2,18},{10... | collective-permute-start | bytes 1179656 | tf_op jit(solution)/shard_map/ppermute | solution.py:493
  4.8 12.2 %collective-permute-start.1 = (bf16[128,1536]{1,0:T(8,128)(2,1)S(1)}, bf16[128,1536]{1,0:T(8,128)(2,1)S(1)}, u32[]{:S(2)}, u32[]{:S(2)}) collective-permute-start(bf16[128,1536]{1,0:T(8,128)(2,1)S(1)} %fusion.2), channel_id=1, source_target_pairs={{0,8},{8,0},{16,24},{24,16},{1,9},{9,1},{17,25},{25,17},{2,10},{10... | collective-permute-start | bytes 1179656 | tf_op jit(solution)/shard_map/ppermute | solution.py:493
  6.3 17.3 %collective-permute-start.3 = (bf16[128,1536]{1,0:T(8,128)(2,1)S(1)}, bf16[128,1536]{1,0:T(8,128)(2,1)S(1)}, u32[]{:S(2)}, u32[]{:S(2)}) collective-permute-start(bf16[128,1536]{1,0:T(8,128)(2,1)S(1)} %fusion.2), channel_id=1, source_target_pairs={{0,24},{8,16},{16,8},{24,0},{1,25},{9,17},{17,9},{25,1},{2,26},{10... | collective-permute-start | bytes 1179656 | tf_op jit(solution)/shard_map/ppermute | solution.py:493
  7.4 9.7 %collective-permute-start = (bf16[512,256]{1,0:T(8,128)(2,1)S(1)}, bf16[512,256]{1,0:T(8,128)(2,1)S(1)}, u32[]{:S(2)}, u32[]{:S(2)}) collective-permute-start(bf16[512,256]{1,0:T(8,128)(2,1)S(1)} %dynamic-slice_bitcast_fusion), channel_id=1, source_target_pairs={{0,4},{1,5},{2,6},{3,7},{8,12},{9,13},{10,14},{11,15},{16,20},{17,... | collective-permute-start | bytes 786440 | tf_op jit(solution)/shard_map/ppermute | solution.py:18
  23.6 3.6 %collective-permute-start.4 = (bf16[128,1536]{1,0:T(8,128)(2,1)S(1)}, bf16[128,1536]{1,0:T(8,128)(2,1)S(1)}, u32[]{:S(2)}, u32[]{:S(2)}) collective-permute-start(bf16[128,1536]{1,0:T(8,128)(2,1)S(1)} %collective-permute-done.1.refs_8_), channel_id=1, source_target_pairs={{0,1},{1,0},{2,3},{3,2},{4,5},{5,4},{6,7},{7,6},{8,9},{9,8},{10,11... | collective-permute-start | bytes 1179656 | tf_op jit(solution)/shard_map/ppermute | solution.py:493
  23.6 4.0 %collective-permute-start.5 = (bf16[128,1536]{1,0:T(8,128)(2,1)S(1)}, bf16[128,1536]{1,0:T(8,128)(2,1)S(1)}, u32[]{:S(2)}, u32[]{:S(2)}) collective-permute-start(bf16[128,1536]{1,0:T(8,128)(2,1)S(1)} %collective-permute-done.2.refs_9_), channel_id=1, source_target_pairs={{0,1},{1,0},{2,3},{3,2},{4,5},{5,4},{6,7},{7,6},{8,9},{9,8},{10,11... | collective-permute-start | bytes 1179656 | tf_op jit(solution)/shard_map/ppermute | solution.py:493
  24.2 3.5 %collective-permute-start.6 = (bf16[128,1536]{1,0:T(8,128)(2,1)S(1)}, bf16[128,1536]{1,0:T(8,128)(2,1)S(1)}, u32[]{:S(2)}, u32[]{:S(2)}) collective-permute-start(bf16[128,1536]{1,0:T(8,128)(2,1)S(1)} %collective-permute-done.3.refs_10_), channel_id=1, source_target_pairs={{0,1},{1,0},{2,3},{3,2},{4,5},{5,4},{6,7},{7,6},{8,9},{9,8},{10,11... | collective-permute-start | bytes 1179656 | tf_op jit(solution)/shard_map/ppermute | solution.py:493
  24.2 12.6 %collective-permute-start.9 = (bf16[512,256]{1,0:T(8,128)(2,1)S(1)}, bf16[512,256]{1,0:T(8,128)(2,1)S(1)}, u32[]{:S(2)}, u32[]{:S(2)}) collective-permute-start(bf16[512,256]{1,0:T(8,128)(2,1)S(1)} %collective-permute-done.refs_3_), channel_id=1, source_target_pairs={{0,24},{8,16},{16,8},{24,0},{1,25},{9,17},{17,9},{25,1},{2,26},{10... | collective-permute-start | bytes 786440 | tf_op jit(solution)/shard_map/ppermute | solution.py:493
  26.8 12.6 %collective-permute-start.8 = (bf16[512,256]{1,0:T(8,128)(2,1)S(1)}, bf16[512,256]{1,0:T(8,128)(2,1)S(1)}, u32[]{:S(2)}, u32[]{:S(2)}) collective-permute-start(bf16[512,256]{1,0:T(8,128)(2,1)S(1)} %collective-permute-done.refs_3_), channel_id=1, source_target_pairs={{0,16},{8,24},{16,0},{24,8},{1,17},{9,25},{17,1},{25,9},{2,18},{10... | collective-permute-start | bytes 786440 | tf_op jit(solution)/shard_map/ppermute | solution.py:493
  27.3 12.4 %collective-permute-start.7 = (bf16[512,256]{1,0:T(8,128)(2,1)S(1)}, bf16[512,256]{1,0:T(8,128)(2,1)S(1)}, u32[]{:S(2)}, u32[]{:S(2)}) collective-permute-start(bf16[512,256]{1,0:T(8,128)(2,1)S(1)} %collective-permute-done.refs_3_), channel_id=1, source_target_pairs={{0,8},{8,0},{16,24},{24,16},{1,9},{9,1},{17,25},{25,17},{2,10},{10... | collective-permute-start | bytes 786440 | tf_op jit(solution)/shard_map/ppermute | solution.py:493
  33.2 16.3 %collective-permute-start.12 = (bf16[512,256]{1,0:T(8,128)(2,1)S(1)}, bf16[512,256]{1,0:T(8,128)(2,1)S(1)}, u32[]{:S(2)}, u32[]{:S(2)}) collective-permute-start(bf16[512,256]{1,0:T(8,128)(2,1)S(1)} %get-tuple-element.94), channel_id=1, source_target_pairs={{4,0},{5,1},{6,2},{7,3},{12,8},{13,9},{14,10},{15,11},{20,16},{21,... | collective-permute-start | bytes 786440 | tf_op jit(solution)/shard_map/ppermute | solution.py:18
  46.7 1.5 %collective-permute-start.10 = (bf16[64,1536]{1,0:T(8,128)(2,1)S(1)}, bf16[64,1536]{1,0:T(8,128)(2,1)S(1)}, u32[]{:S(2)}, u32[]{:S(2)}) collective-permute-start(bf16[64,1536]{1,0:T(8,128)(2,1)S(1)} %get-tuple-element.88), channel_id=1, source_target_pairs={{0,1},{1,0},{2,3},{3,2},{4,5},{5,4},{6,7},{7,6},{8,9},{9,8},{10,11... | collective-permute-start | bytes 589832 | tf_op jit(solution)/shard_map/ppermute | solution.py:493
  46.8 1.7 %collective-permute-start.11 = (bf16[64,1536]{1,0:T(8,128)(2,1)S(1)}, bf16[64,1536]{1,0:T(8,128)(2,1)S(1)}, u32[]{:S(2)}, u32[]{:S(2)}) collective-permute-start(bf16[64,1536]{1,0:T(8,128)(2,1)S(1)} %get-tuple-element.89), channel_id=1, source_target_pairs={{0,1},{1,0},{2,3},{3,2},{4,5},{5,4},{6,7},{7,6},{8,9},{9,8},{10,11... | collective-permute-start | bytes 589832 | tf_op jit(solution)/shard_map/ppermute | solution.py:493
  49.5 7.5 %collective-permute-start.13 = (bf16[32,1536]{1,0:T(8,128)(2,1)S(1)}, bf16[32,1536]{1,0:T(8,128)(2,1)S(1)}, u32[]{:S(2)}, u32[]{:S(2)}) collective-permute-start(bf16[32,1536]{1,0:T(8,128)(2,1)S(1)} %get-tuple-element.95), channel_id=1, source_target_pairs={{0,6},{1,7},{2,4},{3,5},{4,2},{5,3},{6,0},{7,1},{8,14},{9,15},{10,... | collective-permute-start | bytes 294920 | tf_op jit(solution)/shard_map/ppermute | solution.py:493
  52.3 8.7 %collective-permute-start.14 = (bf16[32,1536]{1,0:T(8,128)(2,1)S(1)}, bf16[32,1536]{1,0:T(8,128)(2,1)S(1)}, u32[]{:S(2)}, u32[]{:S(2)}) collective-permute-start(bf16[32,1536]{1,0:T(8,128)(2,1)S(1)} %get-tuple-element.96), channel_id=1, source_target_pairs={{0,4},{1,5},{2,6},{3,7},{4,0},{5,1},{6,2},{7,3},{8,12},{9,13},{10,... | collective-permute-start | bytes 294920 | tf_op jit(solution)/shard_map/ppermute | solution.py:493
  52.3 8.7 %collective-permute-start.15 = (bf16[32,1536]{1,0:T(8,128)(2,1)S(1)}, bf16[32,1536]{1,0:T(8,128)(2,1)S(1)}, u32[]{:S(2)}, u32[]{:S(2)}) collective-permute-start(bf16[32,1536]{1,0:T(8,128)(2,1)S(1)} %get-tuple-element.97), channel_id=1, source_target_pairs={{0,2},{1,3},{2,0},{3,1},{4,6},{5,7},{6,4},{7,5},{8,10},{9,11},{10,... | collective-permute-start | bytes 294920 | tf_op jit(solution)/shard_map/ppermute | solution.py:493
  53.9 9.8 %collective-permute-start.21 = (bf16[512,256]{1,0:T(8,128)(2,1)S(1)}, bf16[512,256]{1,0:T(8,128)(2,1)S(1)}, u32[]{:S(2)}, u32[]{:S(2)}) collective-permute-start(bf16[512,256]{1,0:T(8,128)(2,1)S(1)} %collective-permute-done.12.refs_0_), channel_id=1, source_target_pairs={{24,0},{25,1},{26,2},{27,3}} | collective-permute-start | bytes 786440 | tf_op jit(solution)/shard_map/ppermute | solution.py:497
  55.2 14.0 %collective-permute-start.20 = (bf16[512,256]{1,0:T(8,128)(2,1)S(1)}, bf16[512,256]{1,0:T(8,128)(2,1)S(1)}, u32[]{:S(2)}, u32[]{:S(2)}) collective-permute-start(bf16[512,256]{1,0:T(8,128)(2,1)S(1)} %collective-permute-done.12.refs_0_), channel_id=1, source_target_pairs={{16,0},{17,1},{18,2},{19,3}} | collective-permute-start | bytes 786440 | tf_op jit(solution)/shard_map/ppermute | solution.py:497
  57.0 12.2 %collective-permute-start.19 = (bf16[512,256]{1,0:T(8,128)(2,1)S(1)}, bf16[512,256]{1,0:T(8,128)(2,1)S(1)}, u32[]{:S(2)}, u32[]{:S(2)}) collective-permute-start(bf16[512,256]{1,0:T(8,128)(2,1)S(1)} %collective-permute-done.12.refs_0_), channel_id=1, source_target_pairs={{8,0},{9,1},{10,2},{11,3}} | collective-permute-start | bytes 786440 | tf_op jit(solution)/shard_map/ppermute | solution.py:497
  61.0 9.4 %collective-permute-start.18 = (bf16[32,1536]{1,0:T(8,128)(2,1)S(1)}, bf16[32,1536]{1,0:T(8,128)(2,1)S(1)}, u32[]{:S(2)}, u32[]{:S(2)}) collective-permute-start(bf16[32,1536]{1,0:T(8,128)(2,1)S(1)} %add_convert_fusion.refs_0_), channel_id=1, source_target_pairs={{0,6},{1,7},{2,4},{3,5},{4,2},{5,3},{6,0},{7,1},{8,14},{9,15},{10,... | collective-permute-start | bytes 294920 | tf_op jit(solution)/shard_map/ppermute | solution.py:493
  63.5 8.4 %collective-permute-start.17 = (bf16[32,1536]{1,0:T(8,128)(2,1)S(1)}, bf16[32,1536]{1,0:T(8,128)(2,1)S(1)}, u32[]{:S(2)}, u32[]{:S(2)}) collective-permute-start(bf16[32,1536]{1,0:T(8,128)(2,1)S(1)} %add_convert_fusion.refs_0_), channel_id=1, source_target_pairs={{0,4},{1,5},{2,6},{3,7},{4,0},{5,1},{6,2},{7,3},{8,12},{9,13},{10,... | collective-permute-start | bytes 294920 | tf_op jit(solution)/shard_map/ppermute | solution.py:493
  63.7 8.3 %collective-permute-start.16 = (bf16[32,1536]{1,0:T(8,128)(2,1)S(1)}, bf16[32,1536]{1,0:T(8,128)(2,1)S(1)}, u32[]{:S(2)}, u32[]{:S(2)}) collective-permute-start(bf16[32,1536]{1,0:T(8,128)(2,1)S(1)} %add_convert_fusion.refs_0_), channel_id=1, source_target_pairs={{0,2},{1,3},{2,0},{3,1},{4,6},{5,7},{6,4},{7,5},{8,10},{9,11},{10,... | collective-permute-start | bytes 294920 | tf_op jit(solution)/shard_map/ppermute | solution.py:493
  72.0 1.8 %collective-permute-start.22 = (bf16[4,32,1536]{2,1,0:T(8,128)(2,1)S(1)}, bf16[4,32,1536]{2,1,0:T(8,128)(2,1)S(1)}, u32[]{:S(2)}, u32[]{:S(2)}) collective-permute-start(bf16[4,32,1536]{2,1,0:T(8,128)(2,1)S(1)} %pad_maximum_fusion), channel_id=1, source_target_pairs={{0,1},{1,0},{2,3},{3,2},{4,5},{5,4},{6,7},{7,6},{8,9},{9,8},{10,11... | collective-permute-start | bytes 1179656 | tf_op jit(solution)/shard_map/ppermute | solution.py:493
  (6 other events, 84.7 us)

commit v8 on v7

--- a/solution.py
+++ b/solution.py
@@ -209,11 +209,15 @@
     return local_call(finish_kernel, "finish", [own_skip, gated_all, dz_all, g_all, weights], out_shape)
 
 
+def tap_factor(seq_rows):
+    return jnp.where(lax.axis_index("tm") >= FIRST_DILATION // seq_rows, 1.0, 0.0)
+
+
 def add_products(section, sums, sums_in, tapped, h_all, gated_all, dz_all, g_all, cot):
     channels = tapped.shape[-1]
     for i in range(tapped.shape[0]):
         products = (
-            rows_dot(tapped[i], dz_all[section, i]),
+            rows_dot(tapped[i], dz_all[section, i]) * tap_factor(tapped.shape[1]),
             rows_dot(h_all[section, i], dz_all[section, i]),
             rows_dot(gated_all[section, i], g_all[section + 1, i]),
             rows_dot(gated_all[section, i], cot[i]),
@@ -303,6 +307,8 @@
     for k in range(layers):
         if not last:
             wait_bytes(weights.at[k], weights_here.at[k])
+            if k == 0:
+                weights[0, :, tap] = weights[0, :, tap] * tap_factor(seq_rows).astype(jnp.bfloat16)
         for i in range(seqs):
             if k == 0 and last:
                 pre = ahead_pre[i] + narrow_dot(taps[i][...], weights[0, :, tap])
@@ -461,19 +467,20 @@
                 column += width
 
 
-def add_kernel(own_base, base, *refs):
+def add_kernel(reach, own_base, base, *refs):
     *backs, out = refs
     section = lax.axis_index("section")
-    own = jnp.where(section == 0, 1.0, 0.0)
+    own = jnp.where((section == 0) & (lax.axis_index("tm") < reach), 1.0, 0.0)
     for i, back in enumerate(backs):
         term = back[...].astype(jnp.float32)
         total = base[i - 1] + term if i else own_base[...].astype(jnp.float32) + term * own
         out[0, jnp.bitwise_xor(section, i)] = total.astype(jnp.bfloat16)
 
 
-def add_back(own_base, base, backs):
+def add_back(own_base, base, backs, reach):
     shape = (1, len(backs), *own_base.shape)
-    return local_call(add_kernel, "add_back", [own_base, base, *backs], [jax.ShapeDtypeStruct(shape, jnp.bfloat16)], 2**24)[0]
+    kernel = functools.partial(add_kernel, reach)
+    return local_call(kernel, "add_back", [own_base, base, *backs], [jax.ShapeDtypeStruct(shape, jnp.bfloat16)], 2**24)[0]
 
 
 def local_call(kernel, name, operands, out_shape, weight=0):
@@ -493,6 +500,11 @@
     return lax.ppermute(x, axis, [(i, i ^ by) for i in range(lax.axis_size(axis))])
 
 
+def rotated(x, by):
+    size = lax.axis_size("tm")
+    return lax.ppermute(x, "tm", [(i, (i + by) % size) for i in range(size)])
+
+
 def between(x, shards, pairs, reached):
     return lax.ppermute(x, ("section", "tm"), [(i * shards + t, j * shards + t) for i, j in pairs for t in reached])
 
@@ -529,7 +541,7 @@
     number, seq_rows, channels = signal.shape
     span = FIRST_DILATION // seq_rows
 
-    tap = passed_along(lax.dynamic_index_in_dim(signal, section, 0, False), "tm", span)
+    tap = rotated(lax.dynamic_index_in_dim(signal, section, 0, False), span)
     packed = jnp.concatenate([w_now[0], w_res[0], w_skip[0], w_tap[0]], axis=1)
     half_rows = packed.shape[0] // 2
     own_half = lax.dynamic_slice_in_dim(packed, core * half_rows, half_rows, 0)
@@ -542,7 +554,7 @@
     pieces = [w_now, w_res, w_skip, w_tap, *mine, *other]
     own_skip, own_base, back, weights, *kept_own = layer_stack(own_streams, taps[:1], number, pieces)
     ahead_terms = ahead(taps[0], own_streams[1], kept_own, weights, other_streams)
-    back = passed_along(back, "tm", -span)
+    back = rotated(back, -span)
     gated, dz, g, *sent, kept = layer_stack(other_streams, taps[1:], number, [weights], earlier=ahead_terms)
     got = [swapped(value, "tm", 1) for value in sent]
     own_piece, pieces = spread(got, kept, shards // 2)
@@ -551,7 +563,7 @@
     arrived = [between(back, shards, [(by, 0)], reached) for by in range(1, sections)]
     grad_scale = 1.0 / math.sqrt(number * seq_rows * shards)
     skip_total, base = finish(own_skip, gated, dz, g, weights)
-    input_grads = add_back(own_base, base, [back, *arrived])
+    input_grads = add_back(own_base, base, [back, *arrived], shards - span)
     summed, input_grads = sum_over_chips(own_piece, pieces, grad_scale, input_grads)
     return (skip_total, input_grads, *summed)
 

time: 75.4 us -> 75.6 us (level)
    ppermute x2, waiting for transfers between devices: 1.58 us -> 7.05 us  [rotated(): return lax.ppermute(x, 'tm', [(i, (i + by) % size) for i in range(size)])]
    ppermute x18, waiting for transfers between devices: 17.2 us -> 12.2 us  [swapped(): lax.ppermute(x, axis, [(i, i ^ by) for i in range(lax.axis_size(axis))])]
  transfers between devices with their start and end apart: 23 -> 23, of which waited for: 13 -> 12; matrix products, arithmetic and copies ran while one was open for 1% -> 1% of each run, Pallas kernels for 25% -> 25%
where the time goes in v8:
time: 75.6 us; the launch traced here: 75.3 us
  starting transfers between devices  27.7 us (37%)
  waiting for transfers between devices  20.8 us (28%)
  Pallas kernels  20.1 us (27%)
  local copies, waits for them, and re-layouts  4.66 us (6%)
  other arithmetic  1.22 us (2%)
  between operations  0.83 us (1%)
    ppermute x18, starting transfers between devices, swapped(): lax.ppermute(x, axis, [(i, i ^ by) for i in range(lax.axis_size(axis))])  18 us
    pallas_call x2, Pallas kernels, layer_stack(): pl.pallas_call(functools.partial(stack_kernel, layers, last), in_specs=in...  12.8 us
    ppermute x18, waiting for transfers between devices, swapped(): lax.ppermute(x, axis, [(i, i ^ by) for i in range(lax.axis_size(axis))])  12.2 us
    ppermute x2, waiting for transfers between devices, rotated(): return lax.ppermute(x, 'tm', [(i, (i + by) % size) for i in range(size)])  7.05 us
    pallas_call x5, Pallas kernels, local_call(): pl.pallas_call(kernel, in_specs=[near] * len(operands), out_specs=[near]...  6.93 us
    ppermute x2, starting transfers between devices, rotated(): return lax.ppermute(x, 'tm', [(i, (i + by) % size) for i in range(size)])  5.88 us
    ppermute x3, starting transfers between devices, between(): lax.ppermute(x, ('section', 'tm'), [(i * shards + t, j * shards + t) for...  3.85 us
    unnamed x14, local copies, waits for them, and re-layouts  3.69 us
  transfers between devices with their start and end apart: 23, of which 12 were waited for; matrix products, arithmetic and copies ran while one was open for 1% of the time, Pallas kernels for 25%

profile of v8, /device:TPU:0, one launch (start us, length us, event | category | flops | bytes accessed | tf_op | source)
XLA Modules:
  0.0 75.3 jit_solution(4903713181340117241)
XLA Ops:
  1.8 3.0 %collective-permute-start.2 = (bf16[128,1536]{1,0:T(8,128)(2,1)S(1)}, bf16[128,1536]{1,0:T(8,128)(2,1)S(1)}, u32[]{:S(2)}, u32[]{:S(2)}) collective-permute-start(bf16[128,1536]{1,0:T(8,128)(2,1)S(1)} %fusion.2), channel_id=1, source_target_pairs={{0,16},{8,24},{16,0},{24,8},{1,17},{9,25},{17,1},{25,9},{2,18},{10... | collective-permute-start | bytes 1179656 | tf_op jit(solution)/shard_map/ppermute | solution.py:500
  4.8 1.5 %collective-permute-start.1 = (bf16[128,1536]{1,0:T(8,128)(2,1)S(1)}, bf16[128,1536]{1,0:T(8,128)(2,1)S(1)}, u32[]{:S(2)}, u32[]{:S(2)}) collective-permute-start(bf16[128,1536]{1,0:T(8,128)(2,1)S(1)} %fusion.2), channel_id=1, source_target_pairs={{0,8},{8,0},{16,24},{24,16},{1,9},{9,1},{17,25},{25,17},{2,10},{10... | collective-permute-start | bytes 1179656 | tf_op jit(solution)/shard_map/ppermute | solution.py:500
  7.4 3.1 %collective-permute-start = (bf16[512,256]{1,0:T(8,128)(2,1)S(1)}, bf16[512,256]{1,0:T(8,128)(2,1)S(1)}, u32[]{:S(2)}, u32[]{:S(2)}) collective-permute-start(bf16[512,256]{1,0:T(8,128)(2,1)S(1)} %dynamic-slice_bitcast_fusion), channel_id=1, source_target_pairs={{0,4},{1,5},{2,6},{3,7},{4,0},{5,1},{6,2},{7,3},{8,12},{9,13},{10,... | collective-permute-start | bytes 786440 | tf_op jit(solution)/shard_map/ppermute | solution.py:505
  10.4 1.2 %copy-done = bf16[4,512,256]{2,1,0:T(8,128)(2,1)S(1)} copy-done((bf16[4,512,256]{2,1,0:T(8,128)(2,1)S(1)}, bf16[4,512,256]{2,1,0:T(8,128)(2,1)}, u32[]{:S(2)}) %copy-start) | copy-done | bytes 1048600
  14.5 7.1 %collective-permute-done.refs_3_ = bf16[512,256]{1,0:T(8,128)(2,1)S(1)} collective-permute-done((bf16[512,256]{1,0:T(8,128)(2,1)S(1)}, bf16[512,256]{1,0:T(8,128)(2,1)S(1)}, u32[]{:S(2)}, u32[]{:S(2)}) %collective-permute-start) | collective-permute-done | bytes 262176 | tf_op jit(solution)/shard_map/ppermute | solution.py:505
  21.5 2.1 %collective-permute-done.3.refs_10_ = bf16[128,1536]{1,0:T(8,128)(2,1)S(1)} collective-permute-done((bf16[128,1536]{1,0:T(8,128)(2,1)S(1)}, bf16[128,1536]{1,0:T(8,128)(2,1)S(1)}, u32[]{:S(2)}, u32[]{:S(2)}) %collective-permute-start.3) | collective-permute-done | bytes 393248 | tf_op jit(solution)/shard_map/ppermute | solution.py:500
  24.2 2.6 %collective-permute-start.9 = (bf16[512,256]{1,0:T(8,128)(2,1)S(1)}, bf16[512,256]{1,0:T(8,128)(2,1)S(1)}, u32[]{:S(2)}, u32[]{:S(2)}) collective-permute-start(bf16[512,256]{1,0:T(8,128)(2,1)S(1)} %collective-permute-done.refs_3_), channel_id=1, source_target_pairs={{0,24},{8,16},{16,8},{24,0},{1,25},{9,17},{17,9},{25,1},{2,26},{10... | collective-permute-start | bytes 786440 | tf_op jit(solution)/shard_map/ppermute | solution.py:500
  27.7 5.5 %layer_stack.2 = (bf16[512,256]{1,0:T(8,128)(2,1)S(1)}, bf16[512,256]{1,0:T(8,128)(2,1)S(1)}, bf16[512,256]{1,0:T(8,128)(2,1)S(1)}, bf16[4,256,1536]{2,1,0:T(8,1...) custom-call(bf16[1,512,256]{2,1,0:T(8,128)(2,1)S(1)} %get-tuple-elem, ...), custom_call_target="tpu_custom_call" | custom-call | flops 5905580032 | bytes 2097152 | tf_op jit(solution)/shard_map/layer_stack/pallas_call | solution.py:392
  33.2 2.8 %collective-permute-start.12 = (bf16[512,256]{1,0:T(8,128)(2,1)S(1)}, bf16[512,256]{1,0:T(8,128)(2,1)S(1)}, u32[]{:S(2)}, u32[]{:S(2)}) collective-permute-start(bf16[512,256]{1,0:T(8,128)(2,1)S(1)} %get-tuple-element.94), channel_id=1, source_target_pairs={{0,4},{1,5},{2,6},{3,7},{4,0},{5,1},{6,2},{7,3},{8,12},{9,13},{10,... | collective-permute-start | bytes 786440 | tf_op jit(solution)/shard_map/ppermute | solution.py:505
  36.0 2.1 %ahead.1 = (f32[256,1536]{1,0:T(8,128)S(1)}, f32[3,512,512]{2,1,0:T(8,128)S(1)}, f32[4,3,512,256]{3,2,1,0:T(8,128)S(1)}) custom-call(bf16[1,512,256]{2,1,0:T(8,128)(2,1)S(1)} %bitcast.15, bf16[1,512,256]{2,1,0:T(8,128)(2,1)S(1)} %get-tuple-element.65.refs_1_.cot, bf16[4,1,512,256]{3,2,1,0:T(8,128)(2,1)S(1)} %get-tuple-element.76.h_all, ...), custom_call_target="tpu_custom_call" | custom-call | tf_op jit(solution)/shard_map/ahead/pallas_call | solution.py:488
  38.1 1.3 %collective-permute-done.8.refs_4_ = bf16[512,256]{1,0:T(8,128)(2,1)S(1)} collective-permute-done((bf16[512,256]{1,0:T(8,128)(2,1)S(1)}, bf16[512,256]{1,0:T(8,128)(2,1)S(1)}, u32[]{:S(2)}, u32[]{:S(2)}) %collective-permute-start.8) | collective-permute-done | bytes 262176 | tf_op jit(solution)/shard_map/ppermute | solution.py:500
  39.6 7.3 %layer_stack.3 = (bf16[4,3,512,256]{3,2,1,0:T(8,128)(2,1)S(1)}, bf16[4,3,512,512]{3,2,1,0:T(8,128)(2,1)S(1)}, bf16[5,3,512,256]{3,2,1,0:T(8,128)(2,1)S(1)}, bf16...) custom-call(bf16[3,512,256]{2,1,0:T(8,128)(2,1)S(1)} %get-tuple-element.72.next_signal.refs_0_, ...), custom_call_target="tpu_custom_call" | custom-call | flops 17716740096 | bytes 6291456 | tf_op jit(solution)/shard_map/layer_stack/pallas_call | solution.py:392
  48.8 3.7 %collective-permute-start.13 = (bf16[32,1536]{1,0:T(8,128)(2,1)S(1)}, bf16[32,1536]{1,0:T(8,128)(2,1)S(1)}, u32[]{:S(2)}, u32[]{:S(2)}) collective-permute-start(bf16[32,1536]{1,0:T(8,128)(2,1)S(1)} %get-tuple-element.95), channel_id=1, source_target_pairs={{0,6},{1,7},{2,4},{3,5},{4,2},{5,3},{6,0},{7,1},{8,14},{9,15},{10,... | collective-permute-start | bytes 294920 | tf_op jit(solution)/shard_map/ppermute | solution.py:500
  53.3 1.3 %collective-permute-start.21 = (bf16[512,256]{1,0:T(8,128)(2,1)S(1)}, bf16[512,256]{1,0:T(8,128)(2,1)S(1)}, u32[]{:S(2)}, u32[]{:S(2)}) collective-permute-start(bf16[512,256]{1,0:T(8,128)(2,1)S(1)} %collective-permute-done.12.refs_0_), channel_id=1, source_target_pairs={{24,0},{25,1},{26,2},{27,3}} | collective-permute-start | bytes 786440 | tf_op jit(solution)/shard_map/ppermute | solution.py:509
  54.6 1.3 %collective-permute-start.20 = (bf16[512,256]{1,0:T(8,128)(2,1)S(1)}, bf16[512,256]{1,0:T(8,128)(2,1)S(1)}, u32[]{:S(2)}, u32[]{:S(2)}) collective-permute-start(bf16[512,256]{1,0:T(8,128)(2,1)S(1)} %collective-permute-done.12.refs_0_), channel_id=1, source_target_pairs={{16,0},{17,1},{18,2},{19,3}} | collective-permute-start | bytes 786440 | tf_op jit(solution)/shard_map/ppermute | solution.py:509
  56.4 1.3 %collective-permute-start.19 = (bf16[512,256]{1,0:T(8,128)(2,1)S(1)}, bf16[512,256]{1,0:T(8,128)(2,1)S(1)}, u32[]{:S(2)}, u32[]{:S(2)}) collective-permute-start(bf16[512,256]{1,0:T(8,128)(2,1)S(1)} %collective-permute-done.12.refs_0_), channel_id=1, source_target_pairs={{8,0},{9,1},{10,2},{11,3}} | collective-permute-start | bytes 786440 | tf_op jit(solution)/shard_map/ppermute | solution.py:509
  57.7 3.4 %collective-permute-done.14 = bf16[32,1536]{1,0:T(8,128)(2,1)S(1)} collective-permute-done((bf16[32,1536]{1,0:T(8,128)(2,1)S(1)}, bf16[32,1536]{1,0:T(8,128)(2,1)S(1)}, u32[]{:S(2)}, u32[]{:S(2)}) %collective-permute-start.14) | collective-permute-done | bytes 98336 | tf_op jit(solution)/shard_map/ppermute | solution.py:500
  61.2 2.5 %collective-permute-start.18 = (bf16[32,1536]{1,0:T(8,128)(2,1)S(1)}, bf16[32,1536]{1,0:T(8,128)(2,1)S(1)}, u32[]{:S(2)}, u32[]{:S(2)}) collective-permute-start(bf16[32,1536]{1,0:T(8,128)(2,1)S(1)} %add_convert_fusion.refs_0_), channel_id=1, source_target_pairs={{0,6},{1,7},{2,4},{3,5},{4,2},{5,3},{6,0},{7,1},{8,14},{9,15},{10,... | collective-permute-start | bytes 294920 | tf_op jit(solution)/shard_map/ppermute | solution.py:500
  63.9 1.8 %collective-permute-start.16 = (bf16[32,1536]{1,0:T(8,128)(2,1)S(1)}, bf16[32,1536]{1,0:T(8,128)(2,1)S(1)}, u32[]{:S(2)}, u32[]{:S(2)}) collective-permute-start(bf16[32,1536]{1,0:T(8,128)(2,1)S(1)} %add_convert_fusion.refs_0_), channel_id=1, source_target_pairs={{0,2},{1,3},{2,0},{3,1},{4,6},{5,7},{6,4},{7,5},{8,10},{9,11},{10,... | collective-permute-start | bytes 294920 | tf_op jit(solution)/shard_map/ppermute | solution.py:500
  65.7 2.4 %finish.1 = (bf16[4,512,256]{2,1,0:T(8,128)(2,1)}, f32[3,512,256]{2,1,0:T(8,128)S(1)}) custom-call(bf16[512,256]{1,0:T(8,128)(2,1)S(1)} %get-tuple-element.71.own_skip, bf16[4,3,512,256]{3,2,1,0:T(8,128)(2,1)S(1)} %get-tuple-element.83.gated_all, bf16[4,3,512,512]{3,2,1,0:T(8,128)(2,1)S(1)} %get-tuple-element.84.dz_all, ...), custom_call_target="tpu_custom_call" | custom-call | tf_op jit(solution)/shard_map/finish/pallas_call | solution.py:488
  68.0 1.4 %collective-permute-done.20.refs_2_ = bf16[512,256]{1,0:T(8,128)(2,1)S(1)} collective-permute-done((bf16[512,256]{1,0:T(8,128)(2,1)S(1)}, bf16[512,256]{1,0:T(8,128)(2,1)S(1)}, u32[]{:S(2)}, u32[]{:S(2)}) %collective-permute-start.20) | collective-permute-done | bytes 262176 | tf_op jit(solution)/shard_map/ppermute | solution.py:509
  70.6 1.6 %collective-permute-done.17.refs_2_ = bf16[32,1536]{1,0:T(8,128)(2,1)S(1)} collective-permute-done((bf16[32,1536]{1,0:T(8,128)(2,1)S(1)}, bf16[32,1536]{1,0:T(8,128)(2,1)S(1)}, u32[]{:S(2)}, u32[]{:S(2)}) %collective-permute-start.17) | collective-permute-done | bytes 98336 | tf_op jit(solution)/shard_map/ppermute | solution.py:500
  72.3 1.7 %collective-permute-done.22.refs_4_ = bf16[4,32,1536]{2,1,0:T(8,128)(2,1)S(1)} collective-permute-done((bf16[4,32,1536]{2,1,0:T(8,128)(2,1)S(1)}, bf16[4,32,1536]{2,1,0:T(8,128)(2,1)S(1)}, u32[]{:S(2)}, u32[]{:S(2)}) %collective-permute-start.22) | collective-permute-done | bytes 393248 | tf_op jit(solution)/shard_map/ppermute | solution.py:500
  74.0 1.3 %place_sums.1 = (f32[1,256,512]{2,1,0:T(8,128)}, f32[1,256,512]{2,1,0:T(8,128)}, f32[1,256,256]{2,1,0:T(8,128)}, f32[1,256,256]{2,1,0:T(8,128)}) custom-call(bf16[32,1536]{1,0:T(8,128)(2,1)S(1)} %add_convert_fusion.refs_0_, bf16[32,1536]{1,0:T(8,128)(2,1)S(1)} %collective-permute-done.16.refs_1_, bf16[32,1536]{1,0:T(8,128)(2,1)S(1)} %collective-permute-done.17.refs_2_, ...), custom_call_target="tpu_custom_call" | custom-call | tf_op jit(solution)/shard_map/place_sums/pallas_call | solution.py:488
  (48 shorter events, 11.3 us)
Async XLA Ops:
  0.6 27.0 %copy-start.4 = (bf16[1,256,512]{2,1,0:T(8,128)(2,1)S(1)}, bf16[1,256,512]{2,1,0:T(8,128)(2,1)}, u32[]{:S(2)}) copy-start(bf16[1,256,512]{2,1,0:T(8,128)(2,1)} %refs_7_.1) | copy-start | bytes 786436
  1.8 19.7 %collective-permute-start.2 = (bf16[128,1536]{1,0:T(8,128)(2,1)S(1)}, bf16[128,1536]{1,0:T(8,128)(2,1)S(1)}, u32[]{:S(2)}, u32[]{:S(2)}) collective-permute-start(bf16[128,1536]{1,0:T(8,128)(2,1)S(1)} %fusion.2), channel_id=1, source_target_pairs={{0,16},{8,24},{16,0},{24,8},{1,17},{9,25},{17,1},{25,9},{2,18},{10... | collective-permute-start | bytes 1179656 | tf_op jit(solution)/shard_map/ppermute | solution.py:500
  4.8 16.7 %collective-permute-start.1 = (bf16[128,1536]{1,0:T(8,128)(2,1)S(1)}, bf16[128,1536]{1,0:T(8,128)(2,1)S(1)}, u32[]{:S(2)}, u32[]{:S(2)}) collective-permute-start(bf16[128,1536]{1,0:T(8,128)(2,1)S(1)} %fusion.2), channel_id=1, source_target_pairs={{0,8},{8,0},{16,24},{24,16},{1,9},{9,1},{17,25},{25,17},{2,10},{10... | collective-permute-start | bytes 1179656 | tf_op jit(solution)/shard_map/ppermute | solution.py:500
  6.3 17.3 %collective-permute-start.3 = (bf16[128,1536]{1,0:T(8,128)(2,1)S(1)}, bf16[128,1536]{1,0:T(8,128)(2,1)S(1)}, u32[]{:S(2)}, u32[]{:S(2)}) collective-permute-start(bf16[128,1536]{1,0:T(8,128)(2,1)S(1)} %fusion.2), channel_id=1, source_target_pairs={{0,24},{8,16},{16,8},{24,0},{1,25},{9,17},{17,9},{25,1},{2,26},{10... | collective-permute-start | bytes 1179656 | tf_op jit(solution)/shard_map/ppermute | solution.py:500
  7.4 14.2 %collective-permute-start = (bf16[512,256]{1,0:T(8,128)(2,1)S(1)}, bf16[512,256]{1,0:T(8,128)(2,1)S(1)}, u32[]{:S(2)}, u32[]{:S(2)}) collective-permute-start(bf16[512,256]{1,0:T(8,128)(2,1)S(1)} %dynamic-slice_bitcast_fusion), channel_id=1, source_target_pairs={{0,4},{1,5},{2,6},{3,7},{4,0},{5,1},{6,2},{7,3},{8,12},{9,13},{10,... | collective-permute-start | bytes 786440 | tf_op jit(solution)/shard_map/ppermute | solution.py:505
  23.6 3.6 %collective-permute-start.4 = (bf16[128,1536]{1,0:T(8,128)(2,1)S(1)}, bf16[128,1536]{1,0:T(8,128)(2,1)S(1)}, u32[]{:S(2)}, u32[]{:S(2)}) collective-permute-start(bf16[128,1536]{1,0:T(8,128)(2,1)S(1)} %collective-permute-done.1.refs_8_), channel_id=1, source_target_pairs={{0,1},{1,0},{2,3},{3,2},{4,5},{5,4},{6,7},{7,6},{8,9},{9,8},{10,11... | collective-permute-start | bytes 1179656 | tf_op jit(solution)/shard_map/ppermute | solution.py:500
  23.6 4.0 %collective-permute-start.5 = (bf16[128,1536]{1,0:T(8,128)(2,1)S(1)}, bf16[128,1536]{1,0:T(8,128)(2,1)S(1)}, u32[]{:S(2)}, u32[]{:S(2)}) collective-permute-start(bf16[128,1536]{1,0:T(8,128)(2,1)S(1)} %collective-permute-done.2.refs_9_), channel_id=1, source_target_pairs={{0,1},{1,0},{2,3},{3,2},{4,5},{5,4},{6,7},{7,6},{8,9},{9,8},{10,11... | collective-permute-start | bytes 1179656 | tf_op jit(solution)/shard_map/ppermute | solution.py:500
  24.2 3.5 %collective-permute-start.6 = (bf16[128,1536]{1,0:T(8,128)(2,1)S(1)}, bf16[128,1536]{1,0:T(8,128)(2,1)S(1)}, u32[]{:S(2)}, u32[]{:S(2)}) collective-permute-start(bf16[128,1536]{1,0:T(8,128)(2,1)S(1)} %collective-permute-done.3.refs_10_), channel_id=1, source_target_pairs={{0,1},{1,0},{2,3},{3,2},{4,5},{5,4},{6,7},{7,6},{8,9},{9,8},{10,11... | collective-permute-start | bytes 1179656 | tf_op jit(solution)/shard_map/ppermute | solution.py:500
  24.2 13.9 %collective-permute-start.9 = (bf16[512,256]{1,0:T(8,128)(2,1)S(1)}, bf16[512,256]{1,0:T(8,128)(2,1)S(1)}, u32[]{:S(2)}, u32[]{:S(2)}) collective-permute-start(bf16[512,256]{1,0:T(8,128)(2,1)S(1)} %collective-permute-done.refs_3_), channel_id=1, source_target_pairs={{0,24},{8,16},{16,8},{24,0},{1,25},{9,17},{17,9},{25,1},{2,26},{10... | collective-permute-start | bytes 786440 | tf_op jit(solution)/shard_map/ppermute | solution.py:500
  26.8 12.6 %collective-permute-start.8 = (bf16[512,256]{1,0:T(8,128)(2,1)S(1)}, bf16[512,256]{1,0:T(8,128)(2,1)S(1)}, u32[]{:S(2)}, u32[]{:S(2)}) collective-permute-start(bf16[512,256]{1,0:T(8,128)(2,1)S(1)} %collective-permute-done.refs_3_), channel_id=1, source_target_pairs={{0,16},{8,24},{16,0},{24,8},{1,17},{9,25},{17,1},{25,9},{2,18},{10... | collective-permute-start | bytes 786440 | tf_op jit(solution)/shard_map/ppermute | solution.py:500
  27.3 12.4 %collective-permute-start.7 = (bf16[512,256]{1,0:T(8,128)(2,1)S(1)}, bf16[512,256]{1,0:T(8,128)(2,1)S(1)}, u32[]{:S(2)}, u32[]{:S(2)}) collective-permute-start(bf16[512,256]{1,0:T(8,128)(2,1)S(1)} %collective-permute-done.refs_3_), channel_id=1, source_target_pairs={{0,8},{8,0},{16,24},{24,16},{1,9},{9,1},{17,25},{25,17},{2,10},{10... | collective-permute-start | bytes 786440 | tf_op jit(solution)/shard_map/ppermute | solution.py:500
  33.2 15.6 %collective-permute-start.12 = (bf16[512,256]{1,0:T(8,128)(2,1)S(1)}, bf16[512,256]{1,0:T(8,128)(2,1)S(1)}, u32[]{:S(2)}, u32[]{:S(2)}) collective-permute-start(bf16[512,256]{1,0:T(8,128)(2,1)S(1)} %get-tuple-element.94), channel_id=1, source_target_pairs={{0,4},{1,5},{2,6},{3,7},{4,0},{5,1},{6,2},{7,3},{8,12},{9,13},{10,... | collective-permute-start | bytes 786440 | tf_op jit(solution)/shard_map/ppermute | solution.py:505
  46.9 1.5 %collective-permute-start.10 = (bf16[64,1536]{1,0:T(8,128)(2,1)S(1)}, bf16[64,1536]{1,0:T(8,128)(2,1)S(1)}, u32[]{:S(2)}, u32[]{:S(2)}) collective-permute-start(bf16[64,1536]{1,0:T(8,128)(2,1)S(1)} %get-tuple-element.88), channel_id=1, source_target_pairs={{0,1},{1,0},{2,3},{3,2},{4,5},{5,4},{6,7},{7,6},{8,9},{9,8},{10,11... | collective-permute-start | bytes 589832 | tf_op jit(solution)/shard_map/ppermute | solution.py:500
  47.0 1.7 %collective-permute-start.11 = (bf16[64,1536]{1,0:T(8,128)(2,1)S(1)}, bf16[64,1536]{1,0:T(8,128)(2,1)S(1)}, u32[]{:S(2)}, u32[]{:S(2)}) collective-permute-start(bf16[64,1536]{1,0:T(8,128)(2,1)S(1)} %get-tuple-element.89), channel_id=1, source_target_pairs={{0,1},{1,0},{2,3},{3,2},{4,5},{5,4},{6,7},{7,6},{8,9},{9,8},{10,11... | collective-permute-start | bytes 589832 | tf_op jit(solution)/shard_map/ppermute | solution.py:500
  48.8 7.6 %collective-permute-start.13 = (bf16[32,1536]{1,0:T(8,128)(2,1)S(1)}, bf16[32,1536]{1,0:T(8,128)(2,1)S(1)}, u32[]{:S(2)}, u32[]{:S(2)}) collective-permute-start(bf16[32,1536]{1,0:T(8,128)(2,1)S(1)} %get-tuple-element.95), channel_id=1, source_target_pairs={{0,6},{1,7},{2,4},{3,5},{4,2},{5,3},{6,0},{7,1},{8,14},{9,15},{10,... | collective-permute-start | bytes 294920 | tf_op jit(solution)/shard_map/ppermute | solution.py:500
  52.5 8.7 %collective-permute-start.14 = (bf16[32,1536]{1,0:T(8,128)(2,1)S(1)}, bf16[32,1536]{1,0:T(8,128)(2,1)S(1)}, u32[]{:S(2)}, u32[]{:S(2)}) collective-permute-start(bf16[32,1536]{1,0:T(8,128)(2,1)S(1)} %get-tuple-element.96), channel_id=1, source_target_pairs={{0,4},{1,5},{2,6},{3,7},{4,0},{5,1},{6,2},{7,3},{8,12},{9,13},{10,... | collective-permute-start | bytes 294920 | tf_op jit(solution)/shard_map/ppermute | solution.py:500
  52.5 8.7 %collective-permute-start.15 = (bf16[32,1536]{1,0:T(8,128)(2,1)S(1)}, bf16[32,1536]{1,0:T(8,128)(2,1)S(1)}, u32[]{:S(2)}, u32[]{:S(2)}) collective-permute-start(bf16[32,1536]{1,0:T(8,128)(2,1)S(1)} %get-tuple-element.97), channel_id=1, source_target_pairs={{0,2},{1,3},{2,0},{3,1},{4,6},{5,7},{6,4},{7,5},{8,10},{9,11},{10,... | collective-permute-start | bytes 294920 | tf_op jit(solution)/shard_map/ppermute | solution.py:500
  53.3 10.6 %collective-permute-start.21 = (bf16[512,256]{1,0:T(8,128)(2,1)S(1)}, bf16[512,256]{1,0:T(8,128)(2,1)S(1)}, u32[]{:S(2)}, u32[]{:S(2)}) collective-permute-start(bf16[512,256]{1,0:T(8,128)(2,1)S(1)} %collective-permute-done.12.refs_0_), channel_id=1, source_target_pairs={{24,0},{25,1},{26,2},{27,3}} | collective-permute-start | bytes 786440 | tf_op jit(solution)/shard_map/ppermute | solution.py:509
  54.6 14.8 %collective-permute-start.20 = (bf16[512,256]{1,0:T(8,128)(2,1)S(1)}, bf16[512,256]{1,0:T(8,128)(2,1)S(1)}, u32[]{:S(2)}, u32[]{:S(2)}) collective-permute-start(bf16[512,256]{1,0:T(8,128)(2,1)S(1)} %collective-permute-done.12.refs_0_), channel_id=1, source_target_pairs={{16,0},{17,1},{18,2},{19,3}} | collective-permute-start | bytes 786440 | tf_op jit(solution)/shard_map/ppermute | solution.py:509
  56.4 13.0 %collective-permute-start.19 = (bf16[512,256]{1,0:T(8,128)(2,1)S(1)}, bf16[512,256]{1,0:T(8,128)(2,1)S(1)}, u32[]{:S(2)}, u32[]{:S(2)}) collective-permute-start(bf16[512,256]{1,0:T(8,128)(2,1)S(1)} %collective-permute-done.12.refs_0_), channel_id=1, source_target_pairs={{8,0},{9,1},{10,2},{11,3}} | collective-permute-start | bytes 786440 | tf_op jit(solution)/shard_map/ppermute | solution.py:509
  61.2 9.4 %collective-permute-start.18 = (bf16[32,1536]{1,0:T(8,128)(2,1)S(1)}, bf16[32,1536]{1,0:T(8,128)(2,1)S(1)}, u32[]{:S(2)}, u32[]{:S(2)}) collective-permute-start(bf16[32,1536]{1,0:T(8,128)(2,1)S(1)} %add_convert_fusion.refs_0_), channel_id=1, source_target_pairs={{0,6},{1,7},{2,4},{3,5},{4,2},{5,3},{6,0},{7,1},{8,14},{9,15},{10,... | collective-permute-start | bytes 294920 | tf_op jit(solution)/shard_map/ppermute | solution.py:500
  63.7 8.4 %collective-permute-start.17 = (bf16[32,1536]{1,0:T(8,128)(2,1)S(1)}, bf16[32,1536]{1,0:T(8,128)(2,1)S(1)}, u32[]{:S(2)}, u32[]{:S(2)}) collective-permute-start(bf16[32,1536]{1,0:T(8,128)(2,1)S(1)} %add_convert_fusion.refs_0_), channel_id=1, source_target_pairs={{0,4},{1,5},{2,6},{3,7},{4,0},{5,1},{6,2},{7,3},{8,12},{9,13},{10,... | collective-permute-start | bytes 294920 | tf_op jit(solution)/shard_map/ppermute | solution.py:500
  63.9 8.3 %collective-permute-start.16 = (bf16[32,1536]{1,0:T(8,128)(2,1)S(1)}, bf16[32,1536]{1,0:T(8,128)(2,1)S(1)}, u32[]{:S(2)}, u32[]{:S(2)}) collective-permute-start(bf16[32,1536]{1,0:T(8,128)(2,1)S(1)} %add_convert_fusion.refs_0_), channel_id=1, source_target_pairs={{0,2},{1,3},{2,0},{3,1},{4,6},{5,7},{6,4},{7,5},{8,10},{9,11},{10,... | collective-permute-start | bytes 294920 | tf_op jit(solution)/shard_map/ppermute | solution.py:500
  72.2 1.8 %collective-permute-start.22 = (bf16[4,32,1536]{2,1,0:T(8,128)(2,1)S(1)}, bf16[4,32,1536]{2,1,0:T(8,128)(2,1)S(1)}, u32[]{:S(2)}, u32[]{:S(2)}) collective-permute-start(bf16[4,32,1536]{2,1,0:T(8,128)(2,1)S(1)} %pad_maximum_fusion), channel_id=1, source_target_pairs={{0,1},{1,0},{2,3},{3,2},{4,5},{5,4},{6,7},{7,6},{8,9},{9,8},{10,11... | collective-permute-start | bytes 1179656 | tf_op jit(solution)/shard_map/ppermute | solution.py:500
  (6 other events, 84.7 us)

commit v9 on v7

--- a/solution.py
+++ b/solution.py
@@ -537,7 +537,7 @@
     own_streams, other_streams = order_streams(signal, skip_cot, res_cot)
     tap, mine, own_streams, other_streams = lax.optimization_barrier((tap, mine, own_streams, other_streams))
     other = [swapped(piece, "tm", 1) for piece in mine]
-    taps = [tap] + [swapped(tap, "section", by) for by in range(1, sections)]
+    taps = [tap] + [swapped(tap, "section", by) for by in reversed(range(1, sections))][::-1]
 
     pieces = [w_now, w_res, w_skip, w_tap, *mine, *other]
     own_skip, own_base, back, weights, *kept_own = layer_stack(own_streams, taps[:1], number, pieces)
@@ -548,7 +548,7 @@
     own_piece, pieces = spread(got, kept, shards // 2)
     pieces, back = lax.optimization_barrier((pieces, back))
     reached = range(shards - span)
-    arrived = [between(back, shards, [(by, 0)], reached) for by in range(1, sections)]
+    arrived = [between(back, shards, [(by, 0)], reached) for by in reversed(range(1, sections))][::-1]
     grad_scale = 1.0 / math.sqrt(number * seq_rows * shards)
     skip_total, base = finish(own_skip, gated, dz, g, weights)
     input_grads = add_back(own_base, base, [back, *arrived])

time: 75.4 us -> 75.4 us (level)
  no operation moved by 1% of the time
where the time goes in v9:
time: 75.4 us; the launch traced here: 75 us
  starting transfers between devices  28.2 us (37%)
  waiting for transfers between devices  20.3 us (27%)
  Pallas kernels  19.8 us (26%)
  local copies, waits for them, and re-layouts  4.65 us (6%)
  other arithmetic  1.22 us (2%)
  between operations  0.85 us (1%)
    ppermute x18, starting transfers between devices, swapped(): lax.ppermute(x, axis, [(i, i ^ by) for i in range(lax.axis_size(axis))])  17.9 us
    ppermute x18, waiting for transfers between devices, swapped(): lax.ppermute(x, axis, [(i, i ^ by) for i in range(lax.axis_size(axis))])  17.2 us
    pallas_call x2, Pallas kernels, layer_stack(): pl.pallas_call(functools.partial(stack_kernel, layers, last), in_specs=in...  12.6 us
    pallas_call x5, Pallas kernels, local_call(): pl.pallas_call(kernel, in_specs=[near] * len(operands), out_specs=[near]...  6.94 us
    ppermute x2, starting transfers between devices, passed_along(): return lax.ppermute(x, axis, pairs)  6.41 us
    ppermute x3, starting transfers between devices, between(): lax.ppermute(x, ('section', 'tm'), [(i * shards + t, j * shards + t) for...  3.85 us
    unnamed x14, local copies, waits for them, and re-layouts  3.69 us
    ppermute x2, waiting for transfers between devices, passed_along(): return lax.ppermute(x, axis, pairs)  1.58 us
  transfers between devices with their start and end apart: 23, of which 13 were waited for; matrix products, arithmetic and copies ran while one was open for 1% of the time, Pallas kernels for 25%

profile of v9, /device:TPU:0, one launch (start us, length us, event | category | flops | bytes accessed | tf_op | source)
XLA Modules:
  0.0 75.0 jit_solution(2209240333859794584)
XLA Ops:
  1.8 3.0 %collective-permute-start.2 = (bf16[128,1536]{1,0:T(8,128)(2,1)S(1)}, bf16[128,1536]{1,0:T(8,128)(2,1)S(1)}, u32[]{:S(2)}, u32[]{:S(2)}) collective-permute-start(bf16[128,1536]{1,0:T(8,128)(2,1)S(1)} %fusion.2), channel_id=1, source_target_pairs={{0,16},{8,24},{16,0},{24,8},{1,17},{9,25},{17,1},{25,9},{2,18},{10... | collective-permute-start | bytes 1179656 | tf_op jit(solution)/shard_map/ppermute | solution.py:493
  4.8 1.5 %collective-permute-start.1 = (bf16[128,1536]{1,0:T(8,128)(2,1)S(1)}, bf16[128,1536]{1,0:T(8,128)(2,1)S(1)}, u32[]{:S(2)}, u32[]{:S(2)}) collective-permute-start(bf16[128,1536]{1,0:T(8,128)(2,1)S(1)} %fusion.2), channel_id=1, source_target_pairs={{0,8},{8,0},{16,24},{24,16},{1,9},{9,1},{17,25},{25,17},{2,10},{10... | collective-permute-start | bytes 1179656 | tf_op jit(solution)/shard_map/ppermute | solution.py:493
  7.4 4.9 %collective-permute-start = (bf16[512,256]{1,0:T(8,128)(2,1)S(1)}, bf16[512,256]{1,0:T(8,128)(2,1)S(1)}, u32[]{:S(2)}, u32[]{:S(2)}) collective-permute-start(bf16[512,256]{1,0:T(8,128)(2,1)S(1)} %dynamic-slice_bitcast_fusion), channel_id=1, source_target_pairs={{0,4},{1,5},{2,6},{3,7},{8,12},{9,13},{10,14},{11,15},{16,20},{17,... | collective-permute-start | bytes 786440 | tf_op jit(solution)/shard_map/ppermute | solution.py:18
  13.5 1.2 %copy-done.1 = bf16[4,512,256]{2,1,0:T(8,128)(2,1)S(1)} copy-done((bf16[4,512,256]{2,1,0:T(8,128)(2,1)S(1)}, bf16[4,512,256]{2,1,0:T(8,128)(2,1)}, u32[]{:S(2)}) %copy-start.1) | copy-done | bytes 1048600
  17.0 6.6 %collective-permute-done.3.refs_10_ = bf16[128,1536]{1,0:T(8,128)(2,1)S(1)} collective-permute-done((bf16[128,1536]{1,0:T(8,128)(2,1)S(1)}, bf16[128,1536]{1,0:T(8,128)(2,1)S(1)}, u32[]{:S(2)}, u32[]{:S(2)}) %collective-permute-start.3) | collective-permute-done | bytes 393248 | tf_op jit(solution)/shard_map/ppermute | solution.py:493
  24.2 2.6 %collective-permute-start.9 = (bf16[512,256]{1,0:T(8,128)(2,1)S(1)}, bf16[512,256]{1,0:T(8,128)(2,1)S(1)}, u32[]{:S(2)}, u32[]{:S(2)}) collective-permute-start(bf16[512,256]{1,0:T(8,128)(2,1)S(1)} %collective-permute-done.refs_3_), channel_id=1, source_target_pairs={{0,24},{8,16},{16,8},{24,0},{1,25},{9,17},{17,9},{25,1},{2,26},{10... | collective-permute-start | bytes 786440 | tf_op jit(solution)/shard_map/ppermute | solution.py:493
  27.7 5.5 %layer_stack.2 = (bf16[512,256]{1,0:T(8,128)(2,1)S(1)}, bf16[512,256]{1,0:T(8,128)(2,1)S(1)}, bf16[512,256]{1,0:T(8,128)(2,1)S(1)}, bf16[4,256,1536]{2,1,0:T(8,1...) custom-call(bf16[1,512,256]{2,1,0:T(8,128)(2,1)S(1)} %get-tuple-elem, ...), custom_call_target="tpu_custom_call" | custom-call | flops 5905580032 | bytes 2097152 | tf_op jit(solution)/shard_map/layer_stack/pallas_call | solution.py:386
  33.2 1.5 %collective-permute-start.12 = (bf16[512,256]{1,0:T(8,128)(2,1)S(1)}, bf16[512,256]{1,0:T(8,128)(2,1)S(1)}, u32[]{:S(2)}, u32[]{:S(2)}) collective-permute-start(bf16[512,256]{1,0:T(8,128)(2,1)S(1)} %get-tuple-element.94), channel_id=1, source_target_pairs={{4,0},{5,1},{6,2},{7,3},{12,8},{13,9},{14,10},{15,11},{20,16},{21,... | collective-permute-start | bytes 786440 | tf_op jit(solution)/shard_map/ppermute | solution.py:18
  34.7 2.1 %ahead.1 = (f32[256,1536]{1,0:T(8,128)S(1)}, f32[3,512,512]{2,1,0:T(8,128)S(1)}, f32[4,3,512,256]{3,2,1,0:T(8,128)S(1)}) custom-call(bf16[1,512,256]{2,1,0:T(8,128)(2,1)S(1)} %bitcast.15, bf16[1,512,256]{2,1,0:T(8,128)(2,1)S(1)} %get-tuple-element.65.refs_1_.cot, bf16[4,1,512,256]{3,2,1,0:T(8,128)(2,1)S(1)} %get-tuple-element.76.h_all, ...), custom_call_target="tpu_custom_call" | custom-call | tf_op jit(solution)/shard_map/ahead/pallas_call | solution.py:481
  36.7 2.7 %collective-permute-done.8.refs_4_ = bf16[512,256]{1,0:T(8,128)(2,1)S(1)} collective-permute-done((bf16[512,256]{1,0:T(8,128)(2,1)S(1)}, bf16[512,256]{1,0:T(8,128)(2,1)S(1)}, u32[]{:S(2)}, u32[]{:S(2)}) %collective-permute-start.8) | collective-permute-done | bytes 262176 | tf_op jit(solution)/shard_map/ppermute | solution.py:493
  39.6 7.1 %layer_stack.3 = (bf16[4,3,512,256]{3,2,1,0:T(8,128)(2,1)S(1)}, bf16[4,3,512,512]{3,2,1,0:T(8,128)(2,1)S(1)}, bf16[5,3,512,256]{3,2,1,0:T(8,128)(2,1)S(1)}, bf16...) custom-call(bf16[3,512,256]{2,1,0:T(8,128)(2,1)S(1)} %get-tuple-element.72.next_signal.refs_0_, ...), custom_call_target="tpu_custom_call" | custom-call | flops 17716740096 | bytes 6291456 | tf_op jit(solution)/shard_map/layer_stack/pallas_call | solution.py:386
  49.5 2.8 %collective-permute-start.13 = (bf16[32,1536]{1,0:T(8,128)(2,1)S(1)}, bf16[32,1536]{1,0:T(8,128)(2,1)S(1)}, u32[]{:S(2)}, u32[]{:S(2)}) collective-permute-start(bf16[32,1536]{1,0:T(8,128)(2,1)S(1)} %get-tuple-element.95), channel_id=1, source_target_pairs={{0,6},{1,7},{2,4},{3,5},{4,2},{5,3},{6,0},{7,1},{8,14},{9,15},{10,... | collective-permute-start | bytes 294920 | tf_op jit(solution)/shard_map/ppermute | solution.py:493
  52.3 1.6 %collective-permute-start.15 = (bf16[32,1536]{1,0:T(8,128)(2,1)S(1)}, bf16[32,1536]{1,0:T(8,128)(2,1)S(1)}, u32[]{:S(2)}, u32[]{:S(2)}) collective-permute-start(bf16[32,1536]{1,0:T(8,128)(2,1)S(1)} %get-tuple-element.97), channel_id=1, source_target_pairs={{0,2},{1,3},{2,0},{3,1},{4,6},{5,7},{6,4},{7,5},{8,10},{9,11},{10,... | collective-permute-start | bytes 294920 | tf_op jit(solution)/shard_map/ppermute | solution.py:493
  53.9 1.3 %collective-permute-start.21 = (bf16[512,256]{1,0:T(8,128)(2,1)S(1)}, bf16[512,256]{1,0:T(8,128)(2,1)S(1)}, u32[]{:S(2)}, u32[]{:S(2)}) collective-permute-start(bf16[512,256]{1,0:T(8,128)(2,1)S(1)} %collective-permute-done.12.refs_0_), channel_id=1, source_target_pairs={{24,0},{25,1},{26,2},{27,3}} | collective-permute-start | bytes 786440 | tf_op jit(solution)/shard_map/ppermute | solution.py:497
  55.2 1.3 %collective-permute-start.20 = (bf16[512,256]{1,0:T(8,128)(2,1)S(1)}, bf16[512,256]{1,0:T(8,128)(2,1)S(1)}, u32[]{:S(2)}, u32[]{:S(2)}) collective-permute-start(bf16[512,256]{1,0:T(8,128)(2,1)S(1)} %collective-permute-done.12.refs_0_), channel_id=1, source_target_pairs={{16,0},{17,1},{18,2},{19,3}} | collective-permute-start | bytes 786440 | tf_op jit(solution)/shard_map/ppermute | solution.py:497
  57.0 1.3 %collective-permute-start.19 = (bf16[512,256]{1,0:T(8,128)(2,1)S(1)}, bf16[512,256]{1,0:T(8,128)(2,1)S(1)}, u32[]{:S(2)}, u32[]{:S(2)}) collective-permute-start(bf16[512,256]{1,0:T(8,128)(2,1)S(1)} %collective-permute-done.12.refs_0_), channel_id=1, source_target_pairs={{8,0},{9,1},{10,2},{11,3}} | collective-permute-start | bytes 786440 | tf_op jit(solution)/shard_map/ppermute | solution.py:497
  58.3 2.7 %collective-permute-done.14 = bf16[32,1536]{1,0:T(8,128)(2,1)S(1)} collective-permute-done((bf16[32,1536]{1,0:T(8,128)(2,1)S(1)}, bf16[32,1536]{1,0:T(8,128)(2,1)S(1)}, u32[]{:S(2)}, u32[]{:S(2)}) %collective-permute-start.14) | collective-permute-done | bytes 98336 | tf_op jit(solution)/shard_map/ppermute | solution.py:493
  61.0 2.5 %collective-permute-start.18 = (bf16[32,1536]{1,0:T(8,128)(2,1)S(1)}, bf16[32,1536]{1,0:T(8,128)(2,1)S(1)}, u32[]{:S(2)}, u32[]{:S(2)}) collective-permute-start(bf16[32,1536]{1,0:T(8,128)(2,1)S(1)} %add_convert_fusion.refs_0_), channel_id=1, source_target_pairs={{0,6},{1,7},{2,4},{3,5},{4,2},{5,3},{6,0},{7,1},{8,14},{9,15},{10,... | collective-permute-start | bytes 294920 | tf_op jit(solution)/shard_map/ppermute | solution.py:493
  63.7 1.8 %collective-permute-start.16 = (bf16[32,1536]{1,0:T(8,128)(2,1)S(1)}, bf16[32,1536]{1,0:T(8,128)(2,1)S(1)}, u32[]{:S(2)}, u32[]{:S(2)}) collective-permute-start(bf16[32,1536]{1,0:T(8,128)(2,1)S(1)} %add_convert_fusion.refs_0_), channel_id=1, source_target_pairs={{0,2},{1,3},{2,0},{3,1},{4,6},{5,7},{6,4},{7,5},{8,10},{9,11},{10,... | collective-permute-start | bytes 294920 | tf_op jit(solution)/shard_map/ppermute | solution.py:493
  65.4 2.4 %finish.1 = (bf16[4,512,256]{2,1,0:T(8,128)(2,1)}, f32[3,512,256]{2,1,0:T(8,128)S(1)}) custom-call(bf16[512,256]{1,0:T(8,128)(2,1)S(1)} %get-tuple-element.71.own_skip, bf16[4,3,512,256]{3,2,1,0:T(8,128)(2,1)S(1)} %get-tuple-element.83.gated_all, bf16[4,3,512,512]{3,2,1,0:T(8,128)(2,1)S(1)} %get-tuple-element.84.dz_all, ...), custom_call_target="tpu_custom_call" | custom-call | tf_op jit(solution)/shard_map/finish/pallas_call | solution.py:481
  67.8 1.4 %collective-permute-done.20.refs_2_ = bf16[512,256]{1,0:T(8,128)(2,1)S(1)} collective-permute-done((bf16[512,256]{1,0:T(8,128)(2,1)S(1)}, bf16[512,256]{1,0:T(8,128)(2,1)S(1)}, u32[]{:S(2)}, u32[]{:S(2)}) %collective-permute-start.20) | collective-permute-done | bytes 262176 | tf_op jit(solution)/shard_map/ppermute | solution.py:497
  70.4 1.6 %collective-permute-done.17.refs_2_ = bf16[32,1536]{1,0:T(8,128)(2,1)S(1)} collective-permute-done((bf16[32,1536]{1,0:T(8,128)(2,1)S(1)}, bf16[32,1536]{1,0:T(8,128)(2,1)S(1)}, u32[]{:S(2)}, u32[]{:S(2)}) %collective-permute-start.17) | collective-permute-done | bytes 98336 | tf_op jit(solution)/shard_map/ppermute | solution.py:493
  72.1 1.7 %collective-permute-done.22.refs_4_ = bf16[4,32,1536]{2,1,0:T(8,128)(2,1)S(1)} collective-permute-done((bf16[4,32,1536]{2,1,0:T(8,128)(2,1)S(1)}, bf16[4,32,1536]{2,1,0:T(8,128)(2,1)S(1)}, u32[]{:S(2)}, u32[]{:S(2)}) %collective-permute-start.22) | collective-permute-done | bytes 393248 | tf_op jit(solution)/shard_map/ppermute | solution.py:493
  73.8 1.3 %place_sums.1 = (f32[1,256,512]{2,1,0:T(8,128)}, f32[1,256,512]{2,1,0:T(8,128)}, f32[1,256,256]{2,1,0:T(8,128)}, f32[1,256,256]{2,1,0:T(8,128)}) custom-call(bf16[32,1536]{1,0:T(8,128)(2,1)S(1)} %add_convert_fusion.refs_0_, bf16[32,1536]{1,0:T(8,128)(2,1)S(1)} %collective-permute-done.16.refs_1_, bf16[32,1536]{1,0:T(8,128)(2,1)S(1)} %collective-permute-done.17.refs_2_, ...), custom_call_target="tpu_custom_call" | custom-call | tf_op jit(solution)/shard_map/place_sums/pallas_call | solution.py:481
  (48 shorter events, 12.1 us)
Async XLA Ops:
  0.6 27.0 %copy-start.4 = (bf16[1,256,512]{2,1,0:T(8,128)(2,1)S(1)}, bf16[1,256,512]{2,1,0:T(8,128)(2,1)}, u32[]{:S(2)}) copy-start(bf16[1,256,512]{2,1,0:T(8,128)(2,1)} %refs_7_.1) | copy-start | bytes 786436
  1.8 15.2 %collective-permute-start.2 = (bf16[128,1536]{1,0:T(8,128)(2,1)S(1)}, bf16[128,1536]{1,0:T(8,128)(2,1)S(1)}, u32[]{:S(2)}, u32[]{:S(2)}) collective-permute-start(bf16[128,1536]{1,0:T(8,128)(2,1)S(1)} %fusion.2), channel_id=1, source_target_pairs={{0,16},{8,24},{16,0},{24,8},{1,17},{9,25},{17,1},{25,9},{2,18},{10... | collective-permute-start | bytes 1179656 | tf_op jit(solution)/shard_map/ppermute | solution.py:493
  4.8 12.2 %collective-permute-start.1 = (bf16[128,1536]{1,0:T(8,128)(2,1)S(1)}, bf16[128,1536]{1,0:T(8,128)(2,1)S(1)}, u32[]{:S(2)}, u32[]{:S(2)}) collective-permute-start(bf16[128,1536]{1,0:T(8,128)(2,1)S(1)} %fusion.2), channel_id=1, source_target_pairs={{0,8},{8,0},{16,24},{24,16},{1,9},{9,1},{17,25},{25,17},{2,10},{10... | collective-permute-start | bytes 1179656 | tf_op jit(solution)/shard_map/ppermute | solution.py:493
  6.3 17.3 %collective-permute-start.3 = (bf16[128,1536]{1,0:T(8,128)(2,1)S(1)}, bf16[128,1536]{1,0:T(8,128)(2,1)S(1)}, u32[]{:S(2)}, u32[]{:S(2)}) collective-permute-start(bf16[128,1536]{1,0:T(8,128)(2,1)S(1)} %fusion.2), channel_id=1, source_target_pairs={{0,24},{8,16},{16,8},{24,0},{1,25},{9,17},{17,9},{25,1},{2,26},{10... | collective-permute-start | bytes 1179656 | tf_op jit(solution)/shard_map/ppermute | solution.py:493
  7.4 9.7 %collective-permute-start = (bf16[512,256]{1,0:T(8,128)(2,1)S(1)}, bf16[512,256]{1,0:T(8,128)(2,1)S(1)}, u32[]{:S(2)}, u32[]{:S(2)}) collective-permute-start(bf16[512,256]{1,0:T(8,128)(2,1)S(1)} %dynamic-slice_bitcast_fusion), channel_id=1, source_target_pairs={{0,4},{1,5},{2,6},{3,7},{8,12},{9,13},{10,14},{11,15},{16,20},{17,... | collective-permute-start | bytes 786440 | tf_op jit(solution)/shard_map/ppermute | solution.py:18
  23.6 3.6 %collective-permute-start.4 = (bf16[128,1536]{1,0:T(8,128)(2,1)S(1)}, bf16[128,1536]{1,0:T(8,128)(2,1)S(1)}, u32[]{:S(2)}, u32[]{:S(2)}) collective-permute-start(bf16[128,1536]{1,0:T(8,128)(2,1)S(1)} %collective-permute-done.1.refs_8_), channel_id=1, source_target_pairs={{0,1},{1,0},{2,3},{3,2},{4,5},{5,4},{6,7},{7,6},{8,9},{9,8},{10,11... | collective-permute-start | bytes 1179656 | tf_op jit(solution)/shard_map/ppermute | solution.py:493
  23.6 4.0 %collective-permute-start.5 = (bf16[128,1536]{1,0:T(8,128)(2,1)S(1)}, bf16[128,1536]{1,0:T(8,128)(2,1)S(1)}, u32[]{:S(2)}, u32[]{:S(2)}) collective-permute-start(bf16[128,1536]{1,0:T(8,128)(2,1)S(1)} %collective-permute-done.2.refs_9_), channel_id=1, source_target_pairs={{0,1},{1,0},{2,3},{3,2},{4,5},{5,4},{6,7},{7,6},{8,9},{9,8},{10,11... | collective-permute-start | bytes 1179656 | tf_op jit(solution)/shard_map/ppermute | solution.py:493
  24.2 3.5 %collective-permute-start.6 = (bf16[128,1536]{1,0:T(8,128)(2,1)S(1)}, bf16[128,1536]{1,0:T(8,128)(2,1)S(1)}, u32[]{:S(2)}, u32[]{:S(2)}) collective-permute-start(bf16[128,1536]{1,0:T(8,128)(2,1)S(1)} %collective-permute-done.3.refs_10_), channel_id=1, source_target_pairs={{0,1},{1,0},{2,3},{3,2},{4,5},{5,4},{6,7},{7,6},{8,9},{9,8},{10,11... | collective-permute-start | bytes 1179656 | tf_op jit(solution)/shard_map/ppermute | solution.py:493
  24.2 12.6 %collective-permute-start.9 = (bf16[512,256]{1,0:T(8,128)(2,1)S(1)}, bf16[512,256]{1,0:T(8,128)(2,1)S(1)}, u32[]{:S(2)}, u32[]{:S(2)}) collective-permute-start(bf16[512,256]{1,0:T(8,128)(2,1)S(1)} %collective-permute-done.refs_3_), channel_id=1, source_target_pairs={{0,24},{8,16},{16,8},{24,0},{1,25},{9,17},{17,9},{25,1},{2,26},{10... | collective-permute-start | bytes 786440 | tf_op jit(solution)/shard_map/ppermute | solution.py:493
  26.8 12.6 %collective-permute-start.8 = (bf16[512,256]{1,0:T(8,128)(2,1)S(1)}, bf16[512,256]{1,0:T(8,128)(2,1)S(1)}, u32[]{:S(2)}, u32[]{:S(2)}) collective-permute-start(bf16[512,256]{1,0:T(8,128)(2,1)S(1)} %collective-permute-done.refs_3_), channel_id=1, source_target_pairs={{0,16},{8,24},{16,0},{24,8},{1,17},{9,25},{17,1},{25,9},{2,18},{10... | collective-permute-start | bytes 786440 | tf_op jit(solution)/shard_map/ppermute | solution.py:493
  27.3 12.4 %collective-permute-start.7 = (bf16[512,256]{1,0:T(8,128)(2,1)S(1)}, bf16[512,256]{1,0:T(8,128)(2,1)S(1)}, u32[]{:S(2)}, u32[]{:S(2)}) collective-permute-start(bf16[512,256]{1,0:T(8,128)(2,1)S(1)} %collective-permute-done.refs_3_), channel_id=1, source_target_pairs={{0,8},{8,0},{16,24},{24,16},{1,9},{9,1},{17,25},{25,17},{2,10},{10... | collective-permute-start | bytes 786440 | tf_op jit(solution)/shard_map/ppermute | solution.py:493
  33.2 16.3 %collective-permute-start.12 = (bf16[512,256]{1,0:T(8,128)(2,1)S(1)}, bf16[512,256]{1,0:T(8,128)(2,1)S(1)}, u32[]{:S(2)}, u32[]{:S(2)}) collective-permute-start(bf16[512,256]{1,0:T(8,128)(2,1)S(1)} %get-tuple-element.94), channel_id=1, source_target_pairs={{4,0},{5,1},{6,2},{7,3},{12,8},{13,9},{14,10},{15,11},{20,16},{21,... | collective-permute-start | bytes 786440 | tf_op jit(solution)/shard_map/ppermute | solution.py:18
  46.7 1.5 %collective-permute-start.10 = (bf16[64,1536]{1,0:T(8,128)(2,1)S(1)}, bf16[64,1536]{1,0:T(8,128)(2,1)S(1)}, u32[]{:S(2)}, u32[]{:S(2)}) collective-permute-start(bf16[64,1536]{1,0:T(8,128)(2,1)S(1)} %get-tuple-element.88), channel_id=1, source_target_pairs={{0,1},{1,0},{2,3},{3,2},{4,5},{5,4},{6,7},{7,6},{8,9},{9,8},{10,11... | collective-permute-start | bytes 589832 | tf_op jit(solution)/shard_map/ppermute | solution.py:493
  46.8 1.7 %collective-permute-start.11 = (bf16[64,1536]{1,0:T(8,128)(2,1)S(1)}, bf16[64,1536]{1,0:T(8,128)(2,1)S(1)}, u32[]{:S(2)}, u32[]{:S(2)}) collective-permute-start(bf16[64,1536]{1,0:T(8,128)(2,1)S(1)} %get-tuple-element.89), channel_id=1, source_target_pairs={{0,1},{1,0},{2,3},{3,2},{4,5},{5,4},{6,7},{7,6},{8,9},{9,8},{10,11... | collective-permute-start | bytes 589832 | tf_op jit(solution)/shard_map/ppermute | solution.py:493
  49.5 7.5 %collective-permute-start.13 = (bf16[32,1536]{1,0:T(8,128)(2,1)S(1)}, bf16[32,1536]{1,0:T(8,128)(2,1)S(1)}, u32[]{:S(2)}, u32[]{:S(2)}) collective-permute-start(bf16[32,1536]{1,0:T(8,128)(2,1)S(1)} %get-tuple-element.95), channel_id=1, source_target_pairs={{0,6},{1,7},{2,4},{3,5},{4,2},{5,3},{6,0},{7,1},{8,14},{9,15},{10,... | collective-permute-start | bytes 294920 | tf_op jit(solution)/shard_map/ppermute | solution.py:493
  52.3 8.7 %collective-permute-start.14 = (bf16[32,1536]{1,0:T(8,128)(2,1)S(1)}, bf16[32,1536]{1,0:T(8,128)(2,1)S(1)}, u32[]{:S(2)}, u32[]{:S(2)}) collective-permute-start(bf16[32,1536]{1,0:T(8,128)(2,1)S(1)} %get-tuple-element.96), channel_id=1, source_target_pairs={{0,4},{1,5},{2,6},{3,7},{4,0},{5,1},{6,2},{7,3},{8,12},{9,13},{10,... | collective-permute-start | bytes 294920 | tf_op jit(solution)/shard_map/ppermute | solution.py:493
  52.3 8.7 %collective-permute-start.15 = (bf16[32,1536]{1,0:T(8,128)(2,1)S(1)}, bf16[32,1536]{1,0:T(8,128)(2,1)S(1)}, u32[]{:S(2)}, u32[]{:S(2)}) collective-permute-start(bf16[32,1536]{1,0:T(8,128)(2,1)S(1)} %get-tuple-element.97), channel_id=1, source_target_pairs={{0,2},{1,3},{2,0},{3,1},{4,6},{5,7},{6,4},{7,5},{8,10},{9,11},{10,... | collective-permute-start | bytes 294920 | tf_op jit(solution)/shard_map/ppermute | solution.py:493
  53.9 9.8 %collective-permute-start.21 = (bf16[512,256]{1,0:T(8,128)(2,1)S(1)}, bf16[512,256]{1,0:T(8,128)(2,1)S(1)}, u32[]{:S(2)}, u32[]{:S(2)}) collective-permute-start(bf16[512,256]{1,0:T(8,128)(2,1)S(1)} %collective-permute-done.12.refs_0_), channel_id=1, source_target_pairs={{24,0},{25,1},{26,2},{27,3}} | collective-permute-start | bytes 786440 | tf_op jit(solution)/shard_map/ppermute | solution.py:497
  55.2 14.0 %collective-permute-start.20 = (bf16[512,256]{1,0:T(8,128)(2,1)S(1)}, bf16[512,256]{1,0:T(8,128)(2,1)S(1)}, u32[]{:S(2)}, u32[]{:S(2)}) collective-permute-start(bf16[512,256]{1,0:T(8,128)(2,1)S(1)} %collective-permute-done.12.refs_0_), channel_id=1, source_target_pairs={{16,0},{17,1},{18,2},{19,3}} | collective-permute-start | bytes 786440 | tf_op jit(solution)/shard_map/ppermute | solution.py:497
  57.0 12.2 %collective-permute-start.19 = (bf16[512,256]{1,0:T(8,128)(2,1)S(1)}, bf16[512,256]{1,0:T(8,128)(2,1)S(1)}, u32[]{:S(2)}, u32[]{:S(2)}) collective-permute-start(bf16[512,256]{1,0:T(8,128)(2,1)S(1)} %collective-permute-done.12.refs_0_), channel_id=1, source_target_pairs={{8,0},{9,1},{10,2},{11,3}} | collective-permute-start | bytes 786440 | tf_op jit(solution)/shard_map/ppermute | solution.py:497
  61.0 9.4 %collective-permute-start.18 = (bf16[32,1536]{1,0:T(8,128)(2,1)S(1)}, bf16[32,1536]{1,0:T(8,128)(2,1)S(1)}, u32[]{:S(2)}, u32[]{:S(2)}) collective-permute-start(bf16[32,1536]{1,0:T(8,128)(2,1)S(1)} %add_convert_fusion.refs_0_), channel_id=1, source_target_pairs={{0,6},{1,7},{2,4},{3,5},{4,2},{5,3},{6,0},{7,1},{8,14},{9,15},{10,... | collective-permute-start | bytes 294920 | tf_op jit(solution)/shard_map/ppermute | solution.py:493
  63.5 8.4 %collective-permute-start.17 = (bf16[32,1536]{1,0:T(8,128)(2,1)S(1)}, bf16[32,1536]{1,0:T(8,128)(2,1)S(1)}, u32[]{:S(2)}, u32[]{:S(2)}) collective-permute-start(bf16[32,1536]{1,0:T(8,128)(2,1)S(1)} %add_convert_fusion.refs_0_), channel_id=1, source_target_pairs={{0,4},{1,5},{2,6},{3,7},{4,0},{5,1},{6,2},{7,3},{8,12},{9,13},{10,... | collective-permute-start | bytes 294920 | tf_op jit(solution)/shard_map/ppermute | solution.py:493
  63.7 8.3 %collective-permute-start.16 = (bf16[32,1536]{1,0:T(8,128)(2,1)S(1)}, bf16[32,1536]{1,0:T(8,128)(2,1)S(1)}, u32[]{:S(2)}, u32[]{:S(2)}) collective-permute-start(bf16[32,1536]{1,0:T(8,128)(2,1)S(1)} %add_convert_fusion.refs_0_), channel_id=1, source_target_pairs={{0,2},{1,3},{2,0},{3,1},{4,6},{5,7},{6,4},{7,5},{8,10},{9,11},{10,... | collective-permute-start | bytes 294920 | tf_op jit(solution)/shard_map/ppermute | solution.py:493
  72.0 1.8 %collective-permute-start.22 = (bf16[4,32,1536]{2,1,0:T(8,128)(2,1)S(1)}, bf16[4,32,1536]{2,1,0:T(8,128)(2,1)S(1)}, u32[]{:S(2)}, u32[]{:S(2)}) collective-permute-start(bf16[4,32,1536]{2,1,0:T(8,128)(2,1)S(1)} %pad_maximum_fusion), channel_id=1, source_target_pairs={{0,1},{1,0},{2,3},{3,2},{4,5},{5,4},{6,7},{7,6},{8,9},{9,8},{10,11... | collective-permute-start | bytes 1179656 | tf_op jit(solution)/shard_map/ppermute | solution.py:493
  (6 other events, 84.7 us)
